TPU v7x, 32 devices: a whole 2x2x4 slice. The times are simulated.
32 devices in a mesh: groups: 2 (over y), src: 4 (over x, core), tgt: 4 (over z).
Axes of the slice: x: 2, y: 2, z: 4, core: 2. Of those that a mesh axis runs over, the one named last changes fastest.
Arguments:
- tokens: bfloat16 [8192, 1024], P(('groups', 'src', 'tgt')), parts along dimension 0, may hold values from -6 to 6
- sentence_ids: int32 [32, 256], P(('groups', 'src', 'tgt')), parts along dimension 0, may hold values from 0 to 31, never falling along the last dimension, each value on 1 to 32 neighbouring positions
- inner_weight: bfloat16 [4096, 1024], P(('src', 'tgt')), may hold values from -0.1875 to 0.1875
- outer_weight: bfloat16 [4096, 1024], P(('src', 'tgt')), may hold values from -0.09375 to 0.09375
- grid_rows: int32 [1024], P(('groups', 'src', 'tgt')), parts along dimension 0, may hold values from 0 to 511, as said below
- candidates: int32 [8, 16], P(('groups', 'src')), parts along dimension 0, may hold values from 0 to 63, as said below
- targets: bfloat16 [32768, 1024], P(('groups', 'tgt')), parts along dimension 0, may hold values from -6 to 6
Outputs:
- matched: bfloat16 [1024, 1024], P(('groups', 'src', 'tgt')), parts along dimension 0
- log_mass: float32 [1024], P(('groups', 'src', 'tgt')), parts along dimension 0
There are 2 independent parts, one for each index of `groups`. A program takes and returns all parts, laid end to end along the dimension named above; an argument that names none is the same for every part. Nothing has to cross between parts.
Inputs may be any that keep to these rules, and one draw needn't show every extreme that they name: `grid_rows`: A permutation of the 512 source rows. The sentences of the device at index d along src+tgt take exactly 8 rows of every aligned run of 128 rows, rows d * 8 to d * 8 + 7 of that run. `candidates`: row b lists 16 distinct target blocks for the source rows b * 128 to b * 128 + 127. Block g lies in grid column g // 16. A row names at most 4 blocks of one column, and exactly 4 blocks of some column.
All inputs are finite; a program needn't handle non-finite values.
Results may differ from a plain program's by a relative error of at most 0.0082.
Values may be sent and summed in bfloat16 or wider, within the bound.
No kernel may reach another device: no remote copies, remote signals or barrier semaphores. Data moves between devices by JAX's collectives and lax.ppermute only.
A program may use at most 128 MiB of HBM per device.

v0:
```python
import math

import jax
import jax.numpy as jnp
from jax import lax
from jax.sharding import PartitionSpec as P

SENT_DEV = 32
TBLK = 256
MOST = 4


SCORE_SCALE = 32.0


def unit_rows(values):
    floats = values.astype(jnp.float32)
    square = jnp.mean(floats * floats, axis=-1, keepdims=True)
    return (floats * lax.rsqrt(square + 1e-06) * (1.0 / math.sqrt(values.shape[-1]))).astype(
        jnp.bfloat16
    )


def inner_units(rows, inner):
    product = lax.dot_general(
        rows, inner, (((1,), (1,)), ((), ())), preferred_element_type=jnp.float32
    )
    return jax.nn.gelu(product, approximate=False).astype(jnp.bfloat16)


def layer_norm(summed):
    center = jnp.mean(summed, axis=-1, keepdims=True)
    spread = jnp.mean((summed - center) * (summed - center), axis=-1, keepdims=True)
    return (summed - center) * lax.rsqrt(spread + 1e-05)


def on_device(tokens, sentence_ids, inner_weight, outer_weight, grid_rows, candidates, targets):
    features = tokens.shape[1]
    projected = jnp.dot(
        inner_units(tokens, lax.all_gather(inner_weight, ("src", "tgt"), axis=0, tiled=True)),
        lax.all_gather(outer_weight, ("src", "tgt"), axis=0, tiled=True),
        preferred_element_type=jnp.float32,
    )
    normed = layer_norm(tokens.astype(jnp.float32) + projected)
    members = (sentence_ids[0][None, :] == jnp.arange(SENT_DEV, dtype=jnp.int32)[:, None]).astype(
        jnp.float32
    )
    sums = jnp.dot(members, normed, precision=lax.Precision.HIGHEST)
    unit = unit_rows(sums / jnp.sum(members, axis=1, keepdims=True))
    src_count = lax.axis_size("src")
    tgt_count = lax.axis_size("tgt")
    per_block = SENT_DEV // src_count
    block_rows = tgt_count * SENT_DEV
    order_key = grid_rows // block_rows * per_block + grid_rows % per_block
    reorder = (order_key[None, :] == jnp.arange(SENT_DEV, dtype=jnp.int32)[:, None]).astype(
        jnp.bfloat16
    )
    sorted_units = jnp.dot(reorder, unit, preferred_element_type=jnp.float32).astype(jnp.bfloat16)
    relayed = lax.all_to_all(
        sorted_units.reshape(src_count, per_block, features),
        "src",
        split_axis=0,
        concat_axis=0,
        tiled=True,
    )
    block = lax.all_gather(relayed, "tgt", axis=1, tiled=True).reshape(block_rows, features)
    column_index = lax.axis_index("tgt")
    column_blocks = targets.shape[0] // TBLK
    cand_row = candidates[0]
    listed = (cand_row // column_blocks == column_index).astype(jnp.int32)
    ranks = jnp.cumsum(listed) - 1
    chosen = (
        (listed[None, :] == 1) & (ranks[None, :] == jnp.arange(MOST, dtype=jnp.int32)[:, None])
    ).astype(jnp.int32)
    slot_block = jnp.sum(chosen * (cand_row % column_blocks)[None, :], axis=1)
    valid = jnp.sum(chosen, axis=1).astype(jnp.float32)
    tiles = targets.reshape(column_blocks, TBLK, features)[slot_block]
    target_units = unit_rows(tiles).reshape(MOST * TBLK, features)
    scores = lax.dot_general(
        block, target_units, (((1,), (1,)), ((), ())), preferred_element_type=jnp.float32
    )
    column_valid = jnp.repeat(valid, TBLK)
    expo = jnp.exp(SCORE_SCALE * scores) * column_valid[None, :]
    row_part = jnp.sum(expo, axis=1)
    column_part = jnp.sum(expo, axis=0).reshape(MOST, TBLK)
    picker = (slot_block[:, None] == jnp.arange(column_blocks, dtype=jnp.int32)[None, :]).astype(
        jnp.float32
    )
    column_local = jnp.dot(
        (picker * valid[:, None]).T, column_part, precision=lax.Precision.HIGHEST
    )
    column_total = lax.psum(column_local, "src")
    picked = jnp.dot(picker, column_total, precision=lax.Precision.HIGHEST)
    divisor = jnp.where(valid[:, None] > 0, picked, 1.0).reshape(-1)
    mutual = expo * (expo / divisor[None, :])
    numer = jnp.dot(mutual.astype(jnp.bfloat16), target_units, preferred_element_type=jnp.float32)
    mass_part = jnp.sum(mutual, axis=1)
    row_total = lax.psum(row_part, "tgt")
    numer_rows, mass_rows = (
        lax.psum_scatter(numer, "tgt", scatter_dimension=0, tiled=True),
        lax.psum_scatter(mass_part, "tgt", scatter_dimension=0, tiled=True),
    )
    total_rows = lax.dynamic_slice_in_dim(row_total, column_index * SENT_DEV, SENT_DEV)
    square = jnp.mean(numer_rows * numer_rows, axis=-1, keepdims=True)
    matched = (numer_rows * lax.rsqrt(square + 1e-06)).astype(jnp.bfloat16)
    log_mass = jnp.log(mass_rows / total_rows)
    return (matched, log_mass)


def solution(mesh):
    in_specs = (
        P(("groups", "src", "tgt"), None),
        P(("groups", "src", "tgt"), None),
        P(("src", "tgt"), None),
        P(("src", "tgt"), None),
        P(("groups", "src", "tgt")),
        P(("groups", "src"), None),
        P(("groups", "tgt"), None),
    )
    out_specs = (P(("groups", "src", "tgt"), None), P(("groups", "src", "tgt")))
    return jax.shard_map(
        on_device, mesh=mesh, in_specs=in_specs, out_specs=out_specs, check_vma=False
    )
```

profile of v0, /device:TPU:0, one launch (start us, length us, event | category | flops | bytes accessed | tf_op | source)
XLA Modules:
  0.0 248.9 jit_solution(11889805772872076275)
XLA Ops:
  7.2 0.0 copy-start.1
  7.2 0.0 copy-start.2
  7.2 0.0 all-gather.3.cloned.1.call-start
  7.2 0.7 all-gather.3.cloned.1.call-update
  7.9 0.0 all-gather.5.cloned.1.call-start
  8.0 0.7 all-gather.5.cloned.1.call-update
  8.7 0.7 compare_bitcast_fusion
  9.3 0.1 copy.12
  9.5 0.1 add_reduce_fusion
  9.6 0.7 fusion.70
  10.2 0.1 convert_reduce_fusion.1
  10.4 4.1 %gather_fusion = bf16[4,256,1024]{2,1,0:T(8,128)(2,1)S(1)} fusion(bf16[16,256,1024]{2,1,0:T(8,128)(2,1)} %bitcast.41, s32[1024]{0:T(1024)S(1)} %pad_clamp_fusion), kind=kCustom, calls=%fused_computation | custom fusion | bytes 4194320 | tf_op jit(solution)/shard_map/gather | solution.py:77
  14.5 0.5 multiply_reduce_fusion
  15.0 0.0 copy-done.1
  15.0 0.1 convert_reduce_fusion
  15.1 0.0 copy-done.2
  15.2 0.1 broadcast_bitcast_fusion
  15.2 1.8 multiply_convert_fusion
  17.1 1.9 fusion.4
  19.0 0.0 copy-start
  19.0 68.9 %all-gather.3.cloned.1.call-done = bf16[4096,1024]{1,0:T(8,128)(2,1)} async-done(((bf16[256,1024]{1,0:T(8,128)(2,1)}), bf16[4096,1024]{1,0:T(8,128)(2,1)}) %all-gather.3.cloned.1.call-update) | async-done | bytes 8388624 | tf_op jit(solution)/shard_map/all_gather | solution.py:40
  87.8 75.4 %all-gather.5.cloned.1.call-done = bf16[4096,1024]{1,0:T(8,128)(2,1)} async-done(((bf16[256,1024]{1,0:T(8,128)(2,1)}), bf16[4096,1024]{1,0:T(8,128)(2,1)}) %all-gather.5.cloned.1.call-update) | async-done | bytes 8388624 | tf_op jit(solution)/shard_map/all_gather | solution.py:41
  163.2 19.3 %fusion.106 = (f32[256]{0:T(256)S(1)}, f32[256,1024]{1,0:T(8,128)S(1)}) fusion(bf16[4096,1024]{1,0:T(8,128)(2,1)} %all-gather.5.cloned.1.call-done, bf16[256,1024]{1,0:T(8,128)(2,1)} %param.7, bf16[4096,1024]{1,0:T(8,128)(2,1)} %all-gather.3.cloned.1.call-done), kind=kOutput, calls=%fused_computation.157 | convolution fusion | flops 4363911168 | bytes 18351104 | tf_op jit(solution)/shard_map/dot_general | solution.py:39
  182.6 0.2 multiply_reduce_fusion.1
  182.8 0.7 multiply_reduce_fusion.3
  183.6 0.0 copy-start.3
  183.6 0.8 fusion.49
  184.4 3.3 %all-to-all-start = ((bf16[4,8,1024]{2,1,0:T(8,128)(2,1)}), bf16[4,8,1024]{2,1,0:T(8,128)(2,1)S(1)}, u32[]{:S(2)}, u32[]{:S(2)}) async-start(bf16[4,8,1024]{2,1,0:T(8,128)(2,1)} %fusion.49), calls=%async_computation | async-start | bytes 131072 | tf_op jit(solution)/shard_map/all_to_all | solution.py:59
  187.7 0.0 reduce-scatter.2.cloned.1.call-start
  187.8 4.0 %all-to-all-done = bf16[4,8,1024]{2,1,0:T(8,128)(2,1)S(1)} async-done(((bf16[4,8,1024]{2,1,0:T(8,128)(2,1)}), bf16[4,8,1024]{2,1,0:T(8,128)(2,1)S(1)}, u32[]{:S(2)}, u32[]{:S(2)}) %all-to-all-start) | async-done | bytes 65568 | tf_op jit(solution)/shard_map/all_to_all | solution.py:59
  191.8 14.2 %all_gather.11 = bf16[4,32,1024]{2,1,0:T(8,128)(2,1)S(1)} all-gather(bf16[4,8,1024]{2,1,0:T(8,128)(2,1)S(1)} %all-to-all-done), channel_id=1, replica_groups=mesh['groups'=2,'src'=4,'tgt'=4] {'tgt'}, dimensions={1}, use_global_device_ids=true | all-gather | bytes 327680 | tf_op jit(solution)/shard_map/all_gather | solution.py:66
  206.1 0.0 copy-done
  206.1 0.9 fusion.107
  207.0 0.3 fusion.62
  207.2 10.1 %psum.14 = f32[16,256]{1,0:T(8,128)S(1)} all-reduce(f32[16,256]{1,0:T(8,128)S(1)} %fusion.62), channel_id=1, replica_groups=mesh['groups'=2,'src'=4,'tgt'=4] {'src'}, use_global_device_ids=true, to_apply=%region_9.10 | all-reduce | flops 4096 | bytes 32768 | tf_op jit(solution)/shard_map/psum | solution.py:92
  217.3 0.2 fusion.50
  217.5 2.8 %fusion.55 = f32[128,1024]{1,0:T(8,128)} fusion(bf16[1024,1024]{1,0:T(8,128)(2,1)} %fusion.4, f32[128,1024]{1,0:T(8,128)S(1)} %get-tuple-element.17, f32[1024]{0:T(1024)S(1)} %bitcast.42), kind=kOutput, calls=%fused_computation.71 | convolution fusion | flops 268828672 | bytes 3149824 | tf_op jit(solution)/shard_map/dot_general | solution.py:96
  220.4 0.0 reduce-scatter.2.cloned.1.call-update
  220.4 0.0 copy-done.3
  220.4 0.6 dynamic-slice
  221.6 0.2 fusion.57
  221.8 9.8 %all-reduce.1 = (f32[128]{0:T(128)S(1)}, f32[128]{0:T(128)S(1)}) all-reduce(f32[128]{0:T(128)S(1)} %get-tuple-element.3, f32[128]{0:T(128)S(1)} %get-tuple-element.2), channel_id=1, replica_groups=mesh['groups'=2,'src'=4,'tgt'=4] {'tgt'}, use_global_device_ids=true, to_apply=%region_15.16 | all-reduce | flops 256 | bytes 2048 | tf_op jit(solution)/shard_map/psum | solution.py:98
  231.6 0.6 fusion.72
  232.2 7.6 %reduce-scatter.2.cloned.1.call-done = f32[32,1024]{1,0:T(8,128)} async-done(((f32[128,1024]{1,0:T(8,128)}), f32[32,1024]{1,0:T(8,128)}) %reduce-scatter.2.cloned.1.call-update) | async-done | bytes 131088 | tf_op jit(solution)/shard_map/reduce_scatter | solution.py:100
  239.8 1.0 multiply_reduce_fusion.2
  240.8 1.6 multiply_convert_fusion.1
  (15 shorter events, 0.1 us)
Async XLA Ops:
  7.2 7.8 %copy-start.1 = (s32[1,256]{1,0:T(1,128)S(1)}, s32[1,256]{1,0:T(1,128)}, u32[]{:S(2)}) copy-start(s32[1,256]{1,0:T(1,128)} %param.8) | copy-start | bytes 3076
  7.2 8.0 %copy-start.2 = (s32[32]{0:T(128)S(1)}, s32[32]{0:T(128)}, u32[]{:S(2)}) copy-start(s32[32]{0:T(128)} %param.11) | copy-start | bytes 388
  7.2 80.7 %all-gather.3.cloned.1.call-start = ((), (), s32[]{:S(2)}) async-start(), calls=%async_computation.2 | async-start | bytes 8912896 | tf_op jit(solution)/shard_map/all_gather | solution.py:40
  7.9 155.3 %all-gather.5.cloned.1.call-start = ((), (), s32[]{:S(2)}) async-start(), calls=%async_computation.3 | async-start | bytes 8912896 | tf_op jit(solution)/shard_map/all_gather | solution.py:41
  19.0 187.1 %copy-start = (bf16[4,256,1024]{2,1,0:T(8,128)(2,1)S(1)}, bf16[4,256,1024]{2,1,0:T(8,128)(2,1)}, u32[]{:S(2)}) copy-start(bf16[4,256,1024]{2,1,0:T(8,128)(2,1)} %multiply_convert_fusion) | copy-start | bytes 6291460
  183.6 36.8 %copy-start.3 = (u32[32]{0:T(128)S(1)}, u32[32]{0:T(128)}, u32[]{:S(2)}) copy-start(u32[32]{0:T(128)} %constant.159) | copy-start | bytes 388
  184.4 7.4 %all-to-all-start = ((bf16[4,8,1024]{2,1,0:T(8,128)(2,1)}), bf16[4,8,1024]{2,1,0:T(8,128)(2,1)S(1)}, u32[]{:S(2)}, u32[]{:S(2)}) async-start(bf16[4,8,1024]{2,1,0:T(8,128)(2,1)} %fusion.49), calls=%async_computation | async-start | bytes 131072 | tf_op jit(solution)/shard_map/all_to_all | solution.py:59
  187.7 52.0 %reduce-scatter.2.cloned.1.call-start = ((), (), s32[]{:S(2)}) async-start(), calls=%async_computation.4 | async-start | bytes 655360 | tf_op jit(solution)/shard_map/reduce_scatter | solution.py:100
Sparse Core Ops, SparseCore 0:
  10.2 77.5 all-gather.2
  90.1 73.1 all-gather.4
  220.5 19.2 reduce-scatter.1
where the time goes:
time: 249 us
  waiting for transfers between devices  157 us (63%)
  blocking collectives  34.2 us (14%)
  matrix products  25.1 us (10%)
  between operations  14.6 us (6%)
  other arithmetic  9.67 us (4%)
  local copies, waits for them, and re-layouts  4.84 us (2%)
  starting transfers between devices  3.4 us (1%)
    all_gather x1, waiting for transfers between devices, on_device(): lax.all_gather(outer_weight, ('src', 'tgt'), axis=0, tiled=True)  75.4 us
    all_gather x1, waiting for transfers between devices, on_device(): lax.all_gather(inner_weight, ('src', 'tgt'), axis=0, tiled=True)  68.9 us
    dot_general x1, matrix products, on_device(): jnp.dot(inner_units(tokens, lax.all_gather(inner_weight, ('src', 'tgt'),...  19.3 us
    all_gather x1, blocking collectives, on_device(): lax.all_gather(relayed, 'tgt', axis=1, tiled=True)  14.2 us
    psum x1, blocking collectives, on_device(): column_total = lax.psum(column_local, 'src')  10.1 us
    psum x1, blocking collectives, on_device(): row_total = lax.psum(row_part, 'tgt')  9.79 us
    reduce_scatter x1, waiting for transfers between devices, on_device(): lax.psum_scatter(numer, 'tgt', scatter_dimension=0, tiled=True)  7.57 us
  transfers between devices with their start and end apart: 4, of which 4 were waited for; matrix products, arithmetic and copies ran while one was open for 5% of the time, Pallas kernels for 0%

commit v1 on v0

v1 whole, which is shorter than its diff:
```python
import math

import jax
import jax.numpy as jnp
from jax import lax
from jax.sharding import PartitionSpec as P

SENT_DEV = 32
TBLK = 256
MOST = 4


SCORE_SCALE = 32.0


def bits_of(axis, first):
    size, bit, bits = lax.axis_size(axis), first, []
    while bit < size:
        bits.append(bit)
        bit *= 2
    return bits


def swap(values, axis, offset):
    return lax.ppermute(values, axis, [(i, i ^ offset) for i in range(lax.axis_size(axis))])


def unit_rows(values):
    floats = values.astype(jnp.float32)
    square = jnp.mean(floats * floats, axis=-1, keepdims=True)
    return (floats * lax.rsqrt(square + 1e-06) * (1.0 / math.sqrt(values.shape[-1]))).astype(
        jnp.bfloat16
    )


def inner_units(rows, inner):
    product = lax.dot_general(
        rows, inner, (((1,), (1,)), ((), ())), preferred_element_type=jnp.float32
    )
    return jax.nn.gelu(product, approximate=False).astype(jnp.bfloat16)


def layer_norm(summed):
    center = jnp.mean(summed, axis=-1, keepdims=True)
    spread = jnp.mean((summed - center) * (summed - center), axis=-1, keepdims=True)
    return (summed - center) * lax.rsqrt(spread + 1e-05)


def spread_weight(weight):
    half = weight.shape[0] // 2
    near = [weight, swap(weight, "src", 2)]
    held = [lax.dynamic_slice_in_dim(weight, lax.axis_index("groups") * half, half)]
    for axis, bit in [("tgt", b) for b in bits_of("tgt", 2)] + [("src", b) for b in bits_of("src", 4)]:
        held = held + [swap(piece, axis, bit) for piece in held]
    far = []
    for piece in held[1:]:
        over_x = swap(piece, "src", 2)
        over_y = swap(piece, "groups", 1)
        far += [
            piece,
            over_x,
            over_y,
            swap(over_x[: half // 2], "groups", 1),
            swap(over_y[half // 2 :], "src", 2),
        ]
    return jnp.concatenate(near), jnp.concatenate(far)


def feed_forward(tokens, inner_weight, outer_weight):
    rows = tokens.shape[0]
    pair = jnp.concatenate([tokens, swap(tokens, "tgt", 1)])
    shared = jnp.concatenate([pair, swap(pair, "src", 1)])
    inner_near, inner_far = spread_weight(inner_weight)
    outer_near, outer_far = spread_weight(outer_weight)
    partial = jnp.dot(
        inner_units(shared, inner_near), outer_near, preferred_element_type=jnp.float32
    ) + jnp.dot(inner_units(shared, inner_far), outer_far, preferred_element_type=jnp.float32)
    other = swap(partial[2 * rows :].astype(jnp.bfloat16), "src", 1)
    chip = partial[: 2 * rows] + other.astype(jnp.float32)
    back = swap(chip[rows:].astype(jnp.bfloat16), "tgt", 1)
    return tokens.astype(jnp.float32) + chip[:rows] + back.astype(jnp.float32)


def one_hot(keys, count):
    return keys[None, :] == jnp.arange(count, dtype=jnp.int32)[:, None]


def on_device(tokens, sentence_ids, inner_weight, outer_weight, grid_rows, candidates, targets):
    features = tokens.shape[1]
    src_count = lax.axis_size("src")
    tgt_count = lax.axis_size("tgt")
    src_index = lax.axis_index("src")
    tgt_index = lax.axis_index("tgt")
    per_block = SENT_DEV // src_count
    block_rows = tgt_count * SENT_DEV

    column_blocks = targets.shape[0] // TBLK
    cand_row = candidates[0]
    listed = (cand_row // column_blocks == tgt_index).astype(jnp.int32)
    ranks = jnp.cumsum(listed) - 1
    chosen = (
        (listed[None, :] == 1) & (ranks[None, :] == jnp.arange(MOST, dtype=jnp.int32)[:, None])
    ).astype(jnp.int32)
    slot_block = jnp.sum(chosen * (cand_row % column_blocks)[None, :], axis=1)
    valid = jnp.sum(chosen, axis=1).astype(jnp.float32)
    tiles = targets.reshape(column_blocks, TBLK, features)[slot_block]
    target_units = unit_rows(tiles).reshape(MOST * TBLK, features)

    normed = layer_norm(feed_forward(tokens, inner_weight, outer_weight))
    members = one_hot(sentence_ids[0], SENT_DEV).astype(jnp.float32)
    sums = jnp.dot(members, normed, precision=lax.Precision.HIGHEST)
    unit = unit_rows(sums / jnp.sum(members, axis=1, keepdims=True))

    order_key = (grid_rows // block_rows ^ src_index) * per_block + grid_rows % per_block
    held = jnp.dot(
        one_hot(order_key, SENT_DEV).astype(jnp.bfloat16), unit, preferred_element_type=jnp.float32
    ).astype(jnp.bfloat16)
    held = held.reshape(src_count, 1, per_block, features)
    for bit in reversed(bits_of("src", 1)):
        held = jnp.concatenate([held[:bit], swap(held[bit:], "src", bit)], axis=1)
    mine = held.reshape(SENT_DEV, features)
    parts = jnp.concatenate(
        [mine] + [swap(mine, "tgt", offset) for offset in range(1, tgt_count)]
    )
    origin = jnp.arange(1, dtype=jnp.int32)
    for bit in reversed(bits_of("src", 1)):
        origin = jnp.concatenate([origin, origin ^ bit])
    from_src = (origin ^ src_index)[None, :, None]
    from_tgt = (jnp.arange(tgt_count, dtype=jnp.int32) ^ tgt_index)[:, None, None]
    place = (from_src * tgt_count + from_tgt) * per_block + jnp.arange(per_block, dtype=jnp.int32)
    block = jnp.dot(
        one_hot(place.reshape(-1), block_rows).astype(jnp.bfloat16),
        parts,
        preferred_element_type=jnp.float32,
    ).astype(jnp.bfloat16)

    scores = lax.dot_general(
        block, target_units, (((1,), (1,)), ((), ())), preferred_element_type=jnp.float32
    )
    column_valid = jnp.repeat(valid, TBLK)
    expo = jnp.exp(SCORE_SCALE * scores) * column_valid[None, :]
    row_part = jnp.sum(expo, axis=1)
    column_part = jnp.sum(expo, axis=0).reshape(MOST, TBLK)
    picker = (slot_block[:, None] == jnp.arange(column_blocks, dtype=jnp.int32)[None, :]).astype(
        jnp.float32
    )
    column_total = jnp.dot(
        (picker * valid[:, None]).T, column_part, precision=lax.Precision.HIGHEST
    )
    for bit in bits_of("src", 1):
        column_total = column_total + swap(column_total, "src", bit)
    picked = jnp.dot(picker, column_total, precision=lax.Precision.HIGHEST)
    divisor = jnp.where(valid[:, None] > 0, picked, 1.0).reshape(-1)
    mutual = expo * (expo / divisor[None, :])
    numer = jnp.dot(mutual.astype(jnp.bfloat16), target_units, preferred_element_type=jnp.float32)
    mass_part = jnp.sum(mutual, axis=1)
    sums_part = jnp.stack([mass_part, row_part])

    def rows_of(index):
        return lax.dynamic_slice_in_dim(numer, index * SENT_DEV, SENT_DEV)

    def sums_of(index):
        return lax.dynamic_slice_in_dim(sums_part, index * SENT_DEV, SENT_DEV, axis=1)

    numer_rows, sums_rows = rows_of(tgt_index), sums_of(tgt_index)
    for offset in range(1, tgt_count):
        away = tgt_index ^ offset
        numer_rows = numer_rows + swap(
            rows_of(away).astype(jnp.bfloat16), "tgt", offset
        ).astype(jnp.float32)
        sums_rows = sums_rows + swap(sums_of(away), "tgt", offset)
    square = jnp.mean(numer_rows * numer_rows, axis=-1, keepdims=True)
    matched = (numer_rows * lax.rsqrt(square + 1e-06)).astype(jnp.bfloat16)
    log_mass = jnp.log(sums_rows[0] / sums_rows[1])
    return (matched, log_mass)


def solution(mesh):
    in_specs = (
        P(("groups", "src", "tgt"), None),
        P(("groups", "src", "tgt"), None),
        P(("src", "tgt"), None),
        P(("src", "tgt"), None),
        P(("groups", "src", "tgt")),
        P(("groups", "src"), None),
        P(("groups", "tgt"), None),
    )
    out_specs = (P(("groups", "src", "tgt"), None), P(("groups", "src", "tgt")))
    return jax.shard_map(
        on_device, mesh=mesh, in_specs=in_specs, out_specs=out_specs, check_vma=False
    )
```

time: 249 us -> 144 us (0.58)
  waiting for transfers between devices: 157 us -> 60.2 us
  blocking collectives: 34.2 us -> 0 us
  starting transfers between devices: 3.4 us -> 35.7 us
  between operations: 14.6 us -> 1 us
  local copies, waits for them, and re-layouts: 4.84 us -> 13.6 us
    all_gather x2 -> x0, waiting for transfers between devices: 144 us -> none  [the longest x1 75.4 us: on_device(): lax.all_gather(outer_weight, ('src', 'tgt'), axis=0, tiled=True)]
    ppermute x0 -> x29, waiting for transfers between devices: none -> 60.2 us  [swap(): lax.ppermute(values, axis, [(i, i ^ offset) for i in range(lax.axis_size(...]
    ppermute x0 -> x29, starting transfers between devices: none -> 35.7 us  [swap(): lax.ppermute(values, axis, [(i, i ^ offset) for i in range(lax.axis_size(...]
    psum x2 -> x0, blocking collectives: 19.9 us -> none  [the longest x1 10.1 us: on_device(): column_total = lax.psum(column_local, 'src')]
    all_gather x1 -> x0, blocking collectives: 14.2 us -> none  [on_device(): lax.all_gather(relayed, 'tgt', axis=1, tiled=True)]
    reduce_scatter x1 -> x0, waiting for transfers between devices: 7.57 us -> none  [on_device(): lax.psum_scatter(numer, 'tgt', scatter_dimension=0, tiled=True)]
    all_to_all x1 -> x0, waiting for transfers between devices: 4.01 us -> none  [on_device(): lax.all_to_all(sorted_units.reshape(src_count, per_block, features), 'src...]
    all_to_all x1 -> x0, starting transfers between devices: 3.28 us -> none  [on_device(): lax.all_to_all(sorted_units.reshape(src_count, per_block, features), 'src...]
  transfers between devices with their start and end apart: 4 -> 29, of which waited for: 4 -> 18; matrix products, arithmetic and copies ran while one was open for 5% -> 18% of each run, Pallas kernels for 0% -> 0%
where the time goes in v1:
time: 144 us
  waiting for transfers between devices  60.2 us (42%)
  starting transfers between devices  35.7 us (25%)
  matrix products  24.7 us (17%)
  local copies, waits for them, and re-layouts  13.6 us (9%)
  other arithmetic  8.84 us (6%)
    ppermute x29, waiting for transfers between devices, swap(): lax.ppermute(values, axis, [(i, i ^ offset) for i in range(lax.axis_size(...  60.2 us
    ppermute x29, starting transfers between devices, swap(): lax.ppermute(values, axis, [(i, i ^ offset) for i in range(lax.axis_size(...  35.7 us
    dot_general x1, matrix products, feed_forward(): jnp.dot(inner_units(shared, inner_near), outer_near, preferred_element_ty...  11.6 us
    dot_general x1, matrix products, feed_forward(): jnp.dot(inner_units(shared, inner_far), outer_far, preferred_element_type...  10.1 us
    gather x1, local copies, waits for them, and re-layouts, on_device(): tiles = targets.reshape(column_blocks, TBLK, features)[slot_block]  4.06 us
    unnamed x31, local copies, waits for them, and re-layouts  3.33 us
  transfers between devices with their start and end apart: 29, of which 18 were waited for; matrix products, arithmetic and copies ran while one was open for 18% of the time, Pallas kernels for 0%

profile of v1, /device:TPU:0, one launch (start us, length us, event | category | flops | bytes accessed | tf_op | source)
XLA Modules:
  0.0 144.1 jit_solution(10271375939300311412)
XLA Ops:
  0.6 3.0 %collective-permute-start.2 = (bf16[256,1024]{1,0:T(8,128)(2,1)}, bf16[256,1024]{1,0:T(8,128)(2,1)}, u32[]{:S(2)}, u32[]{:S(2)}) collective-permute-start(bf16[256,1024]{1,0:T(8,128)(2,1)} %param.9), channel_id=1, source_target_pairs={{0,8},{4,12},{8,0},{12,4},{1,9},{5,13},{9,1},{13,5},{2,10},{6,14},... | collective-permute-start | bytes 1572872 | tf_op jit(solution)/shard_map/ppermute | solution.py:25
  3.6 1.0 constant_dynamic-slice_fusion.5
  4.6 2.7 %collective-permute-start.4 = (bf16[128,1024]{1,0:T(8,128)(2,1)S(1)}, bf16[128,1024]{1,0:T(8,128)(2,1)S(1)}, u32[]{:S(2)}, u32[]{:S(2)}) collective-permute-start(bf16[128,1024]{1,0:T(8,128)(2,1)S(1)} %constant_dynamic-slice_fusion.5), channel_id=1, source_target_pairs={{0,2},{1,3},{2,0},{3,1},{4,6},{5,7},{6,4},{7,5},{8,10},{9,11},{10,... | collective-permute-start | bytes 786440 | tf_op jit(solution)/shard_map/ppermute | solution.py:25
  7.8 1.0 constant_dynamic-slice_fusion.4
  9.0 1.8 %collective-permute-start = (bf16[256,1024]{1,0:T(8,128)(2,1)}, bf16[256,1024]{1,0:T(8,128)(2,1)S(1)}, u32[]{:S(2)}, u32[]{:S(2)}) collective-permute-start(bf16[256,1024]{1,0:T(8,128)(2,1)} %param.7), channel_id=1, source_target_pairs={{0,1},{1,0},{2,3},{3,2},{4,5},{5,4},{6,7},{7,6},{8,9},{9,8},{10,11... | collective-permute-start | bytes 1572872 | tf_op jit(solution)/shard_map/ppermute | solution.py:25
  11.5 0.7 compare_bitcast_fusion
  12.5 1.3 copy.13
  13.8 0.8 constant_dynamic-update-slice_fusion.2
  14.7 11.2 %collective-permute-done.4 = bf16[128,1024]{1,0:T(8,128)(2,1)S(1)} collective-permute-done((bf16[128,1024]{1,0:T(8,128)(2,1)S(1)}, bf16[128,1024]{1,0:T(8,128)(2,1)S(1)}, u32[]{:S(2)}, u32[]{:S(2)}) %collective-permute-start.4) | collective-permute-done | bytes 262176 | tf_op jit(solution)/shard_map/ppermute | solution.py:25
  26.4 4.0 %collective-permute-done.9 = bf16[128,1024]{1,0:T(8,128)(2,1)S(1)} collective-permute-done((bf16[128,1024]{1,0:T(8,128)(2,1)S(1)}, bf16[128,1024]{1,0:T(8,128)(2,1)S(1)}, u32[]{:S(2)}, u32[]{:S(2)}) %collective-permute-start.9) | collective-permute-done | bytes 262176 | tf_op jit(solution)/shard_map/ppermute | solution.py:25
  30.3 1.5 %collective-permute-start.6 = (bf16[128,1024]{1,0:T(8,128)(2,1)S(1)}, bf16[128,1024]{1,0:T(8,128)(2,1)S(1)}, u32[]{:S(2)}, u32[]{:S(2)}) collective-permute-start(bf16[128,1024]{1,0:T(8,128)(2,1)S(1)} %collective-permute-done.4), channel_id=1, source_target_pairs={{0,16},{16,0},{1,17},{17,1},{2,18},{18,2},{3,19},{19,3},{4,20},{20... | collective-permute-start | bytes 786440 | tf_op jit(solution)/shard_map/ppermute | solution.py:25
  32.1 1.4 %collective-permute-start.10 = (bf16[128,1024]{1,0:T(8,128)(2,1)S(1)}, bf16[128,1024]{1,0:T(8,128)(2,1)S(1)}, u32[]{:S(2)}, u32[]{:S(2)}) collective-permute-start(bf16[128,1024]{1,0:T(8,128)(2,1)S(1)} %collective-permute-done.9), channel_id=1, source_target_pairs={{0,8},{4,12},{8,0},{12,4},{1,9},{5,13},{9,1},{13,5},{2,10},{6,14},... | collective-permute-start | bytes 786440 | tf_op jit(solution)/shard_map/ppermute | solution.py:25
  33.8 3.7 %collective-permute-done.6 = bf16[128,1024]{1,0:T(8,128)(2,1)S(1)} collective-permute-done((bf16[128,1024]{1,0:T(8,128)(2,1)S(1)}, bf16[128,1024]{1,0:T(8,128)(2,1)S(1)}, u32[]{:S(2)}, u32[]{:S(2)}) %collective-permute-start.6) | collective-permute-done | bytes 262176 | tf_op jit(solution)/shard_map/ppermute | solution.py:25
  37.4 1.5 %collective-permute-start.11 = (bf16[128,1024]{1,0:T(8,128)(2,1)S(1)}, bf16[128,1024]{1,0:T(8,128)(2,1)S(1)}, u32[]{:S(2)}, u32[]{:S(2)}) collective-permute-start(bf16[128,1024]{1,0:T(8,128)(2,1)S(1)} %collective-permute-done.9), channel_id=1, source_target_pairs={{0,16},{16,0},{1,17},{17,1},{2,18},{18,2},{3,19},{19,3},{4,20},{20... | collective-permute-start | bytes 786440 | tf_op jit(solution)/shard_map/ppermute | solution.py:25
  39.0 0.8 constant_dynamic-update-slice_fusion.1
  40.4 4.6 %collective-permute-done.11 = bf16[128,1024]{1,0:T(8,128)(2,1)S(1)} collective-permute-done((bf16[128,1024]{1,0:T(8,128)(2,1)S(1)}, bf16[128,1024]{1,0:T(8,128)(2,1)S(1)}, u32[]{:S(2)}, u32[]{:S(2)}) %collective-permute-start.11) | collective-permute-done | bytes 262176 | tf_op jit(solution)/shard_map/ppermute | solution.py:25
  45.6 1.1 collective-permute-done.7
  46.7 1.5 %collective-permute-start.12 = (bf16[64,1024]{1,0:T(8,128)(2,1)S(1)}, bf16[64,1024]{1,0:T(8,128)(2,1)S(1)}, u32[]{:S(2)}, u32[]{:S(2)}) collective-permute-start(bf16[64,1024]{1,0:T(8,128)(2,1)S(1)} %slice.70), channel_id=1, source_target_pairs={{0,16},{16,0},{1,17},{17,1},{2,18},{18,2},{3,19},{19,3},{4,20},{20... | collective-permute-start | bytes 393224 | tf_op jit(solution)/shard_map/ppermute | solution.py:25
  48.2 1.9 %collective-permute-done.8 = bf16[64,1024]{1,0:T(8,128)(2,1)S(1)} collective-permute-done((bf16[64,1024]{1,0:T(8,128)(2,1)S(1)}, bf16[64,1024]{1,0:T(8,128)(2,1)S(1)}, u32[]{:S(2)}, u32[]{:S(2)}) %collective-permute-start.8) | collective-permute-done | bytes 131104 | tf_op jit(solution)/shard_map/ppermute | solution.py:25
  50.8 0.9 collective-permute-done.12
  51.7 3.5 %collective-permute-done.13 = bf16[64,1024]{1,0:T(8,128)(2,1)S(1)} collective-permute-done((bf16[64,1024]{1,0:T(8,128)(2,1)S(1)}, bf16[64,1024]{1,0:T(8,128)(2,1)S(1)}, u32[]{:S(2)}, u32[]{:S(2)}) %collective-permute-start.13) | collective-permute-done | bytes 131104 | tf_op jit(solution)/shard_map/ppermute | solution.py:25
  55.2 1.1 constant_dynamic-update-slice_fusion
  56.3 10.1 %fusion.26 = f32[1024,1024]{0,1:T(8,128)} fusion(bf16[512,1024]{1,0:T(8,128)(2,1)S(1)} %constant_dynamic-update-slice_fusion.8, bf16[1024,1024]{1,0:T(8,128)(2,1)} %constant_dynamic-update-slice_fusion, bf16[512,1024]{1,0:T(8,128)(2,1)} %copy-done.4), kind=kOutput, calls=%fused_computation.54 | convolution fusion | flops 2181562368 | bytes 8388608 | tf_op jit(solution)/shard_map/dot_general | solution.py:77
  66.4 11.6 %convolution_add_fusion = f32[1024,1024]{0,1:T(8,128)} fusion(f32[1024,1024]{0,1:T(8,128)} %fusion.26, bf16[1024,1024]{1,0:T(8,128)(2,1)} %constant_dynamic-update-slice_fusion, bf16[256,1024]{1,0:T(8,128)(2,1)} %collective-permute-done.2, bf16[256,1024]{1,0:T(8,128)(2,1)S(1)} %copy-done.3, bf16[256,1024]{1,0:T(8,128)(2,1)} %collective-permute-done.3, ...), kind=kOutput, calls=%fused_computation.7 | convolution fusion | flops 2186805248 | bytes 12582912 | tf_op jit(solution)/shard_map/dot_general | solution.py:75
  78.0 2.7 %slice.107 = bf16[512,1024]{0,1:T(8,128)(2,1)} slice(f32[1024,1024]{0,1:T(8,128)} %convolution_add_fusion), slice={[512:1024], [0:1024]} | slice | bytes 2097152 | tf_op jit(solution)/shard_map/slice | solution.py:78
  80.8 4.1 %gather_fusion = bf16[4,256,1024]{2,1,0:T(8,128)(2,1)S(1)} fusion(bf16[16,256,1024]{2,1,0:T(8,128)(2,1)} %bitcast.43, s32[1024]{0:T(1024)S(1)} %pad_clamp_fusion), kind=kCustom, calls=%fused_computation | custom fusion | bytes 4194320 | tf_op jit(solution)/shard_map/gather | solution.py:106
  85.7 2.2 %slice_add_fusion = f32[512,1024]{0,1:T(8,128)S(1)} fusion(f32[1024,1024]{0,1:T(8,128)} %convolution_add_fusion, bf16[512,1024]{0,1:T(8,128)(2,1)} %collective-permute-done.14), kind=kLoop, calls=%fused_computation.15 | loop fusion | flops 1048576 | bytes 5242880 | tf_op jit(solution)/shard_map/add | solution.py:79
  88.0 4.2 %collective-permute-start.15 = (bf16[256,1024]{0,1:T(8,128)(2,1)S(1)}, bf16[256,1024]{0,1:T(8,128)(2,1)S(1)}, u32[]{:S(2)}, u32[]{:S(2)}) collective-permute-start(bf16[256,1024]{0,1:T(8,128)(2,1)S(1)} %slice.108), channel_id=1, source_target_pairs={{0,1},{1,0},{2,3},{3,2},{4,5},{5,4},{6,7},{7,6},{8,9},{9,8},{10,11... | collective-permute-start | bytes 1572872 | tf_op jit(solution)/shard_map/ppermute | solution.py:25
  92.2 1.9 %fusion.1 = bf16[1024,1024]{1,0:T(8,128)(2,1)} fusion(f32[1024]{0:T(1024)S(1)} %bitcast.44, bf16[4,256,1024]{2,1,0:T(8,128)(2,1)S(1)} %gather_fusion), kind=kLoop, calls=%fused_computation.3 | loop fusion | flops 4194304 | bytes 4198400 | tf_op jit(solution)/shard_map/convert_element_type | solution.py:31
  94.1 10.7 %collective-permute-done.15 = bf16[256,1024]{0,1:T(8,128)(2,1)S(1)} collective-permute-done((bf16[256,1024]{0,1:T(8,128)(2,1)S(1)}, bf16[256,1024]{0,1:T(8,128)(2,1)S(1)}, u32[]{:S(2)}, u32[]{:S(2)}) %collective-permute-start.15) | collective-permute-done | bytes 524320 | tf_op jit(solution)/shard_map/ppermute | solution.py:25
  105.4 0.9 multiply_reduce_fusion.3
  107.2 3.3 %collective-permute-done.16 = bf16[2,1,8,1024]{3,2,0,1:T(8,128)(2,1)S(1)} collective-permute-done((bf16[2,1,8,1024]{3,2,0,1:T(8,128)(2,1)S(1)}, bf16[2,1,8,1024]{3,2,0,1:T(8,128)(2,1)S(1)}, u32[]{:S(2)}, u32[]{:S(2)}) %collective-permute-start.16) | collective-permute-done | bytes 32800 | tf_op jit(solution)/shard_map/ppermute | solution.py:25
  110.7 1.1 collective-permute-done.17
  111.8 1.8 %collective-permute-start.18 = (bf16[32,1024]{1,0:T(8,128)(2,1)S(1)}, bf16[32,1024]{1,0:T(8,128)(2,1)S(1)}, u32[]{:S(2)}, u32[]{:S(2)}) collective-permute-start(bf16[32,1024]{1,0:T(8,128)(2,1)S(1)} %maximum_bitcast_fusion), channel_id=1, source_target_pairs={{0,1},{1,0},{2,3},{3,2},{4,5},{5,4},{6,7},{7,6},{8,9},{9,8},{10,11... | collective-permute-start | bytes 196616 | tf_op jit(solution)/shard_map/ppermute | solution.py:25
  113.6 3.3 %collective-permute-start.19 = (bf16[32,1024]{1,0:T(8,128)(2,1)S(1)}, bf16[32,1024]{1,0:T(8,128)(2,1)S(1)}, u32[]{:S(2)}, u32[]{:S(2)}) collective-permute-start(bf16[32,1024]{1,0:T(8,128)(2,1)S(1)} %maximum_bitcast_fusion), channel_id=1, source_target_pairs={{0,2},{1,3},{2,0},{3,1},{4,6},{5,7},{6,4},{7,5},{8,10},{9,11},{10,... | collective-permute-start | bytes 196616 | tf_op jit(solution)/shard_map/ppermute | solution.py:25
  117.1 3.9 %collective-permute-done.19 = bf16[32,1024]{1,0:T(8,128)(2,1)S(1)} collective-permute-done((bf16[32,1024]{1,0:T(8,128)(2,1)S(1)}, bf16[32,1024]{1,0:T(8,128)(2,1)S(1)}, u32[]{:S(2)}, u32[]{:S(2)}) %collective-permute-start.19) | collective-permute-done | bytes 65568 | tf_op jit(solution)/shard_map/ppermute | solution.py:25
  121.0 2.1 %collective-permute-done.20 = bf16[32,1024]{1,0:T(8,128)(2,1)S(1)} collective-permute-done((bf16[32,1024]{1,0:T(8,128)(2,1)S(1)}, bf16[32,1024]{1,0:T(8,128)(2,1)S(1)}, u32[]{:S(2)}, u32[]{:S(2)}) %collective-permute-start.20) | collective-permute-done | bytes 65568 | tf_op jit(solution)/shard_map/ppermute | solution.py:25
  123.1 0.9 fusion.212
  124.4 1.2 collective-permute-done.21
  126.1 3.2 %collective-permute-done.22 = f32[16,256]{1,0:T(8,128)S(1)} collective-permute-done((f32[16,256]{1,0:T(8,128)S(1)}, f32[16,256]{1,0:T(8,128)S(1)}, u32[]{:S(2)}, u32[]{:S(2)}) %collective-permute-start.22) | collective-permute-done | bytes 16416 | tf_op jit(solution)/shard_map/ppermute | solution.py:25
  130.2 0.7 collective-permute-start.26
  130.9 1.7 %collective-permute-start.27 = (f32[2,32]{1,0:T(2,128)S(1)}, f32[2,32]{1,0:T(2,128)S(1)}, u32[]{:S(2)}, u32[]{:S(2)}) collective-permute-start(f32[2,32]{1,0:T(2,128)S(1)} %get-tuple-element.17), channel_id=1, source_target_pairs={{0,2},{1,3},{2,0},{3,1},{4,6},{5,7},{6,4},{7,5},{8,10},{9,11},{10,... | collective-permute-start | bytes 776 | tf_op jit(solution)/shard_map/ppermute | solution.py:25
  132.7 1.9 %collective-permute-start.28 = (f32[2,32]{1,0:T(2,128)S(1)}, f32[2,32]{1,0:T(2,128)S(1)}, u32[]{:S(2)}, u32[]{:S(2)}) collective-permute-start(f32[2,32]{1,0:T(2,128)S(1)} %get-tuple-element.16), channel_id=1, source_target_pairs={{0,3},{1,2},{2,1},{3,0},{4,7},{5,6},{6,5},{7,4},{8,11},{9,10},{10,... | collective-permute-start | bytes 776 | tf_op jit(solution)/shard_map/ppermute | solution.py:25
  134.7 2.5 %collective-permute-start.24 = (bf16[32,1024]{1,0:T(8,128)(2,1)S(1)}, bf16[32,1024]{1,0:T(8,128)(2,1)S(1)}, u32[]{:S(2)}, u32[]{:S(2)}) collective-permute-start(bf16[32,1024]{1,0:T(8,128)(2,1)S(1)} %get-tuple-element.10), channel_id=1, source_target_pairs={{0,2},{1,3},{2,0},{3,1},{4,6},{5,7},{6,4},{7,5},{8,10},{9,11},{10,... | collective-permute-start | bytes 196616 | tf_op jit(solution)/shard_map/ppermute | solution.py:25
  137.1 1.9 %collective-permute-start.25 = (bf16[32,1024]{1,0:T(8,128)(2,1)S(1)}, bf16[32,1024]{1,0:T(8,128)(2,1)S(1)}, u32[]{:S(2)}, u32[]{:S(2)}) collective-permute-start(bf16[32,1024]{1,0:T(8,128)(2,1)S(1)} %get-tuple-element.9), channel_id=1, source_target_pairs={{0,3},{1,2},{2,1},{3,0},{4,7},{5,6},{6,5},{7,4},{8,11},{9,10},{10,... | collective-permute-start | bytes 196616 | tf_op jit(solution)/shard_map/ppermute | solution.py:25
  139.7 0.9 collective-permute-done.24
  140.6 2.6 %collective-permute-done.25 = bf16[32,1024]{1,0:T(8,128)(2,1)S(1)} collective-permute-done((bf16[32,1024]{1,0:T(8,128)(2,1)S(1)}, bf16[32,1024]{1,0:T(8,128)(2,1)S(1)}, u32[]{:S(2)}, u32[]{:S(2)}) %collective-permute-start.25) | collective-permute-done | bytes 65568 | tf_op jit(solution)/shard_map/ppermute | solution.py:25
  143.4 0.7 multiply_convert_fusion
  (101 shorter events, 9.8 us)
Async XLA Ops:
  0.6 13.2 %copy-start = (bf16[256,1024]{1,0:T(8,128)(2,1)S(1)}, bf16[256,1024]{1,0:T(8,128)(2,1)}, u32[]{:S(2)}) copy-start(bf16[256,1024]{1,0:T(8,128)(2,1)} %param.7) | copy-start | bytes 1572868
  0.6 65.7 %collective-permute-start.2 = (bf16[256,1024]{1,0:T(8,128)(2,1)}, bf16[256,1024]{1,0:T(8,128)(2,1)}, u32[]{:S(2)}, u32[]{:S(2)}) collective-permute-start(bf16[256,1024]{1,0:T(8,128)(2,1)} %param.9), channel_id=1, source_target_pairs={{0,8},{4,12},{8,0},{12,4},{1,9},{5,13},{9,1},{13,5},{2,10},{6,14},... | collective-permute-start | bytes 1572872 | tf_op jit(solution)/shard_map/ppermute | solution.py:25
  4.6 21.2 %collective-permute-start.4 = (bf16[128,1024]{1,0:T(8,128)(2,1)S(1)}, bf16[128,1024]{1,0:T(8,128)(2,1)S(1)}, u32[]{:S(2)}, u32[]{:S(2)}) collective-permute-start(bf16[128,1024]{1,0:T(8,128)(2,1)S(1)} %constant_dynamic-slice_fusion.5), channel_id=1, source_target_pairs={{0,2},{1,3},{2,0},{3,1},{4,6},{5,7},{6,4},{7,5},{8,10},{9,11},{10,... | collective-permute-start | bytes 786440 | tf_op jit(solution)/shard_map/ppermute | solution.py:25
  7.3 59.1 %collective-permute-start.3 = (bf16[256,1024]{1,0:T(8,128)(2,1)}, bf16[256,1024]{1,0:T(8,128)(2,1)}, u32[]{:S(2)}, u32[]{:S(2)}) collective-permute-start(bf16[256,1024]{1,0:T(8,128)(2,1)} %param.10), channel_id=1, source_target_pairs={{0,8},{4,12},{8,0},{12,4},{1,9},{5,13},{9,1},{13,5},{2,10},{6,14},... | collective-permute-start | bytes 1572872 | tf_op jit(solution)/shard_map/ppermute | solution.py:25
  8.8 21.5 %collective-permute-start.9 = (bf16[128,1024]{1,0:T(8,128)(2,1)S(1)}, bf16[128,1024]{1,0:T(8,128)(2,1)S(1)}, u32[]{:S(2)}, u32[]{:S(2)}) collective-permute-start(bf16[128,1024]{1,0:T(8,128)(2,1)S(1)} %constant_dynamic-slice_fusion.4), channel_id=1, source_target_pairs={{0,2},{1,3},{2,0},{3,1},{4,6},{5,7},{6,4},{7,5},{8,10},{9,11},{10,... | collective-permute-start | bytes 786440 | tf_op jit(solution)/shard_map/ppermute | solution.py:25
  9.0 23.2 %collective-permute-start = (bf16[256,1024]{1,0:T(8,128)(2,1)}, bf16[256,1024]{1,0:T(8,128)(2,1)S(1)}, u32[]{:S(2)}, u32[]{:S(2)}) collective-permute-start(bf16[256,1024]{1,0:T(8,128)(2,1)} %param.7), channel_id=1, source_target_pairs={{0,1},{1,0},{2,3},{3,2},{4,5},{5,4},{6,7},{7,6},{8,9},{9,8},{10,11... | collective-permute-start | bytes 1572872 | tf_op jit(solution)/shard_map/ppermute | solution.py:25
  25.9 7.8 %collective-permute-start.5 = (bf16[128,1024]{1,0:T(8,128)(2,1)S(1)}, bf16[128,1024]{1,0:T(8,128)(2,1)S(1)}, u32[]{:S(2)}, u32[]{:S(2)}) collective-permute-start(bf16[128,1024]{1,0:T(8,128)(2,1)S(1)} %collective-permute-done.4), channel_id=1, source_target_pairs={{0,8},{4,12},{8,0},{12,4},{1,9},{5,13},{9,1},{13,5},{2,10},{6,14},... | collective-permute-start | bytes 786440 | tf_op jit(solution)/shard_map/ppermute | solution.py:25
  30.3 7.1 %collective-permute-start.6 = (bf16[128,1024]{1,0:T(8,128)(2,1)S(1)}, bf16[128,1024]{1,0:T(8,128)(2,1)S(1)}, u32[]{:S(2)}, u32[]{:S(2)}) collective-permute-start(bf16[128,1024]{1,0:T(8,128)(2,1)S(1)} %collective-permute-done.4), channel_id=1, source_target_pairs={{0,16},{16,0},{1,17},{17,1},{2,18},{18,2},{3,19},{19,3},{4,20},{20... | collective-permute-start | bytes 786440 | tf_op jit(solution)/shard_map/ppermute | solution.py:25
  32.1 7.7 %collective-permute-start.10 = (bf16[128,1024]{1,0:T(8,128)(2,1)S(1)}, bf16[128,1024]{1,0:T(8,128)(2,1)S(1)}, u32[]{:S(2)}, u32[]{:S(2)}) collective-permute-start(bf16[128,1024]{1,0:T(8,128)(2,1)S(1)} %collective-permute-done.9), channel_id=1, source_target_pairs={{0,8},{4,12},{8,0},{12,4},{1,9},{5,13},{9,1},{13,5},{2,10},{6,14},... | collective-permute-start | bytes 786440 | tf_op jit(solution)/shard_map/ppermute | solution.py:25
  33.7 21.5 %collective-permute-start.1 = (bf16[512,1024]{1,0:T(8,128)(2,1)S(1)}, bf16[512,1024]{1,0:T(8,128)(2,1)S(1)}, u32[]{:S(2)}, u32[]{:S(2)}) collective-permute-start(bf16[512,1024]{1,0:T(8,128)(2,1)S(1)} %pad_maximum_fusion), channel_id=1, source_target_pairs={{0,4},{4,0},{8,12},{12,8},{1,5},{5,1},{9,13},{13,9},{2,6},{6,2},{1... | collective-permute-start | bytes 3145736 | tf_op jit(solution)/shard_map/ppermute | solution.py:25
  37.4 7.6 %collective-permute-start.11 = (bf16[128,1024]{1,0:T(8,128)(2,1)S(1)}, bf16[128,1024]{1,0:T(8,128)(2,1)S(1)}, u32[]{:S(2)}, u32[]{:S(2)}) collective-permute-start(bf16[128,1024]{1,0:T(8,128)(2,1)S(1)} %collective-permute-done.9), channel_id=1, source_target_pairs={{0,16},{16,0},{1,17},{17,1},{2,18},{18,2},{3,19},{19,3},{4,20},{20... | collective-permute-start | bytes 786440 | tf_op jit(solution)/shard_map/ppermute | solution.py:25
  39.8 6.9 %collective-permute-start.7 = (bf16[64,1024]{1,0:T(8,128)(2,1)S(1)}, bf16[64,1024]{1,0:T(8,128)(2,1)S(1)}, u32[]{:S(2)}, u32[]{:S(2)}) collective-permute-start(bf16[64,1024]{1,0:T(8,128)(2,1)S(1)} %slice.68), channel_id=1, source_target_pairs={{0,16},{16,0},{1,17},{17,1},{2,18},{18,2},{3,19},{19,3},{4,20},{20... | collective-permute-start | bytes 393224 | tf_op jit(solution)/shard_map/ppermute | solution.py:25
  45.0 5.2 %collective-permute-start.8 = (bf16[64,1024]{1,0:T(8,128)(2,1)S(1)}, bf16[64,1024]{1,0:T(8,128)(2,1)S(1)}, u32[]{:S(2)}, u32[]{:S(2)}) collective-permute-start(bf16[64,1024]{1,0:T(8,128)(2,1)S(1)} %slice.69), channel_id=1, source_target_pairs={{0,8},{4,12},{8,0},{12,4},{1,9},{5,13},{9,1},{13,5},{2,10},{6,14},... | collective-permute-start | bytes 393224 | tf_op jit(solution)/shard_map/ppermute | solution.py:25
  46.7 5.0 %collective-permute-start.12 = (bf16[64,1024]{1,0:T(8,128)(2,1)S(1)}, bf16[64,1024]{1,0:T(8,128)(2,1)S(1)}, u32[]{:S(2)}, u32[]{:S(2)}) collective-permute-start(bf16[64,1024]{1,0:T(8,128)(2,1)S(1)} %slice.70), channel_id=1, source_target_pairs={{0,16},{16,0},{1,17},{17,1},{2,18},{18,2},{3,19},{19,3},{4,20},{20... | collective-permute-start | bytes 393224 | tf_op jit(solution)/shard_map/ppermute | solution.py:25
  50.2 5.0 %collective-permute-start.13 = (bf16[64,1024]{1,0:T(8,128)(2,1)S(1)}, bf16[64,1024]{1,0:T(8,128)(2,1)S(1)}, u32[]{:S(2)}, u32[]{:S(2)}) collective-permute-start(bf16[64,1024]{1,0:T(8,128)(2,1)S(1)} %slice.71), channel_id=1, source_target_pairs={{0,8},{4,12},{8,0},{12,4},{1,9},{5,13},{9,1},{13,5},{2,10},{6,14},... | collective-permute-start | bytes 393224 | tf_op jit(solution)/shard_map/ppermute | solution.py:25
  50.7 4.4 %copy-start.4 = (bf16[512,1024]{1,0:T(8,128)(2,1)}, bf16[512,1024]{1,0:T(8,128)(2,1)S(1)}, u32[]{:S(2)}) copy-start(bf16[512,1024]{1,0:T(8,128)(2,1)S(1)} %constant_dynamic-update-slice_fusion.3) | copy-start | bytes 3145732
  56.3 10.1 %copy-start.2 = (bf16[256,1024]{1,0:T(8,128)(2,1)S(1)}, bf16[256,1024]{1,0:T(8,128)(2,1)}, u32[]{:S(2)}) copy-start(bf16[256,1024]{1,0:T(8,128)(2,1)} %param.10) | copy-start | bytes 1572868
  56.3 10.1 %copy-start.3 = (bf16[256,1024]{1,0:T(8,128)(2,1)S(1)}, bf16[256,1024]{1,0:T(8,128)(2,1)}, u32[]{:S(2)}) copy-start(bf16[256,1024]{1,0:T(8,128)(2,1)} %param.9) | copy-start | bytes 1572868
  80.8 4.9 %collective-permute-start.14 = (bf16[512,1024]{0,1:T(8,128)(2,1)}, bf16[512,1024]{0,1:T(8,128)(2,1)}, u32[]{:S(2)}, u32[]{:S(2)}) collective-permute-start(bf16[512,1024]{0,1:T(8,128)(2,1)} %slice.107), channel_id=1, source_target_pairs={{0,4},{4,0},{8,12},{12,8},{1,5},{5,1},{9,13},{13,9},{2,6},{6,2},{1... | collective-permute-start | bytes 3145736 | tf_op jit(solution)/shard_map/ppermute | solution.py:25
  84.8 0.7 copy-start.6
  84.9 0.8 copy-start.5
  85.7 6.5 %copy-start.7 = (s32[32]{0:T(128)S(1)}, s32[32]{0:T(128)}, u32[]{:S(2)}) copy-start(s32[32]{0:T(128)} %param.11) | copy-start | bytes 388
  88.0 16.8 %collective-permute-start.15 = (bf16[256,1024]{0,1:T(8,128)(2,1)S(1)}, bf16[256,1024]{0,1:T(8,128)(2,1)S(1)}, u32[]{:S(2)}, u32[]{:S(2)}) collective-permute-start(bf16[256,1024]{0,1:T(8,128)(2,1)S(1)} %slice.108), channel_id=1, source_target_pairs={{0,1},{1,0},{2,3},{3,2},{4,5},{5,4},{6,7},{7,6},{8,9},{9,8},{10,11... | collective-permute-start | bytes 1572872 | tf_op jit(solution)/shard_map/ppermute | solution.py:25
  105.1 18.0 %copy-start.1 = (bf16[1024,1024]{1,0:T(8,128)(2,1)S(1)}, bf16[1024,1024]{1,0:T(8,128)(2,1)}, u32[]{:S(2)}) copy-start(bf16[1024,1024]{1,0:T(8,128)(2,1)} %fusion.1) | copy-start | bytes 6291460
  106.6 4.0 %collective-permute-start.16 = (bf16[2,1,8,1024]{3,2,0,1:T(8,128)(2,1)S(1)}, bf16[2,1,8,1024]{3,2,0,1:T(8,128)(2,1)S(1)}, u32[]{:S(2)}, u32[]{:S(2)}) collective-permute-start(bf16[2,1,8,1024]{3,2,0,1:T(8,128)(2,1)S(1)} %get-tuple-element.14), channel_id=1, source_target_pairs={{0,8},{4,12},{8,0},{12,4},{1,9},{5,13},{9,1},{13,5},{2,10},{6,14},... | collective-permute-start | bytes 98312 | tf_op jit(solution)/shard_map/ppermute | solution.py:25
  110.5 1.3 collective-permute-start.17
  111.8 5.2 %collective-permute-start.18 = (bf16[32,1024]{1,0:T(8,128)(2,1)S(1)}, bf16[32,1024]{1,0:T(8,128)(2,1)S(1)}, u32[]{:S(2)}, u32[]{:S(2)}) collective-permute-start(bf16[32,1024]{1,0:T(8,128)(2,1)S(1)} %maximum_bitcast_fusion), channel_id=1, source_target_pairs={{0,1},{1,0},{2,3},{3,2},{4,5},{5,4},{6,7},{7,6},{8,9},{9,8},{10,11... | collective-permute-start | bytes 196616 | tf_op jit(solution)/shard_map/ppermute | solution.py:25
  113.6 7.4 %collective-permute-start.19 = (bf16[32,1024]{1,0:T(8,128)(2,1)S(1)}, bf16[32,1024]{1,0:T(8,128)(2,1)S(1)}, u32[]{:S(2)}, u32[]{:S(2)}) collective-permute-start(bf16[32,1024]{1,0:T(8,128)(2,1)S(1)} %maximum_bitcast_fusion), channel_id=1, source_target_pairs={{0,2},{1,3},{2,0},{3,1},{4,6},{5,7},{6,4},{7,5},{8,10},{9,11},{10,... | collective-permute-start | bytes 196616 | tf_op jit(solution)/shard_map/ppermute | solution.py:25
  116.9 6.2 %collective-permute-start.20 = (bf16[32,1024]{1,0:T(8,128)(2,1)S(1)}, bf16[32,1024]{1,0:T(8,128)(2,1)S(1)}, u32[]{:S(2)}, u32[]{:S(2)}) collective-permute-start(bf16[32,1024]{1,0:T(8,128)(2,1)S(1)} %maximum_bitcast_fusion), channel_id=1, source_target_pairs={{0,3},{1,2},{2,1},{3,0},{4,7},{5,6},{6,5},{7,4},{8,11},{9,10},{10,... | collective-permute-start | bytes 196616 | tf_op jit(solution)/shard_map/ppermute | solution.py:25
  124.3 1.2 collective-permute-start.21
  125.5 3.7 %collective-permute-start.22 = (f32[16,256]{1,0:T(8,128)S(1)}, f32[16,256]{1,0:T(8,128)S(1)}, u32[]{:S(2)}, u32[]{:S(2)}) collective-permute-start(f32[16,256]{1,0:T(8,128)S(1)} %add.193), channel_id=1, source_target_pairs={{0,8},{4,12},{8,0},{12,4},{1,9},{5,13},{9,1},{13,5},{2,10},{6,14},... | collective-permute-start | bytes 49160 | tf_op jit(solution)/shard_map/ppermute | solution.py:25
  130.2 7.0 %collective-permute-start.26 = (f32[2,32]{1,0:T(2,128)S(1)}, f32[2,32]{1,0:T(2,128)S(1)}, u32[]{:S(2)}, u32[]{:S(2)}) collective-permute-start(f32[2,32]{1,0:T(2,128)S(1)} %get-tuple-element.15), channel_id=1, source_target_pairs={{0,1},{1,0},{2,3},{3,2},{4,5},{5,4},{6,7},{7,6},{8,9},{9,8},{10,11... | collective-permute-start | bytes 776 | tf_op jit(solution)/shard_map/ppermute | solution.py:25
  130.9 8.1 %collective-permute-start.27 = (f32[2,32]{1,0:T(2,128)S(1)}, f32[2,32]{1,0:T(2,128)S(1)}, u32[]{:S(2)}, u32[]{:S(2)}) collective-permute-start(f32[2,32]{1,0:T(2,128)S(1)} %get-tuple-element.17), channel_id=1, source_target_pairs={{0,2},{1,3},{2,0},{3,1},{4,6},{5,7},{6,4},{7,5},{8,10},{9,11},{10,... | collective-permute-start | bytes 776 | tf_op jit(solution)/shard_map/ppermute | solution.py:25
  132.7 6.4 %collective-permute-start.28 = (f32[2,32]{1,0:T(2,128)S(1)}, f32[2,32]{1,0:T(2,128)S(1)}, u32[]{:S(2)}, u32[]{:S(2)}) collective-permute-start(f32[2,32]{1,0:T(2,128)S(1)} %get-tuple-element.16), channel_id=1, source_target_pairs={{0,3},{1,2},{2,1},{3,0},{4,7},{5,6},{6,5},{7,4},{8,11},{9,10},{10,... | collective-permute-start | bytes 776 | tf_op jit(solution)/shard_map/ppermute | solution.py:25
  134.6 5.1 %collective-permute-start.23 = (bf16[32,1024]{1,0:T(8,128)(2,1)S(1)}, bf16[32,1024]{1,0:T(8,128)(2,1)S(1)}, u32[]{:S(2)}, u32[]{:S(2)}) collective-permute-start(bf16[32,1024]{1,0:T(8,128)(2,1)S(1)} %get-tuple-element.8), channel_id=1, source_target_pairs={{0,1},{1,0},{2,3},{3,2},{4,5},{5,4},{6,7},{7,6},{8,9},{9,8},{10,11... | collective-permute-start | bytes 196616 | tf_op jit(solution)/shard_map/ppermute | solution.py:25
  134.7 5.9 %collective-permute-start.24 = (bf16[32,1024]{1,0:T(8,128)(2,1)S(1)}, bf16[32,1024]{1,0:T(8,128)(2,1)S(1)}, u32[]{:S(2)}, u32[]{:S(2)}) collective-permute-start(bf16[32,1024]{1,0:T(8,128)(2,1)S(1)} %get-tuple-element.10), channel_id=1, source_target_pairs={{0,2},{1,3},{2,0},{3,1},{4,6},{5,7},{6,4},{7,5},{8,10},{9,11},{10,... | collective-permute-start | bytes 196616 | tf_op jit(solution)/shard_map/ppermute | solution.py:25
  137.1 6.1 %collective-permute-start.25 = (bf16[32,1024]{1,0:T(8,128)(2,1)S(1)}, bf16[32,1024]{1,0:T(8,128)(2,1)S(1)}, u32[]{:S(2)}, u32[]{:S(2)}) collective-permute-start(bf16[32,1024]{1,0:T(8,128)(2,1)S(1)} %get-tuple-element.9), channel_id=1, source_target_pairs={{0,3},{1,2},{2,1},{3,0},{4,7},{5,6},{6,5},{7,4},{8,11},{9,10},{10,... | collective-permute-start | bytes 196616 | tf_op jit(solution)/shard_map/ppermute | solution.py:25

commit v2 on v0

v2 whole, which is shorter than its diff:
```python
import functools
import math

import jax
import jax.numpy as jnp
from jax import lax
from jax.experimental import pallas as pl
from jax.experimental.pallas import tpu as pltpu
from jax.sharding import PartitionSpec as P

SENT_DEV = 32
TBLK = 256
MOST = 4
LANES = 128


SCORE_SCALE = 32.0


def bits_of(axis, first):
    size, bit, bits = lax.axis_size(axis), first, []
    while bit < size:
        bits.append(bit)
        bit *= 2
    return bits


def swap(values, axis, offset):
    return lax.ppermute(values, axis, [(i, i ^ offset) for i in range(lax.axis_size(axis))])


def local_call(kernel, out_shape, args, flops, scratch=(), scalars=0):
    outs = out_shape if isinstance(out_shape, tuple) else (out_shape,)
    moved = sum(math.prod(a.shape) * a.dtype.itemsize for a in (*args, *outs))
    return pl.pallas_call(
        kernel,
        out_shape=out_shape,
        in_specs=[pl.BlockSpec(memory_space=pltpu.SMEM)] * scalars
        + [pl.BlockSpec(memory_space=pltpu.VMEM)] * (len(args) - scalars),
        out_specs=jax.tree.map(lambda _: pl.BlockSpec(memory_space=pltpu.VMEM), out_shape),
        scratch_shapes=scratch,
        compiler_params=pltpu.CompilerParams(vmem_limit_bytes=40 * 2**20),
        cost_estimate=pl.CostEstimate(flops=flops, bytes_accessed=moved, transcendentals=0),
    )(*args)


def shape(dims, dtype):
    return jax.ShapeDtypeStruct(tuple(dims), dtype)


def unit_of(floats):
    square = jnp.mean(floats * floats, axis=-1, keepdims=True)
    return (floats * lax.rsqrt(square + 1e-06) * (1.0 / math.sqrt(floats.shape[-1]))).astype(
        jnp.bfloat16
    )


def dot(left, right, contract, **more):
    return lax.dot_general(
        left, right, ((contract[:1], contract[1:]), ((), ())),
        preferred_element_type=jnp.float32, **more
    )


def gather_refs(refs, held):
    start = 0
    for ref in refs:
        held[start : start + ref.shape[0], :] = ref[...]
        start += ref.shape[0]


def hidden_kernel(count, *refs):
    tokens, weights, (out, rows, held) = refs[:count], refs[count:-3], refs[-3:]
    gather_refs(tokens, rows)
    gather_refs(weights, held)
    step = 256

    @pl.loop(0, out.shape[0] // step)
    def _(index):
        part = pl.ds(pl.multiple_of(index * step, step), step)
        product = dot(rows[part, :], held[...], (1, 1))
        out[part, :] = (
            product * 0.5 * (1.0 + lax.erf(product * math.sqrt(0.5)))
        ).astype(jnp.bfloat16)


def hidden_units(tokens, weights):
    features = weights[0].shape[1]
    rows = sum(t.shape[0] for t in tokens)
    units = sum(w.shape[0] for w in weights)
    return local_call(
        functools.partial(hidden_kernel, len(tokens)),
        shape((rows, units), jnp.bfloat16),
        (*tokens, *weights),
        2 * rows * units * features,
        (pltpu.VMEM((rows, features), jnp.bfloat16), pltpu.VMEM((units, features), jnp.bfloat16)),
    )


def partial_kernel(near_hidden, far_hidden, *refs):
    weights, (own, pair, own_sent, pair_sent, held) = refs[:-5], refs[-5:]
    gather_refs(weights, held)
    near = near_hidden.shape[1]
    rows = own.shape[0]
    for index, out in enumerate((own, pair, own_sent, pair_sent)):
        part = pl.ds(index * rows, rows)
        out[...] = (
            dot(near_hidden[part, :], held[:near, :], (1, 0))
            + dot(far_hidden[part, :], held[near:, :], (1, 0))
        ).astype(out.dtype)


def partial_sums(near_hidden, far_hidden, weights):
    rows, features = near_hidden.shape[0] // 4, weights[0].shape[1]
    units = near_hidden.shape[1] + far_hidden.shape[1]
    kept, sent = shape((rows, features), jnp.float32), shape((rows, features), jnp.bfloat16)
    return local_call(
        partial_kernel,
        (kept, kept, sent, sent),
        (near_hidden, far_hidden, *weights),
        8 * rows * units * features,
        (pltpu.VMEM((units, features), jnp.bfloat16),),
    )


def pool_kernel(count, identity, order, tokens, *refs):
    out, parts = refs[-1], refs[:-1]
    summed = []
    width = tokens.shape[1] // count
    for index in range(count):
        own, core, pair = parts[3 * index : 3 * index + 3]
        summed.append(
            tokens[:, index * width : (index + 1) * width].astype(jnp.float32)
            + (own[...] + core[...].astype(jnp.float32))
            + pair[...].astype(jnp.float32)
        )
    summed = jnp.concatenate(summed, axis=1)
    center = jnp.mean(summed, axis=-1, keepdims=True)
    moved = summed - center
    spread = jnp.mean(moved * moved, axis=-1, keepdims=True)
    normed = moved * lax.rsqrt(spread + 1e-05)
    sentences = out.shape[0]
    members = (
        identity[...] == lax.broadcasted_iota(jnp.int32, (sentences, tokens.shape[0]), 0)
    ).astype(jnp.float32)
    sums = dot(members, normed, (1, 0), precision=lax.Precision.HIGHEST)
    unit = unit_of(sums / jnp.sum(members, axis=1, keepdims=True))
    sort = (order[...] == lax.broadcasted_iota(jnp.int32, (sentences, sentences), 0)).astype(
        jnp.bfloat16
    )
    out[...] = dot(sort, unit, (1, 0)).astype(jnp.bfloat16)


def target_kernel(slots, tiles, out):
    out[...] = unit_of(tiles[...].astype(jnp.float32))


def listed_units(slot_block, targets):
    features = targets.shape[1]
    return pl.pallas_call(
        target_kernel,
        out_shape=shape((MOST * TBLK, features), jnp.bfloat16),
        grid_spec=pltpu.PrefetchScalarGridSpec(
            num_scalar_prefetch=1,
            grid=(MOST,),
            in_specs=[pl.BlockSpec((TBLK, features), lambda slot, slots: (slots[slot], 0))],
            out_specs=pl.BlockSpec((TBLK, features), lambda slot, slots: (slot, 0)),
        ),
        compiler_params=pltpu.CompilerParams(vmem_limit_bytes=40 * 2**20),
        cost_estimate=pl.CostEstimate(
            flops=8 * MOST * TBLK * features,
            bytes_accessed=4 * MOST * TBLK * features,
            transcendentals=0,
        ),
    )(slot_block, targets)


def score_kernel(slots, valid, place, units, *refs):
    parts, (expo, columns, row_total, held) = refs[:-4], refs[-4:]
    gather_refs(parts, held)
    rows = expo.shape[0]
    sort = (place[...] == lax.broadcasted_iota(jnp.int32, (rows, rows), 0)).astype(jnp.bfloat16)
    block = dot(sort, held[...], (1, 0)).astype(jnp.bfloat16)
    columns[...] = jnp.zeros_like(columns)
    total = jnp.zeros((rows, 1), jnp.float32)
    for slot in range(MOST):
        part = pl.ds(slot * TBLK, TBLK)
        weight = valid[slot].astype(jnp.float32)
        values = jnp.exp(SCORE_SCALE * dot(block, units[part, :], (1, 1))) * weight
        expo[:, part] = values
        total = total + jnp.sum(values, axis=1, keepdims=True)
        column = jnp.sum(values, axis=0, keepdims=True)

        @pl.when(valid[slot] > 0)
        def _():
            columns[pl.ds(slots[slot], 1), :] = column

    row_total[...] = total


def extra_columns(values):
    lane = lax.broadcasted_iota(jnp.int32, (values[0].shape[0], LANES), 1)
    out = jnp.zeros(lane.shape, jnp.float32)
    for index, value in enumerate(values):
        out = jnp.where(lane == index, value, out)
    return out


def thirds(value):
    first = value.astype(jnp.bfloat16).astype(jnp.float32)
    second = (value - first).astype(jnp.bfloat16).astype(jnp.float32)
    return [first, second, value - first - second]


def match_kernel(slots, valid, expo, columns, row_total, units, own, sent):
    rows = own.shape[0]
    features = units.shape[1]
    mass = jnp.zeros((expo.shape[0], 1), jnp.float32)
    weights = []
    for slot in range(MOST):
        part = pl.ds(slot * TBLK, TBLK)
        values = expo[:, part]
        listed = valid[slot].astype(jnp.float32)
        divisor = jnp.where(listed > 0, columns[pl.ds(slots[slot], 1), :], 1.0)
        mutual = values * (values / divisor)
        mass = mass + jnp.sum(mutual, axis=1, keepdims=True)
        weights.append(mutual.astype(jnp.bfloat16))
    numer = dot(jnp.concatenate(weights, axis=1), units[...], (1, 0))
    totals = row_total[...]
    zero = jnp.zeros((rows, 1), jnp.float32)
    own[:, :features] = numer[:rows]
    own[:, features:] = extra_columns([mass[:rows], zero, zero, totals[:rows]])
    sent[:, :features] = numer[rows:].astype(jnp.bfloat16)
    sent[:, features:] = extra_columns(thirds(mass[rows:]) + thirds(totals[rows:])).astype(
        jnp.bfloat16
    )


def finish_kernel(own, *refs):
    parts, (matched, log_mass) = refs[:-2], refs[-2:]
    rows, features = matched.shape
    total = own[...]
    for part in parts:
        total = total + part[...].astype(jnp.float32)
    numer = total[:, :features]
    square = jnp.mean(numer * numer, axis=-1, keepdims=True)
    matched[...] = (numer * lax.rsqrt(square + 1e-06)).astype(jnp.bfloat16)
    extra = total[:, features:]
    lane = lax.broadcasted_iota(jnp.int32, extra.shape, 1)
    mass = jnp.sum(jnp.where(lane < 3, extra, 0.0), axis=1, keepdims=True)
    whole = jnp.sum(jnp.where(lane < 3, 0.0, extra), axis=1, keepdims=True)
    ratio = mass / whole
    same = lax.broadcasted_iota(jnp.int32, (rows, rows), 0) == lax.broadcasted_iota(
        jnp.int32, (rows, rows), 1
    )
    log_mass[...] = jnp.log(jnp.sum(jnp.where(same, ratio, 0.0), axis=0, keepdims=True))


def over_square(piece):
    half = piece.shape[0] // 2 // 16 * 16
    over_x = swap(piece, "src", 2)
    over_y = swap(piece, "groups", 1)
    return [
        piece,
        over_x,
        over_y,
        swap(over_x[:half], "groups", 1),
        swap(over_y[half:], "src", 2),
    ]


def far_pieces(half):
    held = half
    for axis, bit in [("tgt", b) for b in bits_of("tgt", 2)] + [("src", b) for b in bits_of("src", 4)]:
        held = jnp.concatenate([held, swap(held, axis, bit)])
    return held[half.shape[0] :]


def feed_forward(tokens, inner_weight, outer_weight, other_work):
    units, features = inner_weight.shape
    half = units // 2
    start = lax.axis_index("groups") * half
    inner_half = lax.dynamic_slice_in_dim(inner_weight, start, half)
    outer_half = lax.dynamic_slice_in_dim(outer_weight, start, half)
    inner_far = over_square(far_pieces(inner_half))
    near_sent = jnp.concatenate([inner_half, outer_half])
    near_x = swap(near_sent, "src", 2)
    near_y = swap(near_x, "groups", 1)
    outer_half, other_work = lax.optimization_barrier((outer_half, other_work))
    columns = 2
    width = features // columns
    outer_far = [
        over_square(far_pieces(outer_half[:, c * width : (c + 1) * width])) for c in range(columns)
    ]
    neighbour = swap(tokens, "tgt", 1)
    shared = [tokens, neighbour, swap(tokens, "src", 1), swap(neighbour, "src", 1)]
    near_hidden = hidden_units(shared, [inner_weight, near_x[:half], near_y[:half]])
    far_hidden = hidden_units(shared, inner_far)
    summands = []
    for c in range(columns):
        near = [
            w[:, c * width : (c + 1) * width]
            for w in (outer_weight, near_x[half:], near_y[half:])
        ]
        own, pair, own_sent, pair_sent = partial_sums(near_hidden, far_hidden, near + outer_far[c])
        pair = pair + swap(pair_sent, "src", 1).astype(jnp.float32)
        summands += [own, swap(own_sent, "src", 1), swap(pair.astype(jnp.bfloat16), "tgt", 1)]
    return summands, other_work


def on_device(tokens, sentence_ids, inner_weight, outer_weight, grid_rows, candidates, targets):
    features = tokens.shape[1]
    src_count = lax.axis_size("src")
    tgt_count = lax.axis_size("tgt")
    src_index = lax.axis_index("src")
    tgt_index = lax.axis_index("tgt")
    per_block = SENT_DEV // src_count
    block_rows = tgt_count * SENT_DEV

    column_blocks = targets.shape[0] // TBLK
    cand_row = candidates[0]
    listed = (cand_row // column_blocks == tgt_index).astype(jnp.int32)
    ranks = jnp.cumsum(listed) - 1
    chosen = (
        (listed[None, :] == 1) & (ranks[None, :] == jnp.arange(MOST, dtype=jnp.int32)[:, None])
    ).astype(jnp.int32)
    slot_block = jnp.sum(chosen * (cand_row % column_blocks)[None, :], axis=1)
    valid = jnp.sum(chosen, axis=1)
    target_units = listed_units(slot_block, targets)

    summands, target_units = feed_forward(tokens, inner_weight, outer_weight, target_units)
    order_key = (grid_rows // block_rows ^ src_index) * per_block + grid_rows % per_block
    held = local_call(
        functools.partial(pool_kernel, len(summands) // 3),
        shape((SENT_DEV, features), jnp.bfloat16),
        (sentence_ids, order_key.reshape(1, -1), tokens, *summands),
        20 * tokens.shape[0] * features,
    )
    held = held.reshape(src_count, 1, per_block, features)
    for bit in reversed(bits_of("src", 1)):
        held = jnp.concatenate([held[:bit], swap(held[bit:], "src", bit)], axis=1)
    mine = held.reshape(SENT_DEV, features)
    parts = [mine] + [swap(mine, "tgt", offset) for offset in range(1, tgt_count)]
    origin = jnp.arange(1, dtype=jnp.int32)
    for bit in reversed(bits_of("src", 1)):
        origin = jnp.concatenate([origin, origin ^ bit])
    from_src = (origin ^ src_index)[None, :, None]
    from_tgt = (jnp.arange(tgt_count, dtype=jnp.int32) ^ tgt_index)[:, None, None]
    place = (from_src * tgt_count + from_tgt) * per_block + jnp.arange(per_block, dtype=jnp.int32)
    place = place.reshape(1, -1) ^ (tgt_index * SENT_DEV)

    pairs = MOST * TBLK
    expo, column_total, row_total = local_call(
        score_kernel,
        (
            shape((block_rows, pairs), jnp.float32),
            shape((column_blocks, TBLK), jnp.float32),
            shape((block_rows, 1), jnp.float32),
        ),
        (slot_block, valid, place, target_units, *parts),
        2 * block_rows * pairs * features,
        (pltpu.VMEM((block_rows, features), jnp.bfloat16),),
        scalars=2,
    )
    for bit in bits_of("src", 1):
        column_total = column_total + swap(column_total, "src", bit)
    own, sent = local_call(
        match_kernel,
        (
            shape((SENT_DEV, features + LANES), jnp.float32),
            shape((block_rows - SENT_DEV, features + LANES), jnp.bfloat16),
        ),
        (slot_block, valid, expo, column_total, row_total, target_units),
        2 * block_rows * pairs * features,
        scalars=2,
    )
    received = [
        swap(sent[(offset - 1) * SENT_DEV : offset * SENT_DEV], "tgt", offset)
        for offset in range(1, tgt_count)
    ]
    matched, log_mass = local_call(
        finish_kernel,
        (shape((SENT_DEV, features), jnp.bfloat16), shape((1, SENT_DEV), jnp.float32)),
        (own, *received),
        8 * SENT_DEV * features,
    )
    return (matched, log_mass.reshape(SENT_DEV))


def solution(mesh):
    in_specs = (
        P(("groups", "src", "tgt"), None),
        P(("groups", "src", "tgt"), None),
        P(("src", "tgt"), None),
        P(("src", "tgt"), None),
        P(("groups", "src", "tgt")),
        P(("groups", "src"), None),
        P(("groups", "tgt"), None),
    )
    out_specs = (P(("groups", "src", "tgt"), None), P(("groups", "src", "tgt")))
    return jax.shard_map(
        on_device, mesh=mesh, in_specs=in_specs, out_specs=out_specs, check_vma=False
    )
```

time: 249 us -> 128 us (0.51)
  waiting for transfers between devices: 157 us -> 58.2 us
  blocking collectives: 34.2 us -> 0 us
  starting transfers between devices: 3.4 us -> 36.7 us
  matrix products: 25.1 us -> 0 us
  Pallas kernels: 0 us -> 16.2 us
  between operations: 14.6 us -> 0.97 us
  local copies, waits for them, and re-layouts: 4.84 us -> 10.2 us
  other arithmetic: 9.67 us -> 5.19 us
    all_gather x2 -> x0, waiting for transfers between devices: 144 us -> none  [the longest x1 75.4 us: on_device(): lax.all_gather(outer_weight, ('src', 'tgt'), axis=0, tiled=True)]
    ppermute x0 -> x36, waiting for transfers between devices: none -> 58.2 us  [swap(): lax.ppermute(values, axis, [(i, i ^ offset) for i in range(lax.axis_size(...]
    ppermute x0 -> x36, starting transfers between devices: none -> 36.7 us  [swap(): lax.ppermute(values, axis, [(i, i ^ offset) for i in range(lax.axis_size(...]
    dot_general x7 -> x0, matrix products: 25.1 us -> none  [the longest x1 19.3 us: on_device(): jnp.dot(inner_units(tokens, lax.all_gather(inner_weight, ('src', 'tgt'),...]
    psum x2 -> x0, blocking collectives: 19.9 us -> none  [the longest x1 10.1 us: on_device(): column_total = lax.psum(column_local, 'src')]
    pallas_call x0 -> x9, Pallas kernels: none -> 16.2 us  [the longest x8 14.8 us: local_call(): pl.pallas_call(kernel, out_shape=out_shape, in_specs=[pl.BlockSpec(memory...]
    all_gather x1 -> x0, blocking collectives: 14.2 us -> none  [on_device(): lax.all_gather(relayed, 'tgt', axis=1, tiled=True)]
    reduce_scatter x1 -> x0, waiting for transfers between devices: 7.57 us -> none  [on_device(): lax.psum_scatter(numer, 'tgt', scatter_dimension=0, tiled=True)]
  transfers between devices with their start and end apart: 4 -> 36, of which waited for: 4 -> 20; matrix products, arithmetic and copies ran while one was open for 5% -> 7% of each run, Pallas kernels for 0% -> 7%
where the time goes in v2:
time: 128 us; the launch traced here: 127 us
  waiting for transfers between devices  58.2 us (45%)
  starting transfers between devices  36.7 us (29%)
  Pallas kernels  16.2 us (13%)
  local copies, waits for them, and re-layouts  10.2 us (8%)
  other arithmetic  5.19 us (4%)
    ppermute x36, waiting for transfers between devices, swap(): lax.ppermute(values, axis, [(i, i ^ offset) for i in range(lax.axis_size(...  58.2 us
    ppermute x36, starting transfers between devices, swap(): lax.ppermute(values, axis, [(i, i ^ offset) for i in range(lax.axis_size(...  36.7 us
    pallas_call x8, Pallas kernels, local_call(): pl.pallas_call(kernel, out_shape=out_shape, in_specs=[pl.BlockSpec(memory...  14.8 us
    unnamed x22, local copies, waits for them, and re-layouts  5.18 us
  transfers between devices with their start and end apart: 36, of which 20 were waited for; matrix products, arithmetic and copies ran while one was open for 7% of the time, Pallas kernels for 7%

profile of v2, /device:TPU:0, one launch (start us, length us, event | category | flops | bytes accessed | tf_op | source)
XLA Modules:
  0.0 127.5 jit_solution(10075519183678726293)
XLA Ops:
  0.6 1.7 %constant_dynamic-slice_fusion = bf16[128,1024]{1,0:T(8,128)(2,1)} fusion(bf16[256,1024]{1,0:T(8,128)(2,1)} %refs_4_.1, s32[]{:T(128)S(6)} %select_n.35), kind=kLoop, calls=%fused_computation.35 | loop fusion | bytes 524292 | tf_op jit(solution)/shard_map/dynamic_slice | solution.py:283
  2.4 4.0 %collective-permute-start.5 = (bf16[128,1024]{1,0:T(8,128)(2,1)}, bf16[128,1024]{1,0:T(8,128)(2,1)S(1)}, u32[]{:S(2)}, u32[]{:S(2)}) collective-permute-start(bf16[128,1024]{1,0:T(8,128)(2,1)} %constant_dynamic-slice_fusion), channel_id=1, source_target_pairs={{0,2},{1,3},{2,0},{3,1},{4,6},{5,7},{6,4},{7,5},{8,10},{9,11},{10,... | collective-permute-start | bytes 786440 | tf_op jit(solution)/shard_map/ppermute | solution.py:29
  6.4 1.6 %collective-permute-start = (bf16[256,1024]{1,0:T(8,128)(2,1)}, bf16[256,1024]{1,0:T(8,128)(2,1)S(1)}, u32[]{:S(2)}, u32[]{:S(2)}) collective-permute-start(bf16[256,1024]{1,0:T(8,128)(2,1)} %tokens.1), channel_id=1, source_target_pairs={{0,1},{1,0},{2,3},{3,2},{4,5},{5,4},{6,7},{7,6},{8,9},{9,8},{10,11... | collective-permute-start | bytes 1572872 | tf_op jit(solution)/shard_map/ppermute | solution.py:29
  8.0 1.0 constant_dynamic-slice_fusion.1
  9.7 1.8 %pad_maximum_fusion = bf16[256,1024]{1,0:T(8,128)(2,1)} fusion(bf16[128,1024]{1,0:T(8,128)(2,1)S(1)} %constant_dynamic-slice_fusion.1, bf16[128,1024]{1,0:T(8,128)(2,1)} %constant_dynamic-slice_fusion), kind=kLoop, calls=%fused_computation | loop fusion | flops 1048576 | bytes 1048576 | tf_op jit(solution)/shard_map/concatenate | solution.py:286
  11.5 1.5 %collective-permute-start.3 = (bf16[256,1024]{1,0:T(8,128)(2,1)}, bf16[256,1024]{1,0:T(8,128)(2,1)}, u32[]{:S(2)}, u32[]{:S(2)}) collective-permute-start(bf16[256,1024]{1,0:T(8,128)(2,1)} %pad_maximum_fusion), channel_id=1, source_target_pairs={{0,8},{4,12},{8,0},{12,4},{1,9},{5,13},{9,1},{13,5},{2,10},{6,14},... | collective-permute-start | bytes 1572872 | tf_op jit(solution)/shard_map/ppermute | solution.py:29
  14.7 3.4 %copy-done = bf16[4096,1024]{1,0:T(8,128)(2,1)S(1)} copy-done((bf16[4096,1024]{1,0:T(8,128)(2,1)S(1)}, bf16[4096,1024]{1,0:T(8,128)(2,1)}, u32[]{:S(2)}) %copy-start) | copy-done | bytes 8388632
  18.1 1.4 %shard_map.86.units = bf16[1024,1024]{1,0:T(8,128)(2,1)S(1)} custom-call(s32[4]{0:T(128)S(1)} %get-tuple-element.37.slots, bf16[4096,1024]{1,0:T(8,128)(2,1)S(1)} %copy-done), custom_call_target="tpu_custom_call" | custom-call | flops 8388608 | bytes 4194304 | tf_op jit(solution)/shard_map/pallas_call | solution.py:160
  20.0 2.6 %collective-permute-start.10 = (bf16[128,512]{1,0:T(8,128)(2,1)S(1)}, bf16[128,512]{1,0:T(8,128)(2,1)S(1)}, u32[]{:S(2)}, u32[]{:S(2)}) collective-permute-start(bf16[128,512]{1,0:T(8,128)(2,1)S(1)} %get-tuple-element.47), channel_id=1, source_target_pairs={{0,2},{1,3},{2,0},{3,1},{4,6},{5,7},{6,4},{7,5},{8,10},{9,11},{10,... | collective-permute-start | bytes 393224 | tf_op jit(solution)/shard_map/ppermute | solution.py:29
  22.6 9.4 %collective-permute-done.18.refs_3_ = bf16[128,512]{1,0:T(8,128)(2,1)S(1)} collective-permute-done((bf16[128,512]{1,0:T(8,128)(2,1)S(1)}, bf16[128,512]{1,0:T(8,128)(2,1)S(1)}, u32[]{:S(2)}, u32[]{:S(2)}) %collective-permute-start.18) | collective-permute-done | bytes 131104 | tf_op jit(solution)/shard_map/ppermute | solution.py:29
  32.5 0.9 collective-permute-done.10.refs_3_
  33.4 1.5 %collective-permute-start.20 = (bf16[128,512]{1,0:T(8,128)(2,1)S(1)}, bf16[128,512]{1,0:T(8,128)(2,1)S(1)}, u32[]{:S(2)}, u32[]{:S(2)}) collective-permute-start(bf16[128,512]{1,0:T(8,128)(2,1)S(1)} %collective-permute-done.18.refs_3_), channel_id=1, source_target_pairs={{0,16},{16,0},{1,17},{17,1},{2,18},{18,2},{3,19},{19,3},{4,20},{20... | collective-permute-start | bytes 393224 | tf_op jit(solution)/shard_map/ppermute | solution.py:29
  36.1 2.3 %collective-permute-done.19.refs_4_ = bf16[128,512]{1,0:T(8,128)(2,1)S(1)} collective-permute-done((bf16[128,512]{1,0:T(8,128)(2,1)S(1)}, bf16[128,512]{1,0:T(8,128)(2,1)S(1)}, u32[]{:S(2)}, u32[]{:S(2)}) %collective-permute-start.19) | collective-permute-done | bytes 131104 | tf_op jit(solution)/shard_map/ppermute | solution.py:29
  38.4 1.5 %collective-permute-start.7 = (bf16[128,1024]{1,0:T(8,128)(2,1)S(1)}, bf16[128,1024]{1,0:T(8,128)(2,1)S(1)}, u32[]{:S(2)}, u32[]{:S(2)}) collective-permute-start(bf16[128,1024]{1,0:T(8,128)(2,1)S(1)} %collective-permute-done.5.refs_4_), channel_id=1, source_target_pairs={{0,16},{16,0},{1,17},{17,1},{2,18},{18,2},{3,19},{19,3},{4,20},{20... | collective-permute-start | bytes 786440 | tf_op jit(solution)/shard_map/ppermute | solution.py:29
  40.5 1.0 slice.108.refs_5_
  41.4 1.2 collective-permute-done.6.refs_5_
  42.9 11.0 %collective-permute-done.7.refs_6_ = bf16[128,1024]{1,0:T(8,128)(2,1)S(1)} collective-permute-done((bf16[128,1024]{1,0:T(8,128)(2,1)S(1)}, bf16[128,1024]{1,0:T(8,128)(2,1)S(1)}, u32[]{:S(2)}, u32[]{:S(2)}) %collective-permute-start.7) | collective-permute-done | bytes 262176 | tf_op jit(solution)/shard_map/ppermute | solution.py:29
  53.9 1.5 %collective-permute-start.8 = (bf16[64,1024]{1,0:T(8,128)(2,1)S(1)}, bf16[64,1024]{1,0:T(8,128)(2,1)S(1)}, u32[]{:S(2)}, u32[]{:S(2)}) collective-permute-start(bf16[64,1024]{1,0:T(8,128)(2,1)S(1)} %slice.110), channel_id=1, source_target_pairs={{0,16},{16,0},{1,17},{17,1},{2,18},{18,2},{3,19},{19,3},{4,20},{20... | collective-permute-start | bytes 393224 | tf_op jit(solution)/shard_map/ppermute | solution.py:29
  55.5 1.0 fusion.6
  57.2 2.4 %collective-permute-done.8.refs_7_ = bf16[64,1024]{1,0:T(8,128)(2,1)S(1)} collective-permute-done((bf16[64,1024]{1,0:T(8,128)(2,1)S(1)}, bf16[64,1024]{1,0:T(8,128)(2,1)S(1)}, u32[]{:S(2)}, u32[]{:S(2)}) %collective-permute-start.8) | collective-permute-done | bytes 131104 | tf_op jit(solution)/shard_map/ppermute | solution.py:29
  59.6 1.5 %collective-permute-start.21 = (bf16[64,512]{1,0:T(8,128)(2,1)S(1)}, bf16[64,512]{1,0:T(8,128)(2,1)S(1)}, u32[]{:S(2)}, u32[]{:S(2)}) collective-permute-start(bf16[64,512]{1,0:T(8,128)(2,1)S(1)} %slice.118), channel_id=1, source_target_pairs={{0,16},{16,0},{1,17},{17,1},{2,18},{18,2},{3,19},{19,3},{4,20},{20... | collective-permute-start | bytes 196616 | tf_op jit(solution)/shard_map/ppermute | solution.py:29
  62.2 2.2 %shard_map.88.far_hidden = bf16[1024,512]{1,0:T(8,128)(2,1)S(1)} custom-call(bf16[256,1024]{1,0:T(8,128)(2,1)S(1)} %copy-done.1, bf16[256,1024]{1,0:T(8,128)(2,1)S(1)} %collective-permute-done.refs_1_, bf16[256,1024]{1,0:T(8,128)(2,1)S(1)} %collective-permute-done.1.refs_2_, bf16[256,1024]{1,0:T(8,128)(2,1)S(1)} %collective-permute-done.2.refs_3_, ...), custom_call_target="tpu_custom_call" | custom-call | flops 1073741824 | bytes 4194304 | tf_op jit(solution)/shard_map/pallas_call | solution.py:35
  64.5 2.2 %shard_map.87.near_hidden = bf16[1024,512]{1,0:T(8,128)(2,1)S(1)} custom-call(bf16[256,1024]{1,0:T(8,128)(2,1)S(1)} %copy-done.1, bf16[256,1024]{1,0:T(8,128)(2,1)S(1)} %collective-permute-done.refs_1_, bf16[256,1024]{1,0:T(8,128)(2,1)S(1)} %collective-permute-done.1.refs_2_, bf16[256,1024]{1,0:T(8,128)(2,1)S(1)} %collective-permute-done.2.refs_3_, ...), custom_call_target="tpu_custom_call" | custom-call | flops 1073741824 | bytes 4194304 | tf_op jit(solution)/shard_map/pallas_call | solution.py:35
  66.7 1.7 %shard_map.90 = (f32[256,512]{1,0:T(8,128)S(1)}, f32[256,512]{1,0:T(8,128)S(1)}, bf16[256,512]{1,0:T(8,128)(2,1)}, bf16[256,512]{1,0:T(8,128)(2,1)S(1)}) custom-call(bf16[1024,512]{1,0:T(8,128)(2,1)S(1)} %shard_map.87.near_hidden, bf16[1024,512]{1,0:T(8,128)(2,1)S(1)} %shard_map.88.far_hidden, bf16[256,512]{1,0:T(8,128)(2,1)S(1)} %get-tuple-element.44.refs_0_, ...), custom_call_target="tpu_custom_call" | custom-call | flops 1073741824 | bytes 4718592 | tf_op jit(solution)/shard_map/pallas_call | solution.py:35
  69.0 1.8 %collective-permute-start.14 = (bf16[64,512]{1,0:T(8,128)(2,1)S(1)}, bf16[64,512]{1,0:T(8,128)(2,1)S(1)}, u32[]{:S(2)}, u32[]{:S(2)}) collective-permute-start(bf16[64,512]{1,0:T(8,128)(2,1)S(1)} %slice.115), channel_id=1, source_target_pairs={{0,8},{4,12},{8,0},{12,4},{1,9},{5,13},{9,1},{13,5},{2,10},{6,14},... | collective-permute-start | bytes 196616 | tf_op jit(solution)/shard_map/ppermute | solution.py:29
  70.8 2.2 %collective-permute-done.13.refs_6_ = bf16[64,512]{1,0:T(8,128)(2,1)S(1)} collective-permute-done((bf16[64,512]{1,0:T(8,128)(2,1)S(1)}, bf16[64,512]{1,0:T(8,128)(2,1)S(1)}, u32[]{:S(2)}, u32[]{:S(2)}) %collective-permute-start.13) | collective-permute-done | bytes 65568 | tf_op jit(solution)/shard_map/ppermute | solution.py:29
  73.3 1.7 %shard_map.89 = (f32[256,512]{1,0:T(8,128)S(1)}, f32[256,512]{1,0:T(8,128)S(1)}, bf16[256,512]{1,0:T(8,128)(2,1)}, bf16[256,512]{1,0:T(8,128)(2,1)S(1)}) custom-call(bf16[1024,512]{1,0:T(8,128)(2,1)S(1)} %shard_map.87.near_hidden, bf16[1024,512]{1,0:T(8,128)(2,1)S(1)} %shard_map.88.far_hidden, bf16[256,512]{1,0:T(8,128)(2,1)S(1)} %get-tuple-element.45.refs_0_, ...), custom_call_target="tpu_custom_call" | custom-call | flops 1073741824 | bytes 4718592 | tf_op jit(solution)/shard_map/pallas_call | solution.py:35
  76.9 0.8 add_convert_fusion.1
  77.7 1.4 %collective-permute-start.17 = (bf16[256,512]{1,0:T(8,128)(2,1)}, bf16[256,512]{1,0:T(8,128)(2,1)}, u32[]{:S(2)}, u32[]{:S(2)}) collective-permute-start(bf16[256,512]{1,0:T(8,128)(2,1)} %add_convert_fusion.1), channel_id=1, source_target_pairs={{0,1},{1,0},{2,3},{3,2},{4,5},{5,4},{6,7},{7,6},{8,9},{9,8},{10,11... | collective-permute-start | bytes 786440 | tf_op jit(solution)/shard_map/ppermute | solution.py:29
  79.2 6.6 %collective-permute-done.25.refs_5_ = bf16[256,512]{1,0:T(8,128)(2,1)} collective-permute-done((bf16[256,512]{1,0:T(8,128)(2,1)}, bf16[256,512]{1,0:T(8,128)(2,1)}, u32[]{:S(2)}, u32[]{:S(2)}) %collective-permute-start.25) | collective-permute-done | bytes 262176 | tf_op jit(solution)/shard_map/ppermute | solution.py:29
  85.8 5.2 %collective-permute-done.17.refs_2_ = bf16[256,512]{1,0:T(8,128)(2,1)} collective-permute-done((bf16[256,512]{1,0:T(8,128)(2,1)}, bf16[256,512]{1,0:T(8,128)(2,1)}, u32[]{:S(2)}, u32[]{:S(2)}) %collective-permute-start.17) | collective-permute-done | bytes 262176 | tf_op jit(solution)/shard_map/ppermute | solution.py:29
  91.0 1.0 copy-done.4
  92.0 2.4 %shard_map.91 = bf16[32,1024]{1,0:T(8,128)(2,1)S(1)} custom-call(s32[1,256]{1,0:T(1,128)S(1)} %copy-done.5, s32[1,32]{1,0:T(1,128)S(1)} %fusion.4.order, bf16[256,1024]{1,0:T(8,128)(2,1)S(1)} %copy-done.1, f32[256,512]{1,0:T(8,128)S(1)} %copy-done.4, bf16[256,512]{1,0:T(8,128)(2,1)} %collective-permute-done.15.refs_1_, ...), custom_call_target="tpu_custom_call" | custom-call | flops 5242880 | bytes 2688128 | tf_op jit(solution)/shard_map/pallas_call | solution.py:35
  94.5 1.8 %collective-permute-start.26 = (bf16[2,1,8,1024]{3,2,1,0:T(8,128)(2,1)S(1)}, bf16[2,1,8,1024]{3,2,1,0:T(8,128)(2,1)S(1)}, u32[]{:S(2)}, u32[]{:S(2)}) collective-permute-start(bf16[2,1,8,1024]{3,2,1,0:T(8,128)(2,1)S(1)} %get-tuple-element.54), channel_id=1, source_target_pairs={{0,8},{4,12},{8,0},{12,4},{1,9},{5,13},{9,1},{13,5},{2,10},{6,14},... | collective-permute-start | bytes 98312 | tf_op jit(solution)/shard_map/ppermute | solution.py:29
  96.3 2.2 %collective-permute-done.26 = bf16[2,1,8,1024]{3,2,1,0:T(8,128)(2,1)S(1)} collective-permute-done((bf16[2,1,8,1024]{3,2,1,0:T(8,128)(2,1)S(1)}, bf16[2,1,8,1024]{3,2,1,0:T(8,128)(2,1)S(1)}, u32[]{:S(2)}, u32[]{:S(2)}) %collective-permute-start.26) | collective-permute-done | bytes 32800 | tf_op jit(solution)/shard_map/ppermute | solution.py:29
  98.6 1.1 collective-permute-done.27
  100.1 1.2 collective-permute-start.29
  101.3 2.9 %collective-permute-start.30 = (bf16[32,1024]{1,0:T(8,128)(2,1)S(1)}, bf16[32,1024]{1,0:T(8,128)(2,1)S(1)}, u32[]{:S(2)}, u32[]{:S(2)}) collective-permute-start(bf16[32,1024]{1,0:T(8,128)(2,1)S(1)} %maximum_bitcast_fusion.refs_0_), channel_id=1, source_target_pairs={{0,3},{1,2},{2,1},{3,0},{4,7},{5,6},{6,5},{7,4},{8,11},{9,10},{10,... | collective-permute-start | bytes 196616 | tf_op jit(solution)/shard_map/ppermute | solution.py:29
  104.9 3.8 %collective-permute-done.29.refs_2_ = bf16[32,1024]{1,0:T(8,128)(2,1)S(1)} collective-permute-done((bf16[32,1024]{1,0:T(8,128)(2,1)S(1)}, bf16[32,1024]{1,0:T(8,128)(2,1)S(1)}, u32[]{:S(2)}, u32[]{:S(2)}) %collective-permute-start.29) | collective-permute-done | bytes 65568 | tf_op jit(solution)/shard_map/ppermute | solution.py:29
  108.7 2.7 %shard_map.92 = (f32[128,1024]{1,0:T(8,128)S(1)}, f32[16,256]{1,0:T(8,128)S(1)}, f32[128,1]{1,0:T(8,128)S(1)}) custom-call(s32[4]{0:T(128)S(1)} %get-tuple-element.37.slots, s32[4]{0:T(128)S(1)} %get-tuple-element.36.valid, s32[1,128]{1,0:T(1,128)S(1)} %xor.32.place, bf16[1024,1024]{1,0:T(8,128)(2,1)S(1)} %shard_map.86.units, ...), custom_call_target="tpu_custom_call" | custom-call | flops 268435456 | bytes 2901024 | tf_op jit(solution)/shard_map/pallas_call | solution.py:35
  111.5 1.2 collective-permute-done.31
  112.7 1.5 %collective-permute-start.32 = (f32[16,256]{1,0:T(8,128)S(1)}, f32[16,256]{1,0:T(8,128)S(1)}, u32[]{:S(2)}, u32[]{:S(2)}) collective-permute-start(f32[16,256]{1,0:T(8,128)S(1)} %add.97), channel_id=1, source_target_pairs={{0,8},{4,12},{8,0},{12,4},{1,9},{5,13},{9,1},{13,5},{2,10},{6,14},... | collective-permute-start | bytes 49160 | tf_op jit(solution)/shard_map/ppermute | solution.py:29
  114.1 2.2 %collective-permute-done.32 = f32[16,256]{1,0:T(8,128)S(1)} collective-permute-done((f32[16,256]{1,0:T(8,128)S(1)}, f32[16,256]{1,0:T(8,128)S(1)}, u32[]{:S(2)}, u32[]{:S(2)}) %collective-permute-start.32) | collective-permute-done | bytes 16416 | tf_op jit(solution)/shard_map/ppermute | solution.py:29
  116.4 1.1 shard_map.93
  117.5 1.4 %collective-permute-start.33 = (bf16[32,1152]{1,0:T(8,128)(2,1)S(1)}, bf16[32,1152]{1,0:T(8,128)(2,1)S(1)}, u32[]{:S(2)}, u32[]{:S(2)}) collective-permute-start(bf16[32,1152]{1,0:T(8,128)(2,1)S(1)} %get-tuple-element.50), channel_id=1, source_target_pairs={{0,1},{1,0},{2,3},{3,2},{4,5},{5,4},{6,7},{7,6},{8,9},{9,8},{10,11... | collective-permute-start | bytes 221192 | tf_op jit(solution)/shard_map/ppermute | solution.py:29
  118.9 1.0 collective-permute-start.34
  119.9 2.0 %collective-permute-start.35 = (bf16[32,1152]{1,0:T(8,128)(2,1)S(1)}, bf16[32,1152]{1,0:T(8,128)(2,1)S(1)}, u32[]{:S(2)}, u32[]{:S(2)}) collective-permute-start(bf16[32,1152]{1,0:T(8,128)(2,1)S(1)} %get-tuple-element.48), channel_id=1, source_target_pairs={{0,3},{1,2},{2,1},{3,0},{4,7},{5,6},{6,5},{7,4},{8,11},{9,10},{10,... | collective-permute-start | bytes 221192 | tf_op jit(solution)/shard_map/ppermute | solution.py:29
  122.1 4.5 %collective-permute-done.34.refs_1_ = bf16[32,1152]{1,0:T(8,128)(2,1)S(1)} collective-permute-done((bf16[32,1152]{1,0:T(8,128)(2,1)S(1)}, bf16[32,1152]{1,0:T(8,128)(2,1)S(1)}, u32[]{:S(2)}, u32[]{:S(2)}) %collective-permute-start.34) | collective-permute-done | bytes 73760 | tf_op jit(solution)/shard_map/ppermute | solution.py:29
  (89 shorter events, 12.3 us)
Async XLA Ops:
  0.6 39.3 %copy-start.1 = (bf16[256,1024]{1,0:T(8,128)(2,1)S(1)}, bf16[256,1024]{1,0:T(8,128)(2,1)}, u32[]{:S(2)}) copy-start(bf16[256,1024]{1,0:T(8,128)(2,1)} %tokens.1) | copy-start | bytes 1572868
  2.4 33.1 %collective-permute-start.5 = (bf16[128,1024]{1,0:T(8,128)(2,1)}, bf16[128,1024]{1,0:T(8,128)(2,1)S(1)}, u32[]{:S(2)}, u32[]{:S(2)}) collective-permute-start(bf16[128,1024]{1,0:T(8,128)(2,1)} %constant_dynamic-slice_fusion), channel_id=1, source_target_pairs={{0,2},{1,3},{2,0},{3,1},{4,6},{5,7},{6,4},{7,5},{8,10},{9,11},{10,... | collective-permute-start | bytes 786440 | tf_op jit(solution)/shard_map/ppermute | solution.py:29
  6.4 33.5 %collective-permute-start = (bf16[256,1024]{1,0:T(8,128)(2,1)}, bf16[256,1024]{1,0:T(8,128)(2,1)S(1)}, u32[]{:S(2)}, u32[]{:S(2)}) collective-permute-start(bf16[256,1024]{1,0:T(8,128)(2,1)} %tokens.1), channel_id=1, source_target_pairs={{0,1},{1,0},{2,3},{3,2},{4,5},{5,4},{6,7},{7,6},{8,9},{9,8},{10,11... | collective-permute-start | bytes 1572872 | tf_op jit(solution)/shard_map/ppermute | solution.py:29
  8.9 0.7 copy-start.6
  11.5 23.5 %collective-permute-start.3 = (bf16[256,1024]{1,0:T(8,128)(2,1)}, bf16[256,1024]{1,0:T(8,128)(2,1)}, u32[]{:S(2)}, u32[]{:S(2)}) collective-permute-start(bf16[256,1024]{1,0:T(8,128)(2,1)} %pad_maximum_fusion), channel_id=1, source_target_pairs={{0,8},{4,12},{8,0},{12,4},{1,9},{5,13},{9,1},{13,5},{2,10},{6,14},... | collective-permute-start | bytes 1572872 | tf_op jit(solution)/shard_map/ppermute | solution.py:29
  14.7 3.4 %copy-start = (bf16[4096,1024]{1,0:T(8,128)(2,1)S(1)}, bf16[4096,1024]{1,0:T(8,128)(2,1)}, u32[]{:S(2)}) copy-start(bf16[4096,1024]{1,0:T(8,128)(2,1)} %tiles.1) | copy-start | bytes 25165828
  18.1 1.5 %copy-start.7 = (bf16[128,1024]{1,0:T(8,128)(2,1)S(1)}, bf16[128,1024]{1,0:T(8,128)(2,1)}, u32[]{:S(2)}) copy-start(bf16[128,1024]{1,0:T(8,128)(2,1)} %copy-done.6) | copy-start | bytes 786436
  18.1 22.3 %copy-start.8 = (bf16[256,1024]{1,0:T(8,128)(2,1)S(1)}, bf16[256,1024]{1,0:T(8,128)(2,1)}, u32[]{:S(2)}) copy-start(bf16[256,1024]{1,0:T(8,128)(2,1)} %param.10) | copy-start | bytes 1572868
  18.1 46.4 %copy-start.2 = (bf16[256,1024]{1,0:T(8,128)(2,1)S(1)}, bf16[256,1024]{1,0:T(8,128)(2,1)}, u32[]{:S(2)}) copy-start(bf16[256,1024]{1,0:T(8,128)(2,1)} %refs_4_.1) | copy-start | bytes 1572868
  19.6 12.4 %collective-permute-start.18 = (bf16[128,512]{1,0:T(8,128)(2,1)S(1)}, bf16[128,512]{1,0:T(8,128)(2,1)S(1)}, u32[]{:S(2)}, u32[]{:S(2)}) collective-permute-start(bf16[128,512]{1,0:T(8,128)(2,1)S(1)} %get-tuple-element.46), channel_id=1, source_target_pairs={{0,2},{1,3},{2,0},{3,1},{4,6},{5,7},{6,4},{7,5},{8,10},{9,11},{10,... | collective-permute-start | bytes 393224 | tf_op jit(solution)/shard_map/ppermute | solution.py:29
  20.0 13.4 %collective-permute-start.10 = (bf16[128,512]{1,0:T(8,128)(2,1)S(1)}, bf16[128,512]{1,0:T(8,128)(2,1)S(1)}, u32[]{:S(2)}, u32[]{:S(2)}) collective-permute-start(bf16[128,512]{1,0:T(8,128)(2,1)S(1)} %get-tuple-element.47), channel_id=1, source_target_pairs={{0,2},{1,3},{2,0},{3,1},{4,6},{5,7},{6,4},{7,5},{8,10},{9,11},{10,... | collective-permute-start | bytes 393224 | tf_op jit(solution)/shard_map/ppermute | solution.py:29
  32.0 6.4 %collective-permute-start.19 = (bf16[128,512]{1,0:T(8,128)(2,1)S(1)}, bf16[128,512]{1,0:T(8,128)(2,1)S(1)}, u32[]{:S(2)}, u32[]{:S(2)}) collective-permute-start(bf16[128,512]{1,0:T(8,128)(2,1)S(1)} %collective-permute-done.18.refs_3_), channel_id=1, source_target_pairs={{0,8},{4,12},{8,0},{12,4},{1,9},{5,13},{9,1},{13,5},{2,10},{6,14},... | collective-permute-start | bytes 393224 | tf_op jit(solution)/shard_map/ppermute | solution.py:29
  33.4 6.5 %collective-permute-start.20 = (bf16[128,512]{1,0:T(8,128)(2,1)S(1)}, bf16[128,512]{1,0:T(8,128)(2,1)S(1)}, u32[]{:S(2)}, u32[]{:S(2)}) collective-permute-start(bf16[128,512]{1,0:T(8,128)(2,1)S(1)} %collective-permute-done.18.refs_3_), channel_id=1, source_target_pairs={{0,16},{16,0},{1,17},{17,1},{2,18},{18,2},{3,19},{19,3},{4,20},{20... | collective-permute-start | bytes 393224 | tf_op jit(solution)/shard_map/ppermute | solution.py:29
  34.9 21.5 %collective-permute-start.4 = (bf16[256,1024]{1,0:T(8,128)(2,1)}, bf16[256,1024]{1,0:T(8,128)(2,1)S(1)}, u32[]{:S(2)}, u32[]{:S(2)}) collective-permute-start(bf16[256,1024]{1,0:T(8,128)(2,1)} %collective-permute-done.3), channel_id=1, source_target_pairs={{0,16},{16,0},{1,17},{17,1},{2,18},{18,2},{3,19},{19,3},{4,20},{20... | collective-permute-start | bytes 1572872 | tf_op jit(solution)/shard_map/ppermute | solution.py:29
  35.4 7.1 %collective-permute-start.6 = (bf16[128,1024]{1,0:T(8,128)(2,1)S(1)}, bf16[128,1024]{1,0:T(8,128)(2,1)S(1)}, u32[]{:S(2)}, u32[]{:S(2)}) collective-permute-start(bf16[128,1024]{1,0:T(8,128)(2,1)S(1)} %collective-permute-done.5.refs_4_), channel_id=1, source_target_pairs={{0,8},{4,12},{8,0},{12,4},{1,9},{5,13},{9,1},{13,5},{2,10},{6,14},... | collective-permute-start | bytes 786440 | tf_op jit(solution)/shard_map/ppermute | solution.py:29
  38.4 15.6 %collective-permute-start.7 = (bf16[128,1024]{1,0:T(8,128)(2,1)S(1)}, bf16[128,1024]{1,0:T(8,128)(2,1)S(1)}, u32[]{:S(2)}, u32[]{:S(2)}) collective-permute-start(bf16[128,1024]{1,0:T(8,128)(2,1)S(1)} %collective-permute-done.5.refs_4_), channel_id=1, source_target_pairs={{0,16},{16,0},{1,17},{17,1},{2,18},{18,2},{3,19},{19,3},{4,20},{20... | collective-permute-start | bytes 786440 | tf_op jit(solution)/shard_map/ppermute | solution.py:29
  39.9 16.7 %collective-permute-start.1 = (bf16[256,1024]{1,0:T(8,128)(2,1)S(1)}, bf16[256,1024]{1,0:T(8,128)(2,1)S(1)}, u32[]{:S(2)}, u32[]{:S(2)}) collective-permute-start(bf16[256,1024]{1,0:T(8,128)(2,1)S(1)} %copy-done.1), channel_id=1, source_target_pairs={{0,4},{4,0},{8,12},{12,8},{1,5},{5,1},{9,13},{13,9},{2,6},{6,2},{1... | collective-permute-start | bytes 1572872 | tf_op jit(solution)/shard_map/ppermute | solution.py:29
  39.9 22.3 %collective-permute-start.2 = (bf16[256,1024]{1,0:T(8,128)(2,1)S(1)}, bf16[256,1024]{1,0:T(8,128)(2,1)S(1)}, u32[]{:S(2)}, u32[]{:S(2)}) collective-permute-start(bf16[256,1024]{1,0:T(8,128)(2,1)S(1)} %collective-permute-done.refs_1_), channel_id=1, source_target_pairs={{0,4},{4,0},{8,12},{12,8},{1,5},{5,1},{9,13},{13,9},{2,6},{6,2},{1... | collective-permute-start | bytes 1572872 | tf_op jit(solution)/shard_map/ppermute | solution.py:29
  42.6 25.8 %collective-permute-start.11 = (bf16[128,512]{1,0:T(8,128)(2,1)S(1)}, bf16[128,512]{1,0:T(8,128)(2,1)S(1)}, u32[]{:S(2)}, u32[]{:S(2)}) collective-permute-start(bf16[128,512]{1,0:T(8,128)(2,1)S(1)} %collective-permute-done.10.refs_3_), channel_id=1, source_target_pairs={{0,8},{4,12},{8,0},{12,4},{1,9},{5,13},{9,1},{13,5},{2,10},{6,14},... | collective-permute-start | bytes 393224 | tf_op jit(solution)/shard_map/ppermute | solution.py:29
  53.9 5.7 %collective-permute-start.8 = (bf16[64,1024]{1,0:T(8,128)(2,1)S(1)}, bf16[64,1024]{1,0:T(8,128)(2,1)S(1)}, u32[]{:S(2)}, u32[]{:S(2)}) collective-permute-start(bf16[64,1024]{1,0:T(8,128)(2,1)S(1)} %slice.110), channel_id=1, source_target_pairs={{0,16},{16,0},{1,17},{17,1},{2,18},{18,2},{3,19},{19,3},{4,20},{20... | collective-permute-start | bytes 393224 | tf_op jit(solution)/shard_map/ppermute | solution.py:29
  56.5 5.3 %collective-permute-start.9 = (bf16[64,1024]{1,0:T(8,128)(2,1)S(1)}, bf16[64,1024]{1,0:T(8,128)(2,1)S(1)}, u32[]{:S(2)}, u32[]{:S(2)}) collective-permute-start(bf16[64,1024]{1,0:T(8,128)(2,1)S(1)} %slice.111), channel_id=1, source_target_pairs={{0,8},{4,12},{8,0},{12,4},{1,9},{5,13},{9,1},{13,5},{2,10},{6,14},... | collective-permute-start | bytes 393224 | tf_op jit(solution)/shard_map/ppermute | solution.py:29
  56.6 22.6 %copy-start.10 = (s32[32]{0:T(128)S(1)}, s32[32]{0:T(128)}, u32[]{:S(2)}) copy-start(s32[32]{0:T(128)} %param.11) | copy-start | bytes 388
  56.6 34.4 %copy-start.5 = (s32[1,256]{1,0:T(1,128)S(1)}, s32[1,256]{1,0:T(1,128)}, u32[]{:S(2)}) copy-start(s32[1,256]{1,0:T(1,128)} %identity.1) | copy-start | bytes 3076
  56.6 12.4 %collective-permute-start.12 = (bf16[128,512]{1,0:T(8,128)(2,1)S(1)}, bf16[128,512]{1,0:T(8,128)(2,1)S(1)}, u32[]{:S(2)}, u32[]{:S(2)}) collective-permute-start(bf16[128,512]{1,0:T(8,128)(2,1)S(1)} %collective-permute-done.10.refs_3_), channel_id=1, source_target_pairs={{0,16},{16,0},{1,17},{17,1},{2,18},{18,2},{3,19},{19,3},{4,20},{20... | collective-permute-start | bytes 393224 | tf_op jit(solution)/shard_map/ppermute | solution.py:29
  59.6 7.1 %collective-permute-start.21 = (bf16[64,512]{1,0:T(8,128)(2,1)S(1)}, bf16[64,512]{1,0:T(8,128)(2,1)S(1)}, u32[]{:S(2)}, u32[]{:S(2)}) collective-permute-start(bf16[64,512]{1,0:T(8,128)(2,1)S(1)} %slice.118), channel_id=1, source_target_pairs={{0,16},{16,0},{1,17},{17,1},{2,18},{18,2},{3,19},{19,3},{4,20},{20... | collective-permute-start | bytes 196616 | tf_op jit(solution)/shard_map/ppermute | solution.py:29
  61.8 4.9 %collective-permute-start.22 = (bf16[64,512]{1,0:T(8,128)(2,1)S(1)}, bf16[64,512]{1,0:T(8,128)(2,1)S(1)}, u32[]{:S(2)}, u32[]{:S(2)}) collective-permute-start(bf16[64,512]{1,0:T(8,128)(2,1)S(1)} %slice.119), channel_id=1, source_target_pairs={{0,8},{4,12},{8,0},{12,4},{1,9},{5,13},{9,1},{13,5},{2,10},{6,14},... | collective-permute-start | bytes 196616 | tf_op jit(solution)/shard_map/ppermute | solution.py:29
  64.4 31.8 %copy-start.9 = (s32[4]{0:T(128)S(1)}, s32[4]{0:T(128)}, u32[]{:S(2)}) copy-start(s32[4]{0:T(128)} %constant.80.clone.1) | copy-start | bytes 52
  68.4 7.1 %collective-permute-start.24 = (bf16[256,512]{1,0:T(8,128)(2,1)S(1)}, bf16[256,512]{1,0:T(8,128)(2,1)S(1)}, u32[]{:S(2)}, u32[]{:S(2)}) collective-permute-start(bf16[256,512]{1,0:T(8,128)(2,1)S(1)} %get-tuple-element.28), channel_id=1, source_target_pairs={{0,4},{4,0},{8,12},{12,8},{1,5},{5,1},{9,13},{13,9},{2,6},{6,2},{1... | collective-permute-start | bytes 786440 | tf_op jit(solution)/shard_map/ppermute | solution.py:29
  68.4 4.6 %collective-permute-start.13 = (bf16[64,512]{1,0:T(8,128)(2,1)S(1)}, bf16[64,512]{1,0:T(8,128)(2,1)S(1)}, u32[]{:S(2)}, u32[]{:S(2)}) collective-permute-start(bf16[64,512]{1,0:T(8,128)(2,1)S(1)} %slice.114), channel_id=1, source_target_pairs={{0,16},{16,0},{1,17},{17,1},{2,18},{18,2},{3,19},{19,3},{4,20},{20... | collective-permute-start | bytes 196616 | tf_op jit(solution)/shard_map/ppermute | solution.py:29
  69.0 4.3 %collective-permute-start.14 = (bf16[64,512]{1,0:T(8,128)(2,1)S(1)}, bf16[64,512]{1,0:T(8,128)(2,1)S(1)}, u32[]{:S(2)}, u32[]{:S(2)}) collective-permute-start(bf16[64,512]{1,0:T(8,128)(2,1)S(1)} %slice.115), channel_id=1, source_target_pairs={{0,8},{4,12},{8,0},{12,4},{1,9},{5,13},{9,1},{13,5},{2,10},{6,14},... | collective-permute-start | bytes 196616 | tf_op jit(solution)/shard_map/ppermute | solution.py:29
  75.1 2.7 %copy-start.3 = (f32[256,512]{1,0:T(8,128)}, f32[256,512]{1,0:T(8,128)S(1)}, u32[]{:S(2)}) copy-start(f32[256,512]{1,0:T(8,128)S(1)} %get-tuple-element.21.refs_0_) | copy-start | bytes 1572868
  75.1 1.9 %collective-permute-start.16 = (bf16[256,512]{1,0:T(8,128)(2,1)S(1)}, bf16[256,512]{1,0:T(8,128)(2,1)S(1)}, u32[]{:S(2)}, u32[]{:S(2)}) collective-permute-start(bf16[256,512]{1,0:T(8,128)(2,1)S(1)} %get-tuple-element.24), channel_id=1, source_target_pairs={{0,4},{4,0},{8,12},{12,8},{1,5},{5,1},{9,13},{13,9},{2,6},{6,2},{1... | collective-permute-start | bytes 786440 | tf_op jit(solution)/shard_map/ppermute | solution.py:29
  75.1 4.1 %collective-permute-start.23 = (bf16[256,512]{1,0:T(8,128)(2,1)}, bf16[256,512]{1,0:T(8,128)(2,1)S(1)}, u32[]{:S(2)}, u32[]{:S(2)}) collective-permute-start(bf16[256,512]{1,0:T(8,128)(2,1)} %get-tuple-element.26), channel_id=1, source_target_pairs={{0,4},{4,0},{8,12},{12,8},{1,5},{5,1},{9,13},{13,9},{2,6},{6,2},{1... | collective-permute-start | bytes 786440 | tf_op jit(solution)/shard_map/ppermute | solution.py:29
  75.6 3.6 %collective-permute-start.15 = (bf16[256,512]{1,0:T(8,128)(2,1)}, bf16[256,512]{1,0:T(8,128)(2,1)}, u32[]{:S(2)}, u32[]{:S(2)}) collective-permute-start(bf16[256,512]{1,0:T(8,128)(2,1)} %get-tuple-element.22), channel_id=1, source_target_pairs={{0,4},{4,0},{8,12},{12,8},{1,5},{5,1},{9,13},{13,9},{2,6},{6,2},{1... | collective-permute-start | bytes 786440 | tf_op jit(solution)/shard_map/ppermute | solution.py:29
  76.4 9.4 %collective-permute-start.25 = (bf16[256,512]{1,0:T(8,128)(2,1)}, bf16[256,512]{1,0:T(8,128)(2,1)}, u32[]{:S(2)}, u32[]{:S(2)}) collective-permute-start(bf16[256,512]{1,0:T(8,128)(2,1)} %add_convert_fusion), channel_id=1, source_target_pairs={{0,1},{1,0},{2,3},{3,2},{4,5},{5,4},{6,7},{7,6},{8,9},{9,8},{10,11... | collective-permute-start | bytes 786440 | tf_op jit(solution)/shard_map/ppermute | solution.py:29
  77.7 13.3 %collective-permute-start.17 = (bf16[256,512]{1,0:T(8,128)(2,1)}, bf16[256,512]{1,0:T(8,128)(2,1)}, u32[]{:S(2)}, u32[]{:S(2)}) collective-permute-start(bf16[256,512]{1,0:T(8,128)(2,1)} %add_convert_fusion.1), channel_id=1, source_target_pairs={{0,1},{1,0},{2,3},{3,2},{4,5},{5,4},{6,7},{7,6},{8,9},{9,8},{10,11... | collective-permute-start | bytes 786440 | tf_op jit(solution)/shard_map/ppermute | solution.py:29
  91.0 1.0 copy-start.4
  94.5 4.0 %collective-permute-start.26 = (bf16[2,1,8,1024]{3,2,1,0:T(8,128)(2,1)S(1)}, bf16[2,1,8,1024]{3,2,1,0:T(8,128)(2,1)S(1)}, u32[]{:S(2)}, u32[]{:S(2)}) collective-permute-start(bf16[2,1,8,1024]{3,2,1,0:T(8,128)(2,1)S(1)} %get-tuple-element.54), channel_id=1, source_target_pairs={{0,8},{4,12},{8,0},{12,4},{1,9},{5,13},{9,1},{13,5},{2,10},{6,14},... | collective-permute-start | bytes 98312 | tf_op jit(solution)/shard_map/ppermute | solution.py:29
  98.5 1.3 collective-permute-start.27
  99.7 5.2 %collective-permute-start.28 = (bf16[32,1024]{1,0:T(8,128)(2,1)S(1)}, bf16[32,1024]{1,0:T(8,128)(2,1)S(1)}, u32[]{:S(2)}, u32[]{:S(2)}) collective-permute-start(bf16[32,1024]{1,0:T(8,128)(2,1)S(1)} %maximum_bitcast_fusion.refs_0_), channel_id=1, source_target_pairs={{0,1},{1,0},{2,3},{3,2},{4,5},{5,4},{6,7},{7,6},{8,9},{9,8},{10,11... | collective-permute-start | bytes 196616 | tf_op jit(solution)/shard_map/ppermute | solution.py:29
  100.1 8.6 %collective-permute-start.29 = (bf16[32,1024]{1,0:T(8,128)(2,1)S(1)}, bf16[32,1024]{1,0:T(8,128)(2,1)S(1)}, u32[]{:S(2)}, u32[]{:S(2)}) collective-permute-start(bf16[32,1024]{1,0:T(8,128)(2,1)S(1)} %maximum_bitcast_fusion.refs_0_), channel_id=1, source_target_pairs={{0,2},{1,3},{2,0},{3,1},{4,6},{5,7},{6,4},{7,5},{8,10},{9,11},{10,... | collective-permute-start | bytes 196616 | tf_op jit(solution)/shard_map/ppermute | solution.py:29
  101.3 7.4 %collective-permute-start.30 = (bf16[32,1024]{1,0:T(8,128)(2,1)S(1)}, bf16[32,1024]{1,0:T(8,128)(2,1)S(1)}, u32[]{:S(2)}, u32[]{:S(2)}) collective-permute-start(bf16[32,1024]{1,0:T(8,128)(2,1)S(1)} %maximum_bitcast_fusion.refs_0_), channel_id=1, source_target_pairs={{0,3},{1,2},{2,1},{3,0},{4,7},{5,6},{6,5},{7,4},{8,11},{9,10},{10,... | collective-permute-start | bytes 196616 | tf_op jit(solution)/shard_map/ppermute | solution.py:29
  111.4 1.2 collective-permute-start.31
  112.7 3.7 %collective-permute-start.32 = (f32[16,256]{1,0:T(8,128)S(1)}, f32[16,256]{1,0:T(8,128)S(1)}, u32[]{:S(2)}, u32[]{:S(2)}) collective-permute-start(f32[16,256]{1,0:T(8,128)S(1)} %add.97), channel_id=1, source_target_pairs={{0,8},{4,12},{8,0},{12,4},{1,9},{5,13},{9,1},{13,5},{2,10},{6,14},... | collective-permute-start | bytes 49160 | tf_op jit(solution)/shard_map/ppermute | solution.py:29
  117.5 4.6 %collective-permute-start.33 = (bf16[32,1152]{1,0:T(8,128)(2,1)S(1)}, bf16[32,1152]{1,0:T(8,128)(2,1)S(1)}, u32[]{:S(2)}, u32[]{:S(2)}) collective-permute-start(bf16[32,1152]{1,0:T(8,128)(2,1)S(1)} %get-tuple-element.50), channel_id=1, source_target_pairs={{0,1},{1,0},{2,3},{3,2},{4,5},{5,4},{6,7},{7,6},{8,9},{9,8},{10,11... | collective-permute-start | bytes 221192 | tf_op jit(solution)/shard_map/ppermute | solution.py:29
  118.9 7.8 %collective-permute-start.34 = (bf16[32,1152]{1,0:T(8,128)(2,1)S(1)}, bf16[32,1152]{1,0:T(8,128)(2,1)S(1)}, u32[]{:S(2)}, u32[]{:S(2)}) collective-permute-start(bf16[32,1152]{1,0:T(8,128)(2,1)S(1)} %get-tuple-element.49), channel_id=1, source_target_pairs={{0,2},{1,3},{2,0},{3,1},{4,6},{5,7},{6,4},{7,5},{8,10},{9,11},{10,... | collective-permute-start | bytes 221192 | tf_op jit(solution)/shard_map/ppermute | solution.py:29
  119.9 6.8 %collective-permute-start.35 = (bf16[32,1152]{1,0:T(8,128)(2,1)S(1)}, bf16[32,1152]{1,0:T(8,128)(2,1)S(1)}, u32[]{:S(2)}, u32[]{:S(2)}) collective-permute-start(bf16[32,1152]{1,0:T(8,128)(2,1)S(1)} %get-tuple-element.48), channel_id=1, source_target_pairs={{0,3},{1,2},{2,1},{3,0},{4,7},{5,6},{6,5},{7,4},{8,11},{9,10},{10,... | collective-permute-start | bytes 221192 | tf_op jit(solution)/shard_map/ppermute | solution.py:29

commit v3 on v2

v3 whole, which is shorter than its diff:
```python
import functools
import math

import jax
import jax.numpy as jnp
from jax import lax
from jax.experimental import pallas as pl
from jax.experimental.pallas import tpu as pltpu
from jax.sharding import PartitionSpec as P

SENT_DEV = 32
TBLK = 256
MOST = 4
LANES = 128


SCORE_SCALE = 32.0


def bits_of(axis, first):
    size, bit, bits = lax.axis_size(axis), first, []
    while bit < size:
        bits.append(bit)
        bit *= 2
    return bits


def swap(values, axis, offset):
    return lax.ppermute(values, axis, [(i, i ^ offset) for i in range(lax.axis_size(axis))])


def local_call(
    kernel, out_shape, args, flops, scratch=(), scalars=0, near=0, place=pltpu.VMEM, vmem=16
):
    outs = out_shape if isinstance(out_shape, tuple) else (out_shape,)
    moved = sum(math.prod(a.shape) * a.dtype.itemsize for a in (*args, *outs))
    return pl.pallas_call(
        kernel,
        out_shape=out_shape,
        in_specs=[pl.BlockSpec(memory_space=pltpu.SMEM)] * scalars
        + [pl.BlockSpec(memory_space=pltpu.VMEM)] * near
        + [pl.BlockSpec(memory_space=place)] * (len(args) - scalars - near),
        out_specs=jax.tree.map(lambda _: pl.BlockSpec(memory_space=pltpu.VMEM), out_shape),
        scratch_shapes=scratch,
        compiler_params=pltpu.CompilerParams(vmem_limit_bytes=vmem * 2**20),
        cost_estimate=pl.CostEstimate(flops=flops, bytes_accessed=moved, transcendentals=0),
    )(*args)


def shape(dims, dtype):
    return jax.ShapeDtypeStruct(tuple(dims), dtype)


def unit_of(floats):
    square = jnp.mean(floats * floats, axis=-1, keepdims=True)
    return (floats * lax.rsqrt(square + 1e-06) * (1.0 / math.sqrt(floats.shape[-1]))).astype(
        jnp.bfloat16
    )


def dot(left, right, contract, **more):
    return lax.dot_general(
        left, right, ((contract[:1], contract[1:]), ((), ())),
        preferred_element_type=jnp.float32, **more
    )


def gather_refs(refs, held):
    start = 0
    for ref in refs:
        held[start : start + ref.shape[0], :] = ref[...]
        start += ref.shape[0]


def fetches(refs, held, sems):
    start, copies = 0, []
    for index, ref in enumerate(refs):
        count = ref.shape[0]
        copies.append(
            pltpu.make_async_copy(ref, held.at[pl.ds(start, count)], sems.at[index])
        )
        start += count
    for copy in copies:
        copy.start()
    return copies


def slice_kernel(inner, outer, inner_half, outer_half, sems):
    half = inner_half.shape[0]
    rows = pl.ds(pl.multiple_of(lax.axis_index("groups") * half, half), half)
    copies = [
        pltpu.make_async_copy(inner.at[rows], inner_half, sems.at[0]),
        pltpu.make_async_copy(outer.at[rows], outer_half, sems.at[1]),
    ]
    for copy in copies:
        copy.start()
    for copy in copies:
        copy.wait()


def weight_halves(inner, outer):
    units, features = inner.shape
    return local_call(
        slice_kernel,
        (shape((units // 2, features), jnp.bfloat16),) * 2,
        (inner, outer),
        0,
        (pltpu.SemaphoreType.DMA((2,)),),
        place=pl.ANY,
        vmem=58,
    )


def hidden_kernel(count, *refs):
    tokens, weights = refs[:count], refs[count:-5]
    out, rows, held, token_sems, weight_sems = refs[-5:]
    weight_copies = fetches(weights, held, weight_sems)
    token_copies = fetches(tokens, rows, token_sems)
    for copy in weight_copies:
        copy.wait()
    start = 0
    for token, copy in zip(tokens, token_copies):
        part = pl.ds(start, token.shape[0])
        copy.wait()
        product = dot(rows[part, :], held[...], (1, 1))
        out[part, :] = (
            product * 0.5 * (1.0 + lax.erf(product * math.sqrt(0.5)))
        ).astype(jnp.bfloat16)
        start += token.shape[0]


def hidden_units(tokens, weights):
    features = weights[0].shape[1]
    rows = sum(t.shape[0] for t in tokens)
    units = sum(w.shape[0] for w in weights)
    return local_call(
        functools.partial(hidden_kernel, len(tokens)),
        shape((rows, units), jnp.bfloat16),
        (*tokens, *weights),
        2 * rows * units * features,
        (
            pltpu.VMEM((rows, features), jnp.bfloat16),
            pltpu.VMEM((units, features), jnp.bfloat16),
            pltpu.SemaphoreType.DMA((len(tokens),)),
            pltpu.SemaphoreType.DMA((len(weights),)),
        ),
        place=pl.ANY,
    )


def partial_kernel(blocks, added, hidden, *refs):
    terms, refs = refs[:added], refs[added:]
    weights, outs, (held, sems) = refs[: -len(blocks) - 2], refs[-len(blocks) - 2 : -2], refs[-2:]
    for copy in fetches(weights, held, sems):
        copy.wait()
    for index, out in zip(blocks, outs):
        rows = out.shape[0]
        sums = dot(hidden[pl.ds(index * rows, rows), :], held[...], (1, 0))
        for term in terms:
            sums = sums + term[...].astype(jnp.float32)
        out[...] = sums.astype(out.dtype)


def partial_sums(hidden, weights, blocks, terms=(), dtype=jnp.bfloat16):
    rows, units, features = hidden.shape[0] // 4, hidden.shape[1], weights[0].shape[1]
    return local_call(
        functools.partial(partial_kernel, blocks, len(terms)),
        (shape((rows, features), dtype),) * len(blocks),
        (hidden, *terms, *weights),
        2 * len(blocks) * rows * units * features,
        (
            pltpu.VMEM((units, features), jnp.bfloat16),
            pltpu.SemaphoreType.DMA((len(weights),)),
        ),
        near=1 + len(terms),
        place=pl.ANY,
    )


def pool_kernel(identity, order, own, back, out):
    summed = own[...] + back[...].astype(jnp.float32)
    center = jnp.mean(summed, axis=-1, keepdims=True)
    moved = summed - center
    spread = jnp.mean(moved * moved, axis=-1, keepdims=True)
    normed = moved * lax.rsqrt(spread + 1e-05)
    sentences = out.shape[0]
    members = (
        identity[...] == lax.broadcasted_iota(jnp.int32, (sentences, own.shape[0]), 0)
    ).astype(jnp.float32)
    sums = dot(members, normed, (1, 0), precision=lax.Precision.HIGHEST)
    unit = unit_of(sums / jnp.sum(members, axis=1, keepdims=True))
    sort = (order[...] == lax.broadcasted_iota(jnp.int32, (sentences, sentences), 0)).astype(
        jnp.bfloat16
    )
    out[...] = dot(sort, unit, (1, 0)).astype(jnp.bfloat16)


def find_slots(listed, slots, valid, blocks):
    column = lax.axis_index("tgt")
    for slot in range(MOST):
        slots[slot] = 0
        valid[slot] = 0
    count = jnp.int32(0)
    for index in range(listed.shape[1]):
        block = listed[0, index]
        here = lax.div(block, blocks) == column

        @pl.when(here)
        def _():
            slots[count] = lax.rem(block, blocks)
            valid[count] = 1

        count = count + here.astype(jnp.int32)


SLOTS = (pltpu.SMEM((MOST,), jnp.int32),) * 2


def target_kernel(listed, targets, out, slots, valid, tiles, sems):
    find_slots(listed, slots, valid, targets.shape[0] // TBLK)
    copies = [
        pltpu.make_async_copy(
            targets.at[pl.ds(pl.multiple_of(slots[slot] * TBLK, TBLK), TBLK)],
            tiles.at[slot],
            sems.at[slot],
        )
        for slot in range(MOST)
    ]
    for copy in copies:
        copy.start()
    for slot, copy in enumerate(copies):
        copy.wait()
        out[slot * TBLK : (slot + 1) * TBLK, :] = unit_of(tiles[slot].astype(jnp.float32))


def listed_units(candidates, targets):
    features = targets.shape[1]
    return local_call(
        target_kernel,
        shape((MOST * TBLK, features), jnp.bfloat16),
        (candidates, targets),
        8 * MOST * TBLK * features,
        (
            *SLOTS,
            pltpu.VMEM((MOST, TBLK, features), jnp.bfloat16),
            pltpu.SemaphoreType.DMA((MOST,)),
        ),
        scalars=1,
        place=pl.ANY,
        vmem=58,
    )


def score_kernel(listed, place, *refs):
    parts, (units_ref, expo, columns, row_total, slots, valid, units, held, sems) = (
        refs[:-9],
        refs[-9:],
    )
    copies = [
        pltpu.make_async_copy(
            units_ref.at[pl.ds(slot * TBLK, TBLK)], units.at[slot], sems.at[slot]
        )
        for slot in range(MOST)
    ]
    for copy in copies:
        copy.start()
    find_slots(listed, slots, valid, columns.shape[0])
    gather_refs(parts, held)
    rows = expo.shape[0]
    sort = (place[...] == lax.broadcasted_iota(jnp.int32, (rows, rows), 0)).astype(jnp.bfloat16)
    block = dot(sort, held[...], (1, 0)).astype(jnp.bfloat16)
    columns[...] = jnp.zeros_like(columns)
    total = jnp.zeros((rows, 1), jnp.float32)
    for slot in range(MOST):
        part = pl.ds(slot * TBLK, TBLK)
        weight = valid[slot].astype(jnp.float32)
        copies[slot].wait()
        values = jnp.exp(SCORE_SCALE * dot(block, units[slot], (1, 1))) * weight
        expo[:, part] = values
        total = total + jnp.sum(values, axis=1, keepdims=True)
        column = jnp.sum(values, axis=0, keepdims=True)

        @pl.when(valid[slot] > 0)
        def _():
            columns[pl.ds(slots[slot], 1), :] = column

    row_total[...] = total


def extra_columns(values):
    lane = lax.broadcasted_iota(jnp.int32, (values[0].shape[0], LANES), 1)
    out = jnp.zeros(lane.shape, jnp.float32)
    for index, value in enumerate(values):
        out = jnp.where(lane == index, value, out)
    return out


def thirds(value):
    first = value.astype(jnp.bfloat16).astype(jnp.float32)
    second = (value - first).astype(jnp.bfloat16).astype(jnp.float32)
    return [first, second, value - first - second]


def match_kernel(listed, expo, columns, row_total, units_ref, own, sent, slots, valid, units, sem):
    copy = pltpu.make_async_copy(units_ref, units, sem)
    copy.start()
    find_slots(listed, slots, valid, columns.shape[0])
    rows = own.shape[0]
    features = units.shape[1]
    mass = jnp.zeros((expo.shape[0], 1), jnp.float32)
    weights = []
    for slot in range(MOST):
        part = pl.ds(slot * TBLK, TBLK)
        values = expo[:, part]
        listed = valid[slot].astype(jnp.float32)
        divisor = jnp.where(listed > 0, columns[pl.ds(slots[slot], 1), :], 1.0)
        mutual = values * (values / divisor)
        mass = mass + jnp.sum(mutual, axis=1, keepdims=True)
        weights.append(mutual.astype(jnp.bfloat16))
    copy.wait()
    numer = dot(jnp.concatenate(weights, axis=1), units[...], (1, 0))
    totals = row_total[...]
    zero = jnp.zeros((rows, 1), jnp.float32)
    own[:, :features] = numer[:rows]
    own[:, features:] = extra_columns([mass[:rows], zero, zero, totals[:rows]])
    sent[:, :features] = numer[rows:].astype(jnp.bfloat16)
    sent[:, features:] = extra_columns(thirds(mass[rows:]) + thirds(totals[rows:])).astype(
        jnp.bfloat16
    )


def finish_kernel(own, *refs):
    parts, (matched, log_mass) = refs[:-2], refs[-2:]
    rows, features = matched.shape
    total = own[...]
    for part in parts:
        total = total + part[...].astype(jnp.float32)
    numer = total[:, :features]
    square = jnp.mean(numer * numer, axis=-1, keepdims=True)
    matched[...] = (numer * lax.rsqrt(square + 1e-06)).astype(jnp.bfloat16)
    extra = total[:, features:]
    lane = lax.broadcasted_iota(jnp.int32, extra.shape, 1)
    mass = jnp.sum(jnp.where(lane < 3, extra, 0.0), axis=1, keepdims=True)
    whole = jnp.sum(jnp.where(lane < 3, 0.0, extra), axis=1, keepdims=True)
    ratio = mass / whole
    same = lax.broadcasted_iota(jnp.int32, (rows, rows), 0) == lax.broadcasted_iota(
        jnp.int32, (rows, rows), 1
    )
    log_mass[...] = jnp.log(jnp.sum(jnp.where(same, ratio, 0.0), axis=0, keepdims=True))


def far_piece(half):
    held = half
    for axis, bit in [("tgt", b) for b in bits_of("tgt", 2)] + [("src", b) for b in bits_of("src", 4)]:
        held = jnp.concatenate([held, swap(held, axis, bit)])
    return held[half.shape[0] :]


def feed_forward(tokens, inner_weight, outer_weight):
    barrier = lax.optimization_barrier
    inner_x, outer_x = swap(inner_weight, "src", 2), swap(outer_weight, "src", 2)
    inner_half, outer_half = weight_halves(inner_weight, outer_weight)
    inner_far, outer_far = far_piece(inner_half), far_piece(outer_half)
    tokens_sent, inner_x = barrier((tokens, inner_x))
    neighbour = swap(tokens_sent, "tgt", 1)
    inner_far_x, inner_far_y = swap(inner_far, "src", 2), swap(inner_far, "groups", 1)

    outer_far, inner_far_x, inner_far_y, outer_x, neighbour = barrier(
        (outer_far, inner_far_x, inner_far_y, outer_x, neighbour)
    )
    outer_far_x, outer_far_y = swap(outer_far, "src", 2), swap(outer_far, "groups", 1)
    inner_square = [inner_far_x, inner_far_y, swap(inner_far_y, "src", 2)]
    outer_square = [outer_far_x, outer_far_y, swap(outer_far_x, "groups", 1)]
    shared = [tokens, neighbour, swap(tokens, "src", 1), swap(neighbour, "src", 1)]
    hidden = hidden_units(shared, [inner_weight, inner_x, inner_far, *inner_square])
    hidden, outer_square = barrier((hidden, outer_square))

    weights = [outer_weight, outer_x, outer_far, *outer_square]
    pair, own = partial_sums(hidden, weights, (3, 2))
    pair, own = swap(pair, "src", 1), swap(own, "src", 1)
    (back,) = partial_sums(hidden, weights, (1,), (pair,))
    back, hidden = barrier((back, hidden))
    back = swap(back, "tgt", 1)
    (own,) = partial_sums(hidden, weights, (0,), (tokens, own), jnp.float32)
    return own, back


def on_device(tokens, sentence_ids, inner_weight, outer_weight, grid_rows, candidates, targets):
    features = tokens.shape[1]
    src_count = lax.axis_size("src")
    tgt_count = lax.axis_size("tgt")
    src_index = lax.axis_index("src")
    tgt_index = lax.axis_index("tgt")
    per_block = SENT_DEV // src_count
    block_rows = tgt_count * SENT_DEV

    column_blocks = targets.shape[0] // TBLK
    target_units = listed_units(candidates, targets)

    summands = feed_forward(tokens, inner_weight, outer_weight)
    order_key = (grid_rows // block_rows ^ src_index) * per_block + grid_rows % per_block
    held = local_call(
        pool_kernel,
        shape((SENT_DEV, features), jnp.bfloat16),
        (sentence_ids, order_key.reshape(1, -1), *summands),
        20 * tokens.shape[0] * features,
    )
    held = held.reshape(src_count, 1, per_block, features)
    for bit in reversed(bits_of("src", 1)):
        held = jnp.concatenate([held[:bit], swap(held[bit:], "src", bit)], axis=1)
    mine = held.reshape(SENT_DEV, features)
    parts = [mine] + [swap(mine, "tgt", offset) for offset in range(1, tgt_count)]
    origin = jnp.arange(1, dtype=jnp.int32)
    for bit in reversed(bits_of("src", 1)):
        origin = jnp.concatenate([origin, origin ^ bit])
    from_src = (origin ^ src_index)[None, :, None]
    from_tgt = (jnp.arange(tgt_count, dtype=jnp.int32) ^ tgt_index)[:, None, None]
    place = (from_src * tgt_count + from_tgt) * per_block + jnp.arange(per_block, dtype=jnp.int32)
    place = place.reshape(1, -1) ^ (tgt_index * SENT_DEV)

    pairs = MOST * TBLK
    expo, column_total, row_total = local_call(
        score_kernel,
        (
            shape((block_rows, pairs), jnp.float32),
            shape((column_blocks, TBLK), jnp.float32),
            shape((block_rows, 1), jnp.float32),
        ),
        (candidates, place, *parts, target_units),
        2 * block_rows * pairs * features,
        (
            *SLOTS,
            pltpu.VMEM((MOST, TBLK, features), jnp.bfloat16),
            pltpu.VMEM((block_rows, features), jnp.bfloat16),
            pltpu.SemaphoreType.DMA((MOST,)),
        ),
        scalars=1,
        near=1 + len(parts),
        place=pl.ANY,
    )
    for bit in bits_of("src", 1):
        column_total = column_total + swap(column_total, "src", bit)
    own, sent = local_call(
        match_kernel,
        (
            shape((SENT_DEV, features + LANES), jnp.float32),
            shape((block_rows - SENT_DEV, features + LANES), jnp.bfloat16),
        ),
        (candidates, expo, column_total, row_total, target_units),
        2 * block_rows * pairs * features,
        (
            *SLOTS,
            pltpu.VMEM((MOST * TBLK, features), jnp.bfloat16),
            pltpu.SemaphoreType.DMA(()),
        ),
        scalars=1,
        near=3,
        place=pl.ANY,
    )
    received = [
        swap(sent[(offset - 1) * SENT_DEV : offset * SENT_DEV], "tgt", offset)
        for offset in range(1, tgt_count)
    ]
    matched, log_mass = local_call(
        finish_kernel,
        (shape((SENT_DEV, features), jnp.bfloat16), shape((1, SENT_DEV), jnp.float32)),
        (own, *received),
        8 * SENT_DEV * features,
    )
    return (matched, log_mass.reshape(SENT_DEV))


def solution(mesh):
    in_specs = (
        P(("groups", "src", "tgt"), None),
        P(("groups", "src", "tgt"), None),
        P(("src", "tgt"), None),
        P(("src", "tgt"), None),
        P(("groups", "src", "tgt")),
        P(("groups", "src"), None),
        P(("groups", "tgt"), None),
    )
    out_specs = (P(("groups", "src", "tgt"), None), P(("groups", "src", "tgt")))
    return jax.shard_map(
        on_device, mesh=mesh, in_specs=in_specs, out_specs=out_specs, check_vma=False
    )
```

time: 128 us -> 117 us (0.914)
  Pallas kernels: 16.2 us -> 23.1 us
  waiting for transfers between devices: 58.2 us -> 52.2 us
  other arithmetic: 5.19 us -> 0.18 us
  starting transfers between devices: 36.7 us -> 32.2 us
  local copies, waits for them, and re-layouts: 10.2 us -> 7.71 us
    pallas_call x8 -> x10, Pallas kernels: 14.8 us -> 23.1 us  [local_call(): pl.pallas_call(kernel, out_shape=out_shape, in_specs=[pl.BlockSpec(memory...]
    ppermute x36 -> x26, waiting for transfers between devices: 58.2 us -> 52.2 us  [swap(): lax.ppermute(values, axis, [(i, i ^ offset) for i in range(lax.axis_size(...]
    ppermute x36 -> x26, starting transfers between devices: 36.7 us -> 32.2 us  [swap(): lax.ppermute(values, axis, [(i, i ^ offset) for i in range(lax.axis_size(...]
    dynamic_slice x2 -> x0, local copies, waits for them, and re-layouts: 2.69 us -> none  [the longest x1 1.72 us: feed_forward(): inner_half = lax.dynamic_slice_in_dim(inner_weight, start, half)]
    unnamed x22 -> x30, local copies, waits for them, and re-layouts: 5.18 us -> 7.59 us
    slice x12 -> x0, local copies, waits for them, and re-layouts: 2.09 us -> none  [the longest x3 1.04 us: feed_forward(): w[:, c * width:(c + 1) * width]]
    concatenate x1 -> x0, other arithmetic: 1.8 us -> none  [feed_forward(): near_sent = jnp.concatenate([inner_half, outer_half])]
    convert_element_type x2 -> x0, other arithmetic: 1.57 us -> none  [feed_forward(): pair.astype(jnp.bfloat16)]
  transfers between devices with their start and end apart: 36 -> 26, of which waited for: 20 -> 15; matrix products, arithmetic and copies ran while one was open for 7% -> 0% of each run, Pallas kernels for 7% -> 12%
where the time goes in v3:
time: 117 us; the launch traced here: 116 us
  waiting for transfers between devices  52.2 us (45%)
  starting transfers between devices  32.2 us (28%)
  Pallas kernels  23.1 us (20%)
  local copies, waits for them, and re-layouts  7.71 us (7%)
    ppermute x26, waiting for transfers between devices, swap(): lax.ppermute(values, axis, [(i, i ^ offset) for i in range(lax.axis_size(...  52.2 us
    ppermute x26, starting transfers between devices, swap(): lax.ppermute(values, axis, [(i, i ^ offset) for i in range(lax.axis_size(...  32.2 us
    pallas_call x10, Pallas kernels, local_call(): pl.pallas_call(kernel, out_shape=out_shape, in_specs=[pl.BlockSpec(memory...  23.1 us
    unnamed x30, local copies, waits for them, and re-layouts  7.59 us
  transfers between devices with their start and end apart: 26, of which 15 were waited for; matrix products, arithmetic and copies ran while one was open for 0% of the time, Pallas kernels for 12%

profile of v3, /device:TPU:0, one launch (start us, length us, event | category | flops | bytes accessed | tf_op | source)
XLA Modules:
  0.0 116.2 jit_solution(14651351433105740004)
XLA Ops:
  0.6 3.0 %collective-permute-start.5 = (bf16[256,1024]{1,0:T(8,128)(2,1)}, bf16[256,1024]{1,0:T(8,128)(2,1)S(1)}, u32[]{:S(2)}, u32[]{:S(2)}) collective-permute-start(bf16[256,1024]{1,0:T(8,128)(2,1)} %refs_4_.1), channel_id=1, source_target_pairs={{0,8},{4,12},{8,0},{12,4},{1,9},{5,13},{9,1},{13,5},{2,10},{6,14},... | collective-permute-start | bytes 1572872 | tf_op jit(solution)/shard_map/ppermute | solution.py:29
  3.7 1.9 %shard_map.86 = (bf16[128,1024]{1,0:T(8,128)(2,1)}, bf16[128,1024]{1,0:T(8,128)(2,1)}) custom-call(bf16[256,1024]{1,0:T(8,128)(2,1)} %refs_4_.1, bf16[256,1024]{1,0:T(8,128)(2,1)} %refs_2_.1), custom_call_target="tpu_custom_call" | custom-call | bytes 1572864 | tf_op jit(solution)/shard_map/pallas_call | solution.py:37
  5.6 3.1 %collective-permute-start.1 = (bf16[128,1024]{1,0:T(8,128)(2,1)}, bf16[128,1024]{1,0:T(8,128)(2,1)S(1)}, u32[]{:S(2)}, u32[]{:S(2)}) collective-permute-start(bf16[128,1024]{1,0:T(8,128)(2,1)} %get-tuple-element.27), channel_id=1, source_target_pairs={{0,2},{1,3},{2,0},{3,1},{4,6},{5,7},{6,4},{7,5},{8,10},{9,11},{10,... | collective-permute-start | bytes 786440 | tf_op jit(solution)/shard_map/ppermute | solution.py:29
  8.7 7.9 %collective-permute-done.5.refs_5_ = bf16[256,1024]{1,0:T(8,128)(2,1)S(1)} collective-permute-done((bf16[256,1024]{1,0:T(8,128)(2,1)}, bf16[256,1024]{1,0:T(8,128)(2,1)S(1)}, u32[]{:S(2)}, u32[]{:S(2)}) %collective-permute-start.5) | collective-permute-done | bytes 524320 | tf_op jit(solution)/shard_map/ppermute | solution.py:29
  16.6 2.1 %collective-permute-start.6 = (bf16[256,1024]{1,0:T(8,128)(2,1)}, bf16[256,1024]{1,0:T(8,128)(2,1)S(1)}, u32[]{:S(2)}, u32[]{:S(2)}) collective-permute-start(bf16[256,1024]{1,0:T(8,128)(2,1)} %refs_0_.5), channel_id=1, source_target_pairs={{0,1},{1,0},{2,3},{3,2},{4,5},{5,4},{6,7},{7,6},{8,9},{9,8},{10,11... | collective-permute-start | bytes 1572872 | tf_op jit(solution)/shard_map/ppermute | solution.py:29
  18.7 2.6 %collective-permute-start = (bf16[128,1024]{1,0:T(8,128)(2,1)}, bf16[128,1024]{1,0:T(8,128)(2,1)S(1)}, u32[]{:S(2)}, u32[]{:S(2)}) collective-permute-start(bf16[128,1024]{1,0:T(8,128)(2,1)} %get-tuple-element.26), channel_id=1, source_target_pairs={{0,2},{1,3},{2,0},{3,1},{4,6},{5,7},{6,4},{7,5},{8,10},{9,11},{10,... | collective-permute-start | bytes 786440 | tf_op jit(solution)/shard_map/ppermute | solution.py:29
  21.3 1.5 %collective-permute-start.2 = (bf16[128,1024]{1,0:T(8,128)(2,1)S(1)}, bf16[128,1024]{1,0:T(8,128)(2,1)S(1)}, u32[]{:S(2)}, u32[]{:S(2)}) collective-permute-start(bf16[128,1024]{1,0:T(8,128)(2,1)S(1)} %collective-permute-done.1.refs_6_), channel_id=1, source_target_pairs={{0,8},{4,12},{8,0},{12,4},{1,9},{5,13},{9,1},{13,5},{2,10},{6,14},... | collective-permute-start | bytes 786440 | tf_op jit(solution)/shard_map/ppermute | solution.py:29
  22.8 1.5 %collective-permute-start.3 = (bf16[128,1024]{1,0:T(8,128)(2,1)S(1)}, bf16[128,1024]{1,0:T(8,128)(2,1)S(1)}, u32[]{:S(2)}, u32[]{:S(2)}) collective-permute-start(bf16[128,1024]{1,0:T(8,128)(2,1)S(1)} %collective-permute-done.1.refs_6_), channel_id=1, source_target_pairs={{0,16},{16,0},{1,17},{17,1},{2,18},{18,2},{3,19},{19,3},{4,20},{20... | collective-permute-start | bytes 786440 | tf_op jit(solution)/shard_map/ppermute | solution.py:29
  24.3 9.5 %collective-permute-done.refs_2_.refs_3_.refs_4_ = bf16[128,1024]{1,0:T(8,128)(2,1)S(1)} collective-permute-done((bf16[128,1024]{1,0:T(8,128)(2,1)}, bf16[128,1024]{1,0:T(8,128)(2,1)S(1)}, u32[]{:S(2)}, u32[]{:S(2)}) %collective-permute-start) | collective-permute-done | bytes 262176 | tf_op jit(solution)/shard_map/ppermute | solution.py:29
  33.9 3.2 %collective-permute-done.6.refs_1_ = bf16[256,1024]{1,0:T(8,128)(2,1)S(1)} collective-permute-done((bf16[256,1024]{1,0:T(8,128)(2,1)}, bf16[256,1024]{1,0:T(8,128)(2,1)S(1)}, u32[]{:S(2)}, u32[]{:S(2)}) %collective-permute-start.6) | collective-permute-done | bytes 524320 | tf_op jit(solution)/shard_map/ppermute | solution.py:29
  37.1 1.5 %collective-permute-start.10 = (bf16[128,1024]{1,0:T(8,128)(2,1)S(1)}, bf16[128,1024]{1,0:T(8,128)(2,1)S(1)}, u32[]{:S(2)}, u32[]{:S(2)}) collective-permute-start(bf16[128,1024]{1,0:T(8,128)(2,1)S(1)} %collective-permute-done.refs_2_.refs_3_.refs_4_), channel_id=1, source_target_pairs={{0,8},{4,12},{8,0},{12,4},{1,9},{5,13},{9,1},{13,5},{2,10},{6,14},... | collective-permute-start | bytes 786440 | tf_op jit(solution)/shard_map/ppermute | solution.py:29
  38.7 0.5 collective-permute-start.9
  39.2 1.6 %collective-permute-start.11 = (bf16[128,1024]{1,0:T(8,128)(2,1)S(1)}, bf16[128,1024]{1,0:T(8,128)(2,1)S(1)}, u32[]{:S(2)}, u32[]{:S(2)}) collective-permute-start(bf16[128,1024]{1,0:T(8,128)(2,1)S(1)} %collective-permute-done.refs_2_.refs_3_.refs_4_), channel_id=1, source_target_pairs={{0,16},{16,0},{1,17},{17,1},{2,18},{18,2},{3,19},{19,3},{4,20},{20... | collective-permute-start | bytes 786440 | tf_op jit(solution)/shard_map/ppermute | solution.py:29
  40.7 5.5 %collective-permute-done.10.refs_3_.refs_4_.refs_5_ = bf16[128,1024]{1,0:T(8,128)(2,1)S(1)} collective-permute-done((bf16[128,1024]{1,0:T(8,128)(2,1)S(1)}, bf16[128,1024]{1,0:T(8,128)(2,1)S(1)}, u32[]{:S(2)}, u32[]{:S(2)}) %collective-permute-start.10) | collective-permute-done | bytes 262176 | tf_op jit(solution)/shard_map/ppermute | solution.py:29
  46.2 1.6 %collective-permute-start.12 = (bf16[128,1024]{1,0:T(8,128)(2,1)S(1)}, bf16[128,1024]{1,0:T(8,128)(2,1)S(1)}, u32[]{:S(2)}, u32[]{:S(2)}) collective-permute-start(bf16[128,1024]{1,0:T(8,128)(2,1)S(1)} %collective-permute-done.10.refs_3_.refs_4_.refs_5_), channel_id=1, source_target_pairs={{0,16},{16,0},{1,17},{17,1},{2,18},{18,2},{3,19},{19,3},{4,20},{20... | collective-permute-start | bytes 786440 | tf_op jit(solution)/shard_map/ppermute | solution.py:29
  47.8 3.6 %collective-permute-done.9.refs_9_ = bf16[128,1024]{1,0:T(8,128)(2,1)S(1)} collective-permute-done((bf16[128,1024]{1,0:T(8,128)(2,1)S(1)}, bf16[128,1024]{1,0:T(8,128)(2,1)S(1)}, u32[]{:S(2)}, u32[]{:S(2)}) %collective-permute-start.9) | collective-permute-done | bytes 262176 | tf_op jit(solution)/shard_map/ppermute | solution.py:29
  51.5 1.0 copy-done.8
  52.5 1.0 copy-done.10
  53.5 3.7 %shard_map.87.hidden = bf16[1024,1024]{1,0:T(8,128)(2,1)S(1)} custom-call(bf16[256,1024]{1,0:T(8,128)(2,1)S(1)} %copy-done.8, bf16[256,1024]{1,0:T(8,128)(2,1)S(1)} %collective-permute-done.6.refs_1_, bf16[256,1024]{1,0:T(8,128)(2,1)S(1)} %collective-permute-done.7.refs_2_, bf16[256,1024]{1,0:T(8,128)(2,1)S(1)} %collective-permute-done.8.refs_3_, ...), custom_call_target="tpu_custom_call" | custom-call | flops 2147483648 | bytes 6291456 | tf_op jit(solution)/shard_map/pallas_call | solution.py:37
  57.3 2.3 %shard_map.88 = (bf16[256,1024]{1,0:T(8,128)(2,1)S(1)}, bf16[256,1024]{1,0:T(8,128)(2,1)}) custom-call(bf16[1024,1024]{1,0:T(8,128)(2,1)S(1)} %shard_map.87.hidden, bf16[256,1024]{1,0:T(8,128)(2,1)S(1)} %copy-done.1, bf16[256,1024]{1,0:T(8,128)(2,1)S(1)} %collective-permute-done.4.refs_1_.refs_2_.refs_3_, ...), custom_call_target="tpu_custom_call" | custom-call | flops 1073741824 | bytes 5242880 | tf_op jit(solution)/shard_map/pallas_call | solution.py:37
  59.7 0.5 collective-permute-start.14
  60.1 1.4 %collective-permute-done.13.refs_0_ = bf16[256,1024]{1,0:T(8,128)(2,1)S(1)} collective-permute-done((bf16[256,1024]{1,0:T(8,128)(2,1)S(1)}, bf16[256,1024]{1,0:T(8,128)(2,1)S(1)}, u32[]{:S(2)}, u32[]{:S(2)}) %collective-permute-start.13) | collective-permute-done | bytes 524320 | tf_op jit(solution)/shard_map/ppermute | solution.py:29
  61.6 1.7 %shard_map.89 = bf16[256,1024]{1,0:T(8,128)(2,1)} custom-call(bf16[1024,1024]{1,0:T(8,128)(2,1)S(1)} %shard_map.87.hidden, bf16[256,1024]{1,0:T(8,128)(2,1)S(1)} %collective-permute-done.13.refs_0_, bf16[256,1024]{1,0:T(8,128)(2,1)S(1)} %copy-done.1, bf16[256,1024]{1,0:T(8,128)(2,1)S(1)} %collective-permute-done.4.refs_1_.refs_2_.refs_3_, ...), custom_call_target="tpu_custom_call" | custom-call | flops 536870912 | bytes 5242880 | tf_op jit(solution)/shard_map/pallas_call | solution.py:37
  63.7 0.9 copy-done.3
  64.6 0.9 copy-done.5
  65.6 0.9 copy-done.7
  66.5 1.0 copy-done.9
  67.6 2.0 %shard_map.90.own = f32[256,1024]{1,0:T(8,128)S(1)} custom-call(bf16[1024,1024]{1,0:T(8,128)(2,1)S(1)} %shard_map.87.hidden, bf16[256,1024]{1,0:T(8,128)(2,1)S(1)} %copy-done.9, bf16[256,1024]{1,0:T(8,128)(2,1)} %collective-permute-done.14.refs_1_, bf16[256,1024]{1,0:T(8,128)(2,1)S(1)} %copy-done.1, ...), custom_call_target="tpu_custom_call" | custom-call | flops 536870912 | bytes 6291456 | tf_op jit(solution)/shard_map/pallas_call | solution.py:37
  69.6 8.1 %collective-permute-done.15.back = bf16[256,1024]{1,0:T(8,128)(2,1)} collective-permute-done((bf16[256,1024]{1,0:T(8,128)(2,1)}, bf16[256,1024]{1,0:T(8,128)(2,1)}, u32[]{:S(2)}, u32[]{:S(2)}) %collective-permute-start.15) | collective-permute-done | bytes 524320 | tf_op jit(solution)/shard_map/ppermute | solution.py:29
  77.6 2.2 %shard_map.91 = bf16[32,1024]{1,0:T(8,128)(2,1)S(1)} custom-call(s32[1,256]{1,0:T(1,128)S(1)} %copy-done.12, s32[1,32]{1,0:T(1,128)S(1)} %fusion.2.order, f32[256,1024]{1,0:T(8,128)S(1)} %shard_map.90.own, bf16[256,1024]{1,0:T(8,128)(2,1)} %collective-permute-done.15.back), custom_call_target="tpu_custom_call" | custom-call | flops 5242880 | bytes 1639552 | tf_op jit(solution)/shard_map/pallas_call | solution.py:37
  79.9 1.6 %collective-permute-start.16 = (bf16[2,1,8,1024]{3,2,1,0:T(8,128)(2,1)S(1)}, bf16[2,1,8,1024]{3,2,1,0:T(8,128)(2,1)S(1)}, u32[]{:S(2)}, u32[]{:S(2)}) collective-permute-start(bf16[2,1,8,1024]{3,2,1,0:T(8,128)(2,1)S(1)} %get-tuple-element.56), channel_id=1, source_target_pairs={{0,8},{4,12},{8,0},{12,4},{1,9},{5,13},{9,1},{13,5},{2,10},{6,14},... | collective-permute-start | bytes 98312 | tf_op jit(solution)/shard_map/ppermute | solution.py:29
  81.5 2.4 %collective-permute-done.16 = bf16[2,1,8,1024]{3,2,1,0:T(8,128)(2,1)S(1)} collective-permute-done((bf16[2,1,8,1024]{3,2,1,0:T(8,128)(2,1)S(1)}, bf16[2,1,8,1024]{3,2,1,0:T(8,128)(2,1)S(1)}, u32[]{:S(2)}, u32[]{:S(2)}) %collective-permute-start.16) | collective-permute-done | bytes 32800 | tf_op jit(solution)/shard_map/ppermute | solution.py:29
  84.0 1.1 collective-permute-done.17
  85.5 3.8 %collective-permute-start.19 = (bf16[32,1024]{1,0:T(8,128)(2,1)S(1)}, bf16[32,1024]{1,0:T(8,128)(2,1)S(1)}, u32[]{:S(2)}, u32[]{:S(2)}) collective-permute-start(bf16[32,1024]{1,0:T(8,128)(2,1)S(1)} %maximum_bitcast_fusion.refs_0_), channel_id=1, source_target_pairs={{0,2},{1,3},{2,0},{3,1},{4,6},{5,7},{6,4},{7,5},{8,10},{9,11},{10,... | collective-permute-start | bytes 196616 | tf_op jit(solution)/shard_map/ppermute | solution.py:29
  89.8 4.1 %shard_map.92.refs_4_.units_ref = bf16[1024,1024]{1,0:T(8,128)(2,1)} custom-call(s32[1,16]{1,0:T(1,128)} %listed.5, bf16[4096,1024]{1,0:T(8,128)(2,1)} %targets.1), custom_call_target="tpu_custom_call" | custom-call | flops 8388608 | bytes 10485824 | tf_op jit(solution)/shard_map/pallas_call | solution.py:37
  94.0 1.5 %collective-permute-done.20.refs_3_ = bf16[32,1024]{1,0:T(8,128)(2,1)S(1)} collective-permute-done((bf16[32,1024]{1,0:T(8,128)(2,1)S(1)}, bf16[32,1024]{1,0:T(8,128)(2,1)S(1)}, u32[]{:S(2)}, u32[]{:S(2)}) %collective-permute-start.20) | collective-permute-done | bytes 65568 | tf_op jit(solution)/shard_map/ppermute | solution.py:29
  95.5 1.6 %copy-done = bf16[1024,1024]{1,0:T(8,128)(2,1)S(1)} copy-done((bf16[1024,1024]{1,0:T(8,128)(2,1)S(1)}, bf16[1024,1024]{1,0:T(8,128)(2,1)}, u32[]{:S(2)}) %copy-start) | copy-done | bytes 2097176
  97.1 3.0 %shard_map.93 = (f32[128,1024]{1,0:T(8,128)S(1)}, f32[16,256]{1,0:T(8,128)S(1)}, f32[128,1]{1,0:T(8,128)S(1)}) custom-call(s32[1,16]{1,0:T(1,128)S(1)} %copy-done.11, s32[1,128]{1,0:T(1,128)S(1)} %xor.32.place, bf16[32,1024]{1,0:T(8,128)(2,1)S(1)} %maximum_bitcast_fusion.refs_0_, bf16[32,1024]{1,0:T(8,128)(2,1)S(1)} %collective-permute-done.18.refs_1_, ...), custom_call_target="tpu_custom_call" | custom-call | flops 268435456 | bytes 2901056 | tf_op jit(solution)/shard_map/pallas_call | solution.py:37
  100.2 1.2 %collective-permute-done.21 = f32[16,256]{1,0:T(8,128)S(1)} collective-permute-done((f32[16,256]{1,0:T(8,128)S(1)}, f32[16,256]{1,0:T(8,128)S(1)}, u32[]{:S(2)}, u32[]{:S(2)}) %collective-permute-start.21) | collective-permute-done | bytes 16416 | tf_op jit(solution)/shard_map/ppermute | solution.py:29
  101.4 1.5 %collective-permute-start.22 = (f32[16,256]{1,0:T(8,128)S(1)}, f32[16,256]{1,0:T(8,128)S(1)}, u32[]{:S(2)}, u32[]{:S(2)}) collective-permute-start(f32[16,256]{1,0:T(8,128)S(1)} %add.64), channel_id=1, source_target_pairs={{0,8},{4,12},{8,0},{12,4},{1,9},{5,13},{9,1},{13,5},{2,10},{6,14},... | collective-permute-start | bytes 49160 | tf_op jit(solution)/shard_map/ppermute | solution.py:29
  102.8 2.3 %collective-permute-done.22 = f32[16,256]{1,0:T(8,128)S(1)} collective-permute-done((f32[16,256]{1,0:T(8,128)S(1)}, f32[16,256]{1,0:T(8,128)S(1)}, u32[]{:S(2)}, u32[]{:S(2)}) %collective-permute-start.22) | collective-permute-done | bytes 16416 | tf_op jit(solution)/shard_map/ppermute | solution.py:29
  105.1 1.4 %shard_map.94 = (f32[32,1152]{1,0:T(8,128)S(1)}, bf16[96,1152]{1,0:T(8,128)(2,1)S(1)}) custom-call(s32[1,16]{1,0:T(1,128)S(1)} %copy-done.11, f32[128,1024]{1,0:T(8,128)S(1)} %get-tuple-element.43.expo, f32[16,256]{1,0:T(8,128)S(1)} %add.65.columns, f32[128,1]{1,0:T(8,128)S(1)} %get-tuple-element.45.row_total, bf16[1024,1024]{1,0:T(8,128)(2,1)S(1)} %copy-done), custom_call_target="tpu_custom_call" | custom-call | flops 268435456 | bytes 3007040 | tf_op jit(solution)/shard_map/pallas_call | solution.py:37
  106.5 0.8 collective-permute-start.23
  107.3 1.8 %collective-permute-start.24 = (bf16[32,1152]{1,0:T(8,128)(2,1)S(1)}, bf16[32,1152]{1,0:T(8,128)(2,1)S(1)}, u32[]{:S(2)}, u32[]{:S(2)}) collective-permute-start(bf16[32,1152]{1,0:T(8,128)(2,1)S(1)} %get-tuple-element.51), channel_id=1, source_target_pairs={{0,2},{1,3},{2,0},{3,1},{4,6},{5,7},{6,4},{7,5},{8,10},{9,11},{10,... | collective-permute-start | bytes 221192 | tf_op jit(solution)/shard_map/ppermute | solution.py:29
  109.2 1.8 %collective-permute-start.25 = (bf16[32,1152]{1,0:T(8,128)(2,1)S(1)}, bf16[32,1152]{1,0:T(8,128)(2,1)S(1)}, u32[]{:S(2)}, u32[]{:S(2)}) collective-permute-start(bf16[32,1152]{1,0:T(8,128)(2,1)S(1)} %get-tuple-element.50), channel_id=1, source_target_pairs={{0,3},{1,2},{2,1},{3,0},{4,7},{5,6},{6,5},{7,4},{8,11},{9,10},{10,... | collective-permute-start | bytes 221192 | tf_op jit(solution)/shard_map/ppermute | solution.py:29
  111.1 3.2 %collective-permute-done.24.refs_1_ = bf16[32,1152]{1,0:T(8,128)(2,1)S(1)} collective-permute-done((bf16[32,1152]{1,0:T(8,128)(2,1)S(1)}, bf16[32,1152]{1,0:T(8,128)(2,1)S(1)}, u32[]{:S(2)}, u32[]{:S(2)}) %collective-permute-start.24) | collective-permute-done | bytes 73760 | tf_op jit(solution)/shard_map/ppermute | solution.py:29
  114.3 1.1 collective-permute-done.25.refs_2_
  115.4 0.8 shard_map.95
  (55 shorter events, 1.8 us)
Async XLA Ops:
  0.6 16.0 %collective-permute-start.5 = (bf16[256,1024]{1,0:T(8,128)(2,1)}, bf16[256,1024]{1,0:T(8,128)(2,1)S(1)}, u32[]{:S(2)}, u32[]{:S(2)}) collective-permute-start(bf16[256,1024]{1,0:T(8,128)(2,1)} %refs_4_.1), channel_id=1, source_target_pairs={{0,8},{4,12},{8,0},{12,4},{1,9},{5,13},{9,1},{13,5},{2,10},{6,14},... | collective-permute-start | bytes 1572872 | tf_op jit(solution)/shard_map/ppermute | solution.py:29
  3.6 30.2 %collective-permute-start.4 = (bf16[256,1024]{1,0:T(8,128)(2,1)}, bf16[256,1024]{1,0:T(8,128)(2,1)S(1)}, u32[]{:S(2)}, u32[]{:S(2)}) collective-permute-start(bf16[256,1024]{1,0:T(8,128)(2,1)} %refs_2_.1), channel_id=1, source_target_pairs={{0,8},{4,12},{8,0},{12,4},{1,9},{5,13},{9,1},{13,5},{2,10},{6,14},... | collective-permute-start | bytes 1572872 | tf_op jit(solution)/shard_map/ppermute | solution.py:29
  5.6 15.8 %collective-permute-start.1 = (bf16[128,1024]{1,0:T(8,128)(2,1)}, bf16[128,1024]{1,0:T(8,128)(2,1)S(1)}, u32[]{:S(2)}, u32[]{:S(2)}) collective-permute-start(bf16[128,1024]{1,0:T(8,128)(2,1)} %get-tuple-element.27), channel_id=1, source_target_pairs={{0,2},{1,3},{2,0},{3,1},{4,6},{5,7},{6,4},{7,5},{8,10},{9,11},{10,... | collective-permute-start | bytes 786440 | tf_op jit(solution)/shard_map/ppermute | solution.py:29
  16.6 20.5 %collective-permute-start.6 = (bf16[256,1024]{1,0:T(8,128)(2,1)}, bf16[256,1024]{1,0:T(8,128)(2,1)S(1)}, u32[]{:S(2)}, u32[]{:S(2)}) collective-permute-start(bf16[256,1024]{1,0:T(8,128)(2,1)} %refs_0_.5), channel_id=1, source_target_pairs={{0,1},{1,0},{2,3},{3,2},{4,5},{5,4},{6,7},{7,6},{8,9},{9,8},{10,11... | collective-permute-start | bytes 1572872 | tf_op jit(solution)/shard_map/ppermute | solution.py:29
  18.7 38.5 %copy-start.1 = (bf16[256,1024]{1,0:T(8,128)(2,1)S(1)}, bf16[256,1024]{1,0:T(8,128)(2,1)}, u32[]{:S(2)}) copy-start(bf16[256,1024]{1,0:T(8,128)(2,1)} %refs_2_.1) | copy-start | bytes 1572868
  18.7 15.1 %collective-permute-start = (bf16[128,1024]{1,0:T(8,128)(2,1)}, bf16[128,1024]{1,0:T(8,128)(2,1)S(1)}, u32[]{:S(2)}, u32[]{:S(2)}) collective-permute-start(bf16[128,1024]{1,0:T(8,128)(2,1)} %get-tuple-element.26), channel_id=1, source_target_pairs={{0,2},{1,3},{2,0},{3,1},{4,6},{5,7},{6,4},{7,5},{8,10},{9,11},{10,... | collective-permute-start | bytes 786440 | tf_op jit(solution)/shard_map/ppermute | solution.py:29
  21.3 12.5 %collective-permute-start.2 = (bf16[128,1024]{1,0:T(8,128)(2,1)S(1)}, bf16[128,1024]{1,0:T(8,128)(2,1)S(1)}, u32[]{:S(2)}, u32[]{:S(2)}) collective-permute-start(bf16[128,1024]{1,0:T(8,128)(2,1)S(1)} %collective-permute-done.1.refs_6_), channel_id=1, source_target_pairs={{0,8},{4,12},{8,0},{12,4},{1,9},{5,13},{9,1},{13,5},{2,10},{6,14},... | collective-permute-start | bytes 786440 | tf_op jit(solution)/shard_map/ppermute | solution.py:29
  22.8 11.0 %collective-permute-start.3 = (bf16[128,1024]{1,0:T(8,128)(2,1)S(1)}, bf16[128,1024]{1,0:T(8,128)(2,1)S(1)}, u32[]{:S(2)}, u32[]{:S(2)}) collective-permute-start(bf16[128,1024]{1,0:T(8,128)(2,1)S(1)} %collective-permute-done.1.refs_6_), channel_id=1, source_target_pairs={{0,16},{16,0},{1,17},{17,1},{2,18},{18,2},{3,19},{19,3},{4,20},{20... | collective-permute-start | bytes 786440 | tf_op jit(solution)/shard_map/ppermute | solution.py:29
  33.8 14.0 %collective-permute-start.7 = (bf16[256,1024]{1,0:T(8,128)(2,1)}, bf16[256,1024]{1,0:T(8,128)(2,1)S(1)}, u32[]{:S(2)}, u32[]{:S(2)}) collective-permute-start(bf16[256,1024]{1,0:T(8,128)(2,1)} %refs_0_.5), channel_id=1, source_target_pairs={{0,4},{4,0},{8,12},{12,8},{1,5},{5,1},{9,13},{13,9},{2,6},{6,2},{1... | collective-permute-start | bytes 1572872 | tf_op jit(solution)/shard_map/ppermute | solution.py:29
  37.1 14.3 %collective-permute-start.8 = (bf16[256,1024]{1,0:T(8,128)(2,1)S(1)}, bf16[256,1024]{1,0:T(8,128)(2,1)S(1)}, u32[]{:S(2)}, u32[]{:S(2)}) collective-permute-start(bf16[256,1024]{1,0:T(8,128)(2,1)S(1)} %collective-permute-done.6.refs_1_), channel_id=1, source_target_pairs={{0,4},{4,0},{8,12},{12,8},{1,5},{5,1},{9,13},{13,9},{2,6},{6,2},{1... | collective-permute-start | bytes 1572872 | tf_op jit(solution)/shard_map/ppermute | solution.py:29
  37.1 9.1 %collective-permute-start.10 = (bf16[128,1024]{1,0:T(8,128)(2,1)S(1)}, bf16[128,1024]{1,0:T(8,128)(2,1)S(1)}, u32[]{:S(2)}, u32[]{:S(2)}) collective-permute-start(bf16[128,1024]{1,0:T(8,128)(2,1)S(1)} %collective-permute-done.refs_2_.refs_3_.refs_4_), channel_id=1, source_target_pairs={{0,8},{4,12},{8,0},{12,4},{1,9},{5,13},{9,1},{13,5},{2,10},{6,14},... | collective-permute-start | bytes 786440 | tf_op jit(solution)/shard_map/ppermute | solution.py:29
  38.7 12.8 %collective-permute-start.9 = (bf16[128,1024]{1,0:T(8,128)(2,1)S(1)}, bf16[128,1024]{1,0:T(8,128)(2,1)S(1)}, u32[]{:S(2)}, u32[]{:S(2)}) collective-permute-start(bf16[128,1024]{1,0:T(8,128)(2,1)S(1)} %collective-permute-done.3.refs_8_), channel_id=1, source_target_pairs={{0,8},{4,12},{8,0},{12,4},{1,9},{5,13},{9,1},{13,5},{2,10},{6,14},... | collective-permute-start | bytes 786440 | tf_op jit(solution)/shard_map/ppermute | solution.py:29
  39.2 18.1 %collective-permute-start.11 = (bf16[128,1024]{1,0:T(8,128)(2,1)S(1)}, bf16[128,1024]{1,0:T(8,128)(2,1)S(1)}, u32[]{:S(2)}, u32[]{:S(2)}) collective-permute-start(bf16[128,1024]{1,0:T(8,128)(2,1)S(1)} %collective-permute-done.refs_2_.refs_3_.refs_4_), channel_id=1, source_target_pairs={{0,16},{16,0},{1,17},{17,1},{2,18},{18,2},{3,19},{19,3},{4,20},{20... | collective-permute-start | bytes 786440 | tf_op jit(solution)/shard_map/ppermute | solution.py:29
  46.2 15.3 %copy-start.2 = (bf16[128,1024]{1,0:T(8,128)(2,1)}, bf16[128,1024]{1,0:T(8,128)(2,1)S(1)}, u32[]{:S(2)}) copy-start(bf16[128,1024]{1,0:T(8,128)(2,1)S(1)} %collective-permute-done.10.refs_3_.refs_4_.refs_5_) | copy-start | bytes 786436
  46.2 11.0 %collective-permute-start.12 = (bf16[128,1024]{1,0:T(8,128)(2,1)S(1)}, bf16[128,1024]{1,0:T(8,128)(2,1)S(1)}, u32[]{:S(2)}, u32[]{:S(2)}) collective-permute-start(bf16[128,1024]{1,0:T(8,128)(2,1)S(1)} %collective-permute-done.10.refs_3_.refs_4_.refs_5_), channel_id=1, source_target_pairs={{0,16},{16,0},{1,17},{17,1},{2,18},{18,2},{3,19},{19,3},{4,20},{20... | collective-permute-start | bytes 786440 | tf_op jit(solution)/shard_map/ppermute | solution.py:29
  51.5 1.0 copy-start.8
  52.5 1.0 copy-start.10
  57.2 4.3 %copy-start.4 = (bf16[128,1024]{1,0:T(8,128)(2,1)}, bf16[128,1024]{1,0:T(8,128)(2,1)S(1)}, u32[]{:S(2)}) copy-start(bf16[128,1024]{1,0:T(8,128)(2,1)S(1)} %collective-permute-done.11.refs_4_.refs_5_.refs_6_) | copy-start | bytes 786436
  57.3 4.3 %copy-start.6 = (bf16[128,1024]{1,0:T(8,128)(2,1)}, bf16[128,1024]{1,0:T(8,128)(2,1)S(1)}, u32[]{:S(2)}) copy-start(bf16[128,1024]{1,0:T(8,128)(2,1)S(1)} %collective-permute-done.12.refs_5_.refs_6_.refs_7_) | copy-start | bytes 786436
  59.6 2.0 %collective-permute-start.13 = (bf16[256,1024]{1,0:T(8,128)(2,1)S(1)}, bf16[256,1024]{1,0:T(8,128)(2,1)S(1)}, u32[]{:S(2)}, u32[]{:S(2)}) collective-permute-start(bf16[256,1024]{1,0:T(8,128)(2,1)S(1)} %get-tuple-element.39), channel_id=1, source_target_pairs={{0,4},{4,0},{8,12},{12,8},{1,5},{5,1},{9,13},{13,9},{2,6},{6,2},{1... | collective-permute-start | bytes 1572872 | tf_op jit(solution)/shard_map/ppermute | solution.py:29
  59.6 4.0 %copy-start.14 = (s32[32]{0:T(128)S(1)}, s32[32]{0:T(128)}, u32[]{:S(2)}) copy-start(s32[32]{0:T(128)} %param.11) | copy-start | bytes 388
  59.7 4.0 %collective-permute-start.14 = (bf16[256,1024]{1,0:T(8,128)(2,1)}, bf16[256,1024]{1,0:T(8,128)(2,1)}, u32[]{:S(2)}, u32[]{:S(2)}) collective-permute-start(bf16[256,1024]{1,0:T(8,128)(2,1)} %get-tuple-element.41), channel_id=1, source_target_pairs={{0,4},{4,0},{8,12},{12,8},{1,5},{5,1},{9,13},{13,9},{2,6},{6,2},{1... | collective-permute-start | bytes 1572872 | tf_op jit(solution)/shard_map/ppermute | solution.py:29
  63.3 14.3 %collective-permute-start.15 = (bf16[256,1024]{1,0:T(8,128)(2,1)}, bf16[256,1024]{1,0:T(8,128)(2,1)}, u32[]{:S(2)}, u32[]{:S(2)}) collective-permute-start(bf16[256,1024]{1,0:T(8,128)(2,1)} %shard_map.89), channel_id=1, source_target_pairs={{0,1},{1,0},{2,3},{3,2},{4,5},{5,4},{6,7},{7,6},{8,9},{9,8},{10,11... | collective-permute-start | bytes 1572872 | tf_op jit(solution)/shard_map/ppermute | solution.py:29
  63.7 1.0 copy-start.3
  64.6 0.9 copy-start.5
  65.6 0.9 copy-start.7
  66.5 1.0 copy-start.9
  67.6 10.1 %copy-start.12 = (s32[1,256]{1,0:T(1,128)S(1)}, s32[1,256]{1,0:T(1,128)}, u32[]{:S(2)}) copy-start(s32[1,256]{1,0:T(1,128)} %identity.1) | copy-start | bytes 3076
  67.6 13.9 %copy-start.13 = (s32[4]{0:T(128)S(1)}, s32[4]{0:T(128)}, u32[]{:S(2)}) copy-start(s32[4]{0:T(128)} %constant.39.clone.1) | copy-start | bytes 52
  79.9 4.0 %collective-permute-start.16 = (bf16[2,1,8,1024]{3,2,1,0:T(8,128)(2,1)S(1)}, bf16[2,1,8,1024]{3,2,1,0:T(8,128)(2,1)S(1)}, u32[]{:S(2)}, u32[]{:S(2)}) collective-permute-start(bf16[2,1,8,1024]{3,2,1,0:T(8,128)(2,1)S(1)} %get-tuple-element.56), channel_id=1, source_target_pairs={{0,8},{4,12},{8,0},{12,4},{1,9},{5,13},{9,1},{13,5},{2,10},{6,14},... | collective-permute-start | bytes 98312 | tf_op jit(solution)/shard_map/ppermute | solution.py:29
  83.9 1.3 %collective-permute-start.17 = (bf16[1,2,8,1024]{3,2,1,0:T(8,128)(2,1)S(1)}, bf16[1,2,8,1024]{3,2,1,0:T(8,128)(2,1)S(1)}, u32[]{:S(2)}, u32[]{:S(2)}) collective-permute-start(bf16[1,2,8,1024]{3,2,1,0:T(8,128)(2,1)S(1)} %get-tuple-element.54), channel_id=1, source_target_pairs={{0,4},{4,0},{8,12},{12,8},{1,5},{5,1},{9,13},{13,9},{2,6},{6,2},{1... | collective-permute-start | bytes 98312 | tf_op jit(solution)/shard_map/ppermute | solution.py:29
  85.2 8.8 %collective-permute-start.18 = (bf16[32,1024]{1,0:T(8,128)(2,1)S(1)}, bf16[32,1024]{1,0:T(8,128)(2,1)S(1)}, u32[]{:S(2)}, u32[]{:S(2)}) collective-permute-start(bf16[32,1024]{1,0:T(8,128)(2,1)S(1)} %maximum_bitcast_fusion.refs_0_), channel_id=1, source_target_pairs={{0,1},{1,0},{2,3},{3,2},{4,5},{5,4},{6,7},{7,6},{8,9},{9,8},{10,11... | collective-permute-start | bytes 196616 | tf_op jit(solution)/shard_map/ppermute | solution.py:29
  85.5 8.4 %collective-permute-start.19 = (bf16[32,1024]{1,0:T(8,128)(2,1)S(1)}, bf16[32,1024]{1,0:T(8,128)(2,1)S(1)}, u32[]{:S(2)}, u32[]{:S(2)}) collective-permute-start(bf16[32,1024]{1,0:T(8,128)(2,1)S(1)} %maximum_bitcast_fusion.refs_0_), channel_id=1, source_target_pairs={{0,2},{1,3},{2,0},{3,1},{4,6},{5,7},{6,4},{7,5},{8,10},{9,11},{10,... | collective-permute-start | bytes 196616 | tf_op jit(solution)/shard_map/ppermute | solution.py:29
  89.3 6.2 %collective-permute-start.20 = (bf16[32,1024]{1,0:T(8,128)(2,1)S(1)}, bf16[32,1024]{1,0:T(8,128)(2,1)S(1)}, u32[]{:S(2)}, u32[]{:S(2)}) collective-permute-start(bf16[32,1024]{1,0:T(8,128)(2,1)S(1)} %maximum_bitcast_fusion.refs_0_), channel_id=1, source_target_pairs={{0,3},{1,2},{2,1},{3,0},{4,7},{5,6},{6,5},{7,4},{8,11},{9,10},{10,... | collective-permute-start | bytes 196616 | tf_op jit(solution)/shard_map/ppermute | solution.py:29
  89.8 5.7 %copy-start.11 = (s32[1,16]{1,0:T(1,128)S(1)}, s32[1,16]{1,0:T(1,128)}, u32[]{:S(2)}) copy-start(s32[1,16]{1,0:T(1,128)} %listed.5) | copy-start | bytes 196
  95.5 1.6 %copy-start = (bf16[1024,1024]{1,0:T(8,128)(2,1)S(1)}, bf16[1024,1024]{1,0:T(8,128)(2,1)}, u32[]{:S(2)}) copy-start(bf16[1024,1024]{1,0:T(8,128)(2,1)} %shard_map.92.refs_4_.units_ref) | copy-start | bytes 6291460
  100.1 1.2 %collective-permute-start.21 = (f32[16,256]{1,0:T(8,128)S(1)}, f32[16,256]{1,0:T(8,128)S(1)}, u32[]{:S(2)}, u32[]{:S(2)}) collective-permute-start(f32[16,256]{1,0:T(8,128)S(1)} %get-tuple-element.44), channel_id=1, source_target_pairs={{0,4},{4,0},{8,12},{12,8},{1,5},{5,1},{9,13},{13,9},{2,6},{6,2},{1... | collective-permute-start | bytes 49160 | tf_op jit(solution)/shard_map/ppermute | solution.py:29
  101.4 3.7 %collective-permute-start.22 = (f32[16,256]{1,0:T(8,128)S(1)}, f32[16,256]{1,0:T(8,128)S(1)}, u32[]{:S(2)}, u32[]{:S(2)}) collective-permute-start(f32[16,256]{1,0:T(8,128)S(1)} %add.64), channel_id=1, source_target_pairs={{0,8},{4,12},{8,0},{12,4},{1,9},{5,13},{9,1},{13,5},{2,10},{6,14},... | collective-permute-start | bytes 49160 | tf_op jit(solution)/shard_map/ppermute | solution.py:29
  106.5 4.6 %collective-permute-start.23 = (bf16[32,1152]{1,0:T(8,128)(2,1)S(1)}, bf16[32,1152]{1,0:T(8,128)(2,1)S(1)}, u32[]{:S(2)}, u32[]{:S(2)}) collective-permute-start(bf16[32,1152]{1,0:T(8,128)(2,1)S(1)} %get-tuple-element.52), channel_id=1, source_target_pairs={{0,1},{1,0},{2,3},{3,2},{4,5},{5,4},{6,7},{7,6},{8,9},{9,8},{10,11... | collective-permute-start | bytes 221192 | tf_op jit(solution)/shard_map/ppermute | solution.py:29
  107.3 7.0 %collective-permute-start.24 = (bf16[32,1152]{1,0:T(8,128)(2,1)S(1)}, bf16[32,1152]{1,0:T(8,128)(2,1)S(1)}, u32[]{:S(2)}, u32[]{:S(2)}) collective-permute-start(bf16[32,1152]{1,0:T(8,128)(2,1)S(1)} %get-tuple-element.51), channel_id=1, source_target_pairs={{0,2},{1,3},{2,0},{3,1},{4,6},{5,7},{6,4},{7,5},{8,10},{9,11},{10,... | collective-permute-start | bytes 221192 | tf_op jit(solution)/shard_map/ppermute | solution.py:29
  109.2 6.3 %collective-permute-start.25 = (bf16[32,1152]{1,0:T(8,128)(2,1)S(1)}, bf16[32,1152]{1,0:T(8,128)(2,1)S(1)}, u32[]{:S(2)}, u32[]{:S(2)}) collective-permute-start(bf16[32,1152]{1,0:T(8,128)(2,1)S(1)} %get-tuple-element.50), channel_id=1, source_target_pairs={{0,3},{1,2},{2,1},{3,0},{4,7},{5,6},{6,5},{7,4},{8,11},{9,10},{10,... | collective-permute-start | bytes 221192 | tf_op jit(solution)/shard_map/ppermute | solution.py:29

commit v4 on v3

--- a/solution.py
+++ b/solution.py
@@ -148,31 +148,34 @@
     )
 
 
-def partial_kernel(blocks, added, hidden, *refs):
+def partial_kernel(blocks, added, near, far, *refs):
     terms, refs = refs[:added], refs[added:]
+    split = near.shape[1]
     weights, outs, (held, sems) = refs[: -len(blocks) - 2], refs[-len(blocks) - 2 : -2], refs[-2:]
     for copy in fetches(weights, held, sems):
         copy.wait()
     for index, out in zip(blocks, outs):
         rows = out.shape[0]
-        sums = dot(hidden[pl.ds(index * rows, rows), :], held[...], (1, 0))
+        part = pl.ds(index * rows, rows)
+        sums = dot(near[part, :], held[:split, :], (1, 0)) + dot(far[part, :], held[split:, :], (1, 0))
         for term in terms:
             sums = sums + term[...].astype(jnp.float32)
         out[...] = sums.astype(out.dtype)
 
 
 def partial_sums(hidden, weights, blocks, terms=(), dtype=jnp.bfloat16):
-    rows, units, features = hidden.shape[0] // 4, hidden.shape[1], weights[0].shape[1]
+    rows, features = hidden[0].shape[0] // 4, weights[0].shape[1]
+    units = hidden[0].shape[1] + hidden[1].shape[1]
     return local_call(
         functools.partial(partial_kernel, blocks, len(terms)),
         (shape((rows, features), dtype),) * len(blocks),
-        (hidden, *terms, *weights),
+        (*hidden, *terms, *weights),
         2 * len(blocks) * rows * units * features,
         (
             pltpu.VMEM((units, features), jnp.bfloat16),
             pltpu.SemaphoreType.DMA((len(weights),)),
         ),
-        near=1 + len(terms),
+        near=2 + len(terms),
         place=pl.ANY,
     )
 
@@ -247,35 +250,22 @@
         ),
         scalars=1,
         place=pl.ANY,
-        vmem=58,
-    )
-
-
-def score_kernel(listed, place, *refs):
-    parts, (units_ref, expo, columns, row_total, slots, valid, units, held, sems) = (
-        refs[:-9],
-        refs[-9:],
-    )
-    copies = [
-        pltpu.make_async_copy(
-            units_ref.at[pl.ds(slot * TBLK, TBLK)], units.at[slot], sems.at[slot]
-        )
-        for slot in range(MOST)
-    ]
-    for copy in copies:
-        copy.start()
+    )
+
+
+def score_kernel(listed, place, units, *refs):
+    parts, (expo, columns, row_total, slots, valid, held) = refs[:-6], refs[-6:]
     find_slots(listed, slots, valid, columns.shape[0])
     gather_refs(parts, held)
     rows = expo.shape[0]
     sort = (place[...] == lax.broadcasted_iota(jnp.int32, (rows, rows), 0)).astype(jnp.bfloat16)
     block = dot(sort, held[...], (1, 0)).astype(jnp.bfloat16)
+    scores = dot(block, units[...], (1, 1))
     columns[...] = jnp.zeros_like(columns)
     total = jnp.zeros((rows, 1), jnp.float32)
     for slot in range(MOST):
-        part = pl.ds(slot * TBLK, TBLK)
-        weight = valid[slot].astype(jnp.float32)
-        copies[slot].wait()
-        values = jnp.exp(SCORE_SCALE * dot(block, units[slot], (1, 1))) * weight
+        part = slice(slot * TBLK, (slot + 1) * TBLK)
+        values = jnp.exp(SCORE_SCALE * scores[:, part]) * valid[slot].astype(jnp.float32)
         expo[:, part] = values
         total = total + jnp.sum(values, axis=1, keepdims=True)
         column = jnp.sum(values, axis=0, keepdims=True)
@@ -301,9 +291,7 @@
     return [first, second, value - first - second]
 
 
-def match_kernel(listed, expo, columns, row_total, units_ref, own, sent, slots, valid, units, sem):
-    copy = pltpu.make_async_copy(units_ref, units, sem)
-    copy.start()
+def match_kernel(listed, expo, columns, row_total, units, own, sent, slots, valid):
     find_slots(listed, slots, valid, columns.shape[0])
     rows = own.shape[0]
     features = units.shape[1]
@@ -317,7 +305,6 @@
         mutual = values * (values / divisor)
         mass = mass + jnp.sum(mutual, axis=1, keepdims=True)
         weights.append(mutual.astype(jnp.bfloat16))
-    copy.wait()
     numer = dot(jnp.concatenate(weights, axis=1), units[...], (1, 0))
     totals = row_total[...]
     zero = jnp.zeros((rows, 1), jnp.float32)
@@ -361,19 +348,18 @@
     inner_x, outer_x = swap(inner_weight, "src", 2), swap(outer_weight, "src", 2)
     inner_half, outer_half = weight_halves(inner_weight, outer_weight)
     inner_far, outer_far = far_piece(inner_half), far_piece(outer_half)
-    tokens_sent, inner_x = barrier((tokens, inner_x))
-    neighbour = swap(tokens_sent, "tgt", 1)
+    neighbour = swap(tokens, "tgt", 1)
     inner_far_x, inner_far_y = swap(inner_far, "src", 2), swap(inner_far, "groups", 1)
 
-    outer_far, inner_far_x, inner_far_y, outer_x, neighbour = barrier(
-        (outer_far, inner_far_x, inner_far_y, outer_x, neighbour)
-    )
+    outer_far, inner_far_y, outer_x, inner_x = barrier((outer_far, inner_far_y, outer_x, inner_x))
     outer_far_x, outer_far_y = swap(outer_far, "src", 2), swap(outer_far, "groups", 1)
     inner_square = [inner_far_x, inner_far_y, swap(inner_far_y, "src", 2)]
     outer_square = [outer_far_x, outer_far_y, swap(outer_far_x, "groups", 1)]
     shared = [tokens, neighbour, swap(tokens, "src", 1), swap(neighbour, "src", 1)]
-    hidden = hidden_units(shared, [inner_weight, inner_x, inner_far, *inner_square])
-    hidden, outer_square = barrier((hidden, outer_square))
+    hidden = [
+        hidden_units(shared, [inner_weight, inner_x]),
+        hidden_units(shared, [inner_far, *inner_square]),
+    ]
 
     weights = [outer_weight, outer_x, outer_far, *outer_square]
     pair, own = partial_sums(hidden, weights, (3, 2))
@@ -426,17 +412,10 @@
             shape((column_blocks, TBLK), jnp.float32),
             shape((block_rows, 1), jnp.float32),
         ),
-        (candidates, place, *parts, target_units),
+        (candidates, place, target_units, *parts),
         2 * block_rows * pairs * features,
-        (
-            *SLOTS,
-            pltpu.VMEM((MOST, TBLK, features), jnp.bfloat16),
-            pltpu.VMEM((block_rows, features), jnp.bfloat16),
-            pltpu.SemaphoreType.DMA((MOST,)),
-        ),
+        (*SLOTS, pltpu.VMEM((block_rows, features), jnp.bfloat16)),
         scalars=1,
-        near=1 + len(parts),
-        place=pl.ANY,
     )
     for bit in bits_of("src", 1):
         column_total = column_total + swap(column_total, "src", bit)
@@ -448,14 +427,8 @@
         ),
         (candidates, expo, column_total, row_total, target_units),
         2 * block_rows * pairs * features,
-        (
-            *SLOTS,
-            pltpu.VMEM((MOST * TBLK, features), jnp.bfloat16),
-            pltpu.SemaphoreType.DMA(()),
-        ),
+        SLOTS,
         scalars=1,
-        near=3,
-        place=pl.ANY,
     )
     received = [
         swap(sent[(offset - 1) * SENT_DEV : offset * SENT_DEV], "tgt", offset)

time: 117 us -> 110 us (0.940)
  Pallas kernels: 23.1 us -> 20 us
  starting transfers between devices: 32.2 us -> 29.4 us
  waiting for transfers between devices: 52.2 us -> 49.4 us
  local copies, waits for them, and re-layouts: 7.71 us -> 9.51 us
    pallas_call x10 -> x11, Pallas kernels: 23.1 us -> 20 us  [local_call(): pl.pallas_call(kernel, out_shape=out_shape, in_specs=[pl.BlockSpec(memory...]
    ppermute x26, waiting for transfers between devices: 52.2 us -> 49.4 us  [swap(): lax.ppermute(values, axis, [(i, i ^ offset) for i in range(lax.axis_size(...]
    ppermute x26, starting transfers between devices: 32.2 us -> 29.4 us  [swap(): lax.ppermute(values, axis, [(i, i ^ offset) for i in range(lax.axis_size(...]
    unnamed x30, local copies, waits for them, and re-layouts: 7.59 us -> 9.39 us
  transfers between devices with their start and end apart: 26 -> 26, of which waited for: 15 -> 13; matrix products, arithmetic and copies ran while one was open for 0% -> 0% of each run, Pallas kernels for 12% -> 11%
where the time goes in v4:
time: 110 us; the launch traced here: 109 us
  waiting for transfers between devices  49.4 us (45%)
  starting transfers between devices  29.4 us (27%)
  Pallas kernels  20 us (18%)
  local copies, waits for them, and re-layouts  9.51 us (9%)
    ppermute x26, waiting for transfers between devices, swap(): lax.ppermute(values, axis, [(i, i ^ offset) for i in range(lax.axis_size(...  49.4 us
    ppermute x26, starting transfers between devices, swap(): lax.ppermute(values, axis, [(i, i ^ offset) for i in range(lax.axis_size(...  29.4 us
    pallas_call x11, Pallas kernels, local_call(): pl.pallas_call(kernel, out_shape=out_shape, in_specs=[pl.BlockSpec(memory...  20 us
    unnamed x30, local copies, waits for them, and re-layouts  9.39 us
  transfers between devices with their start and end apart: 26, of which 13 were waited for; matrix products, arithmetic and copies ran while one was open for 0% of the time, Pallas kernels for 11%

profile of v4, /device:TPU:0, one launch (start us, length us, event | category | flops | bytes accessed | tf_op | source)
XLA Modules:
  0.0 109.5 jit_solution(8762154495349143828)
XLA Ops:
  0.6 3.1 %collective-permute-start = (bf16[256,1024]{1,0:T(8,128)(2,1)}, bf16[256,1024]{1,0:T(8,128)(2,1)S(1)}, u32[]{:S(2)}, u32[]{:S(2)}) collective-permute-start(bf16[256,1024]{1,0:T(8,128)(2,1)} %refs_0_.7), channel_id=1, source_target_pairs={{0,1},{1,0},{2,3},{3,2},{4,5},{5,4},{6,7},{7,6},{8,9},{9,8},{10,11... | collective-permute-start | bytes 1572872 | tf_op jit(solution)/shard_map/ppermute | solution.py:29
  3.7 1.9 %shard_map.87 = (bf16[128,1024]{1,0:T(8,128)(2,1)}, bf16[128,1024]{1,0:T(8,128)(2,1)}) custom-call(bf16[256,1024]{1,0:T(8,128)(2,1)} %refs_4_.1, bf16[256,1024]{1,0:T(8,128)(2,1)} %refs_2_.1), custom_call_target="tpu_custom_call" | custom-call | bytes 1572864 | tf_op jit(solution)/shard_map/pallas_call | solution.py:37
  5.6 2.7 %collective-permute-start.4 = (bf16[128,1024]{1,0:T(8,128)(2,1)}, bf16[128,1024]{1,0:T(8,128)(2,1)S(1)}, u32[]{:S(2)}, u32[]{:S(2)}) collective-permute-start(bf16[128,1024]{1,0:T(8,128)(2,1)} %get-tuple-element.21), channel_id=1, source_target_pairs={{0,2},{1,3},{2,0},{3,1},{4,6},{5,7},{6,4},{7,5},{8,10},{9,11},{10,... | collective-permute-start | bytes 786440 | tf_op jit(solution)/shard_map/ppermute | solution.py:29
  8.2 1.5 %collective-permute-start.6 = (bf16[256,1024]{1,0:T(8,128)(2,1)}, bf16[256,1024]{1,0:T(8,128)(2,1)S(1)}, u32[]{:S(2)}, u32[]{:S(2)}) collective-permute-start(bf16[256,1024]{1,0:T(8,128)(2,1)} %refs_2_.1), channel_id=1, source_target_pairs={{0,8},{4,12},{8,0},{12,4},{1,9},{5,13},{9,1},{13,5},{2,10},{6,14},... | collective-permute-start | bytes 1572872 | tf_op jit(solution)/shard_map/ppermute | solution.py:29
  9.7 0.5 collective-permute-start.7
  10.6 11.4 %collective-permute-done.4.refs_4_ = bf16[128,1024]{1,0:T(8,128)(2,1)S(1)} collective-permute-done((bf16[128,1024]{1,0:T(8,128)(2,1)}, bf16[128,1024]{1,0:T(8,128)(2,1)S(1)}, u32[]{:S(2)}, u32[]{:S(2)}) %collective-permute-start.4) | collective-permute-done | bytes 262176 | tf_op jit(solution)/shard_map/ppermute | solution.py:29
  22.0 1.5 %collective-permute-start.5 = (bf16[128,1024]{1,0:T(8,128)(2,1)S(1)}, bf16[128,1024]{1,0:T(8,128)(2,1)S(1)}, u32[]{:S(2)}, u32[]{:S(2)}) collective-permute-start(bf16[128,1024]{1,0:T(8,128)(2,1)S(1)} %collective-permute-done.4.refs_4_), channel_id=1, source_target_pairs={{0,16},{16,0},{1,17},{17,1},{2,18},{18,2},{3,19},{19,3},{4,20},{20... | collective-permute-start | bytes 786440 | tf_op jit(solution)/shard_map/ppermute | solution.py:29
  23.6 7.9 %collective-permute-done.3.refs_2_.refs_3_.refs_4_ = bf16[128,1024]{1,0:T(8,128)(2,1)S(1)} collective-permute-done((bf16[128,1024]{1,0:T(8,128)(2,1)}, bf16[128,1024]{1,0:T(8,128)(2,1)S(1)}, u32[]{:S(2)}, u32[]{:S(2)}) %collective-permute-start.3) | collective-permute-done | bytes 262176 | tf_op jit(solution)/shard_map/ppermute | solution.py:29
  32.0 0.8 collective-permute-done.7.refs_5_
  32.8 1.5 %collective-permute-start.10 = (bf16[128,1024]{1,0:T(8,128)(2,1)S(1)}, bf16[128,1024]{1,0:T(8,128)(2,1)S(1)}, u32[]{:S(2)}, u32[]{:S(2)}) collective-permute-start(bf16[128,1024]{1,0:T(8,128)(2,1)S(1)} %collective-permute-done.3.refs_2_.refs_3_.refs_4_), channel_id=1, source_target_pairs={{0,8},{4,12},{8,0},{12,4},{1,9},{5,13},{9,1},{13,5},{2,10},{6,14},... | collective-permute-start | bytes 786440 | tf_op jit(solution)/shard_map/ppermute | solution.py:29
  34.3 0.5 collective-permute-start.8
  34.8 1.5 %collective-permute-start.9 = (bf16[128,1024]{1,0:T(8,128)(2,1)S(1)}, bf16[128,1024]{1,0:T(8,128)(2,1)S(1)}, u32[]{:S(2)}, u32[]{:S(2)}) collective-permute-start(bf16[128,1024]{1,0:T(8,128)(2,1)S(1)} %collective-permute-done.5.refs_6_), channel_id=1, source_target_pairs={{0,8},{4,12},{8,0},{12,4},{1,9},{5,13},{9,1},{13,5},{2,10},{6,14},... | collective-permute-start | bytes 786440 | tf_op jit(solution)/shard_map/ppermute | solution.py:29
  36.3 1.5 %collective-permute-start.11 = (bf16[128,1024]{1,0:T(8,128)(2,1)S(1)}, bf16[128,1024]{1,0:T(8,128)(2,1)S(1)}, u32[]{:S(2)}, u32[]{:S(2)}) collective-permute-start(bf16[128,1024]{1,0:T(8,128)(2,1)S(1)} %collective-permute-done.3.refs_2_.refs_3_.refs_4_), channel_id=1, source_target_pairs={{0,16},{16,0},{1,17},{17,1},{2,18},{18,2},{3,19},{19,3},{4,20},{20... | collective-permute-start | bytes 786440 | tf_op jit(solution)/shard_map/ppermute | solution.py:29
  37.8 4.2 %collective-permute-done.10.refs_3_.refs_4_.refs_5_ = bf16[128,1024]{1,0:T(8,128)(2,1)S(1)} collective-permute-done((bf16[128,1024]{1,0:T(8,128)(2,1)S(1)}, bf16[128,1024]{1,0:T(8,128)(2,1)S(1)}, u32[]{:S(2)}, u32[]{:S(2)}) %collective-permute-start.10) | collective-permute-done | bytes 262176 | tf_op jit(solution)/shard_map/ppermute | solution.py:29
  42.0 1.5 %collective-permute-start.12 = (bf16[128,1024]{1,0:T(8,128)(2,1)S(1)}, bf16[128,1024]{1,0:T(8,128)(2,1)S(1)}, u32[]{:S(2)}, u32[]{:S(2)}) collective-permute-start(bf16[128,1024]{1,0:T(8,128)(2,1)S(1)} %collective-permute-done.10.refs_3_.refs_4_.refs_5_), channel_id=1, source_target_pairs={{0,16},{16,0},{1,17},{17,1},{2,18},{18,2},{3,19},{19,3},{4,20},{20... | collective-permute-start | bytes 786440 | tf_op jit(solution)/shard_map/ppermute | solution.py:29
  43.6 1.0 copy-done.2
  44.6 1.0 copy-done.10
  45.7 2.3 %shard_map.88.near = bf16[1024,512]{1,0:T(8,128)(2,1)S(1)} custom-call(bf16[256,1024]{1,0:T(8,128)(2,1)S(1)} %copy-done.2, bf16[256,1024]{1,0:T(8,128)(2,1)S(1)} %collective-permute-done.refs_1_, bf16[256,1024]{1,0:T(8,128)(2,1)S(1)} %collective-permute-done.1.refs_2_, bf16[256,1024]{1,0:T(8,128)(2,1)S(1)} %collective-permute-done.2.refs_3_, ...), custom_call_target="tpu_custom_call" | custom-call | flops 1073741824 | bytes 4194304 | tf_op jit(solution)/shard_map/pallas_call | solution.py:37
  48.0 3.5 %collective-permute-done.9.refs_7_ = bf16[128,1024]{1,0:T(8,128)(2,1)S(1)} collective-permute-done((bf16[128,1024]{1,0:T(8,128)(2,1)S(1)}, bf16[128,1024]{1,0:T(8,128)(2,1)S(1)}, u32[]{:S(2)}, u32[]{:S(2)}) %collective-permute-start.9) | collective-permute-done | bytes 262176 | tf_op jit(solution)/shard_map/ppermute | solution.py:29
  51.5 2.3 %shard_map.89.far = bf16[1024,512]{1,0:T(8,128)(2,1)S(1)} custom-call(bf16[256,1024]{1,0:T(8,128)(2,1)S(1)} %copy-done.2, bf16[256,1024]{1,0:T(8,128)(2,1)S(1)} %collective-permute-done.refs_1_, bf16[256,1024]{1,0:T(8,128)(2,1)S(1)} %collective-permute-done.1.refs_2_, bf16[256,1024]{1,0:T(8,128)(2,1)S(1)} %collective-permute-done.2.refs_3_, ...), custom_call_target="tpu_custom_call" | custom-call | flops 1073741824 | bytes 4194304 | tf_op jit(solution)/shard_map/pallas_call | solution.py:37
  53.9 2.3 %shard_map.90 = (bf16[256,1024]{1,0:T(8,128)(2,1)S(1)}, bf16[256,1024]{1,0:T(8,128)(2,1)}) custom-call(bf16[1024,512]{1,0:T(8,128)(2,1)S(1)} %shard_map.88.near, bf16[1024,512]{1,0:T(8,128)(2,1)S(1)} %shard_map.89.far, bf16[256,1024]{1,0:T(8,128)(2,1)S(1)} %copy-done.1, bf16[256,1024]{1,0:T(8,128)(2,1)S(1)} %collective-permute-done.6.refs_1_.refs_2_.refs_3_, ...), custom_call_target="tpu_custom_call" | custom-call | flops 1073741824 | bytes 5242880 | tf_op jit(solution)/shard_map/pallas_call | solution.py:37
  56.8 1.4 %collective-permute-done.13.refs_0_ = bf16[256,1024]{1,0:T(8,128)(2,1)S(1)} collective-permute-done((bf16[256,1024]{1,0:T(8,128)(2,1)S(1)}, bf16[256,1024]{1,0:T(8,128)(2,1)S(1)}, u32[]{:S(2)}, u32[]{:S(2)}) %collective-permute-start.13) | collective-permute-done | bytes 524320 | tf_op jit(solution)/shard_map/ppermute | solution.py:29
  58.2 1.7 %shard_map.91 = bf16[256,1024]{1,0:T(8,128)(2,1)} custom-call(bf16[1024,512]{1,0:T(8,128)(2,1)S(1)} %shard_map.88.near, bf16[1024,512]{1,0:T(8,128)(2,1)S(1)} %shard_map.89.far, bf16[256,1024]{1,0:T(8,128)(2,1)S(1)} %collective-permute-done.13.refs_0_, bf16[256,1024]{1,0:T(8,128)(2,1)S(1)} %copy-done.1, ...), custom_call_target="tpu_custom_call" | custom-call | flops 536870912 | bytes 5242880 | tf_op jit(solution)/shard_map/pallas_call | solution.py:37
  60.1 1.0 copy-done.3
  61.1 0.9 copy-done.5
  62.0 0.9 copy-done.7
  63.0 0.9 copy-done.9
  63.9 2.0 %shard_map.92.own = f32[256,1024]{1,0:T(8,128)S(1)} custom-call(bf16[1024,512]{1,0:T(8,128)(2,1)S(1)} %shard_map.88.near, bf16[1024,512]{1,0:T(8,128)(2,1)S(1)} %shard_map.89.far, bf16[256,1024]{1,0:T(8,128)(2,1)S(1)} %copy-done.3, bf16[256,1024]{1,0:T(8,128)(2,1)} %collective-permute-done.14.refs_1_, bf16[256,1024]{1,0:T(8,128)(2,1)S(1)} %copy-done.1, ...), custom_call_target="tpu_custom_call" | custom-call | flops 536870912 | bytes 6291456 | tf_op jit(solution)/shard_map/pallas_call | solution.py:37
  65.9 8.3 %collective-permute-done.15.back = bf16[256,1024]{1,0:T(8,128)(2,1)} collective-permute-done((bf16[256,1024]{1,0:T(8,128)(2,1)}, bf16[256,1024]{1,0:T(8,128)(2,1)}, u32[]{:S(2)}, u32[]{:S(2)}) %collective-permute-start.15) | collective-permute-done | bytes 524320 | tf_op jit(solution)/shard_map/ppermute | solution.py:29
  74.3 2.2 %shard_map.93 = bf16[32,1024]{1,0:T(8,128)(2,1)S(1)} custom-call(s32[1,256]{1,0:T(1,128)S(1)} %copy-done.12, s32[1,32]{1,0:T(1,128)S(1)} %fusion.2.order, f32[256,1024]{1,0:T(8,128)S(1)} %shard_map.92.own, bf16[256,1024]{1,0:T(8,128)(2,1)} %collective-permute-done.15.back), custom_call_target="tpu_custom_call" | custom-call | flops 5242880 | bytes 1639552 | tf_op jit(solution)/shard_map/pallas_call | solution.py:37
  76.5 1.6 %collective-permute-start.16 = (bf16[2,1,8,1024]{3,2,1,0:T(8,128)(2,1)S(1)}, bf16[2,1,8,1024]{3,2,1,0:T(8,128)(2,1)S(1)}, u32[]{:S(2)}, u32[]{:S(2)}) collective-permute-start(bf16[2,1,8,1024]{3,2,1,0:T(8,128)(2,1)S(1)} %get-tuple-element.44), channel_id=1, source_target_pairs={{0,8},{4,12},{8,0},{12,4},{1,9},{5,13},{9,1},{13,5},{2,10},{6,14},... | collective-permute-start | bytes 98312 | tf_op jit(solution)/shard_map/ppermute | solution.py:29
  78.1 2.4 %collective-permute-done.16 = bf16[2,1,8,1024]{3,2,1,0:T(8,128)(2,1)S(1)} collective-permute-done((bf16[2,1,8,1024]{3,2,1,0:T(8,128)(2,1)S(1)}, bf16[2,1,8,1024]{3,2,1,0:T(8,128)(2,1)S(1)}, u32[]{:S(2)}, u32[]{:S(2)}) %collective-permute-start.16) | collective-permute-done | bytes 32800 | tf_op jit(solution)/shard_map/ppermute | solution.py:29
  80.6 1.1 %collective-permute-done.17 = bf16[1,2,8,1024]{3,2,1,0:T(8,128)(2,1)S(1)} collective-permute-done((bf16[1,2,8,1024]{3,2,1,0:T(8,128)(2,1)S(1)}, bf16[1,2,8,1024]{3,2,1,0:T(8,128)(2,1)S(1)}, u32[]{:S(2)}, u32[]{:S(2)}) %collective-permute-start.17) | collective-permute-done | bytes 32800 | tf_op jit(solution)/shard_map/ppermute | solution.py:29
  82.1 2.8 %collective-permute-start.19 = (bf16[32,1024]{1,0:T(8,128)(2,1)S(1)}, bf16[32,1024]{1,0:T(8,128)(2,1)S(1)}, u32[]{:S(2)}, u32[]{:S(2)}) collective-permute-start(bf16[32,1024]{1,0:T(8,128)(2,1)S(1)} %maximum_bitcast_fusion.refs_0_), channel_id=1, source_target_pairs={{0,2},{1,3},{2,0},{3,1},{4,6},{5,7},{6,4},{7,5},{8,10},{9,11},{10,... | collective-permute-start | bytes 196616 | tf_op jit(solution)/shard_map/ppermute | solution.py:29
  84.9 1.3 %collective-permute-start.20 = (bf16[32,1024]{1,0:T(8,128)(2,1)S(1)}, bf16[32,1024]{1,0:T(8,128)(2,1)S(1)}, u32[]{:S(2)}, u32[]{:S(2)}) collective-permute-start(bf16[32,1024]{1,0:T(8,128)(2,1)S(1)} %maximum_bitcast_fusion.refs_0_), channel_id=1, source_target_pairs={{0,3},{1,2},{2,1},{3,0},{4,7},{5,6},{6,5},{7,4},{8,11},{9,10},{10,... | collective-permute-start | bytes 196616 | tf_op jit(solution)/shard_map/ppermute | solution.py:29
  86.4 3.4 %copy-done = bf16[4096,1024]{1,0:T(8,128)(2,1)S(1)} copy-done((bf16[4096,1024]{1,0:T(8,128)(2,1)S(1)}, bf16[4096,1024]{1,0:T(8,128)(2,1)}, u32[]{:S(2)}) %copy-start) | copy-done | bytes 8388632
  89.8 1.7 %shard_map.86.units = bf16[1024,1024]{1,0:T(8,128)(2,1)S(1)} custom-call(s32[1,16]{1,0:T(1,128)S(1)} %copy-done.11, bf16[4096,1024]{1,0:T(8,128)(2,1)S(1)} %copy-done), custom_call_target="tpu_custom_call" | custom-call | flops 8388608 | bytes 10485824 | tf_op jit(solution)/shard_map/pallas_call | solution.py:37
  91.5 1.8 %shard_map.94 = (f32[128,1024]{1,0:T(8,128)S(1)}, f32[16,256]{1,0:T(8,128)S(1)}, f32[128,1]{1,0:T(8,128)S(1)}) custom-call(s32[1,16]{1,0:T(1,128)S(1)} %copy-done.11, s32[1,128]{1,0:T(1,128)S(1)} %xor.32.place, bf16[1024,1024]{1,0:T(8,128)(2,1)S(1)} %shard_map.86.units, bf16[32,1024]{1,0:T(8,128)(2,1)S(1)} %maximum_bitcast_fusion.refs_0_, ...), custom_call_target="tpu_custom_call" | custom-call | flops 268435456 | bytes 2901056 | tf_op jit(solution)/shard_map/pallas_call | solution.py:37
  93.3 1.2 %collective-permute-done.21 = f32[16,256]{1,0:T(8,128)S(1)} collective-permute-done((f32[16,256]{1,0:T(8,128)S(1)}, f32[16,256]{1,0:T(8,128)S(1)}, u32[]{:S(2)}, u32[]{:S(2)}) %collective-permute-start.21) | collective-permute-done | bytes 16416 | tf_op jit(solution)/shard_map/ppermute | solution.py:29
  94.5 1.5 %collective-permute-start.22 = (f32[16,256]{1,0:T(8,128)S(1)}, f32[16,256]{1,0:T(8,128)S(1)}, u32[]{:S(2)}, u32[]{:S(2)}) collective-permute-start(f32[16,256]{1,0:T(8,128)S(1)} %add.64), channel_id=1, source_target_pairs={{0,8},{4,12},{8,0},{12,4},{1,9},{5,13},{9,1},{13,5},{2,10},{6,14},... | collective-permute-start | bytes 49160 | tf_op jit(solution)/shard_map/ppermute | solution.py:29
  96.0 2.2 %collective-permute-done.22 = f32[16,256]{1,0:T(8,128)S(1)} collective-permute-done((f32[16,256]{1,0:T(8,128)S(1)}, f32[16,256]{1,0:T(8,128)S(1)}, u32[]{:S(2)}, u32[]{:S(2)}) %collective-permute-start.22) | collective-permute-done | bytes 16416 | tf_op jit(solution)/shard_map/ppermute | solution.py:29
  98.3 1.1 %shard_map.95 = (f32[32,1152]{1,0:T(8,128)S(1)}, bf16[96,1152]{1,0:T(8,128)(2,1)S(1)}) custom-call(s32[1,16]{1,0:T(1,128)S(1)} %copy-done.11, f32[128,1024]{1,0:T(8,128)S(1)} %get-tuple-element.31.expo, f32[16,256]{1,0:T(8,128)S(1)} %add.65.columns, f32[128,1]{1,0:T(8,128)S(1)} %get-tuple-element.33.row_total, bf16[1024,1024]{1,0:T(8,128)(2,1)S(1)} %shard_map.86.units), custom_call_target="tpu_custom_call" | custom-call | flops 268435456 | bytes 3007040 | tf_op jit(solution)/shard_map/pallas_call | solution.py:37
  99.4 0.6 collective-permute-start.23
  100.1 2.5 %collective-permute-start.24 = (bf16[32,1152]{1,0:T(8,128)(2,1)S(1)}, bf16[32,1152]{1,0:T(8,128)(2,1)S(1)}, u32[]{:S(2)}, u32[]{:S(2)}) collective-permute-start(bf16[32,1152]{1,0:T(8,128)(2,1)S(1)} %get-tuple-element.39), channel_id=1, source_target_pairs={{0,2},{1,3},{2,0},{3,1},{4,6},{5,7},{6,4},{7,5},{8,10},{9,11},{10,... | collective-permute-start | bytes 221192 | tf_op jit(solution)/shard_map/ppermute | solution.py:29
  102.5 1.3 %collective-permute-start.25 = (bf16[32,1152]{1,0:T(8,128)(2,1)S(1)}, bf16[32,1152]{1,0:T(8,128)(2,1)S(1)}, u32[]{:S(2)}, u32[]{:S(2)}) collective-permute-start(bf16[32,1152]{1,0:T(8,128)(2,1)S(1)} %get-tuple-element.38), channel_id=1, source_target_pairs={{0,3},{1,2},{2,1},{3,0},{4,7},{5,6},{6,5},{7,4},{8,11},{9,10},{10,... | collective-permute-start | bytes 221192 | tf_op jit(solution)/shard_map/ppermute | solution.py:29
  103.9 3.3 %collective-permute-done.24.refs_1_ = bf16[32,1152]{1,0:T(8,128)(2,1)S(1)} collective-permute-done((bf16[32,1152]{1,0:T(8,128)(2,1)S(1)}, bf16[32,1152]{1,0:T(8,128)(2,1)S(1)}, u32[]{:S(2)}, u32[]{:S(2)}) %collective-permute-start.24) | collective-permute-done | bytes 73760 | tf_op jit(solution)/shard_map/ppermute | solution.py:29
  107.1 1.6 %collective-permute-done.25.refs_2_ = bf16[32,1152]{1,0:T(8,128)(2,1)S(1)} collective-permute-done((bf16[32,1152]{1,0:T(8,128)(2,1)S(1)}, bf16[32,1152]{1,0:T(8,128)(2,1)S(1)}, u32[]{:S(2)}, u32[]{:S(2)}) %collective-permute-start.25) | collective-permute-done | bytes 73760 | tf_op jit(solution)/shard_map/ppermute | solution.py:29
  108.7 0.8 shard_map.96
  (56 shorter events, 2.4 us)
Async XLA Ops:
  0.6 53.2 %copy-start.1 = (bf16[256,1024]{1,0:T(8,128)(2,1)S(1)}, bf16[256,1024]{1,0:T(8,128)(2,1)}, u32[]{:S(2)}) copy-start(bf16[256,1024]{1,0:T(8,128)(2,1)} %refs_2_.1) | copy-start | bytes 1572868
  0.6 30.8 %collective-permute-start = (bf16[256,1024]{1,0:T(8,128)(2,1)}, bf16[256,1024]{1,0:T(8,128)(2,1)S(1)}, u32[]{:S(2)}, u32[]{:S(2)}) collective-permute-start(bf16[256,1024]{1,0:T(8,128)(2,1)} %refs_0_.7), channel_id=1, source_target_pairs={{0,1},{1,0},{2,3},{3,2},{4,5},{5,4},{6,7},{7,6},{8,9},{9,8},{10,11... | collective-permute-start | bytes 1572872 | tf_op jit(solution)/shard_map/ppermute | solution.py:29
  5.6 16.4 %collective-permute-start.4 = (bf16[128,1024]{1,0:T(8,128)(2,1)}, bf16[128,1024]{1,0:T(8,128)(2,1)S(1)}, u32[]{:S(2)}, u32[]{:S(2)}) collective-permute-start(bf16[128,1024]{1,0:T(8,128)(2,1)} %get-tuple-element.21), channel_id=1, source_target_pairs={{0,2},{1,3},{2,0},{3,1},{4,6},{5,7},{6,4},{7,5},{8,10},{9,11},{10,... | collective-permute-start | bytes 786440 | tf_op jit(solution)/shard_map/ppermute | solution.py:29
  8.2 23.7 %collective-permute-start.6 = (bf16[256,1024]{1,0:T(8,128)(2,1)}, bf16[256,1024]{1,0:T(8,128)(2,1)S(1)}, u32[]{:S(2)}, u32[]{:S(2)}) collective-permute-start(bf16[256,1024]{1,0:T(8,128)(2,1)} %refs_2_.1), channel_id=1, source_target_pairs={{0,8},{4,12},{8,0},{12,4},{1,9},{5,13},{9,1},{13,5},{2,10},{6,14},... | collective-permute-start | bytes 1572872 | tf_op jit(solution)/shard_map/ppermute | solution.py:29
  9.7 23.1 %collective-permute-start.7 = (bf16[256,1024]{1,0:T(8,128)(2,1)}, bf16[256,1024]{1,0:T(8,128)(2,1)S(1)}, u32[]{:S(2)}, u32[]{:S(2)}) collective-permute-start(bf16[256,1024]{1,0:T(8,128)(2,1)} %refs_4_.1), channel_id=1, source_target_pairs={{0,8},{4,12},{8,0},{12,4},{1,9},{5,13},{9,1},{13,5},{2,10},{6,14},... | collective-permute-start | bytes 1572872 | tf_op jit(solution)/shard_map/ppermute | solution.py:29
  10.3 49.7 %copy-start.14 = (s32[32]{0:T(128)S(1)}, s32[32]{0:T(128)}, u32[]{:S(2)}) copy-start(s32[32]{0:T(128)} %param.11) | copy-start | bytes 388
  10.3 21.2 %collective-permute-start.3 = (bf16[128,1024]{1,0:T(8,128)(2,1)}, bf16[128,1024]{1,0:T(8,128)(2,1)S(1)}, u32[]{:S(2)}, u32[]{:S(2)}) collective-permute-start(bf16[128,1024]{1,0:T(8,128)(2,1)} %get-tuple-element.20), channel_id=1, source_target_pairs={{0,2},{1,3},{2,0},{3,1},{4,6},{5,7},{6,4},{7,5},{8,10},{9,11},{10,... | collective-permute-start | bytes 786440 | tf_op jit(solution)/shard_map/ppermute | solution.py:29
  22.0 9.9 %collective-permute-start.5 = (bf16[128,1024]{1,0:T(8,128)(2,1)S(1)}, bf16[128,1024]{1,0:T(8,128)(2,1)S(1)}, u32[]{:S(2)}, u32[]{:S(2)}) collective-permute-start(bf16[128,1024]{1,0:T(8,128)(2,1)S(1)} %collective-permute-done.4.refs_4_), channel_id=1, source_target_pairs={{0,16},{16,0},{1,17},{17,1},{2,18},{18,2},{3,19},{19,3},{4,20},{20... | collective-permute-start | bytes 786440 | tf_op jit(solution)/shard_map/ppermute | solution.py:29
  31.4 4.9 %collective-permute-start.1 = (bf16[256,1024]{1,0:T(8,128)(2,1)}, bf16[256,1024]{1,0:T(8,128)(2,1)S(1)}, u32[]{:S(2)}, u32[]{:S(2)}) collective-permute-start(bf16[256,1024]{1,0:T(8,128)(2,1)} %refs_0_.7), channel_id=1, source_target_pairs={{0,4},{4,0},{8,12},{12,8},{1,5},{5,1},{9,13},{13,9},{2,6},{6,2},{1... | collective-permute-start | bytes 1572872 | tf_op jit(solution)/shard_map/ppermute | solution.py:29
  31.4 12.1 %collective-permute-start.2 = (bf16[256,1024]{1,0:T(8,128)(2,1)S(1)}, bf16[256,1024]{1,0:T(8,128)(2,1)S(1)}, u32[]{:S(2)}, u32[]{:S(2)}) collective-permute-start(bf16[256,1024]{1,0:T(8,128)(2,1)S(1)} %collective-permute-done.refs_1_), channel_id=1, source_target_pairs={{0,4},{4,0},{8,12},{12,8},{1,5},{5,1},{9,13},{13,9},{2,6},{6,2},{1... | collective-permute-start | bytes 1572872 | tf_op jit(solution)/shard_map/ppermute | solution.py:29
  32.8 9.2 %collective-permute-start.10 = (bf16[128,1024]{1,0:T(8,128)(2,1)S(1)}, bf16[128,1024]{1,0:T(8,128)(2,1)S(1)}, u32[]{:S(2)}, u32[]{:S(2)}) collective-permute-start(bf16[128,1024]{1,0:T(8,128)(2,1)S(1)} %collective-permute-done.3.refs_2_.refs_3_.refs_4_), channel_id=1, source_target_pairs={{0,8},{4,12},{8,0},{12,4},{1,9},{5,13},{9,1},{13,5},{2,10},{6,14},... | collective-permute-start | bytes 786440 | tf_op jit(solution)/shard_map/ppermute | solution.py:29
  34.3 13.7 %collective-permute-start.8 = (bf16[128,1024]{1,0:T(8,128)(2,1)S(1)}, bf16[128,1024]{1,0:T(8,128)(2,1)S(1)}, u32[]{:S(2)}, u32[]{:S(2)}) collective-permute-start(bf16[128,1024]{1,0:T(8,128)(2,1)S(1)} %collective-permute-done.4.refs_4_), channel_id=1, source_target_pairs={{0,8},{4,12},{8,0},{12,4},{1,9},{5,13},{9,1},{13,5},{2,10},{6,14},... | collective-permute-start | bytes 786440 | tf_op jit(solution)/shard_map/ppermute | solution.py:29
  34.8 16.7 %collective-permute-start.9 = (bf16[128,1024]{1,0:T(8,128)(2,1)S(1)}, bf16[128,1024]{1,0:T(8,128)(2,1)S(1)}, u32[]{:S(2)}, u32[]{:S(2)}) collective-permute-start(bf16[128,1024]{1,0:T(8,128)(2,1)S(1)} %collective-permute-done.5.refs_6_), channel_id=1, source_target_pairs={{0,8},{4,12},{8,0},{12,4},{1,9},{5,13},{9,1},{13,5},{2,10},{6,14},... | collective-permute-start | bytes 786440 | tf_op jit(solution)/shard_map/ppermute | solution.py:29
  36.3 17.5 %collective-permute-start.11 = (bf16[128,1024]{1,0:T(8,128)(2,1)S(1)}, bf16[128,1024]{1,0:T(8,128)(2,1)S(1)}, u32[]{:S(2)}, u32[]{:S(2)}) collective-permute-start(bf16[128,1024]{1,0:T(8,128)(2,1)S(1)} %collective-permute-done.3.refs_2_.refs_3_.refs_4_), channel_id=1, source_target_pairs={{0,16},{16,0},{1,17},{17,1},{2,18},{18,2},{3,19},{19,3},{4,20},{20... | collective-permute-start | bytes 786440 | tf_op jit(solution)/shard_map/ppermute | solution.py:29
  42.0 17.9 %copy-start.4 = (bf16[128,1024]{1,0:T(8,128)(2,1)}, bf16[128,1024]{1,0:T(8,128)(2,1)S(1)}, u32[]{:S(2)}) copy-start(bf16[128,1024]{1,0:T(8,128)(2,1)S(1)} %collective-permute-done.10.refs_3_.refs_4_.refs_5_) | copy-start | bytes 786436
  42.0 11.8 %collective-permute-start.12 = (bf16[128,1024]{1,0:T(8,128)(2,1)S(1)}, bf16[128,1024]{1,0:T(8,128)(2,1)S(1)}, u32[]{:S(2)}, u32[]{:S(2)}) collective-permute-start(bf16[128,1024]{1,0:T(8,128)(2,1)S(1)} %collective-permute-done.10.refs_3_.refs_4_.refs_5_), channel_id=1, source_target_pairs={{0,16},{16,0},{1,17},{17,1},{2,18},{18,2},{3,19},{19,3},{4,20},{20... | collective-permute-start | bytes 786440 | tf_op jit(solution)/shard_map/ppermute | solution.py:29
  43.6 1.0 copy-start.2
  44.6 1.0 copy-start.10
  53.8 20.5 %copy-start.12 = (s32[1,256]{1,0:T(1,128)S(1)}, s32[1,256]{1,0:T(1,128)}, u32[]{:S(2)}) copy-start(s32[1,256]{1,0:T(1,128)} %identity.1) | copy-start | bytes 3076
  53.8 24.3 %copy-start.13 = (s32[4]{0:T(128)S(1)}, s32[4]{0:T(128)}, u32[]{:S(2)}) copy-start(s32[4]{0:T(128)} %constant.39.clone.1) | copy-start | bytes 52
  53.8 32.6 %copy-start.11 = (s32[1,16]{1,0:T(1,128)S(1)}, s32[1,16]{1,0:T(1,128)}, u32[]{:S(2)}) copy-start(s32[1,16]{1,0:T(1,128)} %listed.5) | copy-start | bytes 196
  53.9 6.1 %copy-start.6 = (bf16[128,1024]{1,0:T(8,128)(2,1)}, bf16[128,1024]{1,0:T(8,128)(2,1)S(1)}, u32[]{:S(2)}) copy-start(bf16[128,1024]{1,0:T(8,128)(2,1)S(1)} %collective-permute-done.11.refs_4_.refs_5_.refs_6_) | copy-start | bytes 786436
  53.9 6.1 %copy-start.8 = (bf16[128,1024]{1,0:T(8,128)(2,1)}, bf16[128,1024]{1,0:T(8,128)(2,1)S(1)}, u32[]{:S(2)}) copy-start(bf16[128,1024]{1,0:T(8,128)(2,1)S(1)} %collective-permute-done.12.refs_5_.refs_6_.refs_7_) | copy-start | bytes 786436
  56.2 2.0 %collective-permute-start.13 = (bf16[256,1024]{1,0:T(8,128)(2,1)S(1)}, bf16[256,1024]{1,0:T(8,128)(2,1)S(1)}, u32[]{:S(2)}, u32[]{:S(2)}) collective-permute-start(bf16[256,1024]{1,0:T(8,128)(2,1)S(1)} %get-tuple-element.26), channel_id=1, source_target_pairs={{0,4},{4,0},{8,12},{12,8},{1,5},{5,1},{9,13},{13,9},{2,6},{6,2},{1... | collective-permute-start | bytes 1572872 | tf_op jit(solution)/shard_map/ppermute | solution.py:29
  56.3 3.8 %collective-permute-start.14 = (bf16[256,1024]{1,0:T(8,128)(2,1)}, bf16[256,1024]{1,0:T(8,128)(2,1)}, u32[]{:S(2)}, u32[]{:S(2)}) collective-permute-start(bf16[256,1024]{1,0:T(8,128)(2,1)} %get-tuple-element.29), channel_id=1, source_target_pairs={{0,4},{4,0},{8,12},{12,8},{1,5},{5,1},{9,13},{13,9},{2,6},{6,2},{1... | collective-permute-start | bytes 1572872 | tf_op jit(solution)/shard_map/ppermute | solution.py:29
  59.9 14.3 %collective-permute-start.15 = (bf16[256,1024]{1,0:T(8,128)(2,1)}, bf16[256,1024]{1,0:T(8,128)(2,1)}, u32[]{:S(2)}, u32[]{:S(2)}) collective-permute-start(bf16[256,1024]{1,0:T(8,128)(2,1)} %shard_map.91), channel_id=1, source_target_pairs={{0,1},{1,0},{2,3},{3,2},{4,5},{5,4},{6,7},{7,6},{8,9},{9,8},{10,11... | collective-permute-start | bytes 1572872 | tf_op jit(solution)/shard_map/ppermute | solution.py:29
  60.1 1.0 copy-start.3
  61.1 0.9 copy-start.5
  62.0 0.9 copy-start.7
  63.0 0.9 copy-start.9
  76.5 4.0 %collective-permute-start.16 = (bf16[2,1,8,1024]{3,2,1,0:T(8,128)(2,1)S(1)}, bf16[2,1,8,1024]{3,2,1,0:T(8,128)(2,1)S(1)}, u32[]{:S(2)}, u32[]{:S(2)}) collective-permute-start(bf16[2,1,8,1024]{3,2,1,0:T(8,128)(2,1)S(1)} %get-tuple-element.44), channel_id=1, source_target_pairs={{0,8},{4,12},{8,0},{12,4},{1,9},{5,13},{9,1},{13,5},{2,10},{6,14},... | collective-permute-start | bytes 98312 | tf_op jit(solution)/shard_map/ppermute | solution.py:29
  80.5 1.3 %collective-permute-start.17 = (bf16[1,2,8,1024]{3,2,1,0:T(8,128)(2,1)S(1)}, bf16[1,2,8,1024]{3,2,1,0:T(8,128)(2,1)S(1)}, u32[]{:S(2)}, u32[]{:S(2)}) collective-permute-start(bf16[1,2,8,1024]{3,2,1,0:T(8,128)(2,1)S(1)} %get-tuple-element.42), channel_id=1, source_target_pairs={{0,4},{4,0},{8,12},{12,8},{1,5},{5,1},{9,13},{13,9},{2,6},{6,2},{1... | collective-permute-start | bytes 98312 | tf_op jit(solution)/shard_map/ppermute | solution.py:29
  81.8 9.7 %collective-permute-start.18 = (bf16[32,1024]{1,0:T(8,128)(2,1)S(1)}, bf16[32,1024]{1,0:T(8,128)(2,1)S(1)}, u32[]{:S(2)}, u32[]{:S(2)}) collective-permute-start(bf16[32,1024]{1,0:T(8,128)(2,1)S(1)} %maximum_bitcast_fusion.refs_0_), channel_id=1, source_target_pairs={{0,1},{1,0},{2,3},{3,2},{4,5},{5,4},{6,7},{7,6},{8,9},{9,8},{10,11... | collective-permute-start | bytes 196616 | tf_op jit(solution)/shard_map/ppermute | solution.py:29
  82.1 9.3 %collective-permute-start.19 = (bf16[32,1024]{1,0:T(8,128)(2,1)S(1)}, bf16[32,1024]{1,0:T(8,128)(2,1)S(1)}, u32[]{:S(2)}, u32[]{:S(2)}) collective-permute-start(bf16[32,1024]{1,0:T(8,128)(2,1)S(1)} %maximum_bitcast_fusion.refs_0_), channel_id=1, source_target_pairs={{0,2},{1,3},{2,0},{3,1},{4,6},{5,7},{6,4},{7,5},{8,10},{9,11},{10,... | collective-permute-start | bytes 196616 | tf_op jit(solution)/shard_map/ppermute | solution.py:29
  84.9 6.6 %collective-permute-start.20 = (bf16[32,1024]{1,0:T(8,128)(2,1)S(1)}, bf16[32,1024]{1,0:T(8,128)(2,1)S(1)}, u32[]{:S(2)}, u32[]{:S(2)}) collective-permute-start(bf16[32,1024]{1,0:T(8,128)(2,1)S(1)} %maximum_bitcast_fusion.refs_0_), channel_id=1, source_target_pairs={{0,3},{1,2},{2,1},{3,0},{4,7},{5,6},{6,5},{7,4},{8,11},{9,10},{10,... | collective-permute-start | bytes 196616 | tf_op jit(solution)/shard_map/ppermute | solution.py:29
  86.4 3.4 %copy-start = (bf16[4096,1024]{1,0:T(8,128)(2,1)S(1)}, bf16[4096,1024]{1,0:T(8,128)(2,1)}, u32[]{:S(2)}) copy-start(bf16[4096,1024]{1,0:T(8,128)(2,1)} %targets.1) | copy-start | bytes 25165828
  93.3 1.2 %collective-permute-start.21 = (f32[16,256]{1,0:T(8,128)S(1)}, f32[16,256]{1,0:T(8,128)S(1)}, u32[]{:S(2)}, u32[]{:S(2)}) collective-permute-start(f32[16,256]{1,0:T(8,128)S(1)} %get-tuple-element.32), channel_id=1, source_target_pairs={{0,4},{4,0},{8,12},{12,8},{1,5},{5,1},{9,13},{13,9},{2,6},{6,2},{1... | collective-permute-start | bytes 49160 | tf_op jit(solution)/shard_map/ppermute | solution.py:29
  94.5 3.7 %collective-permute-start.22 = (f32[16,256]{1,0:T(8,128)S(1)}, f32[16,256]{1,0:T(8,128)S(1)}, u32[]{:S(2)}, u32[]{:S(2)}) collective-permute-start(f32[16,256]{1,0:T(8,128)S(1)} %add.64), channel_id=1, source_target_pairs={{0,8},{4,12},{8,0},{12,4},{1,9},{5,13},{9,1},{13,5},{2,10},{6,14},... | collective-permute-start | bytes 49160 | tf_op jit(solution)/shard_map/ppermute | solution.py:29
  99.4 4.5 %collective-permute-start.23 = (bf16[32,1152]{1,0:T(8,128)(2,1)S(1)}, bf16[32,1152]{1,0:T(8,128)(2,1)S(1)}, u32[]{:S(2)}, u32[]{:S(2)}) collective-permute-start(bf16[32,1152]{1,0:T(8,128)(2,1)S(1)} %get-tuple-element.40), channel_id=1, source_target_pairs={{0,1},{1,0},{2,3},{3,2},{4,5},{5,4},{6,7},{7,6},{8,9},{9,8},{10,11... | collective-permute-start | bytes 221192 | tf_op jit(solution)/shard_map/ppermute | solution.py:29
  100.1 7.1 %collective-permute-start.24 = (bf16[32,1152]{1,0:T(8,128)(2,1)S(1)}, bf16[32,1152]{1,0:T(8,128)(2,1)S(1)}, u32[]{:S(2)}, u32[]{:S(2)}) collective-permute-start(bf16[32,1152]{1,0:T(8,128)(2,1)S(1)} %get-tuple-element.39), channel_id=1, source_target_pairs={{0,2},{1,3},{2,0},{3,1},{4,6},{5,7},{6,4},{7,5},{8,10},{9,11},{10,... | collective-permute-start | bytes 221192 | tf_op jit(solution)/shard_map/ppermute | solution.py:29
  102.5 6.2 %collective-permute-start.25 = (bf16[32,1152]{1,0:T(8,128)(2,1)S(1)}, bf16[32,1152]{1,0:T(8,128)(2,1)S(1)}, u32[]{:S(2)}, u32[]{:S(2)}) collective-permute-start(bf16[32,1152]{1,0:T(8,128)(2,1)S(1)} %get-tuple-element.38), channel_id=1, source_target_pairs={{0,3},{1,2},{2,1},{3,0},{4,7},{5,6},{6,5},{7,4},{8,11},{9,10},{10,... | collective-permute-start | bytes 221192 | tf_op jit(solution)/shard_map/ppermute | solution.py:29

commit v5 on v4

--- a/solution.py
+++ b/solution.py
@@ -112,17 +112,13 @@
 
 
 def hidden_kernel(count, *refs):
-    tokens, weights = refs[:count], refs[count:-5]
-    out, rows, held, token_sems, weight_sems = refs[-5:]
-    weight_copies = fetches(weights, held, weight_sems)
-    token_copies = fetches(tokens, rows, token_sems)
-    for copy in weight_copies:
+    tokens, weights, (out, held, sems) = refs[:count], refs[count:-3], refs[-3:]
+    for copy in fetches(weights, held, sems):
         copy.wait()
     start = 0
-    for token, copy in zip(tokens, token_copies):
+    for token in tokens:
         part = pl.ds(start, token.shape[0])
-        copy.wait()
-        product = dot(rows[part, :], held[...], (1, 1))
+        product = dot(token[...], held[...], (1, 1))
         out[part, :] = (
             product * 0.5 * (1.0 + lax.erf(product * math.sqrt(0.5)))
         ).astype(jnp.bfloat16)
@@ -139,11 +135,10 @@
         (*tokens, *weights),
         2 * rows * units * features,
         (
-            pltpu.VMEM((rows, features), jnp.bfloat16),
             pltpu.VMEM((units, features), jnp.bfloat16),
-            pltpu.SemaphoreType.DMA((len(tokens),)),
             pltpu.SemaphoreType.DMA((len(weights),)),
         ),
+        near=len(tokens),
         place=pl.ANY,
     )
 
@@ -362,12 +357,14 @@
     ]
 
     weights = [outer_weight, outer_x, outer_far, *outer_square]
-    pair, own = partial_sums(hidden, weights, (3, 2))
-    pair, own = swap(pair, "src", 1), swap(own, "src", 1)
+    (pair,) = partial_sums(hidden, weights, (3,))
+    hidden, pair = barrier((hidden, pair))
+    (core,) = partial_sums(hidden, weights, (2,))
+    pair, core = barrier((swap(pair, "src", 1), core))
     (back,) = partial_sums(hidden, weights, (1,), (pair,))
-    back, hidden = barrier((back, hidden))
+    back, core, hidden = barrier((back, core, hidden))
     back = swap(back, "tgt", 1)
-    (own,) = partial_sums(hidden, weights, (0,), (tokens, own), jnp.float32)
+    (own,) = partial_sums(hidden, weights, (0,), (tokens, swap(core, "src", 1)), jnp.float32)
     return own, back
 
 

time: 110 us -> 108 us (0.982)
  Pallas kernels: 20 us -> 18.9 us
    pallas_call x11 -> x12, Pallas kernels: 20 us -> 18.9 us  [local_call(): pl.pallas_call(kernel, out_shape=out_shape, in_specs=[pl.BlockSpec(memory...]
  transfers between devices with their start and end apart: 26 -> 26, of which waited for: 13 -> 15; matrix products, arithmetic and copies ran while one was open for 0% -> 0% of each run, Pallas kernels for 11% -> 10%
where the time goes in v5:
time: 108 us
  waiting for transfers between devices  49 us (45%)
  starting transfers between devices  29.3 us (27%)
  Pallas kernels  18.9 us (17%)
  local copies, waits for them, and re-layouts  9.51 us (9%)
    ppermute x26, waiting for transfers between devices, swap(): lax.ppermute(values, axis, [(i, i ^ offset) for i in range(lax.axis_size(...  49 us
    ppermute x26, starting transfers between devices, swap(): lax.ppermute(values, axis, [(i, i ^ offset) for i in range(lax.axis_size(...  29.3 us
    pallas_call x12, Pallas kernels, local_call(): pl.pallas_call(kernel, out_shape=out_shape, in_specs=[pl.BlockSpec(memory...  18.9 us
    unnamed x30, local copies, waits for them, and re-layouts  9.39 us
  transfers between devices with their start and end apart: 26, of which 15 were waited for; matrix products, arithmetic and copies ran while one was open for 0% of the time, Pallas kernels for 10%

profile of v5, /device:TPU:0, one launch (start us, length us, event | category | flops | bytes accessed | tf_op | source)
XLA Modules:
  0.0 107.8 jit_solution(13050847610889073354)
XLA Ops:
  0.6 3.1 %collective-permute-start = (bf16[256,1024]{1,0:T(8,128)(2,1)}, bf16[256,1024]{1,0:T(8,128)(2,1)S(1)}, u32[]{:S(2)}, u32[]{:S(2)}) collective-permute-start(bf16[256,1024]{1,0:T(8,128)(2,1)} %refs_0_.9), channel_id=1, source_target_pairs={{0,1},{1,0},{2,3},{3,2},{4,5},{5,4},{6,7},{7,6},{8,9},{9,8},{10,11... | collective-permute-start | bytes 1572872 | tf_op jit(solution)/shard_map/ppermute | solution.py:29
  3.7 1.8 %shard_map.87 = (bf16[128,1024]{1,0:T(8,128)(2,1)}, bf16[128,1024]{1,0:T(8,128)(2,1)}) custom-call(bf16[256,1024]{1,0:T(8,128)(2,1)} %refs_4_.1, bf16[256,1024]{1,0:T(8,128)(2,1)} %refs_2_.1), custom_call_target="tpu_custom_call" | custom-call | bytes 1572864 | tf_op jit(solution)/shard_map/pallas_call | solution.py:37
  5.6 2.7 %collective-permute-start.4 = (bf16[128,1024]{1,0:T(8,128)(2,1)}, bf16[128,1024]{1,0:T(8,128)(2,1)S(1)}, u32[]{:S(2)}, u32[]{:S(2)}) collective-permute-start(bf16[128,1024]{1,0:T(8,128)(2,1)} %get-tuple-element.25), channel_id=1, source_target_pairs={{0,2},{1,3},{2,0},{3,1},{4,6},{5,7},{6,4},{7,5},{8,10},{9,11},{10,... | collective-permute-start | bytes 786440 | tf_op jit(solution)/shard_map/ppermute | solution.py:29
  8.2 1.5 %collective-permute-start.6 = (bf16[256,1024]{1,0:T(8,128)(2,1)}, bf16[256,1024]{1,0:T(8,128)(2,1)S(1)}, u32[]{:S(2)}, u32[]{:S(2)}) collective-permute-start(bf16[256,1024]{1,0:T(8,128)(2,1)} %refs_2_.1), channel_id=1, source_target_pairs={{0,8},{4,12},{8,0},{12,4},{1,9},{5,13},{9,1},{13,5},{2,10},{6,14},... | collective-permute-start | bytes 1572872 | tf_op jit(solution)/shard_map/ppermute | solution.py:29
  9.7 0.5 collective-permute-start.7
  10.6 11.4 %collective-permute-done.4.refs_4_ = bf16[128,1024]{1,0:T(8,128)(2,1)S(1)} collective-permute-done((bf16[128,1024]{1,0:T(8,128)(2,1)}, bf16[128,1024]{1,0:T(8,128)(2,1)S(1)}, u32[]{:S(2)}, u32[]{:S(2)}) %collective-permute-start.4) | collective-permute-done | bytes 262176 | tf_op jit(solution)/shard_map/ppermute | solution.py:29
  22.0 1.5 %collective-permute-start.5 = (bf16[128,1024]{1,0:T(8,128)(2,1)S(1)}, bf16[128,1024]{1,0:T(8,128)(2,1)S(1)}, u32[]{:S(2)}, u32[]{:S(2)}) collective-permute-start(bf16[128,1024]{1,0:T(8,128)(2,1)S(1)} %collective-permute-done.4.refs_4_), channel_id=1, source_target_pairs={{0,16},{16,0},{1,17},{17,1},{2,18},{18,2},{3,19},{19,3},{4,20},{20... | collective-permute-start | bytes 786440 | tf_op jit(solution)/shard_map/ppermute | solution.py:29
  23.6 7.9 %collective-permute-done.3.refs_2_.refs_3_.refs_4_ = bf16[128,1024]{1,0:T(8,128)(2,1)S(1)} collective-permute-done((bf16[128,1024]{1,0:T(8,128)(2,1)}, bf16[128,1024]{1,0:T(8,128)(2,1)S(1)}, u32[]{:S(2)}, u32[]{:S(2)}) %collective-permute-start.3) | collective-permute-done | bytes 262176 | tf_op jit(solution)/shard_map/ppermute | solution.py:29
  31.9 0.8 collective-permute-done.7.refs_5_
  32.8 1.5 %collective-permute-start.10 = (bf16[128,1024]{1,0:T(8,128)(2,1)S(1)}, bf16[128,1024]{1,0:T(8,128)(2,1)S(1)}, u32[]{:S(2)}, u32[]{:S(2)}) collective-permute-start(bf16[128,1024]{1,0:T(8,128)(2,1)S(1)} %collective-permute-done.3.refs_2_.refs_3_.refs_4_), channel_id=1, source_target_pairs={{0,8},{4,12},{8,0},{12,4},{1,9},{5,13},{9,1},{13,5},{2,10},{6,14},... | collective-permute-start | bytes 786440 | tf_op jit(solution)/shard_map/ppermute | solution.py:29
  34.8 1.5 %collective-permute-start.9 = (bf16[128,1024]{1,0:T(8,128)(2,1)S(1)}, bf16[128,1024]{1,0:T(8,128)(2,1)S(1)}, u32[]{:S(2)}, u32[]{:S(2)}) collective-permute-start(bf16[128,1024]{1,0:T(8,128)(2,1)S(1)} %collective-permute-done.5.refs_6_), channel_id=1, source_target_pairs={{0,8},{4,12},{8,0},{12,4},{1,9},{5,13},{9,1},{13,5},{2,10},{6,14},... | collective-permute-start | bytes 786440 | tf_op jit(solution)/shard_map/ppermute | solution.py:29
  36.3 1.5 %collective-permute-start.11 = (bf16[128,1024]{1,0:T(8,128)(2,1)S(1)}, bf16[128,1024]{1,0:T(8,128)(2,1)S(1)}, u32[]{:S(2)}, u32[]{:S(2)}) collective-permute-start(bf16[128,1024]{1,0:T(8,128)(2,1)S(1)} %collective-permute-done.3.refs_2_.refs_3_.refs_4_), channel_id=1, source_target_pairs={{0,16},{16,0},{1,17},{17,1},{2,18},{18,2},{3,19},{19,3},{4,20},{20... | collective-permute-start | bytes 786440 | tf_op jit(solution)/shard_map/ppermute | solution.py:29
  37.8 4.2 %collective-permute-done.10.refs_3_.refs_4_.refs_5_ = bf16[128,1024]{1,0:T(8,128)(2,1)S(1)} collective-permute-done((bf16[128,1024]{1,0:T(8,128)(2,1)S(1)}, bf16[128,1024]{1,0:T(8,128)(2,1)S(1)}, u32[]{:S(2)}, u32[]{:S(2)}) %collective-permute-start.10) | collective-permute-done | bytes 262176 | tf_op jit(solution)/shard_map/ppermute | solution.py:29
  42.0 1.5 %collective-permute-start.12 = (bf16[128,1024]{1,0:T(8,128)(2,1)S(1)}, bf16[128,1024]{1,0:T(8,128)(2,1)S(1)}, u32[]{:S(2)}, u32[]{:S(2)}) collective-permute-start(bf16[128,1024]{1,0:T(8,128)(2,1)S(1)} %collective-permute-done.10.refs_3_.refs_4_.refs_5_), channel_id=1, source_target_pairs={{0,16},{16,0},{1,17},{17,1},{2,18},{18,2},{3,19},{19,3},{4,20},{20... | collective-permute-start | bytes 786440 | tf_op jit(solution)/shard_map/ppermute | solution.py:29
  43.6 1.0 copy-done.2
  44.6 1.0 copy-done.10
  45.6 1.6 %shard_map.88.near = bf16[1024,512]{1,0:T(8,128)(2,1)S(1)} custom-call(bf16[256,1024]{1,0:T(8,128)(2,1)S(1)} %copy-done.2, bf16[256,1024]{1,0:T(8,128)(2,1)S(1)} %collective-permute-done.refs_1_, bf16[256,1024]{1,0:T(8,128)(2,1)S(1)} %collective-permute-done.1.refs_2_, bf16[256,1024]{1,0:T(8,128)(2,1)S(1)} %collective-permute-done.2.refs_3_, ...), custom_call_target="tpu_custom_call" | custom-call | flops 1073741824 | bytes 4194304 | tf_op jit(solution)/shard_map/pallas_call | solution.py:37
  47.7 3.8 %collective-permute-done.9.refs_7_ = bf16[128,1024]{1,0:T(8,128)(2,1)S(1)} collective-permute-done((bf16[128,1024]{1,0:T(8,128)(2,1)S(1)}, bf16[128,1024]{1,0:T(8,128)(2,1)S(1)}, u32[]{:S(2)}, u32[]{:S(2)}) %collective-permute-start.9) | collective-permute-done | bytes 262176 | tf_op jit(solution)/shard_map/ppermute | solution.py:29
  51.5 1.6 %shard_map.89.far = bf16[1024,512]{1,0:T(8,128)(2,1)S(1)} custom-call(bf16[256,1024]{1,0:T(8,128)(2,1)S(1)} %copy-done.2, bf16[256,1024]{1,0:T(8,128)(2,1)S(1)} %collective-permute-done.refs_1_, bf16[256,1024]{1,0:T(8,128)(2,1)S(1)} %collective-permute-done.1.refs_2_, bf16[256,1024]{1,0:T(8,128)(2,1)S(1)} %collective-permute-done.2.refs_3_, ...), custom_call_target="tpu_custom_call" | custom-call | flops 1073741824 | bytes 4194304 | tf_op jit(solution)/shard_map/pallas_call | solution.py:37
  53.2 0.9 shard_map.90
  54.2 1.7 %shard_map.91 = bf16[256,1024]{1,0:T(8,128)(2,1)} custom-call(bf16[1024,512]{1,0:T(8,128)(2,1)S(1)} %shard_map.88.near, bf16[1024,512]{1,0:T(8,128)(2,1)S(1)} %shard_map.89.far, bf16[256,1024]{1,0:T(8,128)(2,1)S(1)} %copy-done, bf16[256,1024]{1,0:T(8,128)(2,1)S(1)} %collective-permute-done.6.refs_1_.refs_2_.refs_3_, ...), custom_call_target="tpu_custom_call" | custom-call | flops 536870912 | bytes 4718592 | tf_op jit(solution)/shard_map/pallas_call | solution.py:37
  56.1 1.7 %shard_map.92 = bf16[256,1024]{1,0:T(8,128)(2,1)} custom-call(bf16[1024,512]{1,0:T(8,128)(2,1)S(1)} %shard_map.88.near, bf16[1024,512]{1,0:T(8,128)(2,1)S(1)} %shard_map.89.far, bf16[256,1024]{1,0:T(8,128)(2,1)S(1)} %collective-permute-done.13.refs_0_, bf16[256,1024]{1,0:T(8,128)(2,1)S(1)} %copy-done, ...), custom_call_target="tpu_custom_call" | custom-call | flops 536870912 | bytes 5242880 | tf_op jit(solution)/shard_map/pallas_call | solution.py:37
  58.3 1.9 %collective-permute-done.14.refs_1_ = bf16[256,1024]{1,0:T(8,128)(2,1)} collective-permute-done((bf16[256,1024]{1,0:T(8,128)(2,1)}, bf16[256,1024]{1,0:T(8,128)(2,1)}, u32[]{:S(2)}, u32[]{:S(2)}) %collective-permute-start.14) | collective-permute-done | bytes 524320 | tf_op jit(solution)/shard_map/ppermute | solution.py:29
  60.2 1.0 copy-done.3
  61.2 0.9 copy-done.5
  62.1 0.9 copy-done.7
  63.1 0.9 copy-done.9
  64.0 2.0 %shard_map.93.own = f32[256,1024]{1,0:T(8,128)S(1)} custom-call(bf16[1024,512]{1,0:T(8,128)(2,1)S(1)} %shard_map.88.near, bf16[1024,512]{1,0:T(8,128)(2,1)S(1)} %shard_map.89.far, bf16[256,1024]{1,0:T(8,128)(2,1)S(1)} %copy-done.3, bf16[256,1024]{1,0:T(8,128)(2,1)} %collective-permute-done.14.refs_1_, bf16[256,1024]{1,0:T(8,128)(2,1)S(1)} %copy-done, ...), custom_call_target="tpu_custom_call" | custom-call | flops 536870912 | bytes 6291456 | tf_op jit(solution)/shard_map/pallas_call | solution.py:37
  66.0 6.5 %collective-permute-done.15.back = bf16[256,1024]{1,0:T(8,128)(2,1)} collective-permute-done((bf16[256,1024]{1,0:T(8,128)(2,1)}, bf16[256,1024]{1,0:T(8,128)(2,1)}, u32[]{:S(2)}, u32[]{:S(2)}) %collective-permute-start.15) | collective-permute-done | bytes 524320 | tf_op jit(solution)/shard_map/ppermute | solution.py:29
  72.6 2.2 %shard_map.94 = bf16[32,1024]{1,0:T(8,128)(2,1)S(1)} custom-call(s32[1,256]{1,0:T(1,128)S(1)} %copy-done.12, s32[1,32]{1,0:T(1,128)S(1)} %fusion.2.order, f32[256,1024]{1,0:T(8,128)S(1)} %shard_map.93.own, bf16[256,1024]{1,0:T(8,128)(2,1)} %collective-permute-done.15.back), custom_call_target="tpu_custom_call" | custom-call | flops 5242880 | bytes 1639552 | tf_op jit(solution)/shard_map/pallas_call | solution.py:37
  74.8 1.5 %collective-permute-start.16 = (bf16[2,1,8,1024]{3,2,1,0:T(8,128)(2,1)S(1)}, bf16[2,1,8,1024]{3,2,1,0:T(8,128)(2,1)S(1)}, u32[]{:S(2)}, u32[]{:S(2)}) collective-permute-start(bf16[2,1,8,1024]{3,2,1,0:T(8,128)(2,1)S(1)} %get-tuple-element.52), channel_id=1, source_target_pairs={{0,8},{4,12},{8,0},{12,4},{1,9},{5,13},{9,1},{13,5},{2,10},{6,14},... | collective-permute-start | bytes 98312 | tf_op jit(solution)/shard_map/ppermute | solution.py:29
  76.4 2.4 %collective-permute-done.16 = bf16[2,1,8,1024]{3,2,1,0:T(8,128)(2,1)S(1)} collective-permute-done((bf16[2,1,8,1024]{3,2,1,0:T(8,128)(2,1)S(1)}, bf16[2,1,8,1024]{3,2,1,0:T(8,128)(2,1)S(1)}, u32[]{:S(2)}, u32[]{:S(2)}) %collective-permute-start.16) | collective-permute-done | bytes 32800 | tf_op jit(solution)/shard_map/ppermute | solution.py:29
  79.0 1.1 %collective-permute-done.17 = bf16[1,2,8,1024]{3,2,1,0:T(8,128)(2,1)S(1)} collective-permute-done((bf16[1,2,8,1024]{3,2,1,0:T(8,128)(2,1)S(1)}, bf16[1,2,8,1024]{3,2,1,0:T(8,128)(2,1)S(1)}, u32[]{:S(2)}, u32[]{:S(2)}) %collective-permute-start.17) | collective-permute-done | bytes 32800 | tf_op jit(solution)/shard_map/ppermute | solution.py:29
  80.4 2.8 %collective-permute-start.19 = (bf16[32,1024]{1,0:T(8,128)(2,1)S(1)}, bf16[32,1024]{1,0:T(8,128)(2,1)S(1)}, u32[]{:S(2)}, u32[]{:S(2)}) collective-permute-start(bf16[32,1024]{1,0:T(8,128)(2,1)S(1)} %maximum_bitcast_fusion.refs_0_), channel_id=1, source_target_pairs={{0,2},{1,3},{2,0},{3,1},{4,6},{5,7},{6,4},{7,5},{8,10},{9,11},{10,... | collective-permute-start | bytes 196616 | tf_op jit(solution)/shard_map/ppermute | solution.py:29
  83.2 1.3 %collective-permute-start.20 = (bf16[32,1024]{1,0:T(8,128)(2,1)S(1)}, bf16[32,1024]{1,0:T(8,128)(2,1)S(1)}, u32[]{:S(2)}, u32[]{:S(2)}) collective-permute-start(bf16[32,1024]{1,0:T(8,128)(2,1)S(1)} %maximum_bitcast_fusion.refs_0_), channel_id=1, source_target_pairs={{0,3},{1,2},{2,1},{3,0},{4,7},{5,6},{6,5},{7,4},{8,11},{9,10},{10,... | collective-permute-start | bytes 196616 | tf_op jit(solution)/shard_map/ppermute | solution.py:29
  84.7 3.4 %copy-done.1 = bf16[4096,1024]{1,0:T(8,128)(2,1)S(1)} copy-done((bf16[4096,1024]{1,0:T(8,128)(2,1)S(1)}, bf16[4096,1024]{1,0:T(8,128)(2,1)}, u32[]{:S(2)}) %copy-start.1) | copy-done | bytes 8388632
  88.1 1.7 %shard_map.86.units = bf16[1024,1024]{1,0:T(8,128)(2,1)S(1)} custom-call(s32[1,16]{1,0:T(1,128)S(1)} %copy-done.11, bf16[4096,1024]{1,0:T(8,128)(2,1)S(1)} %copy-done.1), custom_call_target="tpu_custom_call" | custom-call | flops 8388608 | bytes 10485824 | tf_op jit(solution)/shard_map/pallas_call | solution.py:37
  89.8 1.8 %shard_map.95 = (f32[128,1024]{1,0:T(8,128)S(1)}, f32[16,256]{1,0:T(8,128)S(1)}, f32[128,1]{1,0:T(8,128)S(1)}) custom-call(s32[1,16]{1,0:T(1,128)S(1)} %copy-done.11, s32[1,128]{1,0:T(1,128)S(1)} %xor.32.place, bf16[1024,1024]{1,0:T(8,128)(2,1)S(1)} %shard_map.86.units, bf16[32,1024]{1,0:T(8,128)(2,1)S(1)} %maximum_bitcast_fusion.refs_0_, ...), custom_call_target="tpu_custom_call" | custom-call | flops 268435456 | bytes 2901056 | tf_op jit(solution)/shard_map/pallas_call | solution.py:37
  91.6 1.2 %collective-permute-done.21 = f32[16,256]{1,0:T(8,128)S(1)} collective-permute-done((f32[16,256]{1,0:T(8,128)S(1)}, f32[16,256]{1,0:T(8,128)S(1)}, u32[]{:S(2)}, u32[]{:S(2)}) %collective-permute-start.21) | collective-permute-done | bytes 16416 | tf_op jit(solution)/shard_map/ppermute | solution.py:29
  92.8 1.5 %collective-permute-start.22 = (f32[16,256]{1,0:T(8,128)S(1)}, f32[16,256]{1,0:T(8,128)S(1)}, u32[]{:S(2)}, u32[]{:S(2)}) collective-permute-start(f32[16,256]{1,0:T(8,128)S(1)} %add.64), channel_id=1, source_target_pairs={{0,8},{4,12},{8,0},{12,4},{1,9},{5,13},{9,1},{13,5},{2,10},{6,14},... | collective-permute-start | bytes 49160 | tf_op jit(solution)/shard_map/ppermute | solution.py:29
  94.3 2.3 %collective-permute-done.22 = f32[16,256]{1,0:T(8,128)S(1)} collective-permute-done((f32[16,256]{1,0:T(8,128)S(1)}, f32[16,256]{1,0:T(8,128)S(1)}, u32[]{:S(2)}, u32[]{:S(2)}) %collective-permute-start.22) | collective-permute-done | bytes 16416 | tf_op jit(solution)/shard_map/ppermute | solution.py:29
  96.6 1.1 %shard_map.96 = (f32[32,1152]{1,0:T(8,128)S(1)}, bf16[96,1152]{1,0:T(8,128)(2,1)S(1)}) custom-call(s32[1,16]{1,0:T(1,128)S(1)} %copy-done.11, f32[128,1024]{1,0:T(8,128)S(1)} %get-tuple-element.39.expo, f32[16,256]{1,0:T(8,128)S(1)} %add.65.columns, f32[128,1]{1,0:T(8,128)S(1)} %get-tuple-element.41.row_total, bf16[1024,1024]{1,0:T(8,128)(2,1)S(1)} %shard_map.86.units), custom_call_target="tpu_custom_call" | custom-call | flops 268435456 | bytes 3007040 | tf_op jit(solution)/shard_map/pallas_call | solution.py:37
  97.7 0.6 collective-permute-start.23
  98.4 2.5 %collective-permute-start.24 = (bf16[32,1152]{1,0:T(8,128)(2,1)S(1)}, bf16[32,1152]{1,0:T(8,128)(2,1)S(1)}, u32[]{:S(2)}, u32[]{:S(2)}) collective-permute-start(bf16[32,1152]{1,0:T(8,128)(2,1)S(1)} %get-tuple-element.47), channel_id=1, source_target_pairs={{0,2},{1,3},{2,0},{3,1},{4,6},{5,7},{6,4},{7,5},{8,10},{9,11},{10,... | collective-permute-start | bytes 221192 | tf_op jit(solution)/shard_map/ppermute | solution.py:29
  100.8 1.3 %collective-permute-start.25 = (bf16[32,1152]{1,0:T(8,128)(2,1)S(1)}, bf16[32,1152]{1,0:T(8,128)(2,1)S(1)}, u32[]{:S(2)}, u32[]{:S(2)}) collective-permute-start(bf16[32,1152]{1,0:T(8,128)(2,1)S(1)} %get-tuple-element.46), channel_id=1, source_target_pairs={{0,3},{1,2},{2,1},{3,0},{4,7},{5,6},{6,5},{7,4},{8,11},{9,10},{10,... | collective-permute-start | bytes 221192 | tf_op jit(solution)/shard_map/ppermute | solution.py:29
  102.2 3.3 %collective-permute-done.24.refs_1_ = bf16[32,1152]{1,0:T(8,128)(2,1)S(1)} collective-permute-done((bf16[32,1152]{1,0:T(8,128)(2,1)S(1)}, bf16[32,1152]{1,0:T(8,128)(2,1)S(1)}, u32[]{:S(2)}, u32[]{:S(2)}) %collective-permute-start.24) | collective-permute-done | bytes 73760 | tf_op jit(solution)/shard_map/ppermute | solution.py:29
  105.4 1.6 %collective-permute-done.25.refs_2_ = bf16[32,1152]{1,0:T(8,128)(2,1)S(1)} collective-permute-done((bf16[32,1152]{1,0:T(8,128)(2,1)S(1)}, bf16[32,1152]{1,0:T(8,128)(2,1)S(1)}, u32[]{:S(2)}, u32[]{:S(2)}) %collective-permute-start.25) | collective-permute-done | bytes 73760 | tf_op jit(solution)/shard_map/ppermute | solution.py:29
  107.0 0.8 shard_map.97
  (57 shorter events, 3.3 us)
Async XLA Ops:
  0.6 52.5 %copy-start = (bf16[256,1024]{1,0:T(8,128)(2,1)S(1)}, bf16[256,1024]{1,0:T(8,128)(2,1)}, u32[]{:S(2)}) copy-start(bf16[256,1024]{1,0:T(8,128)(2,1)} %refs_2_.1) | copy-start | bytes 1572868
  0.6 30.8 %collective-permute-start = (bf16[256,1024]{1,0:T(8,128)(2,1)}, bf16[256,1024]{1,0:T(8,128)(2,1)S(1)}, u32[]{:S(2)}, u32[]{:S(2)}) collective-permute-start(bf16[256,1024]{1,0:T(8,128)(2,1)} %refs_0_.9), channel_id=1, source_target_pairs={{0,1},{1,0},{2,3},{3,2},{4,5},{5,4},{6,7},{7,6},{8,9},{9,8},{10,11... | collective-permute-start | bytes 1572872 | tf_op jit(solution)/shard_map/ppermute | solution.py:29
  5.6 16.5 %collective-permute-start.4 = (bf16[128,1024]{1,0:T(8,128)(2,1)}, bf16[128,1024]{1,0:T(8,128)(2,1)S(1)}, u32[]{:S(2)}, u32[]{:S(2)}) collective-permute-start(bf16[128,1024]{1,0:T(8,128)(2,1)} %get-tuple-element.25), channel_id=1, source_target_pairs={{0,2},{1,3},{2,0},{3,1},{4,6},{5,7},{6,4},{7,5},{8,10},{9,11},{10,... | collective-permute-start | bytes 786440 | tf_op jit(solution)/shard_map/ppermute | solution.py:29
  8.2 23.7 %collective-permute-start.6 = (bf16[256,1024]{1,0:T(8,128)(2,1)}, bf16[256,1024]{1,0:T(8,128)(2,1)S(1)}, u32[]{:S(2)}, u32[]{:S(2)}) collective-permute-start(bf16[256,1024]{1,0:T(8,128)(2,1)} %refs_2_.1), channel_id=1, source_target_pairs={{0,8},{4,12},{8,0},{12,4},{1,9},{5,13},{9,1},{13,5},{2,10},{6,14},... | collective-permute-start | bytes 1572872 | tf_op jit(solution)/shard_map/ppermute | solution.py:29
  9.7 23.1 %collective-permute-start.7 = (bf16[256,1024]{1,0:T(8,128)(2,1)}, bf16[256,1024]{1,0:T(8,128)(2,1)S(1)}, u32[]{:S(2)}, u32[]{:S(2)}) collective-permute-start(bf16[256,1024]{1,0:T(8,128)(2,1)} %refs_4_.1), channel_id=1, source_target_pairs={{0,8},{4,12},{8,0},{12,4},{1,9},{5,13},{9,1},{13,5},{2,10},{6,14},... | collective-permute-start | bytes 1572872 | tf_op jit(solution)/shard_map/ppermute | solution.py:29
  10.3 21.2 %collective-permute-start.3 = (bf16[128,1024]{1,0:T(8,128)(2,1)}, bf16[128,1024]{1,0:T(8,128)(2,1)S(1)}, u32[]{:S(2)}, u32[]{:S(2)}) collective-permute-start(bf16[128,1024]{1,0:T(8,128)(2,1)} %get-tuple-element.24), channel_id=1, source_target_pairs={{0,2},{1,3},{2,0},{3,1},{4,6},{5,7},{6,4},{7,5},{8,10},{9,11},{10,... | collective-permute-start | bytes 786440 | tf_op jit(solution)/shard_map/ppermute | solution.py:29
  22.0 9.9 %collective-permute-start.5 = (bf16[128,1024]{1,0:T(8,128)(2,1)S(1)}, bf16[128,1024]{1,0:T(8,128)(2,1)S(1)}, u32[]{:S(2)}, u32[]{:S(2)}) collective-permute-start(bf16[128,1024]{1,0:T(8,128)(2,1)S(1)} %collective-permute-done.4.refs_4_), channel_id=1, source_target_pairs={{0,16},{16,0},{1,17},{17,1},{2,18},{18,2},{3,19},{19,3},{4,20},{20... | collective-permute-start | bytes 786440 | tf_op jit(solution)/shard_map/ppermute | solution.py:29
  31.4 4.9 %collective-permute-start.1 = (bf16[256,1024]{1,0:T(8,128)(2,1)}, bf16[256,1024]{1,0:T(8,128)(2,1)S(1)}, u32[]{:S(2)}, u32[]{:S(2)}) collective-permute-start(bf16[256,1024]{1,0:T(8,128)(2,1)} %refs_0_.9), channel_id=1, source_target_pairs={{0,4},{4,0},{8,12},{12,8},{1,5},{5,1},{9,13},{13,9},{2,6},{6,2},{1... | collective-permute-start | bytes 1572872 | tf_op jit(solution)/shard_map/ppermute | solution.py:29
  31.4 12.1 %collective-permute-start.2 = (bf16[256,1024]{1,0:T(8,128)(2,1)S(1)}, bf16[256,1024]{1,0:T(8,128)(2,1)S(1)}, u32[]{:S(2)}, u32[]{:S(2)}) collective-permute-start(bf16[256,1024]{1,0:T(8,128)(2,1)S(1)} %collective-permute-done.refs_1_), channel_id=1, source_target_pairs={{0,4},{4,0},{8,12},{12,8},{1,5},{5,1},{9,13},{13,9},{2,6},{6,2},{1... | collective-permute-start | bytes 1572872 | tf_op jit(solution)/shard_map/ppermute | solution.py:29
  32.8 9.2 %collective-permute-start.10 = (bf16[128,1024]{1,0:T(8,128)(2,1)S(1)}, bf16[128,1024]{1,0:T(8,128)(2,1)S(1)}, u32[]{:S(2)}, u32[]{:S(2)}) collective-permute-start(bf16[128,1024]{1,0:T(8,128)(2,1)S(1)} %collective-permute-done.3.refs_2_.refs_3_.refs_4_), channel_id=1, source_target_pairs={{0,8},{4,12},{8,0},{12,4},{1,9},{5,13},{9,1},{13,5},{2,10},{6,14},... | collective-permute-start | bytes 786440 | tf_op jit(solution)/shard_map/ppermute | solution.py:29
  34.3 13.4 %collective-permute-start.8 = (bf16[128,1024]{1,0:T(8,128)(2,1)S(1)}, bf16[128,1024]{1,0:T(8,128)(2,1)S(1)}, u32[]{:S(2)}, u32[]{:S(2)}) collective-permute-start(bf16[128,1024]{1,0:T(8,128)(2,1)S(1)} %collective-permute-done.4.refs_4_), channel_id=1, source_target_pairs={{0,8},{4,12},{8,0},{12,4},{1,9},{5,13},{9,1},{13,5},{2,10},{6,14},... | collective-permute-start | bytes 786440 | tf_op jit(solution)/shard_map/ppermute | solution.py:29
  34.8 16.7 %collective-permute-start.9 = (bf16[128,1024]{1,0:T(8,128)(2,1)S(1)}, bf16[128,1024]{1,0:T(8,128)(2,1)S(1)}, u32[]{:S(2)}, u32[]{:S(2)}) collective-permute-start(bf16[128,1024]{1,0:T(8,128)(2,1)S(1)} %collective-permute-done.5.refs_6_), channel_id=1, source_target_pairs={{0,8},{4,12},{8,0},{12,4},{1,9},{5,13},{9,1},{13,5},{2,10},{6,14},... | collective-permute-start | bytes 786440 | tf_op jit(solution)/shard_map/ppermute | solution.py:29
  36.3 16.8 %collective-permute-start.11 = (bf16[128,1024]{1,0:T(8,128)(2,1)S(1)}, bf16[128,1024]{1,0:T(8,128)(2,1)S(1)}, u32[]{:S(2)}, u32[]{:S(2)}) collective-permute-start(bf16[128,1024]{1,0:T(8,128)(2,1)S(1)} %collective-permute-done.3.refs_2_.refs_3_.refs_4_), channel_id=1, source_target_pairs={{0,16},{16,0},{1,17},{17,1},{2,18},{18,2},{3,19},{19,3},{4,20},{20... | collective-permute-start | bytes 786440 | tf_op jit(solution)/shard_map/ppermute | solution.py:29
  42.0 14.1 %copy-start.4 = (bf16[128,1024]{1,0:T(8,128)(2,1)}, bf16[128,1024]{1,0:T(8,128)(2,1)S(1)}, u32[]{:S(2)}) copy-start(bf16[128,1024]{1,0:T(8,128)(2,1)S(1)} %collective-permute-done.10.refs_3_.refs_4_.refs_5_) | copy-start | bytes 786436
  42.0 11.1 %collective-permute-start.12 = (bf16[128,1024]{1,0:T(8,128)(2,1)S(1)}, bf16[128,1024]{1,0:T(8,128)(2,1)S(1)}, u32[]{:S(2)}, u32[]{:S(2)}) collective-permute-start(bf16[128,1024]{1,0:T(8,128)(2,1)S(1)} %collective-permute-done.10.refs_3_.refs_4_.refs_5_), channel_id=1, source_target_pairs={{0,16},{16,0},{1,17},{17,1},{2,18},{18,2},{3,19},{19,3},{4,20},{20... | collective-permute-start | bytes 786440 | tf_op jit(solution)/shard_map/ppermute | solution.py:29
  43.6 1.0 copy-start.2
  44.6 1.0 copy-start.10
  53.1 5.2 %copy-start.14 = (s32[32]{0:T(128)S(1)}, s32[32]{0:T(128)}, u32[]{:S(2)}) copy-start(s32[32]{0:T(128)} %param.11) | copy-start | bytes 388
  53.1 4.7 %copy-start.6 = (bf16[128,1024]{1,0:T(8,128)(2,1)}, bf16[128,1024]{1,0:T(8,128)(2,1)S(1)}, u32[]{:S(2)}) copy-start(bf16[128,1024]{1,0:T(8,128)(2,1)S(1)} %collective-permute-done.11.refs_4_.refs_5_.refs_6_) | copy-start | bytes 786436
  53.1 5.1 %copy-start.8 = (bf16[128,1024]{1,0:T(8,128)(2,1)}, bf16[128,1024]{1,0:T(8,128)(2,1)S(1)}, u32[]{:S(2)}) copy-start(bf16[128,1024]{1,0:T(8,128)(2,1)S(1)} %collective-permute-done.12.refs_5_.refs_6_.refs_7_) | copy-start | bytes 786436
  54.1 18.5 %copy-start.12 = (s32[1,256]{1,0:T(1,128)S(1)}, s32[1,256]{1,0:T(1,128)}, u32[]{:S(2)}) copy-start(s32[1,256]{1,0:T(1,128)} %identity.1) | copy-start | bytes 3076
  54.1 22.3 %copy-start.13 = (s32[4]{0:T(128)S(1)}, s32[4]{0:T(128)}, u32[]{:S(2)}) copy-start(s32[4]{0:T(128)} %constant.39.clone.1) | copy-start | bytes 52
  54.1 30.6 %copy-start.11 = (s32[1,16]{1,0:T(1,128)S(1)}, s32[1,16]{1,0:T(1,128)}, u32[]{:S(2)}) copy-start(s32[1,16]{1,0:T(1,128)} %listed.5) | copy-start | bytes 196
  54.1 2.0 %collective-permute-start.13 = (bf16[256,1024]{1,0:T(8,128)(2,1)S(1)}, bf16[256,1024]{1,0:T(8,128)(2,1)S(1)}, u32[]{:S(2)}, u32[]{:S(2)}) collective-permute-start(bf16[256,1024]{1,0:T(8,128)(2,1)S(1)} %shard_map.90), channel_id=1, source_target_pairs={{0,4},{4,0},{8,12},{12,8},{1,5},{5,1},{9,13},{13,9},{2,6},{6,2},{1... | collective-permute-start | bytes 1572872 | tf_op jit(solution)/shard_map/ppermute | solution.py:29
  57.8 2.3 %collective-permute-start.14 = (bf16[256,1024]{1,0:T(8,128)(2,1)}, bf16[256,1024]{1,0:T(8,128)(2,1)}, u32[]{:S(2)}, u32[]{:S(2)}) collective-permute-start(bf16[256,1024]{1,0:T(8,128)(2,1)} %shard_map.91), channel_id=1, source_target_pairs={{0,4},{4,0},{8,12},{12,8},{1,5},{5,1},{9,13},{13,9},{2,6},{6,2},{1... | collective-permute-start | bytes 1572872 | tf_op jit(solution)/shard_map/ppermute | solution.py:29
  58.3 14.3 %collective-permute-start.15 = (bf16[256,1024]{1,0:T(8,128)(2,1)}, bf16[256,1024]{1,0:T(8,128)(2,1)}, u32[]{:S(2)}, u32[]{:S(2)}) collective-permute-start(bf16[256,1024]{1,0:T(8,128)(2,1)} %shard_map.92), channel_id=1, source_target_pairs={{0,1},{1,0},{2,3},{3,2},{4,5},{5,4},{6,7},{7,6},{8,9},{9,8},{10,11... | collective-permute-start | bytes 1572872 | tf_op jit(solution)/shard_map/ppermute | solution.py:29
  60.2 1.0 copy-start.3
  61.2 0.9 copy-start.5
  62.1 0.9 copy-start.7
  63.1 0.9 copy-start.9
  74.8 4.0 %collective-permute-start.16 = (bf16[2,1,8,1024]{3,2,1,0:T(8,128)(2,1)S(1)}, bf16[2,1,8,1024]{3,2,1,0:T(8,128)(2,1)S(1)}, u32[]{:S(2)}, u32[]{:S(2)}) collective-permute-start(bf16[2,1,8,1024]{3,2,1,0:T(8,128)(2,1)S(1)} %get-tuple-element.52), channel_id=1, source_target_pairs={{0,8},{4,12},{8,0},{12,4},{1,9},{5,13},{9,1},{13,5},{2,10},{6,14},... | collective-permute-start | bytes 98312 | tf_op jit(solution)/shard_map/ppermute | solution.py:29
  78.8 1.3 %collective-permute-start.17 = (bf16[1,2,8,1024]{3,2,1,0:T(8,128)(2,1)S(1)}, bf16[1,2,8,1024]{3,2,1,0:T(8,128)(2,1)S(1)}, u32[]{:S(2)}, u32[]{:S(2)}) collective-permute-start(bf16[1,2,8,1024]{3,2,1,0:T(8,128)(2,1)S(1)} %get-tuple-element.50), channel_id=1, source_target_pairs={{0,4},{4,0},{8,12},{12,8},{1,5},{5,1},{9,13},{13,9},{2,6},{6,2},{1... | collective-permute-start | bytes 98312 | tf_op jit(solution)/shard_map/ppermute | solution.py:29
  80.1 9.7 %collective-permute-start.18 = (bf16[32,1024]{1,0:T(8,128)(2,1)S(1)}, bf16[32,1024]{1,0:T(8,128)(2,1)S(1)}, u32[]{:S(2)}, u32[]{:S(2)}) collective-permute-start(bf16[32,1024]{1,0:T(8,128)(2,1)S(1)} %maximum_bitcast_fusion.refs_0_), channel_id=1, source_target_pairs={{0,1},{1,0},{2,3},{3,2},{4,5},{5,4},{6,7},{7,6},{8,9},{9,8},{10,11... | collective-permute-start | bytes 196616 | tf_op jit(solution)/shard_map/ppermute | solution.py:29
  80.4 9.3 %collective-permute-start.19 = (bf16[32,1024]{1,0:T(8,128)(2,1)S(1)}, bf16[32,1024]{1,0:T(8,128)(2,1)S(1)}, u32[]{:S(2)}, u32[]{:S(2)}) collective-permute-start(bf16[32,1024]{1,0:T(8,128)(2,1)S(1)} %maximum_bitcast_fusion.refs_0_), channel_id=1, source_target_pairs={{0,2},{1,3},{2,0},{3,1},{4,6},{5,7},{6,4},{7,5},{8,10},{9,11},{10,... | collective-permute-start | bytes 196616 | tf_op jit(solution)/shard_map/ppermute | solution.py:29
  83.2 6.6 %collective-permute-start.20 = (bf16[32,1024]{1,0:T(8,128)(2,1)S(1)}, bf16[32,1024]{1,0:T(8,128)(2,1)S(1)}, u32[]{:S(2)}, u32[]{:S(2)}) collective-permute-start(bf16[32,1024]{1,0:T(8,128)(2,1)S(1)} %maximum_bitcast_fusion.refs_0_), channel_id=1, source_target_pairs={{0,3},{1,2},{2,1},{3,0},{4,7},{5,6},{6,5},{7,4},{8,11},{9,10},{10,... | collective-permute-start | bytes 196616 | tf_op jit(solution)/shard_map/ppermute | solution.py:29
  84.7 3.4 %copy-start.1 = (bf16[4096,1024]{1,0:T(8,128)(2,1)S(1)}, bf16[4096,1024]{1,0:T(8,128)(2,1)}, u32[]{:S(2)}) copy-start(bf16[4096,1024]{1,0:T(8,128)(2,1)} %targets.1) | copy-start | bytes 25165828
  91.6 1.2 %collective-permute-start.21 = (f32[16,256]{1,0:T(8,128)S(1)}, f32[16,256]{1,0:T(8,128)S(1)}, u32[]{:S(2)}, u32[]{:S(2)}) collective-permute-start(f32[16,256]{1,0:T(8,128)S(1)} %get-tuple-element.40), channel_id=1, source_target_pairs={{0,4},{4,0},{8,12},{12,8},{1,5},{5,1},{9,13},{13,9},{2,6},{6,2},{1... | collective-permute-start | bytes 49160 | tf_op jit(solution)/shard_map/ppermute | solution.py:29
  92.8 3.7 %collective-permute-start.22 = (f32[16,256]{1,0:T(8,128)S(1)}, f32[16,256]{1,0:T(8,128)S(1)}, u32[]{:S(2)}, u32[]{:S(2)}) collective-permute-start(f32[16,256]{1,0:T(8,128)S(1)} %add.64), channel_id=1, source_target_pairs={{0,8},{4,12},{8,0},{12,4},{1,9},{5,13},{9,1},{13,5},{2,10},{6,14},... | collective-permute-start | bytes 49160 | tf_op jit(solution)/shard_map/ppermute | solution.py:29
  97.7 4.5 %collective-permute-start.23 = (bf16[32,1152]{1,0:T(8,128)(2,1)S(1)}, bf16[32,1152]{1,0:T(8,128)(2,1)S(1)}, u32[]{:S(2)}, u32[]{:S(2)}) collective-permute-start(bf16[32,1152]{1,0:T(8,128)(2,1)S(1)} %get-tuple-element.48), channel_id=1, source_target_pairs={{0,1},{1,0},{2,3},{3,2},{4,5},{5,4},{6,7},{7,6},{8,9},{9,8},{10,11... | collective-permute-start | bytes 221192 | tf_op jit(solution)/shard_map/ppermute | solution.py:29
  98.4 7.1 %collective-permute-start.24 = (bf16[32,1152]{1,0:T(8,128)(2,1)S(1)}, bf16[32,1152]{1,0:T(8,128)(2,1)S(1)}, u32[]{:S(2)}, u32[]{:S(2)}) collective-permute-start(bf16[32,1152]{1,0:T(8,128)(2,1)S(1)} %get-tuple-element.47), channel_id=1, source_target_pairs={{0,2},{1,3},{2,0},{3,1},{4,6},{5,7},{6,4},{7,5},{8,10},{9,11},{10,... | collective-permute-start | bytes 221192 | tf_op jit(solution)/shard_map/ppermute | solution.py:29
  100.8 6.2 %collective-permute-start.25 = (bf16[32,1152]{1,0:T(8,128)(2,1)S(1)}, bf16[32,1152]{1,0:T(8,128)(2,1)S(1)}, u32[]{:S(2)}, u32[]{:S(2)}) collective-permute-start(bf16[32,1152]{1,0:T(8,128)(2,1)S(1)} %get-tuple-element.46), channel_id=1, source_target_pairs={{0,3},{1,2},{2,1},{3,0},{4,7},{5,6},{6,5},{7,4},{8,11},{9,10},{10,... | collective-permute-start | bytes 221192 | tf_op jit(solution)/shard_map/ppermute | solution.py:29

commit v6 on v5

--- a/solution.py
+++ b/solution.py
@@ -72,12 +72,17 @@
         start += ref.shape[0]
 
 
-def fetches(refs, held, sems):
+def fetches(refs, held, sems, paired=None):
     start, copies = 0, []
     for index, ref in enumerate(refs):
         count = ref.shape[0]
+        place = start
+        if paired is not None and index in (paired, paired + 1):
+            first = lax.axis_index("groups")
+            step = first if index == paired else -first
+            place = pl.multiple_of(start + step * count, count)
         copies.append(
-            pltpu.make_async_copy(ref, held.at[pl.ds(start, count)], sems.at[index])
+            pltpu.make_async_copy(ref, held.at[pl.ds(place, count)], sems.at[index])
         )
         start += count
     for copy in copies:
@@ -147,7 +152,7 @@
     terms, refs = refs[:added], refs[added:]
     split = near.shape[1]
     weights, outs, (held, sems) = refs[: -len(blocks) - 2], refs[-len(blocks) - 2 : -2], refs[-2:]
-    for copy in fetches(weights, held, sems):
+    for copy in fetches(weights, held, sems, paired=1):
         copy.wait()
     for index, out in zip(blocks, outs):
         rows = out.shape[0]
@@ -158,6 +163,36 @@
         out[...] = sums.astype(out.dtype)
 
 
+def return_kernel(near, far, core, *refs):
+    weights, (first, second, held, sems) = refs[:-4], refs[-4:]
+    for copy in fetches(weights, held, sems, paired=1):
+        copy.wait()
+    rows, split = first.shape[0], near.shape[1]
+    for index, out in enumerate((first, second)):
+        part = pl.ds((2 + index) * rows, rows)
+        sums = dot(near[part, :], held[:split, :], (1, 0)) + dot(far[part, :], held[split:, :], (1, 0))
+        out[...] = (sums + core[index * rows : (index + 1) * rows, :].astype(jnp.float32)).astype(
+            out.dtype
+        )
+
+
+def return_sums(hidden, weights, core):
+    rows, features = core.shape
+    units = hidden[0].shape[1] + hidden[1].shape[1]
+    return local_call(
+        return_kernel,
+        (shape((rows // 2, features), jnp.bfloat16),) * 2,
+        (*hidden, core, *weights),
+        2 * rows * units * features,
+        (
+            pltpu.VMEM((units, features), jnp.bfloat16),
+            pltpu.SemaphoreType.DMA((len(weights),)),
+        ),
+        near=3,
+        place=pl.ANY,
+    )
+
+
 def partial_sums(hidden, weights, blocks, terms=(), dtype=jnp.bfloat16):
     rows, features = hidden[0].shape[0] // 4, weights[0].shape[1]
     units = hidden[0].shape[1] + hidden[1].shape[1]
@@ -175,8 +210,8 @@
     )
 
 
-def pool_kernel(identity, order, own, back, out):
-    summed = own[...] + back[...].astype(jnp.float32)
+def pool_kernel(identity, order, own, first, second, out):
+    summed = own[...] + jnp.concatenate([first[...], second[...]], axis=0).astype(jnp.float32)
     center = jnp.mean(summed, axis=-1, keepdims=True)
     moved = summed - center
     spread = jnp.mean(moved * moved, axis=-1, keepdims=True)
@@ -340,32 +375,37 @@
 
 def feed_forward(tokens, inner_weight, outer_weight):
     barrier = lax.optimization_barrier
-    inner_x, outer_x = swap(inner_weight, "src", 2), swap(outer_weight, "src", 2)
     inner_half, outer_half = weight_halves(inner_weight, outer_weight)
+    inner_x, outer_x = swap(inner_weight, "src", 2), swap(outer_half, "src", 2)
     inner_far, outer_far = far_piece(inner_half), far_piece(outer_half)
     neighbour = swap(tokens, "tgt", 1)
-    inner_far_x, inner_far_y = swap(inner_far, "src", 2), swap(inner_far, "groups", 1)
-
-    outer_far, inner_far_y, outer_x, inner_x = barrier((outer_far, inner_far_y, outer_x, inner_x))
+    inner_far_x = swap(inner_far, "src", 2)
+
+    outer_y = swap(outer_x, "groups", 1)
+    inner_far, outer_far, inner_far_x, outer_y, inner_x = barrier(
+        (inner_far, outer_far, inner_far_x, outer_y, inner_x)
+    )
+    inner_far_y = swap(inner_far, "groups", 1)
     outer_far_x, outer_far_y = swap(outer_far, "src", 2), swap(outer_far, "groups", 1)
     inner_square = [inner_far_x, inner_far_y, swap(inner_far_y, "src", 2)]
     outer_square = [outer_far_x, outer_far_y, swap(outer_far_x, "groups", 1)]
     shared = [tokens, neighbour, swap(tokens, "src", 1), swap(neighbour, "src", 1)]
+    inner_square[2], outer_square[1] = barrier((inner_square[2], outer_square[1]))
     hidden = [
-        hidden_units(shared, [inner_weight, inner_x]),
-        hidden_units(shared, [inner_far, *inner_square]),
+        hidden_units(shared, [inner_weight, inner_x, inner_far, inner_square[0]]),
+        hidden_units(shared, inner_square[1:]),
     ]
 
-    weights = [outer_weight, outer_x, outer_far, *outer_square]
+    weights = [outer_weight, outer_x, outer_y, outer_far, *outer_square]
     (pair,) = partial_sums(hidden, weights, (3,))
     hidden, pair = barrier((hidden, pair))
     (core,) = partial_sums(hidden, weights, (2,))
     pair, core = barrier((swap(pair, "src", 1), core))
-    (back,) = partial_sums(hidden, weights, (1,), (pair,))
+    back = return_sums(hidden, weights, pair)
     back, core, hidden = barrier((back, core, hidden))
-    back = swap(back, "tgt", 1)
+    back = [swap(sums, "tgt", 1) for sums in back]
     (own,) = partial_sums(hidden, weights, (0,), (tokens, swap(core, "src", 1)), jnp.float32)
-    return own, back
+    return own, *back
 
 
 def on_device(tokens, sentence_ids, inner_weight, outer_weight, grid_rows, candidates, targets):

time: 108 us -> 106 us (0.981)
  Pallas kernels: 18.9 us -> 17.3 us
    pallas_call x12, Pallas kernels: 18.9 us -> 17.3 us  [local_call(): pl.pallas_call(kernel, out_shape=out_shape, in_specs=[pl.BlockSpec(memory...]
    ppermute x26 -> x28, starting transfers between devices: 29.3 us -> 28.3 us  [swap(): lax.ppermute(values, axis, [(i, i ^ offset) for i in range(lax.axis_size(...]
    unnamed x30 -> x36, local copies, waits for them, and re-layouts: 9.39 us -> 9.77 us
    ppermute x26 -> x28, waiting for transfers between devices: 49 us -> 49.2 us  [swap(): lax.ppermute(values, axis, [(i, i ^ offset) for i in range(lax.axis_size(...]
  transfers between devices with their start and end apart: 26 -> 28, of which waited for: 15 -> 17; matrix products, arithmetic and copies ran while one was open for 0% -> 0% of each run, Pallas kernels for 10% -> 8%
where the time goes in v6:
time: 106 us
  waiting for transfers between devices  49.2 us (46%)
  starting transfers between devices  28.3 us (27%)
  Pallas kernels  17.3 us (16%)
  local copies, waits for them, and re-layouts  9.89 us (9%)
    ppermute x28, waiting for transfers between devices, swap(): lax.ppermute(values, axis, [(i, i ^ offset) for i in range(lax.axis_size(...  49.2 us
    ppermute x28, starting transfers between devices, swap(): lax.ppermute(values, axis, [(i, i ^ offset) for i in range(lax.axis_size(...  28.3 us
    pallas_call x12, Pallas kernels, local_call(): pl.pallas_call(kernel, out_shape=out_shape, in_specs=[pl.BlockSpec(memory...  17.3 us
    unnamed x36, local copies, waits for them, and re-layouts  9.77 us
  transfers between devices with their start and end apart: 28, of which 17 were waited for; matrix products, arithmetic and copies ran while one was open for 0% of the time, Pallas kernels for 8%

profile of v6, /device:TPU:0, one launch (start us, length us, event | category | flops | bytes accessed | tf_op | source)
XLA Modules:
  0.0 105.8 jit_solution(18231109784458574534)
XLA Ops:
  0.7 1.9 %shard_map.87 = (bf16[128,1024]{1,0:T(8,128)(2,1)}, bf16[128,1024]{1,0:T(8,128)(2,1)}) custom-call(bf16[256,1024]{1,0:T(8,128)(2,1)} %refs_4_.1, bf16[256,1024]{1,0:T(8,128)(2,1)} %refs_2_.1), custom_call_target="tpu_custom_call" | custom-call | bytes 1572864 | tf_op jit(solution)/shard_map/pallas_call | solution.py:37
  2.6 3.0 %collective-permute-start.6 = (bf16[128,1024]{1,0:T(8,128)(2,1)}, bf16[128,1024]{1,0:T(8,128)(2,1)S(1)}, u32[]{:S(2)}, u32[]{:S(2)}) collective-permute-start(bf16[128,1024]{1,0:T(8,128)(2,1)} %get-tuple-element.31), channel_id=1, source_target_pairs={{0,8},{4,12},{8,0},{12,4},{1,9},{5,13},{9,1},{13,5},{2,10},{6,14},... | collective-permute-start | bytes 786440 | tf_op jit(solution)/shard_map/ppermute | solution.py:29
  5.6 2.6 %collective-permute-start.3 = (bf16[128,1024]{1,0:T(8,128)(2,1)}, bf16[128,1024]{1,0:T(8,128)(2,1)S(1)}, u32[]{:S(2)}, u32[]{:S(2)}) collective-permute-start(bf16[128,1024]{1,0:T(8,128)(2,1)} %get-tuple-element.30), channel_id=1, source_target_pairs={{0,2},{1,3},{2,0},{3,1},{4,6},{5,7},{6,4},{7,5},{8,10},{9,11},{10,... | collective-permute-start | bytes 786440 | tf_op jit(solution)/shard_map/ppermute | solution.py:29
  8.7 1.6 %collective-permute-start = (bf16[256,1024]{1,0:T(8,128)(2,1)}, bf16[256,1024]{1,0:T(8,128)(2,1)S(1)}, u32[]{:S(2)}, u32[]{:S(2)}) collective-permute-start(bf16[256,1024]{1,0:T(8,128)(2,1)} %refs_0_.11), channel_id=1, source_target_pairs={{0,1},{1,0},{2,3},{3,2},{4,5},{5,4},{6,7},{7,6},{8,9},{9,8},{10,11... | collective-permute-start | bytes 1572872 | tf_op jit(solution)/shard_map/ppermute | solution.py:29
  10.6 2.3 %collective-permute-done.6.refs_1_.refs_3_ = bf16[128,1024]{1,0:T(8,128)(2,1)S(1)} collective-permute-done((bf16[128,1024]{1,0:T(8,128)(2,1)}, bf16[128,1024]{1,0:T(8,128)(2,1)S(1)}, u32[]{:S(2)}, u32[]{:S(2)}) %collective-permute-start.6) | collective-permute-done | bytes 262176 | tf_op jit(solution)/shard_map/ppermute | solution.py:29
  12.9 2.1 %collective-permute-start.7 = (bf16[128,1024]{1,0:T(8,128)(2,1)S(1)}, bf16[128,1024]{1,0:T(8,128)(2,1)S(1)}, u32[]{:S(2)}, u32[]{:S(2)}) collective-permute-start(bf16[128,1024]{1,0:T(8,128)(2,1)S(1)} %collective-permute-done.6.refs_1_.refs_3_), channel_id=1, source_target_pairs={{0,16},{16,0},{1,17},{17,1},{2,18},{18,2},{3,19},{19,3},{4,20},{20... | collective-permute-start | bytes 786440 | tf_op jit(solution)/shard_map/ppermute | solution.py:29
  15.0 6.3 %collective-permute-done.3.refs_6_ = bf16[128,1024]{1,0:T(8,128)(2,1)S(1)} collective-permute-done((bf16[128,1024]{1,0:T(8,128)(2,1)}, bf16[128,1024]{1,0:T(8,128)(2,1)S(1)}, u32[]{:S(2)}, u32[]{:S(2)}) %collective-permute-start.3) | collective-permute-done | bytes 262176 | tf_op jit(solution)/shard_map/ppermute | solution.py:29
  21.8 8.9 %collective-permute-done.4.refs_3_.refs_5_ = bf16[128,1024]{1,0:T(8,128)(2,1)S(1)} collective-permute-done((bf16[128,1024]{1,0:T(8,128)(2,1)}, bf16[128,1024]{1,0:T(8,128)(2,1)S(1)}, u32[]{:S(2)}, u32[]{:S(2)}) %collective-permute-start.4) | collective-permute-done | bytes 262176 | tf_op jit(solution)/shard_map/ppermute | solution.py:29
  30.7 1.6 %collective-permute-start.9 = (bf16[128,1024]{1,0:T(8,128)(2,1)S(1)}, bf16[128,1024]{1,0:T(8,128)(2,1)S(1)}, u32[]{:S(2)}, u32[]{:S(2)}) collective-permute-start(bf16[128,1024]{1,0:T(8,128)(2,1)S(1)} %collective-permute-done.3.refs_6_), channel_id=1, source_target_pairs={{0,16},{16,0},{1,17},{17,1},{2,18},{18,2},{3,19},{19,3},{4,20},{20... | collective-permute-start | bytes 786440 | tf_op jit(solution)/shard_map/ppermute | solution.py:29
  33.3 1.6 %collective-permute-start.11 = (bf16[128,1024]{1,0:T(8,128)(2,1)S(1)}, bf16[128,1024]{1,0:T(8,128)(2,1)S(1)}, u32[]{:S(2)}, u32[]{:S(2)}) collective-permute-start(bf16[128,1024]{1,0:T(8,128)(2,1)S(1)} %collective-permute-done.4.refs_3_.refs_5_), channel_id=1, source_target_pairs={{0,16},{16,0},{1,17},{17,1},{2,18},{18,2},{3,19},{19,3},{4,20},{20... | collective-permute-start | bytes 786440 | tf_op jit(solution)/shard_map/ppermute | solution.py:29
  34.9 4.1 %collective-permute-done.9.refs_4_ = bf16[128,1024]{1,0:T(8,128)(2,1)S(1)} collective-permute-done((bf16[128,1024]{1,0:T(8,128)(2,1)S(1)}, bf16[128,1024]{1,0:T(8,128)(2,1)S(1)}, u32[]{:S(2)}, u32[]{:S(2)}) %collective-permute-start.9) | collective-permute-done | bytes 262176 | tf_op jit(solution)/shard_map/ppermute | solution.py:29
  39.1 2.9 %collective-permute-done.12.refs_4_.refs_6_ = bf16[128,1024]{1,0:T(8,128)(2,1)S(1)} collective-permute-done((bf16[128,1024]{1,0:T(8,128)(2,1)S(1)}, bf16[128,1024]{1,0:T(8,128)(2,1)S(1)}, u32[]{:S(2)}, u32[]{:S(2)}) %collective-permute-start.12) | collective-permute-done | bytes 262176 | tf_op jit(solution)/shard_map/ppermute | solution.py:29
  42.5 1.1 %collective-permute-done.11.refs_5_.refs_7_ = bf16[128,1024]{1,0:T(8,128)(2,1)S(1)} collective-permute-done((bf16[128,1024]{1,0:T(8,128)(2,1)S(1)}, bf16[128,1024]{1,0:T(8,128)(2,1)S(1)}, u32[]{:S(2)}, u32[]{:S(2)}) %collective-permute-start.11) | collective-permute-done | bytes 262176 | tf_op jit(solution)/shard_map/ppermute | solution.py:29
  43.7 3.0 %collective-permute-done.10.refs_5_ = bf16[128,1024]{1,0:T(8,128)(2,1)S(1)} collective-permute-done((bf16[128,1024]{1,0:T(8,128)(2,1)S(1)}, bf16[128,1024]{1,0:T(8,128)(2,1)S(1)}, u32[]{:S(2)}, u32[]{:S(2)}) %collective-permute-start.10) | collective-permute-done | bytes 262176 | tf_op jit(solution)/shard_map/ppermute | solution.py:29
  46.6 1.0 copy-done.8
  47.7 0.9 shard_map.89.far
  48.6 2.2 %shard_map.88.near = bf16[1024,768]{1,0:T(8,128)(2,1)S(1)} custom-call(bf16[256,1024]{1,0:T(8,128)(2,1)S(1)} %copy-done.9, bf16[256,1024]{1,0:T(8,128)(2,1)S(1)} %collective-permute-done.refs_1_, bf16[256,1024]{1,0:T(8,128)(2,1)S(1)} %collective-permute-done.1.refs_2_, bf16[256,1024]{1,0:T(8,128)(2,1)S(1)} %collective-permute-done.2.refs_3_, ...), custom_call_target="tpu_custom_call" | custom-call | flops 1610612736 | bytes 5242880 | tf_op jit(solution)/shard_map/pallas_call | solution.py:37
  50.9 1.0 shard_map.90
  51.9 1.7 %shard_map.91 = bf16[256,1024]{1,0:T(8,128)(2,1)} custom-call(bf16[1024,768]{1,0:T(8,128)(2,1)S(1)} %shard_map.88.near, bf16[1024,256]{1,0:T(8,128)(2,1)S(1)} %shard_map.89.far, bf16[256,1024]{1,0:T(8,128)(2,1)S(1)} %copy-done, bf16[128,1024]{1,0:T(8,128)(2,1)S(1)} %collective-permute-done.6.refs_1_.refs_3_, ...), custom_call_target="tpu_custom_call" | custom-call | flops 536870912 | bytes 4718592 | tf_op jit(solution)/shard_map/pallas_call | solution.py:37
  53.8 1.0 shard_map.92
  54.8 0.7 copy-done.14
  55.5 0.7 copy-done.15
  56.6 2.3 %collective-permute-start.16 = (bf16[128,1024]{1,0:T(8,128)(2,1)}, bf16[128,1024]{1,0:T(8,128)(2,1)S(1)}, u32[]{:S(2)}, u32[]{:S(2)}) collective-permute-start(bf16[128,1024]{1,0:T(8,128)(2,1)} %copy-done.15), channel_id=1, source_target_pairs={{0,1},{1,0},{2,3},{3,2},{4,5},{5,4},{6,7},{7,6},{8,9},{9,8},{10,11... | collective-permute-start | bytes 786440 | tf_op jit(solution)/shard_map/ppermute | solution.py:29
  59.0 0.9 copy-done.3
  59.9 0.9 copy-done.5
  60.9 0.9 copy-done.7
  61.8 1.0 copy-done.10
  62.9 2.0 %shard_map.93.own = f32[256,1024]{1,0:T(8,128)S(1)} custom-call(bf16[1024,768]{1,0:T(8,128)(2,1)S(1)} %shard_map.88.near, bf16[1024,256]{1,0:T(8,128)(2,1)S(1)} %shard_map.89.far, bf16[256,1024]{1,0:T(8,128)(2,1)S(1)} %copy-done.10, bf16[256,1024]{1,0:T(8,128)(2,1)} %collective-permute-done.15.refs_1_, bf16[256,1024]{1,0:T(8,128)(2,1)S(1)} %copy-done, ...), custom_call_target="tpu_custom_call" | custom-call | flops 536870912 | bytes 6291456 | tf_op jit(solution)/shard_map/pallas_call | solution.py:37
  64.9 1.3 %collective-permute-done.16.first = bf16[128,1024]{1,0:T(8,128)(2,1)S(1)} collective-permute-done((bf16[128,1024]{1,0:T(8,128)(2,1)}, bf16[128,1024]{1,0:T(8,128)(2,1)S(1)}, u32[]{:S(2)}, u32[]{:S(2)}) %collective-permute-start.16) | collective-permute-done | bytes 262176 | tf_op jit(solution)/shard_map/ppermute | solution.py:29
  66.2 5.1 %collective-permute-done.17.second = bf16[128,1024]{1,0:T(8,128)(2,1)S(1)} collective-permute-done((bf16[128,1024]{1,0:T(8,128)(2,1)}, bf16[128,1024]{1,0:T(8,128)(2,1)S(1)}, u32[]{:S(2)}, u32[]{:S(2)}) %collective-permute-start.17) | collective-permute-done | bytes 262176 | tf_op jit(solution)/shard_map/ppermute | solution.py:29
  71.4 1.2 %shard_map.94 = bf16[32,1024]{1,0:T(8,128)(2,1)S(1)} custom-call(s32[1,256]{1,0:T(1,128)S(1)} %copy-done.13, s32[1,32]{1,0:T(1,128)S(1)} %fusion.2.order, f32[256,1024]{1,0:T(8,128)S(1)} %shard_map.93.own, bf16[128,1024]{1,0:T(8,128)(2,1)S(1)} %collective-permute-done.16.first, bf16[128,1024]{1,0:T(8,128)(2,1)S(1)} %collective-permute-done.17.second), custom_call_target="tpu_custom_call" | custom-call | flops 5242880 | bytes 1639552 | tf_op jit(solution)/shard_map/pallas_call | solution.py:37
  72.6 0.6 collective-permute-start.18
  73.2 3.4 %collective-permute-done.18 = bf16[2,1,8,1024]{3,2,1,0:T(8,128)(2,1)S(1)} collective-permute-done((bf16[2,1,8,1024]{3,2,1,0:T(8,128)(2,1)S(1)}, bf16[2,1,8,1024]{3,2,1,0:T(8,128)(2,1)S(1)}, u32[]{:S(2)}, u32[]{:S(2)}) %collective-permute-start.18) | collective-permute-done | bytes 32800 | tf_op jit(solution)/shard_map/ppermute | solution.py:29
  76.7 1.1 %collective-permute-done.19 = bf16[1,2,8,1024]{3,2,1,0:T(8,128)(2,1)S(1)} collective-permute-done((bf16[1,2,8,1024]{3,2,1,0:T(8,128)(2,1)S(1)}, bf16[1,2,8,1024]{3,2,1,0:T(8,128)(2,1)S(1)}, u32[]{:S(2)}, u32[]{:S(2)}) %collective-permute-start.19) | collective-permute-done | bytes 32800 | tf_op jit(solution)/shard_map/ppermute | solution.py:29
  77.8 1.8 %collective-permute-start.20 = (bf16[32,1024]{1,0:T(8,128)(2,1)S(1)}, bf16[32,1024]{1,0:T(8,128)(2,1)S(1)}, u32[]{:S(2)}, u32[]{:S(2)}) collective-permute-start(bf16[32,1024]{1,0:T(8,128)(2,1)S(1)} %maximum_bitcast_fusion.refs_0_), channel_id=1, source_target_pairs={{0,1},{1,0},{2,3},{3,2},{4,5},{5,4},{6,7},{7,6},{8,9},{9,8},{10,11... | collective-permute-start | bytes 196616 | tf_op jit(solution)/shard_map/ppermute | solution.py:29
  79.7 1.3 %collective-permute-start.21 = (bf16[32,1024]{1,0:T(8,128)(2,1)S(1)}, bf16[32,1024]{1,0:T(8,128)(2,1)S(1)}, u32[]{:S(2)}, u32[]{:S(2)}) collective-permute-start(bf16[32,1024]{1,0:T(8,128)(2,1)S(1)} %maximum_bitcast_fusion.refs_0_), channel_id=1, source_target_pairs={{0,2},{1,3},{2,0},{3,1},{4,6},{5,7},{6,4},{7,5},{8,10},{9,11},{10,... | collective-permute-start | bytes 196616 | tf_op jit(solution)/shard_map/ppermute | solution.py:29
  80.9 1.3 %collective-permute-start.22 = (bf16[32,1024]{1,0:T(8,128)(2,1)S(1)}, bf16[32,1024]{1,0:T(8,128)(2,1)S(1)}, u32[]{:S(2)}, u32[]{:S(2)}) collective-permute-start(bf16[32,1024]{1,0:T(8,128)(2,1)S(1)} %maximum_bitcast_fusion.refs_0_), channel_id=1, source_target_pairs={{0,3},{1,2},{2,1},{3,0},{4,7},{5,6},{6,5},{7,4},{8,11},{9,10},{10,... | collective-permute-start | bytes 196616 | tf_op jit(solution)/shard_map/ppermute | solution.py:29
  82.5 3.4 %copy-done.1 = bf16[4096,1024]{1,0:T(8,128)(2,1)S(1)} copy-done((bf16[4096,1024]{1,0:T(8,128)(2,1)S(1)}, bf16[4096,1024]{1,0:T(8,128)(2,1)}, u32[]{:S(2)}) %copy-start.1) | copy-done | bytes 8388632
  85.9 1.7 %shard_map.86.units = bf16[1024,1024]{1,0:T(8,128)(2,1)S(1)} custom-call(s32[1,16]{1,0:T(1,128)S(1)} %copy-done.12, bf16[4096,1024]{1,0:T(8,128)(2,1)S(1)} %copy-done.1), custom_call_target="tpu_custom_call" | custom-call | flops 8388608 | bytes 10485824 | tf_op jit(solution)/shard_map/pallas_call | solution.py:37
  87.9 1.8 %shard_map.95 = (f32[128,1024]{1,0:T(8,128)S(1)}, f32[16,256]{1,0:T(8,128)S(1)}, f32[128,1]{1,0:T(8,128)S(1)}) custom-call(s32[1,16]{1,0:T(1,128)S(1)} %copy-done.12, s32[1,128]{1,0:T(1,128)S(1)} %xor.32.place, bf16[1024,1024]{1,0:T(8,128)(2,1)S(1)} %shard_map.86.units, bf16[32,1024]{1,0:T(8,128)(2,1)S(1)} %maximum_bitcast_fusion.refs_0_, ...), custom_call_target="tpu_custom_call" | custom-call | flops 268435456 | bytes 2901056 | tf_op jit(solution)/shard_map/pallas_call | solution.py:37
  89.7 1.2 %collective-permute-done.23 = f32[16,256]{1,0:T(8,128)S(1)} collective-permute-done((f32[16,256]{1,0:T(8,128)S(1)}, f32[16,256]{1,0:T(8,128)S(1)}, u32[]{:S(2)}, u32[]{:S(2)}) %collective-permute-start.23) | collective-permute-done | bytes 16416 | tf_op jit(solution)/shard_map/ppermute | solution.py:29
  91.5 3.2 %collective-permute-done.24 = f32[16,256]{1,0:T(8,128)S(1)} collective-permute-done((f32[16,256]{1,0:T(8,128)S(1)}, f32[16,256]{1,0:T(8,128)S(1)}, u32[]{:S(2)}, u32[]{:S(2)}) %collective-permute-start.24) | collective-permute-done | bytes 16416 | tf_op jit(solution)/shard_map/ppermute | solution.py:29
  94.7 1.1 %shard_map.96 = (f32[32,1152]{1,0:T(8,128)S(1)}, bf16[96,1152]{1,0:T(8,128)(2,1)S(1)}) custom-call(s32[1,16]{1,0:T(1,128)S(1)} %copy-done.12, f32[128,1024]{1,0:T(8,128)S(1)} %get-tuple-element.51.expo, f32[16,256]{1,0:T(8,128)S(1)} %add.65.columns, f32[128,1]{1,0:T(8,128)S(1)} %get-tuple-element.53.row_total, bf16[1024,1024]{1,0:T(8,128)(2,1)S(1)} %shard_map.86.units), custom_call_target="tpu_custom_call" | custom-call | flops 268435456 | bytes 3007040 | tf_op jit(solution)/shard_map/pallas_call | solution.py:37
  95.8 1.4 %collective-permute-start.25 = (bf16[32,1152]{1,0:T(8,128)(2,1)S(1)}, bf16[32,1152]{1,0:T(8,128)(2,1)S(1)}, u32[]{:S(2)}, u32[]{:S(2)}) collective-permute-start(bf16[32,1152]{1,0:T(8,128)(2,1)S(1)} %get-tuple-element.60), channel_id=1, source_target_pairs={{0,1},{1,0},{2,3},{3,2},{4,5},{5,4},{6,7},{7,6},{8,9},{9,8},{10,11... | collective-permute-start | bytes 221192 | tf_op jit(solution)/shard_map/ppermute | solution.py:29
  97.2 1.3 %collective-permute-start.26 = (bf16[32,1152]{1,0:T(8,128)(2,1)S(1)}, bf16[32,1152]{1,0:T(8,128)(2,1)S(1)}, u32[]{:S(2)}, u32[]{:S(2)}) collective-permute-start(bf16[32,1152]{1,0:T(8,128)(2,1)S(1)} %get-tuple-element.59), channel_id=1, source_target_pairs={{0,2},{1,3},{2,0},{3,1},{4,6},{5,7},{6,4},{7,5},{8,10},{9,11},{10,... | collective-permute-start | bytes 221192 | tf_op jit(solution)/shard_map/ppermute | solution.py:29
  98.6 1.7 %collective-permute-start.27 = (bf16[32,1152]{1,0:T(8,128)(2,1)S(1)}, bf16[32,1152]{1,0:T(8,128)(2,1)S(1)}, u32[]{:S(2)}, u32[]{:S(2)}) collective-permute-start(bf16[32,1152]{1,0:T(8,128)(2,1)S(1)} %get-tuple-element.58), channel_id=1, source_target_pairs={{0,3},{1,2},{2,1},{3,0},{4,7},{5,6},{6,5},{7,4},{8,11},{9,10},{10,... | collective-permute-start | bytes 221192 | tf_op jit(solution)/shard_map/ppermute | solution.py:29
  100.8 4.2 %collective-permute-done.26.refs_1_ = bf16[32,1152]{1,0:T(8,128)(2,1)S(1)} collective-permute-done((bf16[32,1152]{1,0:T(8,128)(2,1)S(1)}, bf16[32,1152]{1,0:T(8,128)(2,1)S(1)}, u32[]{:S(2)}, u32[]{:S(2)}) %collective-permute-start.26) | collective-permute-done | bytes 73760 | tf_op jit(solution)/shard_map/ppermute | solution.py:29
  105.0 0.8 shard_map.97
  (67 shorter events, 5.5 us)
Async XLA Ops:
  0.6 48.0 %copy-start.11 = (bf16[256,1024]{1,0:T(8,128)(2,1)S(1)}, bf16[256,1024]{1,0:T(8,128)(2,1)}, u32[]{:S(2)}) copy-start(bf16[256,1024]{1,0:T(8,128)(2,1)} %refs_4_.1) | copy-start | bytes 1572868
  0.6 48.0 %copy-start.9 = (bf16[256,1024]{1,0:T(8,128)(2,1)S(1)}, bf16[256,1024]{1,0:T(8,128)(2,1)}, u32[]{:S(2)}) copy-start(bf16[256,1024]{1,0:T(8,128)(2,1)} %refs_0_.11) | copy-start | bytes 1572868
  2.6 10.3 %collective-permute-start.6 = (bf16[128,1024]{1,0:T(8,128)(2,1)}, bf16[128,1024]{1,0:T(8,128)(2,1)S(1)}, u32[]{:S(2)}, u32[]{:S(2)}) collective-permute-start(bf16[128,1024]{1,0:T(8,128)(2,1)} %get-tuple-element.31), channel_id=1, source_target_pairs={{0,8},{4,12},{8,0},{12,4},{1,9},{5,13},{9,1},{13,5},{2,10},{6,14},... | collective-permute-start | bytes 786440 | tf_op jit(solution)/shard_map/ppermute | solution.py:29
  5.6 15.8 %collective-permute-start.3 = (bf16[128,1024]{1,0:T(8,128)(2,1)}, bf16[128,1024]{1,0:T(8,128)(2,1)S(1)}, u32[]{:S(2)}, u32[]{:S(2)}) collective-permute-start(bf16[128,1024]{1,0:T(8,128)(2,1)} %get-tuple-element.30), channel_id=1, source_target_pairs={{0,2},{1,3},{2,0},{3,1},{4,6},{5,7},{6,4},{7,5},{8,10},{9,11},{10,... | collective-permute-start | bytes 786440 | tf_op jit(solution)/shard_map/ppermute | solution.py:29
  8.2 22.5 %collective-permute-start.8 = (bf16[256,1024]{1,0:T(8,128)(2,1)}, bf16[256,1024]{1,0:T(8,128)(2,1)S(1)}, u32[]{:S(2)}, u32[]{:S(2)}) collective-permute-start(bf16[256,1024]{1,0:T(8,128)(2,1)} %refs_4_.1), channel_id=1, source_target_pairs={{0,8},{4,12},{8,0},{12,4},{1,9},{5,13},{9,1},{13,5},{2,10},{6,14},... | collective-permute-start | bytes 1572872 | tf_op jit(solution)/shard_map/ppermute | solution.py:29
  8.7 23.6 %collective-permute-start = (bf16[256,1024]{1,0:T(8,128)(2,1)}, bf16[256,1024]{1,0:T(8,128)(2,1)S(1)}, u32[]{:S(2)}, u32[]{:S(2)}) collective-permute-start(bf16[256,1024]{1,0:T(8,128)(2,1)} %refs_0_.11), channel_id=1, source_target_pairs={{0,1},{1,0},{2,3},{3,2},{4,5},{5,4},{6,7},{7,6},{8,9},{9,8},{10,11... | collective-permute-start | bytes 1572872 | tf_op jit(solution)/shard_map/ppermute | solution.py:29
  10.3 20.4 %collective-permute-start.4 = (bf16[128,1024]{1,0:T(8,128)(2,1)}, bf16[128,1024]{1,0:T(8,128)(2,1)S(1)}, u32[]{:S(2)}, u32[]{:S(2)}) collective-permute-start(bf16[128,1024]{1,0:T(8,128)(2,1)} %get-tuple-element.31), channel_id=1, source_target_pairs={{0,2},{1,3},{2,0},{3,1},{4,6},{5,7},{6,4},{7,5},{8,10},{9,11},{10,... | collective-permute-start | bytes 786440 | tf_op jit(solution)/shard_map/ppermute | solution.py:29
  12.9 17.7 %collective-permute-start.7 = (bf16[128,1024]{1,0:T(8,128)(2,1)S(1)}, bf16[128,1024]{1,0:T(8,128)(2,1)S(1)}, u32[]{:S(2)}, u32[]{:S(2)}) collective-permute-start(bf16[128,1024]{1,0:T(8,128)(2,1)S(1)} %collective-permute-done.6.refs_1_.refs_3_), channel_id=1, source_target_pairs={{0,16},{16,0},{1,17},{17,1},{2,18},{18,2},{3,19},{19,3},{4,20},{20... | collective-permute-start | bytes 786440 | tf_op jit(solution)/shard_map/ppermute | solution.py:29
  21.4 9.3 %collective-permute-start.5 = (bf16[128,1024]{1,0:T(8,128)(2,1)S(1)}, bf16[128,1024]{1,0:T(8,128)(2,1)S(1)}, u32[]{:S(2)}, u32[]{:S(2)}) collective-permute-start(bf16[128,1024]{1,0:T(8,128)(2,1)S(1)} %collective-permute-done.3.refs_6_), channel_id=1, source_target_pairs={{0,8},{4,12},{8,0},{12,4},{1,9},{5,13},{9,1},{13,5},{2,10},{6,14},... | collective-permute-start | bytes 786440 | tf_op jit(solution)/shard_map/ppermute | solution.py:29
  30.7 8.3 %collective-permute-start.9 = (bf16[128,1024]{1,0:T(8,128)(2,1)S(1)}, bf16[128,1024]{1,0:T(8,128)(2,1)S(1)}, u32[]{:S(2)}, u32[]{:S(2)}) collective-permute-start(bf16[128,1024]{1,0:T(8,128)(2,1)S(1)} %collective-permute-done.3.refs_6_), channel_id=1, source_target_pairs={{0,16},{16,0},{1,17},{17,1},{2,18},{18,2},{3,19},{19,3},{4,20},{20... | collective-permute-start | bytes 786440 | tf_op jit(solution)/shard_map/ppermute | solution.py:29
  32.3 14.3 %collective-permute-start.1 = (bf16[256,1024]{1,0:T(8,128)(2,1)}, bf16[256,1024]{1,0:T(8,128)(2,1)S(1)}, u32[]{:S(2)}, u32[]{:S(2)}) collective-permute-start(bf16[256,1024]{1,0:T(8,128)(2,1)} %refs_0_.11), channel_id=1, source_target_pairs={{0,4},{4,0},{8,12},{12,8},{1,5},{5,1},{9,13},{13,9},{2,6},{6,2},{1... | collective-permute-start | bytes 1572872 | tf_op jit(solution)/shard_map/ppermute | solution.py:29
  32.3 14.3 %collective-permute-start.2 = (bf16[256,1024]{1,0:T(8,128)(2,1)S(1)}, bf16[256,1024]{1,0:T(8,128)(2,1)S(1)}, u32[]{:S(2)}, u32[]{:S(2)}) collective-permute-start(bf16[256,1024]{1,0:T(8,128)(2,1)S(1)} %collective-permute-done.refs_1_), channel_id=1, source_target_pairs={{0,4},{4,0},{8,12},{12,8},{1,5},{5,1},{9,13},{13,9},{2,6},{6,2},{1... | collective-permute-start | bytes 1572872 | tf_op jit(solution)/shard_map/ppermute | solution.py:29
  32.8 9.2 %collective-permute-start.12 = (bf16[128,1024]{1,0:T(8,128)(2,1)S(1)}, bf16[128,1024]{1,0:T(8,128)(2,1)S(1)}, u32[]{:S(2)}, u32[]{:S(2)}) collective-permute-start(bf16[128,1024]{1,0:T(8,128)(2,1)S(1)} %collective-permute-done.4.refs_3_.refs_5_), channel_id=1, source_target_pairs={{0,8},{4,12},{8,0},{12,4},{1,9},{5,13},{9,1},{13,5},{2,10},{6,14},... | collective-permute-start | bytes 786440 | tf_op jit(solution)/shard_map/ppermute | solution.py:29
  33.3 10.3 %collective-permute-start.11 = (bf16[128,1024]{1,0:T(8,128)(2,1)S(1)}, bf16[128,1024]{1,0:T(8,128)(2,1)S(1)}, u32[]{:S(2)}, u32[]{:S(2)}) collective-permute-start(bf16[128,1024]{1,0:T(8,128)(2,1)S(1)} %collective-permute-done.4.refs_3_.refs_5_), channel_id=1, source_target_pairs={{0,16},{16,0},{1,17},{17,1},{2,18},{18,2},{3,19},{19,3},{4,20},{20... | collective-permute-start | bytes 786440 | tf_op jit(solution)/shard_map/ppermute | solution.py:29
  39.0 7.6 %collective-permute-start.10 = (bf16[128,1024]{1,0:T(8,128)(2,1)S(1)}, bf16[128,1024]{1,0:T(8,128)(2,1)S(1)}, u32[]{:S(2)}, u32[]{:S(2)}) collective-permute-start(bf16[128,1024]{1,0:T(8,128)(2,1)S(1)} %collective-permute-done.9.refs_4_), channel_id=1, source_target_pairs={{0,8},{4,12},{8,0},{12,4},{1,9},{5,13},{9,1},{13,5},{2,10},{6,14},... | collective-permute-start | bytes 786440 | tf_op jit(solution)/shard_map/ppermute | solution.py:29
  42.0 11.8 %copy-start.2 = (bf16[128,1024]{1,0:T(8,128)(2,1)}, bf16[128,1024]{1,0:T(8,128)(2,1)S(1)}, u32[]{:S(2)}) copy-start(bf16[128,1024]{1,0:T(8,128)(2,1)S(1)} %collective-permute-done.12.refs_4_.refs_6_) | copy-start | bytes 786436
  42.0 8.9 %collective-permute-start.13 = (bf16[128,1024]{1,0:T(8,128)(2,1)S(1)}, bf16[128,1024]{1,0:T(8,128)(2,1)S(1)}, u32[]{:S(2)}, u32[]{:S(2)}) collective-permute-start(bf16[128,1024]{1,0:T(8,128)(2,1)S(1)} %collective-permute-done.12.refs_4_.refs_6_), channel_id=1, source_target_pairs={{0,16},{16,0},{1,17},{17,1},{2,18},{18,2},{3,19},{19,3},{4,20},{20... | collective-permute-start | bytes 786440 | tf_op jit(solution)/shard_map/ppermute | solution.py:29
  43.7 10.2 %copy-start.4 = (bf16[128,1024]{1,0:T(8,128)(2,1)}, bf16[128,1024]{1,0:T(8,128)(2,1)S(1)}, u32[]{:S(2)}) copy-start(bf16[128,1024]{1,0:T(8,128)(2,1)S(1)} %collective-permute-done.11.refs_5_.refs_7_) | copy-start | bytes 786436
  46.6 1.0 copy-start.8
  48.6 2.3 %copy-start = (bf16[256,1024]{1,0:T(8,128)(2,1)S(1)}, bf16[256,1024]{1,0:T(8,128)(2,1)}, u32[]{:S(2)}) copy-start(bf16[256,1024]{1,0:T(8,128)(2,1)} %refs_2_.1) | copy-start | bytes 1572868
  50.9 3.0 %copy-start.6 = (bf16[128,1024]{1,0:T(8,128)(2,1)}, bf16[128,1024]{1,0:T(8,128)(2,1)S(1)}, u32[]{:S(2)}) copy-start(bf16[128,1024]{1,0:T(8,128)(2,1)S(1)} %collective-permute-done.13.refs_6_.refs_8_) | copy-start | bytes 786436
  51.8 2.0 %collective-permute-start.14 = (bf16[256,1024]{1,0:T(8,128)(2,1)S(1)}, bf16[256,1024]{1,0:T(8,128)(2,1)S(1)}, u32[]{:S(2)}, u32[]{:S(2)}) collective-permute-start(bf16[256,1024]{1,0:T(8,128)(2,1)S(1)} %shard_map.90), channel_id=1, source_target_pairs={{0,4},{4,0},{8,12},{12,8},{1,5},{5,1},{9,13},{13,9},{2,6},{6,2},{1... | collective-permute-start | bytes 1572872 | tf_op jit(solution)/shard_map/ppermute | solution.py:29
  53.7 5.3 %copy-start.17 = (s32[32]{0:T(128)S(1)}, s32[32]{0:T(128)}, u32[]{:S(2)}) copy-start(s32[32]{0:T(128)} %param.11) | copy-start | bytes 388
  54.8 0.7 copy-start.14
  55.5 0.7 copy-start.15
  56.3 2.7 %collective-permute-start.15 = (bf16[256,1024]{1,0:T(8,128)(2,1)}, bf16[256,1024]{1,0:T(8,128)(2,1)}, u32[]{:S(2)}, u32[]{:S(2)}) collective-permute-start(bf16[256,1024]{1,0:T(8,128)(2,1)} %shard_map.91), channel_id=1, source_target_pairs={{0,4},{4,0},{8,12},{12,8},{1,5},{5,1},{9,13},{13,9},{2,6},{6,2},{1... | collective-permute-start | bytes 1572872 | tf_op jit(solution)/shard_map/ppermute | solution.py:29
  56.6 9.6 %collective-permute-start.16 = (bf16[128,1024]{1,0:T(8,128)(2,1)}, bf16[128,1024]{1,0:T(8,128)(2,1)S(1)}, u32[]{:S(2)}, u32[]{:S(2)}) collective-permute-start(bf16[128,1024]{1,0:T(8,128)(2,1)} %copy-done.15), channel_id=1, source_target_pairs={{0,1},{1,0},{2,3},{3,2},{4,5},{5,4},{6,7},{7,6},{8,9},{9,8},{10,11... | collective-permute-start | bytes 786440 | tf_op jit(solution)/shard_map/ppermute | solution.py:29
  58.9 12.4 %collective-permute-start.17 = (bf16[128,1024]{1,0:T(8,128)(2,1)}, bf16[128,1024]{1,0:T(8,128)(2,1)S(1)}, u32[]{:S(2)}, u32[]{:S(2)}) collective-permute-start(bf16[128,1024]{1,0:T(8,128)(2,1)} %copy-done.14), channel_id=1, source_target_pairs={{0,1},{1,0},{2,3},{3,2},{4,5},{5,4},{6,7},{7,6},{8,9},{9,8},{10,11... | collective-permute-start | bytes 786440 | tf_op jit(solution)/shard_map/ppermute | solution.py:29
  59.0 1.0 copy-start.3
  59.9 0.9 copy-start.5
  60.9 0.9 copy-start.7
  61.8 1.0 copy-start.10
  62.9 8.5 %copy-start.13 = (s32[1,256]{1,0:T(1,128)S(1)}, s32[1,256]{1,0:T(1,128)}, u32[]{:S(2)}) copy-start(s32[1,256]{1,0:T(1,128)} %identity.1) | copy-start | bytes 3076
  62.9 10.3 %copy-start.16 = (s32[4]{0:T(128)S(1)}, s32[4]{0:T(128)}, u32[]{:S(2)}) copy-start(s32[4]{0:T(128)} %constant.39.clone.1) | copy-start | bytes 52
  62.9 19.6 %copy-start.12 = (s32[1,16]{1,0:T(1,128)S(1)}, s32[1,16]{1,0:T(1,128)}, u32[]{:S(2)}) copy-start(s32[1,16]{1,0:T(1,128)} %listed.5) | copy-start | bytes 196
  72.6 4.0 %collective-permute-start.18 = (bf16[2,1,8,1024]{3,2,1,0:T(8,128)(2,1)S(1)}, bf16[2,1,8,1024]{3,2,1,0:T(8,128)(2,1)S(1)}, u32[]{:S(2)}, u32[]{:S(2)}) collective-permute-start(bf16[2,1,8,1024]{3,2,1,0:T(8,128)(2,1)S(1)} %get-tuple-element.64), channel_id=1, source_target_pairs={{0,8},{4,12},{8,0},{12,4},{1,9},{5,13},{9,1},{13,5},{2,10},{6,14},... | collective-permute-start | bytes 98312 | tf_op jit(solution)/shard_map/ppermute | solution.py:29
  76.6 1.3 %collective-permute-start.19 = (bf16[1,2,8,1024]{3,2,1,0:T(8,128)(2,1)S(1)}, bf16[1,2,8,1024]{3,2,1,0:T(8,128)(2,1)S(1)}, u32[]{:S(2)}, u32[]{:S(2)}) collective-permute-start(bf16[1,2,8,1024]{3,2,1,0:T(8,128)(2,1)S(1)} %get-tuple-element.62), channel_id=1, source_target_pairs={{0,4},{4,0},{8,12},{12,8},{1,5},{5,1},{9,13},{13,9},{2,6},{6,2},{1... | collective-permute-start | bytes 98312 | tf_op jit(solution)/shard_map/ppermute | solution.py:29
  77.8 9.7 %collective-permute-start.20 = (bf16[32,1024]{1,0:T(8,128)(2,1)S(1)}, bf16[32,1024]{1,0:T(8,128)(2,1)S(1)}, u32[]{:S(2)}, u32[]{:S(2)}) collective-permute-start(bf16[32,1024]{1,0:T(8,128)(2,1)S(1)} %maximum_bitcast_fusion.refs_0_), channel_id=1, source_target_pairs={{0,1},{1,0},{2,3},{3,2},{4,5},{5,4},{6,7},{7,6},{8,9},{9,8},{10,11... | collective-permute-start | bytes 196616 | tf_op jit(solution)/shard_map/ppermute | solution.py:29
  79.7 8.2 %collective-permute-start.21 = (bf16[32,1024]{1,0:T(8,128)(2,1)S(1)}, bf16[32,1024]{1,0:T(8,128)(2,1)S(1)}, u32[]{:S(2)}, u32[]{:S(2)}) collective-permute-start(bf16[32,1024]{1,0:T(8,128)(2,1)S(1)} %maximum_bitcast_fusion.refs_0_), channel_id=1, source_target_pairs={{0,2},{1,3},{2,0},{3,1},{4,6},{5,7},{6,4},{7,5},{8,10},{9,11},{10,... | collective-permute-start | bytes 196616 | tf_op jit(solution)/shard_map/ppermute | solution.py:29
  80.9 7.0 %collective-permute-start.22 = (bf16[32,1024]{1,0:T(8,128)(2,1)S(1)}, bf16[32,1024]{1,0:T(8,128)(2,1)S(1)}, u32[]{:S(2)}, u32[]{:S(2)}) collective-permute-start(bf16[32,1024]{1,0:T(8,128)(2,1)S(1)} %maximum_bitcast_fusion.refs_0_), channel_id=1, source_target_pairs={{0,3},{1,2},{2,1},{3,0},{4,7},{5,6},{6,5},{7,4},{8,11},{9,10},{10,... | collective-permute-start | bytes 196616 | tf_op jit(solution)/shard_map/ppermute | solution.py:29
  82.5 3.4 %copy-start.1 = (bf16[4096,1024]{1,0:T(8,128)(2,1)S(1)}, bf16[4096,1024]{1,0:T(8,128)(2,1)}, u32[]{:S(2)}) copy-start(bf16[4096,1024]{1,0:T(8,128)(2,1)} %targets.1) | copy-start | bytes 25165828
  89.7 1.2 %collective-permute-start.23 = (f32[16,256]{1,0:T(8,128)S(1)}, f32[16,256]{1,0:T(8,128)S(1)}, u32[]{:S(2)}, u32[]{:S(2)}) collective-permute-start(f32[16,256]{1,0:T(8,128)S(1)} %get-tuple-element.52), channel_id=1, source_target_pairs={{0,4},{4,0},{8,12},{12,8},{1,5},{5,1},{9,13},{13,9},{2,6},{6,2},{1... | collective-permute-start | bytes 49160 | tf_op jit(solution)/shard_map/ppermute | solution.py:29
  90.9 3.7 %collective-permute-start.24 = (f32[16,256]{1,0:T(8,128)S(1)}, f32[16,256]{1,0:T(8,128)S(1)}, u32[]{:S(2)}, u32[]{:S(2)}) collective-permute-start(f32[16,256]{1,0:T(8,128)S(1)} %add.64), channel_id=1, source_target_pairs={{0,8},{4,12},{8,0},{12,4},{1,9},{5,13},{9,1},{13,5},{2,10},{6,14},... | collective-permute-start | bytes 49160 | tf_op jit(solution)/shard_map/ppermute | solution.py:29
  95.8 5.0 %collective-permute-start.25 = (bf16[32,1152]{1,0:T(8,128)(2,1)S(1)}, bf16[32,1152]{1,0:T(8,128)(2,1)S(1)}, u32[]{:S(2)}, u32[]{:S(2)}) collective-permute-start(bf16[32,1152]{1,0:T(8,128)(2,1)S(1)} %get-tuple-element.60), channel_id=1, source_target_pairs={{0,1},{1,0},{2,3},{3,2},{4,5},{5,4},{6,7},{7,6},{8,9},{9,8},{10,11... | collective-permute-start | bytes 221192 | tf_op jit(solution)/shard_map/ppermute | solution.py:29
  97.2 7.8 %collective-permute-start.26 = (bf16[32,1152]{1,0:T(8,128)(2,1)S(1)}, bf16[32,1152]{1,0:T(8,128)(2,1)S(1)}, u32[]{:S(2)}, u32[]{:S(2)}) collective-permute-start(bf16[32,1152]{1,0:T(8,128)(2,1)S(1)} %get-tuple-element.59), channel_id=1, source_target_pairs={{0,2},{1,3},{2,0},{3,1},{4,6},{5,7},{6,4},{7,5},{8,10},{9,11},{10,... | collective-permute-start | bytes 221192 | tf_op jit(solution)/shard_map/ppermute | solution.py:29
  98.6 6.4 %collective-permute-start.27 = (bf16[32,1152]{1,0:T(8,128)(2,1)S(1)}, bf16[32,1152]{1,0:T(8,128)(2,1)S(1)}, u32[]{:S(2)}, u32[]{:S(2)}) collective-permute-start(bf16[32,1152]{1,0:T(8,128)(2,1)S(1)} %get-tuple-element.58), channel_id=1, source_target_pairs={{0,3},{1,2},{2,1},{3,0},{4,7},{5,6},{6,5},{7,4},{8,11},{9,10},{10,... | collective-permute-start | bytes 221192 | tf_op jit(solution)/shard_map/ppermute | solution.py:29

commit v7 on v6

--- a/solution.py
+++ b/solution.py
@@ -378,7 +378,7 @@
     inner_half, outer_half = weight_halves(inner_weight, outer_weight)
     inner_x, outer_x = swap(inner_weight, "src", 2), swap(outer_half, "src", 2)
     inner_far, outer_far = far_piece(inner_half), far_piece(outer_half)
-    neighbour = swap(tokens, "tgt", 1)
+    neighbour = swap(barrier((tokens, inner_half))[0], "tgt", 1)
     inner_far_x = swap(inner_far, "src", 2)
 
     outer_y = swap(outer_x, "groups", 1)
@@ -428,14 +428,12 @@
         (sentence_ids, order_key.reshape(1, -1), *summands),
         20 * tokens.shape[0] * features,
     )
-    held = held.reshape(src_count, 1, per_block, features)
-    for bit in reversed(bits_of("src", 1)):
-        held = jnp.concatenate([held[:bit], swap(held[bit:], "src", bit)], axis=1)
-    mine = held.reshape(SENT_DEV, features)
+    held = held.reshape(src_count, per_block, features)
+    mine = jnp.concatenate(
+        [held[0]] + [swap(held[offset], "src", offset) for offset in range(1, src_count)]
+    )
     parts = [mine] + [swap(mine, "tgt", offset) for offset in range(1, tgt_count)]
-    origin = jnp.arange(1, dtype=jnp.int32)
-    for bit in reversed(bits_of("src", 1)):
-        origin = jnp.concatenate([origin, origin ^ bit])
+    origin = jnp.arange(src_count, dtype=jnp.int32)
     from_src = (origin ^ src_index)[None, :, None]
     from_tgt = (jnp.arange(tgt_count, dtype=jnp.int32) ^ tgt_index)[:, None, None]
     place = (from_src * tgt_count + from_tgt) * per_block + jnp.arange(per_block, dtype=jnp.int32)

time: 106 us -> 105 us (level)
  waiting for transfers between devices: 49.2 us -> 45.8 us
  starting transfers between devices: 28.3 us -> 30.4 us
    ppermute x28 -> x29, waiting for transfers between devices: 49.2 us -> 45.8 us  [swap(): lax.ppermute(values, axis, [(i, i ^ offset) for i in range(lax.axis_size(...]
    ppermute x28 -> x29, starting transfers between devices: 28.3 us -> 30.4 us  [swap(): lax.ppermute(values, axis, [(i, i ^ offset) for i in range(lax.axis_size(...]
    unnamed x36 -> x34, local copies, waits for them, and re-layouts: 9.77 us -> 9.74 us
  transfers between devices with their start and end apart: 28 -> 29, of which waited for: 17 -> 16; matrix products, arithmetic and copies ran while one was open for 0% -> 0% of each run, Pallas kernels for 8% -> 8%
where the time goes in v7:
time: 105 us; the launch traced here: 104 us
  waiting for transfers between devices  45.8 us (44%)
  starting transfers between devices  30.4 us (29%)
  Pallas kernels  17.3 us (16%)
  local copies, waits for them, and re-layouts  9.86 us (9%)
    ppermute x29, waiting for transfers between devices, swap(): lax.ppermute(values, axis, [(i, i ^ offset) for i in range(lax.axis_size(...  45.8 us
    ppermute x29, starting transfers between devices, swap(): lax.ppermute(values, axis, [(i, i ^ offset) for i in range(lax.axis_size(...  30.4 us
    pallas_call x12, Pallas kernels, local_call(): pl.pallas_call(kernel, out_shape=out_shape, in_specs=[pl.BlockSpec(memory...  17.3 us
    unnamed x34, local copies, waits for them, and re-layouts  9.74 us
  transfers between devices with their start and end apart: 29, of which 16 were waited for; matrix products, arithmetic and copies ran while one was open for 0% of the time, Pallas kernels for 8%

profile of v7, /device:TPU:0, one launch (start us, length us, event | category | flops | bytes accessed | tf_op | source)
XLA Modules:
  0.0 104.4 jit_solution(1312668510669863718)
XLA Ops:
  0.7 1.9 %shard_map.87 = (bf16[128,1024]{1,0:T(8,128)(2,1)}, bf16[128,1024]{1,0:T(8,128)(2,1)}) custom-call(bf16[256,1024]{1,0:T(8,128)(2,1)} %refs_4_.1, bf16[256,1024]{1,0:T(8,128)(2,1)} %refs_2_.1), custom_call_target="tpu_custom_call" | custom-call | bytes 1572864 | tf_op jit(solution)/shard_map/pallas_call | solution.py:37
  2.6 3.0 %collective-permute-start.6 = (bf16[128,1024]{1,0:T(8,128)(2,1)}, bf16[128,1024]{1,0:T(8,128)(2,1)S(1)}, u32[]{:S(2)}, u32[]{:S(2)}) collective-permute-start(bf16[128,1024]{1,0:T(8,128)(2,1)} %get-tuple-element.33), channel_id=1, source_target_pairs={{0,8},{4,12},{8,0},{12,4},{1,9},{5,13},{9,1},{13,5},{2,10},{6,14},... | collective-permute-start | bytes 786440 | tf_op jit(solution)/shard_map/ppermute | solution.py:29
  5.6 2.6 %collective-permute-start.3 = (bf16[128,1024]{1,0:T(8,128)(2,1)}, bf16[128,1024]{1,0:T(8,128)(2,1)S(1)}, u32[]{:S(2)}, u32[]{:S(2)}) collective-permute-start(bf16[128,1024]{1,0:T(8,128)(2,1)} %get-tuple-element.31), channel_id=1, source_target_pairs={{0,2},{1,3},{2,0},{3,1},{4,6},{5,7},{6,4},{7,5},{8,10},{9,11},{10,... | collective-permute-start | bytes 786440 | tf_op jit(solution)/shard_map/ppermute | solution.py:29
  8.7 1.6 %collective-permute-start = (bf16[256,1024]{1,0:T(8,128)(2,1)}, bf16[256,1024]{1,0:T(8,128)(2,1)S(1)}, u32[]{:S(2)}, u32[]{:S(2)}) collective-permute-start(bf16[256,1024]{1,0:T(8,128)(2,1)} %refs_0_.11), channel_id=1, source_target_pairs={{0,1},{1,0},{2,3},{3,2},{4,5},{5,4},{6,7},{7,6},{8,9},{9,8},{10,11... | collective-permute-start | bytes 1572872 | tf_op jit(solution)/shard_map/ppermute | solution.py:29
  10.6 2.3 %collective-permute-done.6.refs_1_.refs_3_ = bf16[128,1024]{1,0:T(8,128)(2,1)S(1)} collective-permute-done((bf16[128,1024]{1,0:T(8,128)(2,1)}, bf16[128,1024]{1,0:T(8,128)(2,1)S(1)}, u32[]{:S(2)}, u32[]{:S(2)}) %collective-permute-start.6) | collective-permute-done | bytes 262176 | tf_op jit(solution)/shard_map/ppermute | solution.py:29
  12.9 2.1 %collective-permute-start.7 = (bf16[128,1024]{1,0:T(8,128)(2,1)S(1)}, bf16[128,1024]{1,0:T(8,128)(2,1)S(1)}, u32[]{:S(2)}, u32[]{:S(2)}) collective-permute-start(bf16[128,1024]{1,0:T(8,128)(2,1)S(1)} %collective-permute-done.6.refs_1_.refs_3_), channel_id=1, source_target_pairs={{0,16},{16,0},{1,17},{17,1},{2,18},{18,2},{3,19},{19,3},{4,20},{20... | collective-permute-start | bytes 786440 | tf_op jit(solution)/shard_map/ppermute | solution.py:29
  15.0 6.3 %collective-permute-done.3.refs_6_ = bf16[128,1024]{1,0:T(8,128)(2,1)S(1)} collective-permute-done((bf16[128,1024]{1,0:T(8,128)(2,1)}, bf16[128,1024]{1,0:T(8,128)(2,1)S(1)}, u32[]{:S(2)}, u32[]{:S(2)}) %collective-permute-start.3) | collective-permute-done | bytes 262176 | tf_op jit(solution)/shard_map/ppermute | solution.py:29
  21.8 8.9 %collective-permute-done.4.refs_3_.refs_5_ = bf16[128,1024]{1,0:T(8,128)(2,1)S(1)} collective-permute-done((bf16[128,1024]{1,0:T(8,128)(2,1)}, bf16[128,1024]{1,0:T(8,128)(2,1)S(1)}, u32[]{:S(2)}, u32[]{:S(2)}) %collective-permute-start.4) | collective-permute-done | bytes 262176 | tf_op jit(solution)/shard_map/ppermute | solution.py:29
  30.7 1.6 %collective-permute-start.9 = (bf16[128,1024]{1,0:T(8,128)(2,1)S(1)}, bf16[128,1024]{1,0:T(8,128)(2,1)S(1)}, u32[]{:S(2)}, u32[]{:S(2)}) collective-permute-start(bf16[128,1024]{1,0:T(8,128)(2,1)S(1)} %collective-permute-done.3.refs_6_), channel_id=1, source_target_pairs={{0,16},{16,0},{1,17},{17,1},{2,18},{18,2},{3,19},{19,3},{4,20},{20... | collective-permute-start | bytes 786440 | tf_op jit(solution)/shard_map/ppermute | solution.py:29
  33.3 1.6 %collective-permute-start.11 = (bf16[128,1024]{1,0:T(8,128)(2,1)S(1)}, bf16[128,1024]{1,0:T(8,128)(2,1)S(1)}, u32[]{:S(2)}, u32[]{:S(2)}) collective-permute-start(bf16[128,1024]{1,0:T(8,128)(2,1)S(1)} %collective-permute-done.4.refs_3_.refs_5_), channel_id=1, source_target_pairs={{0,16},{16,0},{1,17},{17,1},{2,18},{18,2},{3,19},{19,3},{4,20},{20... | collective-permute-start | bytes 786440 | tf_op jit(solution)/shard_map/ppermute | solution.py:29
  34.9 4.1 %collective-permute-done.9.refs_4_ = bf16[128,1024]{1,0:T(8,128)(2,1)S(1)} collective-permute-done((bf16[128,1024]{1,0:T(8,128)(2,1)S(1)}, bf16[128,1024]{1,0:T(8,128)(2,1)S(1)}, u32[]{:S(2)}, u32[]{:S(2)}) %collective-permute-start.9) | collective-permute-done | bytes 262176 | tf_op jit(solution)/shard_map/ppermute | solution.py:29
  39.1 2.9 %collective-permute-done.12.refs_4_.refs_6_ = bf16[128,1024]{1,0:T(8,128)(2,1)S(1)} collective-permute-done((bf16[128,1024]{1,0:T(8,128)(2,1)S(1)}, bf16[128,1024]{1,0:T(8,128)(2,1)S(1)}, u32[]{:S(2)}, u32[]{:S(2)}) %collective-permute-start.12) | collective-permute-done | bytes 262176 | tf_op jit(solution)/shard_map/ppermute | solution.py:29
  42.5 1.1 %collective-permute-done.11.refs_5_.refs_7_ = bf16[128,1024]{1,0:T(8,128)(2,1)S(1)} collective-permute-done((bf16[128,1024]{1,0:T(8,128)(2,1)S(1)}, bf16[128,1024]{1,0:T(8,128)(2,1)S(1)}, u32[]{:S(2)}, u32[]{:S(2)}) %collective-permute-start.11) | collective-permute-done | bytes 262176 | tf_op jit(solution)/shard_map/ppermute | solution.py:29
  43.6 3.0 %collective-permute-done.10.refs_5_ = bf16[128,1024]{1,0:T(8,128)(2,1)S(1)} collective-permute-done((bf16[128,1024]{1,0:T(8,128)(2,1)S(1)}, bf16[128,1024]{1,0:T(8,128)(2,1)S(1)}, u32[]{:S(2)}, u32[]{:S(2)}) %collective-permute-start.10) | collective-permute-done | bytes 262176 | tf_op jit(solution)/shard_map/ppermute | solution.py:29
  46.6 1.0 copy-done.8
  47.7 0.9 shard_map.89.far
  48.6 2.2 %shard_map.88.near = bf16[1024,768]{1,0:T(8,128)(2,1)S(1)} custom-call(bf16[256,1024]{1,0:T(8,128)(2,1)S(1)} %copy-done.9, bf16[256,1024]{1,0:T(8,128)(2,1)S(1)} %collective-permute-done.refs_1_, bf16[256,1024]{1,0:T(8,128)(2,1)S(1)} %collective-permute-done.1.refs_2_, bf16[256,1024]{1,0:T(8,128)(2,1)S(1)} %collective-permute-done.2.refs_3_, ...), custom_call_target="tpu_custom_call" | custom-call | flops 1610612736 | bytes 5242880 | tf_op jit(solution)/shard_map/pallas_call | solution.py:37
  50.9 1.0 shard_map.90
  51.9 1.8 %shard_map.91 = bf16[256,1024]{1,0:T(8,128)(2,1)} custom-call(bf16[1024,768]{1,0:T(8,128)(2,1)S(1)} %shard_map.88.near, bf16[1024,256]{1,0:T(8,128)(2,1)S(1)} %shard_map.89.far, bf16[256,1024]{1,0:T(8,128)(2,1)S(1)} %copy-done, bf16[128,1024]{1,0:T(8,128)(2,1)S(1)} %collective-permute-done.6.refs_1_.refs_3_, ...), custom_call_target="tpu_custom_call" | custom-call | flops 536870912 | bytes 4718592 | tf_op jit(solution)/shard_map/pallas_call | solution.py:37
  53.8 1.0 shard_map.92
  54.9 0.7 copy-done.14
  55.5 0.7 copy-done.15
  56.6 2.3 %collective-permute-start.16 = (bf16[128,1024]{1,0:T(8,128)(2,1)}, bf16[128,1024]{1,0:T(8,128)(2,1)S(1)}, u32[]{:S(2)}, u32[]{:S(2)}) collective-permute-start(bf16[128,1024]{1,0:T(8,128)(2,1)} %copy-done.15), channel_id=1, source_target_pairs={{0,1},{1,0},{2,3},{3,2},{4,5},{5,4},{6,7},{7,6},{8,9},{9,8},{10,11... | collective-permute-start | bytes 786440 | tf_op jit(solution)/shard_map/ppermute | solution.py:29
  59.0 0.9 copy-done.3
  59.9 0.9 copy-done.5
  60.9 0.9 copy-done.7
  61.8 1.0 copy-done.10
  62.9 2.0 %shard_map.93.own = f32[256,1024]{1,0:T(8,128)S(1)} custom-call(bf16[1024,768]{1,0:T(8,128)(2,1)S(1)} %shard_map.88.near, bf16[1024,256]{1,0:T(8,128)(2,1)S(1)} %shard_map.89.far, bf16[256,1024]{1,0:T(8,128)(2,1)S(1)} %copy-done.10, bf16[256,1024]{1,0:T(8,128)(2,1)} %collective-permute-done.15.refs_1_, bf16[256,1024]{1,0:T(8,128)(2,1)S(1)} %copy-done, ...), custom_call_target="tpu_custom_call" | custom-call | flops 536870912 | bytes 6291456 | tf_op jit(solution)/shard_map/pallas_call | solution.py:37
  64.9 1.3 %collective-permute-done.16.first = bf16[128,1024]{1,0:T(8,128)(2,1)S(1)} collective-permute-done((bf16[128,1024]{1,0:T(8,128)(2,1)}, bf16[128,1024]{1,0:T(8,128)(2,1)S(1)}, u32[]{:S(2)}, u32[]{:S(2)}) %collective-permute-start.16) | collective-permute-done | bytes 262176 | tf_op jit(solution)/shard_map/ppermute | solution.py:29
  66.2 5.1 %collective-permute-done.17.second = bf16[128,1024]{1,0:T(8,128)(2,1)S(1)} collective-permute-done((bf16[128,1024]{1,0:T(8,128)(2,1)}, bf16[128,1024]{1,0:T(8,128)(2,1)S(1)}, u32[]{:S(2)}, u32[]{:S(2)}) %collective-permute-start.17) | collective-permute-done | bytes 262176 | tf_op jit(solution)/shard_map/ppermute | solution.py:29
  71.3 1.2 %shard_map.94 = bf16[32,1024]{1,0:T(8,128)(2,1)S(1)} custom-call(s32[1,256]{1,0:T(1,128)S(1)} %copy-done.13, s32[1,32]{1,0:T(1,128)S(1)} %fusion.1.order, f32[256,1024]{1,0:T(8,128)S(1)} %shard_map.93.own, bf16[128,1024]{1,0:T(8,128)(2,1)S(1)} %collective-permute-done.16.first, bf16[128,1024]{1,0:T(8,128)(2,1)S(1)} %collective-permute-done.17.second), custom_call_target="tpu_custom_call" | custom-call | flops 5242880 | bytes 1639552 | tf_op jit(solution)/shard_map/pallas_call | solution.py:37
  73.2 1.3 %collective-permute-start.20 = (bf16[8,1024]{1,0:T(8,128)(2,1)S(1)}, bf16[8,1024]{1,0:T(8,128)(2,1)S(1)}, u32[]{:S(2)}, u32[]{:S(2)}) collective-permute-start(bf16[8,1024]{1,0:T(8,128)(2,1)S(1)} %get-tuple-element.64), channel_id=1, source_target_pairs={{0,12},{4,8},{8,4},{12,0},{1,13},{5,9},{9,5},{13,1},{2,14},{6,10},... | collective-permute-start | bytes 49160 | tf_op jit(solution)/shard_map/ppermute | solution.py:29
  74.5 2.0 %collective-permute-done.19 = bf16[8,1024]{1,0:T(8,128)(2,1)S(1)} collective-permute-done((bf16[8,1024]{1,0:T(8,128)(2,1)S(1)}, bf16[8,1024]{1,0:T(8,128)(2,1)S(1)}, u32[]{:S(2)}, u32[]{:S(2)}) %collective-permute-start.19) | collective-permute-done | bytes 16416 | tf_op jit(solution)/shard_map/ppermute | solution.py:29
  76.5 1.8 %collective-permute-start.21 = (bf16[32,1024]{1,0:T(8,128)(2,1)S(1)}, bf16[32,1024]{1,0:T(8,128)(2,1)S(1)}, u32[]{:S(2)}, u32[]{:S(2)}) collective-permute-start(bf16[32,1024]{1,0:T(8,128)(2,1)S(1)} %pad_maximum_fusion.refs_0_), channel_id=1, source_target_pairs={{0,1},{1,0},{2,3},{3,2},{4,5},{5,4},{6,7},{7,6},{8,9},{9,8},{10,11... | collective-permute-start | bytes 196616 | tf_op jit(solution)/shard_map/ppermute | solution.py:29
  78.4 1.3 %collective-permute-start.22 = (bf16[32,1024]{1,0:T(8,128)(2,1)S(1)}, bf16[32,1024]{1,0:T(8,128)(2,1)S(1)}, u32[]{:S(2)}, u32[]{:S(2)}) collective-permute-start(bf16[32,1024]{1,0:T(8,128)(2,1)S(1)} %pad_maximum_fusion.refs_0_), channel_id=1, source_target_pairs={{0,2},{1,3},{2,0},{3,1},{4,6},{5,7},{6,4},{7,5},{8,10},{9,11},{10,... | collective-permute-start | bytes 196616 | tf_op jit(solution)/shard_map/ppermute | solution.py:29
  79.7 1.3 %collective-permute-start.23 = (bf16[32,1024]{1,0:T(8,128)(2,1)S(1)}, bf16[32,1024]{1,0:T(8,128)(2,1)S(1)}, u32[]{:S(2)}, u32[]{:S(2)}) collective-permute-start(bf16[32,1024]{1,0:T(8,128)(2,1)S(1)} %pad_maximum_fusion.refs_0_), channel_id=1, source_target_pairs={{0,3},{1,2},{2,1},{3,0},{4,7},{5,6},{6,5},{7,4},{8,11},{9,10},{10,... | collective-permute-start | bytes 196616 | tf_op jit(solution)/shard_map/ppermute | solution.py:29
  81.2 3.4 %copy-done.1 = bf16[4096,1024]{1,0:T(8,128)(2,1)S(1)} copy-done((bf16[4096,1024]{1,0:T(8,128)(2,1)S(1)}, bf16[4096,1024]{1,0:T(8,128)(2,1)}, u32[]{:S(2)}) %copy-start.1) | copy-done | bytes 8388632
  84.6 1.7 %shard_map.86.units = bf16[1024,1024]{1,0:T(8,128)(2,1)S(1)} custom-call(s32[1,16]{1,0:T(1,128)S(1)} %copy-done.12, bf16[4096,1024]{1,0:T(8,128)(2,1)S(1)} %copy-done.1), custom_call_target="tpu_custom_call" | custom-call | flops 8388608 | bytes 10485824 | tf_op jit(solution)/shard_map/pallas_call | solution.py:37
  86.5 1.8 %shard_map.95 = (f32[128,1024]{1,0:T(8,128)S(1)}, f32[16,256]{1,0:T(8,128)S(1)}, f32[128,1]{1,0:T(8,128)S(1)}) custom-call(s32[1,16]{1,0:T(1,128)S(1)} %copy-done.12, s32[1,128]{1,0:T(1,128)S(1)} %xor.40.place, bf16[1024,1024]{1,0:T(8,128)(2,1)S(1)} %shard_map.86.units, bf16[32,1024]{1,0:T(8,128)(2,1)S(1)} %pad_maximum_fusion.refs_0_, ...), custom_call_target="tpu_custom_call" | custom-call | flops 268435456 | bytes 2901056 | tf_op jit(solution)/shard_map/pallas_call | solution.py:37
  88.4 1.2 %collective-permute-done.24 = f32[16,256]{1,0:T(8,128)S(1)} collective-permute-done((f32[16,256]{1,0:T(8,128)S(1)}, f32[16,256]{1,0:T(8,128)S(1)}, u32[]{:S(2)}, u32[]{:S(2)}) %collective-permute-start.24) | collective-permute-done | bytes 16416 | tf_op jit(solution)/shard_map/ppermute | solution.py:29
  89.5 1.3 %collective-permute-start.25 = (f32[16,256]{1,0:T(8,128)S(1)}, f32[16,256]{1,0:T(8,128)S(1)}, u32[]{:S(2)}, u32[]{:S(2)}) collective-permute-start(f32[16,256]{1,0:T(8,128)S(1)} %add.64), channel_id=1, source_target_pairs={{0,8},{4,12},{8,0},{12,4},{1,9},{5,13},{9,1},{13,5},{2,10},{6,14},... | collective-permute-start | bytes 49160 | tf_op jit(solution)/shard_map/ppermute | solution.py:29
  90.9 2.4 %collective-permute-done.25 = f32[16,256]{1,0:T(8,128)S(1)} collective-permute-done((f32[16,256]{1,0:T(8,128)S(1)}, f32[16,256]{1,0:T(8,128)S(1)}, u32[]{:S(2)}, u32[]{:S(2)}) %collective-permute-start.25) | collective-permute-done | bytes 16416 | tf_op jit(solution)/shard_map/ppermute | solution.py:29
  93.3 1.1 %shard_map.96 = (f32[32,1152]{1,0:T(8,128)S(1)}, bf16[96,1152]{1,0:T(8,128)(2,1)S(1)}) custom-call(s32[1,16]{1,0:T(1,128)S(1)} %copy-done.12, f32[128,1024]{1,0:T(8,128)S(1)} %get-tuple-element.53.expo, f32[16,256]{1,0:T(8,128)S(1)} %add.65.columns, f32[128,1]{1,0:T(8,128)S(1)} %get-tuple-element.55.row_total, bf16[1024,1024]{1,0:T(8,128)(2,1)S(1)} %shard_map.86.units), custom_call_target="tpu_custom_call" | custom-call | flops 268435456 | bytes 3007040 | tf_op jit(solution)/shard_map/pallas_call | solution.py:37
  94.4 1.4 %collective-permute-start.26 = (bf16[32,1152]{1,0:T(8,128)(2,1)S(1)}, bf16[32,1152]{1,0:T(8,128)(2,1)S(1)}, u32[]{:S(2)}, u32[]{:S(2)}) collective-permute-start(bf16[32,1152]{1,0:T(8,128)(2,1)S(1)} %get-tuple-element.62), channel_id=1, source_target_pairs={{0,1},{1,0},{2,3},{3,2},{4,5},{5,4},{6,7},{7,6},{8,9},{9,8},{10,11... | collective-permute-start | bytes 221192 | tf_op jit(solution)/shard_map/ppermute | solution.py:29
  95.8 1.5 %collective-permute-start.27 = (bf16[32,1152]{1,0:T(8,128)(2,1)S(1)}, bf16[32,1152]{1,0:T(8,128)(2,1)S(1)}, u32[]{:S(2)}, u32[]{:S(2)}) collective-permute-start(bf16[32,1152]{1,0:T(8,128)(2,1)S(1)} %get-tuple-element.61), channel_id=1, source_target_pairs={{0,2},{1,3},{2,0},{3,1},{4,6},{5,7},{6,4},{7,5},{8,10},{9,11},{10,... | collective-permute-start | bytes 221192 | tf_op jit(solution)/shard_map/ppermute | solution.py:29
  97.3 1.6 %collective-permute-start.28 = (bf16[32,1152]{1,0:T(8,128)(2,1)S(1)}, bf16[32,1152]{1,0:T(8,128)(2,1)S(1)}, u32[]{:S(2)}, u32[]{:S(2)}) collective-permute-start(bf16[32,1152]{1,0:T(8,128)(2,1)S(1)} %get-tuple-element.60), channel_id=1, source_target_pairs={{0,3},{1,2},{2,1},{3,0},{4,7},{5,6},{6,5},{7,4},{8,11},{9,10},{10,... | collective-permute-start | bytes 221192 | tf_op jit(solution)/shard_map/ppermute | solution.py:29
  99.4 4.2 %collective-permute-done.27.refs_1_ = bf16[32,1152]{1,0:T(8,128)(2,1)S(1)} collective-permute-done((bf16[32,1152]{1,0:T(8,128)(2,1)S(1)}, bf16[32,1152]{1,0:T(8,128)(2,1)S(1)}, u32[]{:S(2)}, u32[]{:S(2)}) %collective-permute-start.27) | collective-permute-done | bytes 73760 | tf_op jit(solution)/shard_map/ppermute | solution.py:29
  103.6 0.8 shard_map.97
  (66 shorter events, 5.5 us)
Async XLA Ops:
  0.6 47.9 %copy-start.11 = (bf16[256,1024]{1,0:T(8,128)(2,1)S(1)}, bf16[256,1024]{1,0:T(8,128)(2,1)}, u32[]{:S(2)}) copy-start(bf16[256,1024]{1,0:T(8,128)(2,1)} %refs_4_.1) | copy-start | bytes 1572868
  0.6 47.9 %copy-start.9 = (bf16[256,1024]{1,0:T(8,128)(2,1)S(1)}, bf16[256,1024]{1,0:T(8,128)(2,1)}, u32[]{:S(2)}) copy-start(bf16[256,1024]{1,0:T(8,128)(2,1)} %refs_0_.11) | copy-start | bytes 1572868
  2.6 10.3 %collective-permute-start.6 = (bf16[128,1024]{1,0:T(8,128)(2,1)}, bf16[128,1024]{1,0:T(8,128)(2,1)S(1)}, u32[]{:S(2)}, u32[]{:S(2)}) collective-permute-start(bf16[128,1024]{1,0:T(8,128)(2,1)} %get-tuple-element.33), channel_id=1, source_target_pairs={{0,8},{4,12},{8,0},{12,4},{1,9},{5,13},{9,1},{13,5},{2,10},{6,14},... | collective-permute-start | bytes 786440 | tf_op jit(solution)/shard_map/ppermute | solution.py:29
  5.6 15.8 %collective-permute-start.3 = (bf16[128,1024]{1,0:T(8,128)(2,1)}, bf16[128,1024]{1,0:T(8,128)(2,1)S(1)}, u32[]{:S(2)}, u32[]{:S(2)}) collective-permute-start(bf16[128,1024]{1,0:T(8,128)(2,1)} %get-tuple-element.31), channel_id=1, source_target_pairs={{0,2},{1,3},{2,0},{3,1},{4,6},{5,7},{6,4},{7,5},{8,10},{9,11},{10,... | collective-permute-start | bytes 786440 | tf_op jit(solution)/shard_map/ppermute | solution.py:29
  8.2 22.5 %collective-permute-start.8 = (bf16[256,1024]{1,0:T(8,128)(2,1)}, bf16[256,1024]{1,0:T(8,128)(2,1)S(1)}, u32[]{:S(2)}, u32[]{:S(2)}) collective-permute-start(bf16[256,1024]{1,0:T(8,128)(2,1)} %refs_4_.1), channel_id=1, source_target_pairs={{0,8},{4,12},{8,0},{12,4},{1,9},{5,13},{9,1},{13,5},{2,10},{6,14},... | collective-permute-start | bytes 1572872 | tf_op jit(solution)/shard_map/ppermute | solution.py:29
  8.7 23.6 %collective-permute-start = (bf16[256,1024]{1,0:T(8,128)(2,1)}, bf16[256,1024]{1,0:T(8,128)(2,1)S(1)}, u32[]{:S(2)}, u32[]{:S(2)}) collective-permute-start(bf16[256,1024]{1,0:T(8,128)(2,1)} %refs_0_.11), channel_id=1, source_target_pairs={{0,1},{1,0},{2,3},{3,2},{4,5},{5,4},{6,7},{7,6},{8,9},{9,8},{10,11... | collective-permute-start | bytes 1572872 | tf_op jit(solution)/shard_map/ppermute | solution.py:29
  10.3 20.4 %collective-permute-start.4 = (bf16[128,1024]{1,0:T(8,128)(2,1)}, bf16[128,1024]{1,0:T(8,128)(2,1)S(1)}, u32[]{:S(2)}, u32[]{:S(2)}) collective-permute-start(bf16[128,1024]{1,0:T(8,128)(2,1)} %get-tuple-element.33), channel_id=1, source_target_pairs={{0,2},{1,3},{2,0},{3,1},{4,6},{5,7},{6,4},{7,5},{8,10},{9,11},{10,... | collective-permute-start | bytes 786440 | tf_op jit(solution)/shard_map/ppermute | solution.py:29
  12.9 17.7 %collective-permute-start.7 = (bf16[128,1024]{1,0:T(8,128)(2,1)S(1)}, bf16[128,1024]{1,0:T(8,128)(2,1)S(1)}, u32[]{:S(2)}, u32[]{:S(2)}) collective-permute-start(bf16[128,1024]{1,0:T(8,128)(2,1)S(1)} %collective-permute-done.6.refs_1_.refs_3_), channel_id=1, source_target_pairs={{0,16},{16,0},{1,17},{17,1},{2,18},{18,2},{3,19},{19,3},{4,20},{20... | collective-permute-start | bytes 786440 | tf_op jit(solution)/shard_map/ppermute | solution.py:29
  21.4 9.3 %collective-permute-start.5 = (bf16[128,1024]{1,0:T(8,128)(2,1)S(1)}, bf16[128,1024]{1,0:T(8,128)(2,1)S(1)}, u32[]{:S(2)}, u32[]{:S(2)}) collective-permute-start(bf16[128,1024]{1,0:T(8,128)(2,1)S(1)} %collective-permute-done.3.refs_6_), channel_id=1, source_target_pairs={{0,8},{4,12},{8,0},{12,4},{1,9},{5,13},{9,1},{13,5},{2,10},{6,14},... | collective-permute-start | bytes 786440 | tf_op jit(solution)/shard_map/ppermute | solution.py:29
  30.7 8.3 %collective-permute-start.9 = (bf16[128,1024]{1,0:T(8,128)(2,1)S(1)}, bf16[128,1024]{1,0:T(8,128)(2,1)S(1)}, u32[]{:S(2)}, u32[]{:S(2)}) collective-permute-start(bf16[128,1024]{1,0:T(8,128)(2,1)S(1)} %collective-permute-done.3.refs_6_), channel_id=1, source_target_pairs={{0,16},{16,0},{1,17},{17,1},{2,18},{18,2},{3,19},{19,3},{4,20},{20... | collective-permute-start | bytes 786440 | tf_op jit(solution)/shard_map/ppermute | solution.py:29
  32.3 14.3 %collective-permute-start.1 = (bf16[256,1024]{1,0:T(8,128)(2,1)}, bf16[256,1024]{1,0:T(8,128)(2,1)S(1)}, u32[]{:S(2)}, u32[]{:S(2)}) collective-permute-start(bf16[256,1024]{1,0:T(8,128)(2,1)} %refs_0_.11), channel_id=1, source_target_pairs={{0,4},{4,0},{8,12},{12,8},{1,5},{5,1},{9,13},{13,9},{2,6},{6,2},{1... | collective-permute-start | bytes 1572872 | tf_op jit(solution)/shard_map/ppermute | solution.py:29
  32.3 14.3 %collective-permute-start.2 = (bf16[256,1024]{1,0:T(8,128)(2,1)S(1)}, bf16[256,1024]{1,0:T(8,128)(2,1)S(1)}, u32[]{:S(2)}, u32[]{:S(2)}) collective-permute-start(bf16[256,1024]{1,0:T(8,128)(2,1)S(1)} %collective-permute-done.refs_1_), channel_id=1, source_target_pairs={{0,4},{4,0},{8,12},{12,8},{1,5},{5,1},{9,13},{13,9},{2,6},{6,2},{1... | collective-permute-start | bytes 1572872 | tf_op jit(solution)/shard_map/ppermute | solution.py:29
  32.8 9.2 %collective-permute-start.12 = (bf16[128,1024]{1,0:T(8,128)(2,1)S(1)}, bf16[128,1024]{1,0:T(8,128)(2,1)S(1)}, u32[]{:S(2)}, u32[]{:S(2)}) collective-permute-start(bf16[128,1024]{1,0:T(8,128)(2,1)S(1)} %collective-permute-done.4.refs_3_.refs_5_), channel_id=1, source_target_pairs={{0,8},{4,12},{8,0},{12,4},{1,9},{5,13},{9,1},{13,5},{2,10},{6,14},... | collective-permute-start | bytes 786440 | tf_op jit(solution)/shard_map/ppermute | solution.py:29
  33.3 10.3 %collective-permute-start.11 = (bf16[128,1024]{1,0:T(8,128)(2,1)S(1)}, bf16[128,1024]{1,0:T(8,128)(2,1)S(1)}, u32[]{:S(2)}, u32[]{:S(2)}) collective-permute-start(bf16[128,1024]{1,0:T(8,128)(2,1)S(1)} %collective-permute-done.4.refs_3_.refs_5_), channel_id=1, source_target_pairs={{0,16},{16,0},{1,17},{17,1},{2,18},{18,2},{3,19},{19,3},{4,20},{20... | collective-permute-start | bytes 786440 | tf_op jit(solution)/shard_map/ppermute | solution.py:29
  39.0 7.6 %collective-permute-start.10 = (bf16[128,1024]{1,0:T(8,128)(2,1)S(1)}, bf16[128,1024]{1,0:T(8,128)(2,1)S(1)}, u32[]{:S(2)}, u32[]{:S(2)}) collective-permute-start(bf16[128,1024]{1,0:T(8,128)(2,1)S(1)} %collective-permute-done.9.refs_4_), channel_id=1, source_target_pairs={{0,8},{4,12},{8,0},{12,4},{1,9},{5,13},{9,1},{13,5},{2,10},{6,14},... | collective-permute-start | bytes 786440 | tf_op jit(solution)/shard_map/ppermute | solution.py:29
  42.0 11.9 %copy-start.2 = (bf16[128,1024]{1,0:T(8,128)(2,1)}, bf16[128,1024]{1,0:T(8,128)(2,1)S(1)}, u32[]{:S(2)}) copy-start(bf16[128,1024]{1,0:T(8,128)(2,1)S(1)} %collective-permute-done.12.refs_4_.refs_6_) | copy-start | bytes 786436
  42.0 8.9 %collective-permute-start.13 = (bf16[128,1024]{1,0:T(8,128)(2,1)S(1)}, bf16[128,1024]{1,0:T(8,128)(2,1)S(1)}, u32[]{:S(2)}, u32[]{:S(2)}) collective-permute-start(bf16[128,1024]{1,0:T(8,128)(2,1)S(1)} %collective-permute-done.12.refs_4_.refs_6_), channel_id=1, source_target_pairs={{0,16},{16,0},{1,17},{17,1},{2,18},{18,2},{3,19},{19,3},{4,20},{20... | collective-permute-start | bytes 786440 | tf_op jit(solution)/shard_map/ppermute | solution.py:29
  43.6 10.2 %copy-start.4 = (bf16[128,1024]{1,0:T(8,128)(2,1)}, bf16[128,1024]{1,0:T(8,128)(2,1)S(1)}, u32[]{:S(2)}) copy-start(bf16[128,1024]{1,0:T(8,128)(2,1)S(1)} %collective-permute-done.11.refs_5_.refs_7_) | copy-start | bytes 786436
  46.6 1.0 %copy-start.8 = (bf16[256,1024]{1,0:T(8,128)(2,1)S(1)}, bf16[256,1024]{1,0:T(8,128)(2,1)}, u32[]{:S(2)}) copy-start(bf16[256,1024]{1,0:T(8,128)(2,1)} %refs_0_.11) | copy-start | bytes 1572868
  48.6 2.3 %copy-start = (bf16[256,1024]{1,0:T(8,128)(2,1)S(1)}, bf16[256,1024]{1,0:T(8,128)(2,1)}, u32[]{:S(2)}) copy-start(bf16[256,1024]{1,0:T(8,128)(2,1)} %refs_2_.1) | copy-start | bytes 1572868
  50.9 3.0 %copy-start.6 = (bf16[128,1024]{1,0:T(8,128)(2,1)}, bf16[128,1024]{1,0:T(8,128)(2,1)S(1)}, u32[]{:S(2)}) copy-start(bf16[128,1024]{1,0:T(8,128)(2,1)S(1)} %collective-permute-done.13.refs_6_.refs_8_) | copy-start | bytes 786436
  51.8 2.0 %collective-permute-start.14 = (bf16[256,1024]{1,0:T(8,128)(2,1)S(1)}, bf16[256,1024]{1,0:T(8,128)(2,1)S(1)}, u32[]{:S(2)}, u32[]{:S(2)}) collective-permute-start(bf16[256,1024]{1,0:T(8,128)(2,1)S(1)} %shard_map.90), channel_id=1, source_target_pairs={{0,4},{4,0},{8,12},{12,8},{1,5},{5,1},{9,13},{13,9},{2,6},{6,2},{1... | collective-permute-start | bytes 1572872 | tf_op jit(solution)/shard_map/ppermute | solution.py:29
  53.7 5.2 %copy-start.16 = (s32[32]{0:T(128)S(1)}, s32[32]{0:T(128)}, u32[]{:S(2)}) copy-start(s32[32]{0:T(128)} %param.11) | copy-start | bytes 388
  54.8 0.7 copy-start.14
  55.5 0.7 copy-start.15
  56.2 2.7 %collective-permute-start.15 = (bf16[256,1024]{1,0:T(8,128)(2,1)}, bf16[256,1024]{1,0:T(8,128)(2,1)}, u32[]{:S(2)}, u32[]{:S(2)}) collective-permute-start(bf16[256,1024]{1,0:T(8,128)(2,1)} %shard_map.91), channel_id=1, source_target_pairs={{0,4},{4,0},{8,12},{12,8},{1,5},{5,1},{9,13},{13,9},{2,6},{6,2},{1... | collective-permute-start | bytes 1572872 | tf_op jit(solution)/shard_map/ppermute | solution.py:29
  56.6 9.6 %collective-permute-start.16 = (bf16[128,1024]{1,0:T(8,128)(2,1)}, bf16[128,1024]{1,0:T(8,128)(2,1)S(1)}, u32[]{:S(2)}, u32[]{:S(2)}) collective-permute-start(bf16[128,1024]{1,0:T(8,128)(2,1)} %copy-done.15), channel_id=1, source_target_pairs={{0,1},{1,0},{2,3},{3,2},{4,5},{5,4},{6,7},{7,6},{8,9},{9,8},{10,11... | collective-permute-start | bytes 786440 | tf_op jit(solution)/shard_map/ppermute | solution.py:29
  58.9 12.4 %collective-permute-start.17 = (bf16[128,1024]{1,0:T(8,128)(2,1)}, bf16[128,1024]{1,0:T(8,128)(2,1)S(1)}, u32[]{:S(2)}, u32[]{:S(2)}) collective-permute-start(bf16[128,1024]{1,0:T(8,128)(2,1)} %copy-done.14), channel_id=1, source_target_pairs={{0,1},{1,0},{2,3},{3,2},{4,5},{5,4},{6,7},{7,6},{8,9},{9,8},{10,11... | collective-permute-start | bytes 786440 | tf_op jit(solution)/shard_map/ppermute | solution.py:29
  59.0 1.0 copy-start.3
  59.9 0.9 copy-start.5
  60.9 0.9 copy-start.7
  61.8 1.0 copy-start.10
  62.8 8.5 %copy-start.13 = (s32[1,256]{1,0:T(1,128)S(1)}, s32[1,256]{1,0:T(1,128)}, u32[]{:S(2)}) copy-start(s32[1,256]{1,0:T(1,128)} %identity.1) | copy-start | bytes 3076
  62.9 18.3 %copy-start.12 = (s32[1,16]{1,0:T(1,128)S(1)}, s32[1,16]{1,0:T(1,128)}, u32[]{:S(2)}) copy-start(s32[1,16]{1,0:T(1,128)} %listed.5) | copy-start | bytes 196
  72.5 2.0 %collective-permute-start.18 = (bf16[8,1024]{1,0:T(8,128)(2,1)S(1)}, bf16[8,1024]{1,0:T(8,128)(2,1)S(1)}, u32[]{:S(2)}, u32[]{:S(2)}) collective-permute-start(bf16[8,1024]{1,0:T(8,128)(2,1)S(1)} %get-tuple-element.66), channel_id=1, source_target_pairs={{0,4},{4,0},{8,12},{12,8},{1,5},{5,1},{9,13},{13,9},{2,6},{6,2},{1... | collective-permute-start | bytes 49160 | tf_op jit(solution)/shard_map/ppermute | solution.py:29
  72.6 3.9 %collective-permute-start.19 = (bf16[8,1024]{1,0:T(8,128)(2,1)S(1)}, bf16[8,1024]{1,0:T(8,128)(2,1)S(1)}, u32[]{:S(2)}, u32[]{:S(2)}) collective-permute-start(bf16[8,1024]{1,0:T(8,128)(2,1)S(1)} %get-tuple-element.65), channel_id=1, source_target_pairs={{0,8},{4,12},{8,0},{12,4},{1,9},{5,13},{9,1},{13,5},{2,10},{6,14},... | collective-permute-start | bytes 49160 | tf_op jit(solution)/shard_map/ppermute | solution.py:29
  73.2 3.3 %collective-permute-start.20 = (bf16[8,1024]{1,0:T(8,128)(2,1)S(1)}, bf16[8,1024]{1,0:T(8,128)(2,1)S(1)}, u32[]{:S(2)}, u32[]{:S(2)}) collective-permute-start(bf16[8,1024]{1,0:T(8,128)(2,1)S(1)} %get-tuple-element.64), channel_id=1, source_target_pairs={{0,12},{4,8},{8,4},{12,0},{1,13},{5,9},{9,5},{13,1},{2,14},{6,10},... | collective-permute-start | bytes 49160 | tf_op jit(solution)/shard_map/ppermute | solution.py:29
  76.5 9.7 %collective-permute-start.21 = (bf16[32,1024]{1,0:T(8,128)(2,1)S(1)}, bf16[32,1024]{1,0:T(8,128)(2,1)S(1)}, u32[]{:S(2)}, u32[]{:S(2)}) collective-permute-start(bf16[32,1024]{1,0:T(8,128)(2,1)S(1)} %pad_maximum_fusion.refs_0_), channel_id=1, source_target_pairs={{0,1},{1,0},{2,3},{3,2},{4,5},{5,4},{6,7},{7,6},{8,9},{9,8},{10,11... | collective-permute-start | bytes 196616 | tf_op jit(solution)/shard_map/ppermute | solution.py:29
  78.4 8.2 %collective-permute-start.22 = (bf16[32,1024]{1,0:T(8,128)(2,1)S(1)}, bf16[32,1024]{1,0:T(8,128)(2,1)S(1)}, u32[]{:S(2)}, u32[]{:S(2)}) collective-permute-start(bf16[32,1024]{1,0:T(8,128)(2,1)S(1)} %pad_maximum_fusion.refs_0_), channel_id=1, source_target_pairs={{0,2},{1,3},{2,0},{3,1},{4,6},{5,7},{6,4},{7,5},{8,10},{9,11},{10,... | collective-permute-start | bytes 196616 | tf_op jit(solution)/shard_map/ppermute | solution.py:29
  79.7 6.8 %collective-permute-start.23 = (bf16[32,1024]{1,0:T(8,128)(2,1)S(1)}, bf16[32,1024]{1,0:T(8,128)(2,1)S(1)}, u32[]{:S(2)}, u32[]{:S(2)}) collective-permute-start(bf16[32,1024]{1,0:T(8,128)(2,1)S(1)} %pad_maximum_fusion.refs_0_), channel_id=1, source_target_pairs={{0,3},{1,2},{2,1},{3,0},{4,7},{5,6},{6,5},{7,4},{8,11},{9,10},{10,... | collective-permute-start | bytes 196616 | tf_op jit(solution)/shard_map/ppermute | solution.py:29
  81.2 3.4 %copy-start.1 = (bf16[4096,1024]{1,0:T(8,128)(2,1)S(1)}, bf16[4096,1024]{1,0:T(8,128)(2,1)}, u32[]{:S(2)}) copy-start(bf16[4096,1024]{1,0:T(8,128)(2,1)} %targets.1) | copy-start | bytes 25165828
  88.3 1.2 %collective-permute-start.24 = (f32[16,256]{1,0:T(8,128)S(1)}, f32[16,256]{1,0:T(8,128)S(1)}, u32[]{:S(2)}, u32[]{:S(2)}) collective-permute-start(f32[16,256]{1,0:T(8,128)S(1)} %get-tuple-element.54), channel_id=1, source_target_pairs={{0,4},{4,0},{8,12},{12,8},{1,5},{5,1},{9,13},{13,9},{2,6},{6,2},{1... | collective-permute-start | bytes 49160 | tf_op jit(solution)/shard_map/ppermute | solution.py:29
  89.5 3.7 %collective-permute-start.25 = (f32[16,256]{1,0:T(8,128)S(1)}, f32[16,256]{1,0:T(8,128)S(1)}, u32[]{:S(2)}, u32[]{:S(2)}) collective-permute-start(f32[16,256]{1,0:T(8,128)S(1)} %add.64), channel_id=1, source_target_pairs={{0,8},{4,12},{8,0},{12,4},{1,9},{5,13},{9,1},{13,5},{2,10},{6,14},... | collective-permute-start | bytes 49160 | tf_op jit(solution)/shard_map/ppermute | solution.py:29
  94.4 5.0 %collective-permute-start.26 = (bf16[32,1152]{1,0:T(8,128)(2,1)S(1)}, bf16[32,1152]{1,0:T(8,128)(2,1)S(1)}, u32[]{:S(2)}, u32[]{:S(2)}) collective-permute-start(bf16[32,1152]{1,0:T(8,128)(2,1)S(1)} %get-tuple-element.62), channel_id=1, source_target_pairs={{0,1},{1,0},{2,3},{3,2},{4,5},{5,4},{6,7},{7,6},{8,9},{9,8},{10,11... | collective-permute-start | bytes 221192 | tf_op jit(solution)/shard_map/ppermute | solution.py:29
  95.8 7.8 %collective-permute-start.27 = (bf16[32,1152]{1,0:T(8,128)(2,1)S(1)}, bf16[32,1152]{1,0:T(8,128)(2,1)S(1)}, u32[]{:S(2)}, u32[]{:S(2)}) collective-permute-start(bf16[32,1152]{1,0:T(8,128)(2,1)S(1)} %get-tuple-element.61), channel_id=1, source_target_pairs={{0,2},{1,3},{2,0},{3,1},{4,6},{5,7},{6,4},{7,5},{8,10},{9,11},{10,... | collective-permute-start | bytes 221192 | tf_op jit(solution)/shard_map/ppermute | solution.py:29
  97.3 6.3 %collective-permute-start.28 = (bf16[32,1152]{1,0:T(8,128)(2,1)S(1)}, bf16[32,1152]{1,0:T(8,128)(2,1)S(1)}, u32[]{:S(2)}, u32[]{:S(2)}) collective-permute-start(bf16[32,1152]{1,0:T(8,128)(2,1)S(1)} %get-tuple-element.60), channel_id=1, source_target_pairs={{0,3},{1,2},{2,1},{3,0},{4,7},{5,6},{6,5},{7,4},{8,11},{9,10},{10,... | collective-permute-start | bytes 221192 | tf_op jit(solution)/shard_map/ppermute | solution.py:29

commit v8 on v7

--- a/solution.py
+++ b/solution.py
@@ -432,7 +432,8 @@
     mine = jnp.concatenate(
         [held[0]] + [swap(held[offset], "src", offset) for offset in range(1, src_count)]
     )
-    parts = [mine] + [swap(mine, "tgt", offset) for offset in range(1, tgt_count)]
+    parts = [swap(mine, "tgt", offset) for offset in reversed(range(1, tgt_count))]
+    parts = [mine, *reversed(parts)]
     origin = jnp.arange(src_count, dtype=jnp.int32)
     from_src = (origin ^ src_index)[None, :, None]
     from_tgt = (jnp.arange(tgt_count, dtype=jnp.int32) ^ tgt_index)[:, None, None]
@@ -467,7 +468,7 @@
     )
     received = [
         swap(sent[(offset - 1) * SENT_DEV : offset * SENT_DEV], "tgt", offset)
-        for offset in range(1, tgt_count)
+        for offset in reversed(range(1, tgt_count))
     ]
     matched, log_mass = local_call(
         finish_kernel,

time: 105 us -> 105 us (level)
  no operation moved by 1% of the time
where the time goes in v8:
time: 105 us; the launch traced here: 104 us
  waiting for transfers between devices  45.7 us (44%)
  starting transfers between devices  30.4 us (29%)
  Pallas kernels  17.3 us (16%)
  local copies, waits for them, and re-layouts  9.86 us (9%)
    ppermute x29, waiting for transfers between devices, swap(): lax.ppermute(values, axis, [(i, i ^ offset) for i in range(lax.axis_size(...  45.7 us
    ppermute x29, starting transfers between devices, swap(): lax.ppermute(values, axis, [(i, i ^ offset) for i in range(lax.axis_size(...  30.4 us
    pallas_call x12, Pallas kernels, local_call(): pl.pallas_call(kernel, out_shape=out_shape, in_specs=[pl.BlockSpec(memory...  17.3 us
    unnamed x34, local copies, waits for them, and re-layouts  9.74 us
  transfers between devices with their start and end apart: 29, of which 16 were waited for; matrix products, arithmetic and copies ran while one was open for 0% of the time, Pallas kernels for 8%

profile of v8, /device:TPU:0, one launch (start us, length us, event | category | flops | bytes accessed | tf_op | source)
XLA Modules:
  0.0 104.3 jit_solution(7366806062985561791)
XLA Ops:
  0.7 1.9 %shard_map.87 = (bf16[128,1024]{1,0:T(8,128)(2,1)}, bf16[128,1024]{1,0:T(8,128)(2,1)}) custom-call(bf16[256,1024]{1,0:T(8,128)(2,1)} %refs_4_.1, bf16[256,1024]{1,0:T(8,128)(2,1)} %refs_2_.1), custom_call_target="tpu_custom_call" | custom-call | bytes 1572864 | tf_op jit(solution)/shard_map/pallas_call | solution.py:37
  2.6 3.0 %collective-permute-start.6 = (bf16[128,1024]{1,0:T(8,128)(2,1)}, bf16[128,1024]{1,0:T(8,128)(2,1)S(1)}, u32[]{:S(2)}, u32[]{:S(2)}) collective-permute-start(bf16[128,1024]{1,0:T(8,128)(2,1)} %get-tuple-element.33), channel_id=1, source_target_pairs={{0,8},{4,12},{8,0},{12,4},{1,9},{5,13},{9,1},{13,5},{2,10},{6,14},... | collective-permute-start | bytes 786440 | tf_op jit(solution)/shard_map/ppermute | solution.py:29
  5.6 2.6 %collective-permute-start.3 = (bf16[128,1024]{1,0:T(8,128)(2,1)}, bf16[128,1024]{1,0:T(8,128)(2,1)S(1)}, u32[]{:S(2)}, u32[]{:S(2)}) collective-permute-start(bf16[128,1024]{1,0:T(8,128)(2,1)} %get-tuple-element.31), channel_id=1, source_target_pairs={{0,2},{1,3},{2,0},{3,1},{4,6},{5,7},{6,4},{7,5},{8,10},{9,11},{10,... | collective-permute-start | bytes 786440 | tf_op jit(solution)/shard_map/ppermute | solution.py:29
  8.7 1.6 %collective-permute-start = (bf16[256,1024]{1,0:T(8,128)(2,1)}, bf16[256,1024]{1,0:T(8,128)(2,1)S(1)}, u32[]{:S(2)}, u32[]{:S(2)}) collective-permute-start(bf16[256,1024]{1,0:T(8,128)(2,1)} %refs_0_.11), channel_id=1, source_target_pairs={{0,1},{1,0},{2,3},{3,2},{4,5},{5,4},{6,7},{7,6},{8,9},{9,8},{10,11... | collective-permute-start | bytes 1572872 | tf_op jit(solution)/shard_map/ppermute | solution.py:29
  10.6 2.3 %collective-permute-done.6.refs_1_.refs_3_ = bf16[128,1024]{1,0:T(8,128)(2,1)S(1)} collective-permute-done((bf16[128,1024]{1,0:T(8,128)(2,1)}, bf16[128,1024]{1,0:T(8,128)(2,1)S(1)}, u32[]{:S(2)}, u32[]{:S(2)}) %collective-permute-start.6) | collective-permute-done | bytes 262176 | tf_op jit(solution)/shard_map/ppermute | solution.py:29
  12.9 2.1 %collective-permute-start.7 = (bf16[128,1024]{1,0:T(8,128)(2,1)S(1)}, bf16[128,1024]{1,0:T(8,128)(2,1)S(1)}, u32[]{:S(2)}, u32[]{:S(2)}) collective-permute-start(bf16[128,1024]{1,0:T(8,128)(2,1)S(1)} %collective-permute-done.6.refs_1_.refs_3_), channel_id=1, source_target_pairs={{0,16},{16,0},{1,17},{17,1},{2,18},{18,2},{3,19},{19,3},{4,20},{20... | collective-permute-start | bytes 786440 | tf_op jit(solution)/shard_map/ppermute | solution.py:29
  15.0 6.3 %collective-permute-done.3.refs_6_ = bf16[128,1024]{1,0:T(8,128)(2,1)S(1)} collective-permute-done((bf16[128,1024]{1,0:T(8,128)(2,1)}, bf16[128,1024]{1,0:T(8,128)(2,1)S(1)}, u32[]{:S(2)}, u32[]{:S(2)}) %collective-permute-start.3) | collective-permute-done | bytes 262176 | tf_op jit(solution)/shard_map/ppermute | solution.py:29
  21.8 8.9 %collective-permute-done.4.refs_3_.refs_5_ = bf16[128,1024]{1,0:T(8,128)(2,1)S(1)} collective-permute-done((bf16[128,1024]{1,0:T(8,128)(2,1)}, bf16[128,1024]{1,0:T(8,128)(2,1)S(1)}, u32[]{:S(2)}, u32[]{:S(2)}) %collective-permute-start.4) | collective-permute-done | bytes 262176 | tf_op jit(solution)/shard_map/ppermute | solution.py:29
  30.7 1.6 %collective-permute-start.9 = (bf16[128,1024]{1,0:T(8,128)(2,1)S(1)}, bf16[128,1024]{1,0:T(8,128)(2,1)S(1)}, u32[]{:S(2)}, u32[]{:S(2)}) collective-permute-start(bf16[128,1024]{1,0:T(8,128)(2,1)S(1)} %collective-permute-done.3.refs_6_), channel_id=1, source_target_pairs={{0,16},{16,0},{1,17},{17,1},{2,18},{18,2},{3,19},{19,3},{4,20},{20... | collective-permute-start | bytes 786440 | tf_op jit(solution)/shard_map/ppermute | solution.py:29
  33.3 1.6 %collective-permute-start.11 = (bf16[128,1024]{1,0:T(8,128)(2,1)S(1)}, bf16[128,1024]{1,0:T(8,128)(2,1)S(1)}, u32[]{:S(2)}, u32[]{:S(2)}) collective-permute-start(bf16[128,1024]{1,0:T(8,128)(2,1)S(1)} %collective-permute-done.4.refs_3_.refs_5_), channel_id=1, source_target_pairs={{0,16},{16,0},{1,17},{17,1},{2,18},{18,2},{3,19},{19,3},{4,20},{20... | collective-permute-start | bytes 786440 | tf_op jit(solution)/shard_map/ppermute | solution.py:29
  34.9 4.1 %collective-permute-done.9.refs_4_ = bf16[128,1024]{1,0:T(8,128)(2,1)S(1)} collective-permute-done((bf16[128,1024]{1,0:T(8,128)(2,1)S(1)}, bf16[128,1024]{1,0:T(8,128)(2,1)S(1)}, u32[]{:S(2)}, u32[]{:S(2)}) %collective-permute-start.9) | collective-permute-done | bytes 262176 | tf_op jit(solution)/shard_map/ppermute | solution.py:29
  39.1 2.9 %collective-permute-done.12.refs_4_.refs_6_ = bf16[128,1024]{1,0:T(8,128)(2,1)S(1)} collective-permute-done((bf16[128,1024]{1,0:T(8,128)(2,1)S(1)}, bf16[128,1024]{1,0:T(8,128)(2,1)S(1)}, u32[]{:S(2)}, u32[]{:S(2)}) %collective-permute-start.12) | collective-permute-done | bytes 262176 | tf_op jit(solution)/shard_map/ppermute | solution.py:29
  42.5 1.1 %collective-permute-done.11.refs_5_.refs_7_ = bf16[128,1024]{1,0:T(8,128)(2,1)S(1)} collective-permute-done((bf16[128,1024]{1,0:T(8,128)(2,1)S(1)}, bf16[128,1024]{1,0:T(8,128)(2,1)S(1)}, u32[]{:S(2)}, u32[]{:S(2)}) %collective-permute-start.11) | collective-permute-done | bytes 262176 | tf_op jit(solution)/shard_map/ppermute | solution.py:29
  43.6 3.0 %collective-permute-done.10.refs_5_ = bf16[128,1024]{1,0:T(8,128)(2,1)S(1)} collective-permute-done((bf16[128,1024]{1,0:T(8,128)(2,1)S(1)}, bf16[128,1024]{1,0:T(8,128)(2,1)S(1)}, u32[]{:S(2)}, u32[]{:S(2)}) %collective-permute-start.10) | collective-permute-done | bytes 262176 | tf_op jit(solution)/shard_map/ppermute | solution.py:29
  46.6 1.0 copy-done.8
  47.7 0.9 shard_map.89.far
  48.6 2.2 %shard_map.88.near = bf16[1024,768]{1,0:T(8,128)(2,1)S(1)} custom-call(bf16[256,1024]{1,0:T(8,128)(2,1)S(1)} %copy-done.9, bf16[256,1024]{1,0:T(8,128)(2,1)S(1)} %collective-permute-done.refs_1_, bf16[256,1024]{1,0:T(8,128)(2,1)S(1)} %collective-permute-done.1.refs_2_, bf16[256,1024]{1,0:T(8,128)(2,1)S(1)} %collective-permute-done.2.refs_3_, ...), custom_call_target="tpu_custom_call" | custom-call | flops 1610612736 | bytes 5242880 | tf_op jit(solution)/shard_map/pallas_call | solution.py:37
  50.9 1.0 shard_map.90
  51.9 1.8 %shard_map.91 = bf16[256,1024]{1,0:T(8,128)(2,1)} custom-call(bf16[1024,768]{1,0:T(8,128)(2,1)S(1)} %shard_map.88.near, bf16[1024,256]{1,0:T(8,128)(2,1)S(1)} %shard_map.89.far, bf16[256,1024]{1,0:T(8,128)(2,1)S(1)} %copy-done, bf16[128,1024]{1,0:T(8,128)(2,1)S(1)} %collective-permute-done.6.refs_1_.refs_3_, ...), custom_call_target="tpu_custom_call" | custom-call | flops 536870912 | bytes 4718592 | tf_op jit(solution)/shard_map/pallas_call | solution.py:37
  53.8 1.0 shard_map.92
  54.9 0.7 copy-done.14
  55.5 0.7 copy-done.15
  56.6 2.3 %collective-permute-start.16 = (bf16[128,1024]{1,0:T(8,128)(2,1)}, bf16[128,1024]{1,0:T(8,128)(2,1)S(1)}, u32[]{:S(2)}, u32[]{:S(2)}) collective-permute-start(bf16[128,1024]{1,0:T(8,128)(2,1)} %copy-done.15), channel_id=1, source_target_pairs={{0,1},{1,0},{2,3},{3,2},{4,5},{5,4},{6,7},{7,6},{8,9},{9,8},{10,11... | collective-permute-start | bytes 786440 | tf_op jit(solution)/shard_map/ppermute | solution.py:29
  59.0 0.9 copy-done.3
  59.9 0.9 copy-done.5
  60.9 0.9 copy-done.7
  61.8 1.0 copy-done.10
  62.9 2.0 %shard_map.93.own = f32[256,1024]{1,0:T(8,128)S(1)} custom-call(bf16[1024,768]{1,0:T(8,128)(2,1)S(1)} %shard_map.88.near, bf16[1024,256]{1,0:T(8,128)(2,1)S(1)} %shard_map.89.far, bf16[256,1024]{1,0:T(8,128)(2,1)S(1)} %copy-done.10, bf16[256,1024]{1,0:T(8,128)(2,1)} %collective-permute-done.15.refs_1_, bf16[256,1024]{1,0:T(8,128)(2,1)S(1)} %copy-done, ...), custom_call_target="tpu_custom_call" | custom-call | flops 536870912 | bytes 6291456 | tf_op jit(solution)/shard_map/pallas_call | solution.py:37
  64.9 1.3 %collective-permute-done.16.first = bf16[128,1024]{1,0:T(8,128)(2,1)S(1)} collective-permute-done((bf16[128,1024]{1,0:T(8,128)(2,1)}, bf16[128,1024]{1,0:T(8,128)(2,1)S(1)}, u32[]{:S(2)}, u32[]{:S(2)}) %collective-permute-start.16) | collective-permute-done | bytes 262176 | tf_op jit(solution)/shard_map/ppermute | solution.py:29
  66.2 5.1 %collective-permute-done.17.second = bf16[128,1024]{1,0:T(8,128)(2,1)S(1)} collective-permute-done((bf16[128,1024]{1,0:T(8,128)(2,1)}, bf16[128,1024]{1,0:T(8,128)(2,1)S(1)}, u32[]{:S(2)}, u32[]{:S(2)}) %collective-permute-start.17) | collective-permute-done | bytes 262176 | tf_op jit(solution)/shard_map/ppermute | solution.py:29
  71.3 1.2 %shard_map.94 = bf16[32,1024]{1,0:T(8,128)(2,1)S(1)} custom-call(s32[1,256]{1,0:T(1,128)S(1)} %copy-done.13, s32[1,32]{1,0:T(1,128)S(1)} %fusion.1.order, f32[256,1024]{1,0:T(8,128)S(1)} %shard_map.93.own, bf16[128,1024]{1,0:T(8,128)(2,1)S(1)} %collective-permute-done.16.first, bf16[128,1024]{1,0:T(8,128)(2,1)S(1)} %collective-permute-done.17.second), custom_call_target="tpu_custom_call" | custom-call | flops 5242880 | bytes 1639552 | tf_op jit(solution)/shard_map/pallas_call | solution.py:37
  73.2 1.3 %collective-permute-start.20 = (bf16[8,1024]{1,0:T(8,128)(2,1)S(1)}, bf16[8,1024]{1,0:T(8,128)(2,1)S(1)}, u32[]{:S(2)}, u32[]{:S(2)}) collective-permute-start(bf16[8,1024]{1,0:T(8,128)(2,1)S(1)} %get-tuple-element.64), channel_id=1, source_target_pairs={{0,12},{4,8},{8,4},{12,0},{1,13},{5,9},{9,5},{13,1},{2,14},{6,10},... | collective-permute-start | bytes 49160 | tf_op jit(solution)/shard_map/ppermute | solution.py:29
  74.5 2.0 %collective-permute-done.19 = bf16[8,1024]{1,0:T(8,128)(2,1)S(1)} collective-permute-done((bf16[8,1024]{1,0:T(8,128)(2,1)S(1)}, bf16[8,1024]{1,0:T(8,128)(2,1)S(1)}, u32[]{:S(2)}, u32[]{:S(2)}) %collective-permute-start.19) | collective-permute-done | bytes 16416 | tf_op jit(solution)/shard_map/ppermute | solution.py:29
  76.5 1.8 %collective-permute-start.21 = (bf16[32,1024]{1,0:T(8,128)(2,1)S(1)}, bf16[32,1024]{1,0:T(8,128)(2,1)S(1)}, u32[]{:S(2)}, u32[]{:S(2)}) collective-permute-start(bf16[32,1024]{1,0:T(8,128)(2,1)S(1)} %pad_maximum_fusion.refs_0_), channel_id=1, source_target_pairs={{0,1},{1,0},{2,3},{3,2},{4,5},{5,4},{6,7},{7,6},{8,9},{9,8},{10,11... | collective-permute-start | bytes 196616 | tf_op jit(solution)/shard_map/ppermute | solution.py:29
  78.4 1.3 %collective-permute-start.22 = (bf16[32,1024]{1,0:T(8,128)(2,1)S(1)}, bf16[32,1024]{1,0:T(8,128)(2,1)S(1)}, u32[]{:S(2)}, u32[]{:S(2)}) collective-permute-start(bf16[32,1024]{1,0:T(8,128)(2,1)S(1)} %pad_maximum_fusion.refs_0_), channel_id=1, source_target_pairs={{0,2},{1,3},{2,0},{3,1},{4,6},{5,7},{6,4},{7,5},{8,10},{9,11},{10,... | collective-permute-start | bytes 196616 | tf_op jit(solution)/shard_map/ppermute | solution.py:29
  79.7 1.3 %collective-permute-start.23 = (bf16[32,1024]{1,0:T(8,128)(2,1)S(1)}, bf16[32,1024]{1,0:T(8,128)(2,1)S(1)}, u32[]{:S(2)}, u32[]{:S(2)}) collective-permute-start(bf16[32,1024]{1,0:T(8,128)(2,1)S(1)} %pad_maximum_fusion.refs_0_), channel_id=1, source_target_pairs={{0,3},{1,2},{2,1},{3,0},{4,7},{5,6},{6,5},{7,4},{8,11},{9,10},{10,... | collective-permute-start | bytes 196616 | tf_op jit(solution)/shard_map/ppermute | solution.py:29
  81.2 3.4 %copy-done.1 = bf16[4096,1024]{1,0:T(8,128)(2,1)S(1)} copy-done((bf16[4096,1024]{1,0:T(8,128)(2,1)S(1)}, bf16[4096,1024]{1,0:T(8,128)(2,1)}, u32[]{:S(2)}) %copy-start.1) | copy-done | bytes 8388632
  84.6 1.7 %shard_map.86.units = bf16[1024,1024]{1,0:T(8,128)(2,1)S(1)} custom-call(s32[1,16]{1,0:T(1,128)S(1)} %copy-done.12, bf16[4096,1024]{1,0:T(8,128)(2,1)S(1)} %copy-done.1), custom_call_target="tpu_custom_call" | custom-call | flops 8388608 | bytes 10485824 | tf_op jit(solution)/shard_map/pallas_call | solution.py:37
  86.5 1.8 %shard_map.95 = (f32[128,1024]{1,0:T(8,128)S(1)}, f32[16,256]{1,0:T(8,128)S(1)}, f32[128,1]{1,0:T(8,128)S(1)}) custom-call(s32[1,16]{1,0:T(1,128)S(1)} %copy-done.12, s32[1,128]{1,0:T(1,128)S(1)} %xor.40.place, bf16[1024,1024]{1,0:T(8,128)(2,1)S(1)} %shard_map.86.units, bf16[32,1024]{1,0:T(8,128)(2,1)S(1)} %pad_maximum_fusion.refs_0_, ...), custom_call_target="tpu_custom_call" | custom-call | flops 268435456 | bytes 2901056 | tf_op jit(solution)/shard_map/pallas_call | solution.py:37
  88.4 1.2 %collective-permute-done.24 = f32[16,256]{1,0:T(8,128)S(1)} collective-permute-done((f32[16,256]{1,0:T(8,128)S(1)}, f32[16,256]{1,0:T(8,128)S(1)}, u32[]{:S(2)}, u32[]{:S(2)}) %collective-permute-start.24) | collective-permute-done | bytes 16416 | tf_op jit(solution)/shard_map/ppermute | solution.py:29
  89.5 1.3 %collective-permute-start.25 = (f32[16,256]{1,0:T(8,128)S(1)}, f32[16,256]{1,0:T(8,128)S(1)}, u32[]{:S(2)}, u32[]{:S(2)}) collective-permute-start(f32[16,256]{1,0:T(8,128)S(1)} %add.64), channel_id=1, source_target_pairs={{0,8},{4,12},{8,0},{12,4},{1,9},{5,13},{9,1},{13,5},{2,10},{6,14},... | collective-permute-start | bytes 49160 | tf_op jit(solution)/shard_map/ppermute | solution.py:29
  90.9 2.4 %collective-permute-done.25 = f32[16,256]{1,0:T(8,128)S(1)} collective-permute-done((f32[16,256]{1,0:T(8,128)S(1)}, f32[16,256]{1,0:T(8,128)S(1)}, u32[]{:S(2)}, u32[]{:S(2)}) %collective-permute-start.25) | collective-permute-done | bytes 16416 | tf_op jit(solution)/shard_map/ppermute | solution.py:29
  93.3 1.1 %shard_map.96 = (f32[32,1152]{1,0:T(8,128)S(1)}, bf16[96,1152]{1,0:T(8,128)(2,1)S(1)}) custom-call(s32[1,16]{1,0:T(1,128)S(1)} %copy-done.12, f32[128,1024]{1,0:T(8,128)S(1)} %get-tuple-element.53.expo, f32[16,256]{1,0:T(8,128)S(1)} %add.65.columns, f32[128,1]{1,0:T(8,128)S(1)} %get-tuple-element.55.row_total, bf16[1024,1024]{1,0:T(8,128)(2,1)S(1)} %shard_map.86.units), custom_call_target="tpu_custom_call" | custom-call | flops 268435456 | bytes 3007040 | tf_op jit(solution)/shard_map/pallas_call | solution.py:37
  94.4 2.3 %collective-permute-start.26 = (bf16[32,1152]{1,0:T(8,128)(2,1)S(1)}, bf16[32,1152]{1,0:T(8,128)(2,1)S(1)}, u32[]{:S(2)}, u32[]{:S(2)}) collective-permute-start(bf16[32,1152]{1,0:T(8,128)(2,1)S(1)} %get-tuple-element.62), channel_id=1, source_target_pairs={{0,3},{1,2},{2,1},{3,0},{4,7},{5,6},{6,5},{7,4},{8,11},{9,10},{10,... | collective-permute-start | bytes 221192 | tf_op jit(solution)/shard_map/ppermute | solution.py:29
  97.3 1.6 %collective-permute-start.28 = (bf16[32,1152]{1,0:T(8,128)(2,1)S(1)}, bf16[32,1152]{1,0:T(8,128)(2,1)S(1)}, u32[]{:S(2)}, u32[]{:S(2)}) collective-permute-start(bf16[32,1152]{1,0:T(8,128)(2,1)S(1)} %get-tuple-element.60), channel_id=1, source_target_pairs={{0,1},{1,0},{2,3},{3,2},{4,5},{5,4},{6,7},{7,6},{8,9},{9,8},{10,11... | collective-permute-start | bytes 221192 | tf_op jit(solution)/shard_map/ppermute | solution.py:29
  98.9 2.3 %collective-permute-done.26.refs_0_ = bf16[32,1152]{1,0:T(8,128)(2,1)S(1)} collective-permute-done((bf16[32,1152]{1,0:T(8,128)(2,1)S(1)}, bf16[32,1152]{1,0:T(8,128)(2,1)S(1)}, u32[]{:S(2)}, u32[]{:S(2)}) %collective-permute-start.26) | collective-permute-done | bytes 73760 | tf_op jit(solution)/shard_map/ppermute | solution.py:29
  101.2 2.4 %collective-permute-done.27.refs_1_ = bf16[32,1152]{1,0:T(8,128)(2,1)S(1)} collective-permute-done((bf16[32,1152]{1,0:T(8,128)(2,1)S(1)}, bf16[32,1152]{1,0:T(8,128)(2,1)S(1)}, u32[]{:S(2)}, u32[]{:S(2)}) %collective-permute-start.27) | collective-permute-done | bytes 73760 | tf_op jit(solution)/shard_map/ppermute | solution.py:29
  103.6 0.8 shard_map.97
  (66 shorter events, 5.5 us)
Async XLA Ops:
  0.6 47.9 %copy-start.11 = (bf16[256,1024]{1,0:T(8,128)(2,1)S(1)}, bf16[256,1024]{1,0:T(8,128)(2,1)}, u32[]{:S(2)}) copy-start(bf16[256,1024]{1,0:T(8,128)(2,1)} %refs_4_.1) | copy-start | bytes 1572868
  0.6 47.9 %copy-start.9 = (bf16[256,1024]{1,0:T(8,128)(2,1)S(1)}, bf16[256,1024]{1,0:T(8,128)(2,1)}, u32[]{:S(2)}) copy-start(bf16[256,1024]{1,0:T(8,128)(2,1)} %refs_0_.11) | copy-start | bytes 1572868
  2.6 10.3 %collective-permute-start.6 = (bf16[128,1024]{1,0:T(8,128)(2,1)}, bf16[128,1024]{1,0:T(8,128)(2,1)S(1)}, u32[]{:S(2)}, u32[]{:S(2)}) collective-permute-start(bf16[128,1024]{1,0:T(8,128)(2,1)} %get-tuple-element.33), channel_id=1, source_target_pairs={{0,8},{4,12},{8,0},{12,4},{1,9},{5,13},{9,1},{13,5},{2,10},{6,14},... | collective-permute-start | bytes 786440 | tf_op jit(solution)/shard_map/ppermute | solution.py:29
  5.6 15.8 %collective-permute-start.3 = (bf16[128,1024]{1,0:T(8,128)(2,1)}, bf16[128,1024]{1,0:T(8,128)(2,1)S(1)}, u32[]{:S(2)}, u32[]{:S(2)}) collective-permute-start(bf16[128,1024]{1,0:T(8,128)(2,1)} %get-tuple-element.31), channel_id=1, source_target_pairs={{0,2},{1,3},{2,0},{3,1},{4,6},{5,7},{6,4},{7,5},{8,10},{9,11},{10,... | collective-permute-start | bytes 786440 | tf_op jit(solution)/shard_map/ppermute | solution.py:29
  8.2 22.5 %collective-permute-start.8 = (bf16[256,1024]{1,0:T(8,128)(2,1)}, bf16[256,1024]{1,0:T(8,128)(2,1)S(1)}, u32[]{:S(2)}, u32[]{:S(2)}) collective-permute-start(bf16[256,1024]{1,0:T(8,128)(2,1)} %refs_4_.1), channel_id=1, source_target_pairs={{0,8},{4,12},{8,0},{12,4},{1,9},{5,13},{9,1},{13,5},{2,10},{6,14},... | collective-permute-start | bytes 1572872 | tf_op jit(solution)/shard_map/ppermute | solution.py:29
  8.7 23.6 %collective-permute-start = (bf16[256,1024]{1,0:T(8,128)(2,1)}, bf16[256,1024]{1,0:T(8,128)(2,1)S(1)}, u32[]{:S(2)}, u32[]{:S(2)}) collective-permute-start(bf16[256,1024]{1,0:T(8,128)(2,1)} %refs_0_.11), channel_id=1, source_target_pairs={{0,1},{1,0},{2,3},{3,2},{4,5},{5,4},{6,7},{7,6},{8,9},{9,8},{10,11... | collective-permute-start | bytes 1572872 | tf_op jit(solution)/shard_map/ppermute | solution.py:29
  10.3 20.4 %collective-permute-start.4 = (bf16[128,1024]{1,0:T(8,128)(2,1)}, bf16[128,1024]{1,0:T(8,128)(2,1)S(1)}, u32[]{:S(2)}, u32[]{:S(2)}) collective-permute-start(bf16[128,1024]{1,0:T(8,128)(2,1)} %get-tuple-element.33), channel_id=1, source_target_pairs={{0,2},{1,3},{2,0},{3,1},{4,6},{5,7},{6,4},{7,5},{8,10},{9,11},{10,... | collective-permute-start | bytes 786440 | tf_op jit(solution)/shard_map/ppermute | solution.py:29
  12.9 17.7 %collective-permute-start.7 = (bf16[128,1024]{1,0:T(8,128)(2,1)S(1)}, bf16[128,1024]{1,0:T(8,128)(2,1)S(1)}, u32[]{:S(2)}, u32[]{:S(2)}) collective-permute-start(bf16[128,1024]{1,0:T(8,128)(2,1)S(1)} %collective-permute-done.6.refs_1_.refs_3_), channel_id=1, source_target_pairs={{0,16},{16,0},{1,17},{17,1},{2,18},{18,2},{3,19},{19,3},{4,20},{20... | collective-permute-start | bytes 786440 | tf_op jit(solution)/shard_map/ppermute | solution.py:29
  21.4 9.3 %collective-permute-start.5 = (bf16[128,1024]{1,0:T(8,128)(2,1)S(1)}, bf16[128,1024]{1,0:T(8,128)(2,1)S(1)}, u32[]{:S(2)}, u32[]{:S(2)}) collective-permute-start(bf16[128,1024]{1,0:T(8,128)(2,1)S(1)} %collective-permute-done.3.refs_6_), channel_id=1, source_target_pairs={{0,8},{4,12},{8,0},{12,4},{1,9},{5,13},{9,1},{13,5},{2,10},{6,14},... | collective-permute-start | bytes 786440 | tf_op jit(solution)/shard_map/ppermute | solution.py:29
  30.7 8.3 %collective-permute-start.9 = (bf16[128,1024]{1,0:T(8,128)(2,1)S(1)}, bf16[128,1024]{1,0:T(8,128)(2,1)S(1)}, u32[]{:S(2)}, u32[]{:S(2)}) collective-permute-start(bf16[128,1024]{1,0:T(8,128)(2,1)S(1)} %collective-permute-done.3.refs_6_), channel_id=1, source_target_pairs={{0,16},{16,0},{1,17},{17,1},{2,18},{18,2},{3,19},{19,3},{4,20},{20... | collective-permute-start | bytes 786440 | tf_op jit(solution)/shard_map/ppermute | solution.py:29
  32.3 14.3 %collective-permute-start.1 = (bf16[256,1024]{1,0:T(8,128)(2,1)}, bf16[256,1024]{1,0:T(8,128)(2,1)S(1)}, u32[]{:S(2)}, u32[]{:S(2)}) collective-permute-start(bf16[256,1024]{1,0:T(8,128)(2,1)} %refs_0_.11), channel_id=1, source_target_pairs={{0,4},{4,0},{8,12},{12,8},{1,5},{5,1},{9,13},{13,9},{2,6},{6,2},{1... | collective-permute-start | bytes 1572872 | tf_op jit(solution)/shard_map/ppermute | solution.py:29
  32.3 14.3 %collective-permute-start.2 = (bf16[256,1024]{1,0:T(8,128)(2,1)S(1)}, bf16[256,1024]{1,0:T(8,128)(2,1)S(1)}, u32[]{:S(2)}, u32[]{:S(2)}) collective-permute-start(bf16[256,1024]{1,0:T(8,128)(2,1)S(1)} %collective-permute-done.refs_1_), channel_id=1, source_target_pairs={{0,4},{4,0},{8,12},{12,8},{1,5},{5,1},{9,13},{13,9},{2,6},{6,2},{1... | collective-permute-start | bytes 1572872 | tf_op jit(solution)/shard_map/ppermute | solution.py:29
  32.8 9.2 %collective-permute-start.12 = (bf16[128,1024]{1,0:T(8,128)(2,1)S(1)}, bf16[128,1024]{1,0:T(8,128)(2,1)S(1)}, u32[]{:S(2)}, u32[]{:S(2)}) collective-permute-start(bf16[128,1024]{1,0:T(8,128)(2,1)S(1)} %collective-permute-done.4.refs_3_.refs_5_), channel_id=1, source_target_pairs={{0,8},{4,12},{8,0},{12,4},{1,9},{5,13},{9,1},{13,5},{2,10},{6,14},... | collective-permute-start | bytes 786440 | tf_op jit(solution)/shard_map/ppermute | solution.py:29
  33.3 10.3 %collective-permute-start.11 = (bf16[128,1024]{1,0:T(8,128)(2,1)S(1)}, bf16[128,1024]{1,0:T(8,128)(2,1)S(1)}, u32[]{:S(2)}, u32[]{:S(2)}) collective-permute-start(bf16[128,1024]{1,0:T(8,128)(2,1)S(1)} %collective-permute-done.4.refs_3_.refs_5_), channel_id=1, source_target_pairs={{0,16},{16,0},{1,17},{17,1},{2,18},{18,2},{3,19},{19,3},{4,20},{20... | collective-permute-start | bytes 786440 | tf_op jit(solution)/shard_map/ppermute | solution.py:29
  39.0 7.6 %collective-permute-start.10 = (bf16[128,1024]{1,0:T(8,128)(2,1)S(1)}, bf16[128,1024]{1,0:T(8,128)(2,1)S(1)}, u32[]{:S(2)}, u32[]{:S(2)}) collective-permute-start(bf16[128,1024]{1,0:T(8,128)(2,1)S(1)} %collective-permute-done.9.refs_4_), channel_id=1, source_target_pairs={{0,8},{4,12},{8,0},{12,4},{1,9},{5,13},{9,1},{13,5},{2,10},{6,14},... | collective-permute-start | bytes 786440 | tf_op jit(solution)/shard_map/ppermute | solution.py:29
  42.0 11.9 %copy-start.2 = (bf16[128,1024]{1,0:T(8,128)(2,1)}, bf16[128,1024]{1,0:T(8,128)(2,1)S(1)}, u32[]{:S(2)}) copy-start(bf16[128,1024]{1,0:T(8,128)(2,1)S(1)} %collective-permute-done.12.refs_4_.refs_6_) | copy-start | bytes 786436
  42.0 8.9 %collective-permute-start.13 = (bf16[128,1024]{1,0:T(8,128)(2,1)S(1)}, bf16[128,1024]{1,0:T(8,128)(2,1)S(1)}, u32[]{:S(2)}, u32[]{:S(2)}) collective-permute-start(bf16[128,1024]{1,0:T(8,128)(2,1)S(1)} %collective-permute-done.12.refs_4_.refs_6_), channel_id=1, source_target_pairs={{0,16},{16,0},{1,17},{17,1},{2,18},{18,2},{3,19},{19,3},{4,20},{20... | collective-permute-start | bytes 786440 | tf_op jit(solution)/shard_map/ppermute | solution.py:29
  43.6 10.2 %copy-start.4 = (bf16[128,1024]{1,0:T(8,128)(2,1)}, bf16[128,1024]{1,0:T(8,128)(2,1)S(1)}, u32[]{:S(2)}) copy-start(bf16[128,1024]{1,0:T(8,128)(2,1)S(1)} %collective-permute-done.11.refs_5_.refs_7_) | copy-start | bytes 786436
  46.6 1.0 %copy-start.8 = (bf16[256,1024]{1,0:T(8,128)(2,1)S(1)}, bf16[256,1024]{1,0:T(8,128)(2,1)}, u32[]{:S(2)}) copy-start(bf16[256,1024]{1,0:T(8,128)(2,1)} %refs_0_.11) | copy-start | bytes 1572868
  48.6 2.3 %copy-start = (bf16[256,1024]{1,0:T(8,128)(2,1)S(1)}, bf16[256,1024]{1,0:T(8,128)(2,1)}, u32[]{:S(2)}) copy-start(bf16[256,1024]{1,0:T(8,128)(2,1)} %refs_2_.1) | copy-start | bytes 1572868
  50.9 3.0 %copy-start.6 = (bf16[128,1024]{1,0:T(8,128)(2,1)}, bf16[128,1024]{1,0:T(8,128)(2,1)S(1)}, u32[]{:S(2)}) copy-start(bf16[128,1024]{1,0:T(8,128)(2,1)S(1)} %collective-permute-done.13.refs_6_.refs_8_) | copy-start | bytes 786436
  51.8 2.0 %collective-permute-start.14 = (bf16[256,1024]{1,0:T(8,128)(2,1)S(1)}, bf16[256,1024]{1,0:T(8,128)(2,1)S(1)}, u32[]{:S(2)}, u32[]{:S(2)}) collective-permute-start(bf16[256,1024]{1,0:T(8,128)(2,1)S(1)} %shard_map.90), channel_id=1, source_target_pairs={{0,4},{4,0},{8,12},{12,8},{1,5},{5,1},{9,13},{13,9},{2,6},{6,2},{1... | collective-permute-start | bytes 1572872 | tf_op jit(solution)/shard_map/ppermute | solution.py:29
  53.7 5.2 %copy-start.16 = (s32[32]{0:T(128)S(1)}, s32[32]{0:T(128)}, u32[]{:S(2)}) copy-start(s32[32]{0:T(128)} %param.11) | copy-start | bytes 388
  54.8 0.7 copy-start.14
  55.5 0.7 copy-start.15
  56.2 2.7 %collective-permute-start.15 = (bf16[256,1024]{1,0:T(8,128)(2,1)}, bf16[256,1024]{1,0:T(8,128)(2,1)}, u32[]{:S(2)}, u32[]{:S(2)}) collective-permute-start(bf16[256,1024]{1,0:T(8,128)(2,1)} %shard_map.91), channel_id=1, source_target_pairs={{0,4},{4,0},{8,12},{12,8},{1,5},{5,1},{9,13},{13,9},{2,6},{6,2},{1... | collective-permute-start | bytes 1572872 | tf_op jit(solution)/shard_map/ppermute | solution.py:29
  56.6 9.6 %collective-permute-start.16 = (bf16[128,1024]{1,0:T(8,128)(2,1)}, bf16[128,1024]{1,0:T(8,128)(2,1)S(1)}, u32[]{:S(2)}, u32[]{:S(2)}) collective-permute-start(bf16[128,1024]{1,0:T(8,128)(2,1)} %copy-done.15), channel_id=1, source_target_pairs={{0,1},{1,0},{2,3},{3,2},{4,5},{5,4},{6,7},{7,6},{8,9},{9,8},{10,11... | collective-permute-start | bytes 786440 | tf_op jit(solution)/shard_map/ppermute | solution.py:29
  58.9 12.4 %collective-permute-start.17 = (bf16[128,1024]{1,0:T(8,128)(2,1)}, bf16[128,1024]{1,0:T(8,128)(2,1)S(1)}, u32[]{:S(2)}, u32[]{:S(2)}) collective-permute-start(bf16[128,1024]{1,0:T(8,128)(2,1)} %copy-done.14), channel_id=1, source_target_pairs={{0,1},{1,0},{2,3},{3,2},{4,5},{5,4},{6,7},{7,6},{8,9},{9,8},{10,11... | collective-permute-start | bytes 786440 | tf_op jit(solution)/shard_map/ppermute | solution.py:29
  59.0 1.0 copy-start.3
  59.9 0.9 copy-start.5
  60.9 0.9 copy-start.7
  61.8 1.0 copy-start.10
  62.8 8.5 %copy-start.13 = (s32[1,256]{1,0:T(1,128)S(1)}, s32[1,256]{1,0:T(1,128)}, u32[]{:S(2)}) copy-start(s32[1,256]{1,0:T(1,128)} %identity.1) | copy-start | bytes 3076
  62.9 18.3 %copy-start.12 = (s32[1,16]{1,0:T(1,128)S(1)}, s32[1,16]{1,0:T(1,128)}, u32[]{:S(2)}) copy-start(s32[1,16]{1,0:T(1,128)} %listed.5) | copy-start | bytes 196
  72.5 2.0 %collective-permute-start.18 = (bf16[8,1024]{1,0:T(8,128)(2,1)S(1)}, bf16[8,1024]{1,0:T(8,128)(2,1)S(1)}, u32[]{:S(2)}, u32[]{:S(2)}) collective-permute-start(bf16[8,1024]{1,0:T(8,128)(2,1)S(1)} %get-tuple-element.66), channel_id=1, source_target_pairs={{0,4},{4,0},{8,12},{12,8},{1,5},{5,1},{9,13},{13,9},{2,6},{6,2},{1... | collective-permute-start | bytes 49160 | tf_op jit(solution)/shard_map/ppermute | solution.py:29
  72.6 3.9 %collective-permute-start.19 = (bf16[8,1024]{1,0:T(8,128)(2,1)S(1)}, bf16[8,1024]{1,0:T(8,128)(2,1)S(1)}, u32[]{:S(2)}, u32[]{:S(2)}) collective-permute-start(bf16[8,1024]{1,0:T(8,128)(2,1)S(1)} %get-tuple-element.65), channel_id=1, source_target_pairs={{0,8},{4,12},{8,0},{12,4},{1,9},{5,13},{9,1},{13,5},{2,10},{6,14},... | collective-permute-start | bytes 49160 | tf_op jit(solution)/shard_map/ppermute | solution.py:29
  73.2 3.3 %collective-permute-start.20 = (bf16[8,1024]{1,0:T(8,128)(2,1)S(1)}, bf16[8,1024]{1,0:T(8,128)(2,1)S(1)}, u32[]{:S(2)}, u32[]{:S(2)}) collective-permute-start(bf16[8,1024]{1,0:T(8,128)(2,1)S(1)} %get-tuple-element.64), channel_id=1, source_target_pairs={{0,12},{4,8},{8,4},{12,0},{1,13},{5,9},{9,5},{13,1},{2,14},{6,10},... | collective-permute-start | bytes 49160 | tf_op jit(solution)/shard_map/ppermute | solution.py:29
  76.5 9.7 %collective-permute-start.21 = (bf16[32,1024]{1,0:T(8,128)(2,1)S(1)}, bf16[32,1024]{1,0:T(8,128)(2,1)S(1)}, u32[]{:S(2)}, u32[]{:S(2)}) collective-permute-start(bf16[32,1024]{1,0:T(8,128)(2,1)S(1)} %pad_maximum_fusion.refs_0_), channel_id=1, source_target_pairs={{0,1},{1,0},{2,3},{3,2},{4,5},{5,4},{6,7},{7,6},{8,9},{9,8},{10,11... | collective-permute-start | bytes 196616 | tf_op jit(solution)/shard_map/ppermute | solution.py:29
  78.4 8.2 %collective-permute-start.22 = (bf16[32,1024]{1,0:T(8,128)(2,1)S(1)}, bf16[32,1024]{1,0:T(8,128)(2,1)S(1)}, u32[]{:S(2)}, u32[]{:S(2)}) collective-permute-start(bf16[32,1024]{1,0:T(8,128)(2,1)S(1)} %pad_maximum_fusion.refs_0_), channel_id=1, source_target_pairs={{0,2},{1,3},{2,0},{3,1},{4,6},{5,7},{6,4},{7,5},{8,10},{9,11},{10,... | collective-permute-start | bytes 196616 | tf_op jit(solution)/shard_map/ppermute | solution.py:29
  79.7 6.8 %collective-permute-start.23 = (bf16[32,1024]{1,0:T(8,128)(2,1)S(1)}, bf16[32,1024]{1,0:T(8,128)(2,1)S(1)}, u32[]{:S(2)}, u32[]{:S(2)}) collective-permute-start(bf16[32,1024]{1,0:T(8,128)(2,1)S(1)} %pad_maximum_fusion.refs_0_), channel_id=1, source_target_pairs={{0,3},{1,2},{2,1},{3,0},{4,7},{5,6},{6,5},{7,4},{8,11},{9,10},{10,... | collective-permute-start | bytes 196616 | tf_op jit(solution)/shard_map/ppermute | solution.py:29
  81.2 3.4 %copy-start.1 = (bf16[4096,1024]{1,0:T(8,128)(2,1)S(1)}, bf16[4096,1024]{1,0:T(8,128)(2,1)}, u32[]{:S(2)}) copy-start(bf16[4096,1024]{1,0:T(8,128)(2,1)} %targets.1) | copy-start | bytes 25165828
  88.3 1.2 %collective-permute-start.24 = (f32[16,256]{1,0:T(8,128)S(1)}, f32[16,256]{1,0:T(8,128)S(1)}, u32[]{:S(2)}, u32[]{:S(2)}) collective-permute-start(f32[16,256]{1,0:T(8,128)S(1)} %get-tuple-element.54), channel_id=1, source_target_pairs={{0,4},{4,0},{8,12},{12,8},{1,5},{5,1},{9,13},{13,9},{2,6},{6,2},{1... | collective-permute-start | bytes 49160 | tf_op jit(solution)/shard_map/ppermute | solution.py:29
  89.5 3.7 %collective-permute-start.25 = (f32[16,256]{1,0:T(8,128)S(1)}, f32[16,256]{1,0:T(8,128)S(1)}, u32[]{:S(2)}, u32[]{:S(2)}) collective-permute-start(f32[16,256]{1,0:T(8,128)S(1)} %add.64), channel_id=1, source_target_pairs={{0,8},{4,12},{8,0},{12,4},{1,9},{5,13},{9,1},{13,5},{2,10},{6,14},... | collective-permute-start | bytes 49160 | tf_op jit(solution)/shard_map/ppermute | solution.py:29
  94.4 6.7 %collective-permute-start.26 = (bf16[32,1152]{1,0:T(8,128)(2,1)S(1)}, bf16[32,1152]{1,0:T(8,128)(2,1)S(1)}, u32[]{:S(2)}, u32[]{:S(2)}) collective-permute-start(bf16[32,1152]{1,0:T(8,128)(2,1)S(1)} %get-tuple-element.62), channel_id=1, source_target_pairs={{0,3},{1,2},{2,1},{3,0},{4,7},{5,6},{6,5},{7,4},{8,11},{9,10},{10,... | collective-permute-start | bytes 221192 | tf_op jit(solution)/shard_map/ppermute | solution.py:29
  96.8 6.8 %collective-permute-start.27 = (bf16[32,1152]{1,0:T(8,128)(2,1)S(1)}, bf16[32,1152]{1,0:T(8,128)(2,1)S(1)}, u32[]{:S(2)}, u32[]{:S(2)}) collective-permute-start(bf16[32,1152]{1,0:T(8,128)(2,1)S(1)} %get-tuple-element.61), channel_id=1, source_target_pairs={{0,2},{1,3},{2,0},{3,1},{4,6},{5,7},{6,4},{7,5},{8,10},{9,11},{10,... | collective-permute-start | bytes 221192 | tf_op jit(solution)/shard_map/ppermute | solution.py:29
  97.3 6.3 %collective-permute-start.28 = (bf16[32,1152]{1,0:T(8,128)(2,1)S(1)}, bf16[32,1152]{1,0:T(8,128)(2,1)S(1)}, u32[]{:S(2)}, u32[]{:S(2)}) collective-permute-start(bf16[32,1152]{1,0:T(8,128)(2,1)S(1)} %get-tuple-element.60), channel_id=1, source_target_pairs={{0,1},{1,0},{2,3},{3,2},{4,5},{5,4},{6,7},{7,6},{8,9},{9,8},{10,11... | collective-permute-start | bytes 221192 | tf_op jit(solution)/shard_map/ppermute | solution.py:29
